TPU v7x, 32 devices: a whole 2x2x4 slice. The times are simulated.
32 devices in a mesh: pipe: 4 (over y, core), section: 2 (over x), tp: 4 (over z).
Axes of the slice: x: 2, y: 2, z: 4, core: 2. Of those that a mesh axis runs over, the one named last changes fastest.
Arguments:
- weights: bfloat16 [4, 2, 2, 4096, 512], P('pipe', 'section', None, 'tp'), may hold values from -6 to 6
- first_moment: float32 [4, 2, 2, 4096, 512], P('pipe', 'section', None, 'tp'), may hold values from -4 to 4
- second_moment: float32 [4, 2, 2, 4096, 512], P('pipe', 'section', None, 'tp'), may hold values from 0.1 to 2
- gradients: bfloat16 [4, 2, 2, 4096, 512], P('pipe', 'section', None, 'tp'), may hold values from -6 to 6
- old_section: int32 [4, 3], replicated, may hold values from 0 to 1, as said below
- new_section: int32 [3], replicated, may hold values from 0 to 1, as said below
- lost_pipe: int32 [4], replicated, may hold values from 0 to 3, each once
- donor_offset: int32 [3], replicated, may hold values from 1 to 3
Outputs:
- new_weights: bfloat16 [4, 2, 2, 4096, 512], P('pipe', 'section', None, 'tp')
- new_first: float32 [4, 2, 2, 4096, 512], P('pipe', 'section', None, 'tp')
- new_second: float32 [4, 2, 2, 4096, 512], P('pipe', 'section', None, 'tp')
Inputs may be any that keep to these rules, and one draw needn't show every extreme that they name: `old_section`: each row places layers in section order (a layer's section never falls with the layer); 1 section of each row hold exactly 2 layers and the others one each. `new_section`: layers in any order; no section holds more than 2 layers, and some section holds exactly 2.
All inputs are finite; a program needn't handle non-finite values.
Results may differ from a plain program's by a relative error of at most 0.0075.
Values may be sent and summed in bfloat16 or wider, within the bound.
No kernel may reach another device: no remote copies, remote signals or barrier semaphores. Data moves between devices by JAX's collectives and lax.ppermute only.
A program may use at most 64 MiB of HBM per device.

v0:
```python
import math

import jax
import jax.numpy as jnp
from jax import lax
from jax.experimental import pallas as pl
from jax.experimental.pallas import tpu as pltpu
from jax.sharding import PartitionSpec as P

LEARN_RATE = 0.01
BETA_ONE = 0.9
BETA_TWO = 0.95
EPSILON = 1e-08
DECAY_RATE = 0.1

CORES = 2
CHUNKS = 4
VMEM = 24 * 1024 * 1024
AXES = ("pipe", "section")


def both(*terms):
    out = terms[0]
    for term in terms[1:]:
        out = jnp.logical_and(out, term)
    return out


def as_int(flag):
    return jnp.where(flag, 1, 0).astype(jnp.int32)


def total(terms):
    out = jnp.int32(0)
    for term in terms:
        out = out + term
    return out


class Sizes:
    def __init__(self, weights, new_section):
        self.pipes = lax.axis_size("pipe")
        self.sections = lax.axis_size("section")
        self.groups = self.pipes // CORES
        self.slots = weights.shape[2]
        self.rows = weights.shape[3]
        self.cols = weights.shape[4]
        self.layers = new_section.shape[0]
        self.half = self.rows // CORES
        self.band = self.half // self.sections
        self.chunks = max(1, min(CHUNKS, self.band // 32))
        self.sub = self.band // self.chunks
        doubles = self.layers - self.sections
        widest = 0
        for at in range(self.sections):
            low = at + max(0, doubles - (self.sections - at))
            high = min(self.layers - self.sections + at, at + min(at, doubles) + 1)
            widest = max(widest, high - low + 1)
        self.channels = min(widest, CORES * self.slots)

    def send(self, value, target, group=None):
        pairs = []
        for pipe in range(self.pipes):
            if group is not None and pipe // CORES != group:
                continue
            for section in range(self.sections):
                group_to, core, to = target(pipe // CORES, pipe % CORES, section)
                pipe_to = group_to * CORES + core
                pairs.append((pipe * self.sections + section, pipe_to * self.sections + to))
        return lax.ppermute(value, AXES, pairs)

    def to_core(self, value, group=None):
        return self.send(value, lambda g, c, s: (g, 1 - c, s), group)

    def to_group(self, value, shift, group=None):
        return self.send(value, lambda g, c, s: ((g + shift) % self.groups, c, s), group)

    def to_section(self, value, shift, group=None):
        return self.send(value, lambda g, c, s: (g, c, (s + shift) % self.sections), group)


def plan_tables(z, pipe, section, old, new, lost_pipe, offset):
    layers = range(z.layers)
    lost = lost_pipe(0)
    group, core = pipe // CORES, pipe % CORES
    sibling = group * CORES + (1 - core)
    lost_group = lost // CORES
    tables = {}

    def now_of(at):
        return [jnp.where(at == lost, new(l), old(at, l)) for l in layers]

    def slots_of(sections):
        return [total(as_int(sections[k] == sections[l]) for k in range(l)) for l in layers]

    def layer_at(sections, slots, at, slot):
        hits = [both(sections[l] == at, slots[l] == slot) for l in layers]
        index = total(jnp.where(hits[l], l, 0) for l in layers)
        return index, total(as_int(hit) for hit in hits)

    def lookup(values, index):
        out = values[0]
        for l in layers[1:]:
            out = jnp.where(index == l, values[l], out)
        return out

    my_now = now_of(pipe)
    my_slot = slots_of(my_now)
    sib_now = now_of(sibling)
    sib_slot = slots_of(sib_now)
    new_list = [new(l) for l in layers]
    new_slot = slots_of(new_list)

    donor = [lost_pipe(offset(l)) for l in layers]
    source_section = [old(donor[l], l) for l in layers]
    source_slot = [
        total(as_int(old(donor[l], k) == source_section[l]) for k in range(l)) for l in layers
    ]
    source_group = [donor[l] // CORES for l in layers]
    crosses = [as_int(source_group[l] != lost_group) for l in layers]
    rank = [total(crosses[k] for k in range(l)) for l in layers]
    channel = [
        total(
            as_int(both(source_group[k] == source_group[l], source_section[k] == source_section[l]))
            for k in range(l)
        )
        for l in layers
    ]
    tables["branch"] = [[(lost_group, total(crosses))]]

    for first, parts, me in (("group", z.groups, group), ("section", z.sections, section)):

        def grad_unit(l, band):
            return [
                (as_int(my_now[l] == section), my_slot[l] * parts + band),
                (as_int(sib_now[l] == section), sib_slot[l] * parts + band),
            ]

        for shift in range(1, parts):
            band = lax.rem(me + shift, parts)
            tables["grad_out", first, shift] = [grad_unit(l, band) for l in layers]
        tables["grad_sum", first] = [
            grad_unit(l, me) + [(1, l)] * (parts - 1) for l in layers
        ]
        other = z.sections if first == "group" else z.groups
        tables["grad_mean", first] = [[(1, l)] * other for l in layers]
        for name, sections, slots in (("mine", my_now, my_slot), ("sibling", sib_now, sib_slot)):
            units = []
            for slot in range(z.slots):
                index, found = layer_at(sections, slots, section, slot)
                for band in range(parts):
                    unit = []
                    for shift in range(parts):
                        sender = lax.rem(me + parts - shift, parts)
                        unit.append((found * as_int(sender == band), index))
                    units.append(unit)
            tables[name, first] = units

    here = [as_int(source_group[l] == group) for l in layers]
    my_chip = [here[l] * as_int(source_section[l] == section) for l in layers]
    from_me = [as_int(donor[l] == pipe) for l in layers]

    for shift in range(1, z.sections):
        band = lax.rem(section + shift, z.sections)
        units = []
        for k in range(z.channels):
            hit = [my_chip[l] * as_int(channel[l] == k) for l in layers]
            slot = total(hit[l] * source_slot[l] for l in layers)
            mine = total(hit[l] * from_me[l] for l in layers)
            found = total(hit)
            index = slot * z.sections + band
            units.append([(mine, index), (found - mine, index)])
        tables["spread", shift] = units

    def held(l_my_chip, l_from_me, l_slot, l_here, l_channel, l_section):
        index = l_slot * z.sections + section
        unit = [(l_my_chip * l_from_me, index), (l_my_chip * (1 - l_from_me), index)]
        for shift in range(1, z.sections):
            sender = lax.rem(section + z.sections - shift, z.sections)
            unit.append((l_here * as_int(l_section == sender), l_channel))
        return unit

    def held_at(index):
        return held(
            *(
                lookup(values, index)
                for values in (my_chip, from_me, source_slot, here, channel, source_section)
            )
        )

    units = []
    for u in range(z.layers):
        hit = [crosses[l] * as_int(rank[l] == u) for l in layers]
        index = total(hit[l] * l for l in layers)
        found = total(hit)
        units.append([(flag * found, at) for flag, at in held_at(index)])
    tables["across"] = units

    def arrived(index, found):
        found = found * as_int(group == lost_group)
        unit = [(flag * found, at) for flag, at in held_at(index)]
        from_group = lookup(source_group, index)
        for shift in range(1, z.groups):
            sender = lax.rem(group + z.groups - shift, z.groups)
            unit.append((found * as_int(from_group == sender), lookup(rank, index)))
        return unit

    for shift in range(1, z.sections):
        target = lax.rem(section + shift, z.sections)
        tables["deliver", shift] = [
            arrived(*layer_at(new_list, new_slot, target, slot)) for slot in range(z.slots)
        ]
    units = []
    for slot in range(z.slots):
        own = arrived(*layer_at(new_list, new_slot, section, slot))
        for band in range(z.sections):
            mine = as_int(section == band)
            unit = [(flag * mine, at) for flag, at in own]
            for shift in range(1, z.sections):
                sender = lax.rem(section + z.sections - shift, z.sections)
                unit.append((as_int(both(sender == band, group == lost_group)), slot))
            units.append(unit)
    tables["collect"] = units

    last = [as_int(pipe == lost), core]
    for slot in range(z.slots):
        last.append(layer_at(my_now, my_slot, section, slot)[1])
    tables["update"] = [[tuple(last)]]
    return tables


def table_size(z):
    sources = z.sections + z.groups + z.sections + 2
    units = (z.sections + z.groups) * (4 * z.layers + 4 * z.slots)
    units += z.sections * (z.channels + 2 * z.slots) + z.layers
    return -(-(2 * units * sources + z.slots + 8) // 1024) * 1024


def make_plan(z, place, old_section, new_section, lost_pipe, donor_offset):
    starts = {}
    size = table_size(z)

    def kernel(place_ref, old_ref, new_ref, lost_ref, offset_ref, table_ref):
        tables = plan_tables(
            z,
            place_ref[0],
            place_ref[1],
            lambda at, l: old_ref[at, l],
            lambda l: new_ref[l],
            lambda rank: lost_ref[rank],
            lambda l: offset_ref[l],
        )
        at = 0
        for name, units in tables.items():
            starts[name] = at
            for unit in units:
                for entry in unit:
                    for value in entry:
                        table_ref[at] = jnp.int32(value)
                        at += 1
        assert at <= size

    smem = pl.BlockSpec(memory_space=pltpu.SMEM)
    table = pl.pallas_call(
        kernel,
        out_shape=jax.ShapeDtypeStruct((size,), jnp.int32),
        in_specs=[smem] * 5,
        out_specs=smem,
        name="plan",
    )(place, old_section, new_section, lost_pipe, donor_offset)
    return table, starts


SMEM_SPEC = pl.BlockSpec(memory_space=pltpu.SMEM)
VMEM_SPEC = pl.BlockSpec(memory_space=pltpu.VMEM)


def cost(operands, results):
    moved = sum(math.prod(a.shape) * a.dtype.itemsize for a in (*operands, *results))
    return pl.CostEstimate(flops=moved // 4, bytes_accessed=moved, transcendentals=0)


class Order:
    def __init__(self):
        self.last = []

    def specs(self):
        return [pl.BlockSpec(memory_space=pl.ANY)] * len(self.last)

    def then(self, result):
        self.last = [result[-1] if isinstance(result, (tuple, list)) else result]
        return result


def pack(z, order, table, start, units, sources, name):
    count = len(sources)
    arrays, _, rows, cols = sources[0].shape

    def kernel(table_ref, *refs):
        out_ref = refs[-1]
        for unit in range(units):
            for source, ref in enumerate(refs[:count]):
                at = start + (unit * count + source) * 2

                @pl.when(table_ref[at] != 0)
                def _(unit=unit, ref=ref, at=at):
                    out_ref[:, pl.ds(unit, 1)] = ref[:, pl.ds(table_ref[at + 1], 1)]

    out = jax.ShapeDtypeStruct((arrays, units, rows, cols), jnp.bfloat16)
    call = pl.pallas_call(
        kernel,
        out_shape=out,
        in_specs=[SMEM_SPEC] + [VMEM_SPEC] * count + order.specs(),
        out_specs=VMEM_SPEC,
        compiler_params=pltpu.CompilerParams(vmem_limit_bytes=VMEM),
        cost_estimate=cost([out], [out]),
        name=name,
    )
    return order.then(call(table, *sources, *order.last))


def add_up(z, order, table, start, units, sources, name):
    count = len(sources)
    _, rows, cols = sources[0].shape

    def kernel(table_ref, *refs):
        out_ref = refs[-1]
        for unit in range(units):
            out = jnp.zeros((rows, cols), jnp.float32)
            for source, ref in enumerate(refs[:count]):
                at = start + (unit * count + source) * 2
                block = ref[table_ref[at + 1]].astype(jnp.float32)
                out = out + jnp.where(table_ref[at] != 0, block, 0.0)
            out_ref[unit] = out.astype(out_ref.dtype)

    out = jax.ShapeDtypeStruct((units, rows, cols), jnp.bfloat16)
    call = pl.pallas_call(
        kernel,
        out_shape=out,
        in_specs=[SMEM_SPEC] + [VMEM_SPEC] * count + order.specs(),
        out_specs=VMEM_SPEC,
        compiler_params=pltpu.CompilerParams(vmem_limit_bytes=VMEM),
        cost_estimate=cost([out] * 2, [out]),
        name=name,
    )
    return order.then(call(table, *sources, *order.last))


def halve(z, order, place, arrays, chunk, chunks, name):
    sub = z.band // chunks
    count = len(arrays)
    views = [a.reshape(z.slots, CORES, z.sections, chunks, sub, z.cols) for a in arrays]

    def kernel(place_ref, *refs):
        own_refs, their_refs = refs[:count], refs[count : 2 * count]
        own_out, their_out = refs[-2:]
        for at in range(count):
            own_out[at] = own_refs[at][:, 0, :, 0].astype(jnp.bfloat16)
            their_out[at] = their_refs[at][:, 0, :, 0].astype(jnp.bfloat16)

    def spec(own):
        def index_map(step, place_ref):
            core = lax.rem(place_ref[0], CORES)
            return (0, core if own else 1 - core, 0, chunk, 0, 0)

        return pl.BlockSpec((z.slots, 1, z.sections, 1, sub, z.cols), index_map)

    shape = (count, z.slots, z.sections, sub, z.cols)
    out = jax.ShapeDtypeStruct(shape, jnp.bfloat16)
    out_spec = pl.BlockSpec(shape, lambda step, place_ref: (0, 0, 0, 0, 0))
    call = pl.pallas_call(
        kernel,
        grid_spec=pltpu.PrefetchScalarGridSpec(
            num_scalar_prefetch=1,
            grid=(1,),
            in_specs=[spec(True)] * count + [spec(False)] * count + order.specs(),
            out_specs=[out_spec] * 2,
        ),
        out_shape=(out, out),
        compiler_params=pltpu.CompilerParams(vmem_limit_bytes=VMEM),
        cost_estimate=cost([out] * 4, [out] * 2),
        name=name,
    )
    return order.then(call(place, *views, *views, *order.last))


def update(z, order, table, start, chunk, state, rebuilt, mean, outs):
    views = [a.reshape(z.slots, CORES, z.sections, z.chunks, z.sub, z.cols) for a in state]
    rebuilt = [a.reshape(3, z.slots, z.sections, z.sub, z.cols) for a in rebuilt]
    mean = [a.reshape(z.slots, z.sections, z.chunks, z.sub, z.cols) for a in mean]
    outs = [] if outs is None else list(outs)

    def kernel(table_ref, *refs):
        local_refs, lost_refs, mean_refs = refs[:3], refs[3:5], refs[5:7]
        out_w, out_one, out_two = refs[-3:]
        slot = pl.program_id(0)
        is_lost = table_ref[start] != 0
        core = table_ref[start + 1]
        found = table_ref[start + 2 + slot] != 0

        def step(half, band, weight, one, two, grad):
            grad = grad.astype(jnp.float32) * (1.0 / z.pipes)
            weight = weight.astype(jnp.float32)
            next_one = BETA_ONE * one.astype(jnp.float32) + (1.0 - BETA_ONE) * grad
            next_two = BETA_TWO * two.astype(jnp.float32) + (1.0 - BETA_TWO) * grad * grad
            move = next_one / (jnp.sqrt(next_two) + EPSILON) + DECAY_RATE * weight
            out_w[0, half, band, 0] = (weight - LEARN_RATE * move).astype(out_w.dtype)
            out_one[0, half, band, 0] = next_one
            out_two[0, half, band, 0] = next_two

        for half in range(CORES):
            for source in range(2):
                mine = both(found, (core == half) == (source == 0))

                @pl.when(both(mine, is_lost))
                def _(half=half, source=source):
                    for band in range(z.sections):
                        ref = lost_refs[source]
                        step(
                            half, band, ref[0, 0, band], ref[1, 0, band], ref[2, 0, band],
                            mean_refs[source][0, band, 0],
                        )

                @pl.when(both(mine, jnp.logical_not(is_lost)))
                def _(half=half, source=source):
                    for band in range(z.sections):
                        step(
                            half, band, *(ref[0, half, band, 0] for ref in local_refs),
                            mean_refs[source][0, band, 0],
                        )

        @pl.when(jnp.logical_not(found))
        def _():
            for ref in (out_w, out_one, out_two):
                ref[...] = jnp.zeros(ref.shape, ref.dtype)

    def local(slot, table_ref):
        return (slot * (1 - table_ref[start]), 0, 0, chunk, 0, 0)

    def lost(slot, table_ref):
        return (0, slot * table_ref[start], 0, 0, 0)

    state_block = (1, CORES, z.sections, 1, z.sub, z.cols)
    state_spec = pl.BlockSpec(state_block, local)
    lost_spec = pl.BlockSpec((3, 1, z.sections, z.sub, z.cols), lost)
    mean_spec = pl.BlockSpec(
        (1, z.sections, 1, z.sub, z.cols), lambda slot, table_ref: (slot, 0, chunk, 0, 0)
    )
    out_spec = pl.BlockSpec(state_block, lambda slot, table_ref: (slot, 0, 0, chunk, 0, 0))
    shape = views[0].shape
    elements = z.slots * z.rows * z.cols // z.chunks
    call = pl.pallas_call(
        kernel,
        grid_spec=pltpu.PrefetchScalarGridSpec(
            num_scalar_prefetch=1,
            grid=(z.slots,),
            in_specs=[state_spec] * 3
            + [lost_spec] * 2
            + [mean_spec] * 2
            + [pl.BlockSpec(memory_space=pl.ANY)] * len(outs)
            + order.specs(),
            out_specs=[out_spec] * 3,
        ),
        out_shape=(
            jax.ShapeDtypeStruct(shape, jnp.bfloat16),
            jax.ShapeDtypeStruct(shape, jnp.float32),
            jax.ShapeDtypeStruct(shape, jnp.float32),
        ),
        input_output_aliases={8 + at: at for at in range(len(outs))},
        compiler_params=pltpu.CompilerParams(vmem_limit_bytes=VMEM),
        cost_estimate=pl.CostEstimate(
            flops=elements * 14, bytes_accessed=elements * 22, transcendentals=elements * 2
        ),
        name="update",
    )
    return call(table, *views, *rebuilt, *mean, *outs, *order.last)


class Gradients:
    def __init__(self, z, order, table, starts, first, pair):
        self.z, self.order, self.table, self.starts, self.first = z, order, table, starts, first
        if first == "group":
            self.parts, self.other = z.groups, z.sections
            self.send_first, self.send_other = z.to_group, z.to_section
        else:
            self.parts, self.other = z.sections, z.groups
            self.send_first, self.send_other = z.to_section, z.to_group
        rows = z.half // self.parts
        self.held = [a.reshape(z.slots * self.parts, rows, z.cols) for a in pair]

    def summed(self, name, sources):
        return add_up(
            self.z, self.order, self.table, self.starts[name], self.z.layers, sources, name[0]
        )

    def scatter(self):
        self.arrived = []
        for shift in range(1, self.parts):
            part = self.summed(("grad_out", self.first, shift), self.held)
            self.arrived.append(self.send_first(part, shift))

    def exchange(self):
        part = self.summed(("grad_sum", self.first), self.held + self.arrived)
        self.whole = [part] + [self.send_other(part, shift) for shift in range(1, self.other)]

    def gather(self):
        whole = self.summed(("grad_mean", self.first), self.whole)
        bands = [whole] + [self.send_first(whole, shift) for shift in range(1, self.parts)]
        self.bands = [band[None] for band in bands]

    def finish(self):
        z = self.z
        theirs, mine = (
            pack(
                z,
                self.order,
                self.table,
                self.starts[name, self.first],
                z.slots * self.parts,
                self.bands,
                name + "_mean",
            )
            for name in ("sibling", "mine")
        )
        return mine, z.to_core(theirs)


class Donated:
    def __init__(self, z, order, table, starts, pair):
        self.z, self.order, self.table, self.starts = z, order, table, starts
        self.held = [a.reshape(3, z.slots * z.sections, z.sub, z.cols) for a in pair]

    def packed(self, name, units, sources):
        label = name if isinstance(name, str) else name[0]
        return pack(self.z, self.order, self.table, self.starts[name], units, sources, label)

    def spread(self):
        z = self.z
        own = self.held[:2]
        for shift in range(1, z.sections):
            sent = self.packed(("spread", shift), z.channels, own)
            self.held.append(z.to_section(sent, shift))

    def across(self):
        crossed = self.packed("across", self.z.layers, self.held)
        for shift in range(1, self.z.groups):
            self.held.append(self.z.to_group(crossed, shift))

    def deliver(self):
        z = self.z
        arrived = []
        for shift in range(1, z.sections):
            sent = self.packed(("deliver", shift), z.slots, self.held)
            arrived.append(z.to_section(sent, shift))
        self.held = self.held + arrived

    def collect(self):
        z = self.z
        half = self.packed("collect", z.slots * z.sections, self.held)
        self.rebuilt = (half, z.to_core(half))


def per_device(
    weights,
    first_moment,
    second_moment,
    gradients,
    old_section,
    new_section,
    lost_pipe,
    donor_offset,
):
    z = Sizes(weights, new_section)
    order = Order()
    place = jnp.stack([lax.axis_index("pipe"), lax.axis_index("section")]).astype(jnp.int32)
    state = (weights[0, 0], first_moment[0, 0], second_moment[0, 0])

    def swap(arrays, chunk, chunks, name):
        own, theirs = halve(z, order, place, arrays, chunk, chunks, name)
        return own, z.to_core(theirs)

    pair = swap((gradients[0, 0],), 0, 1, "halve_gradients")
    chunk_pairs = [swap(state, 0, z.chunks, "halve_state")]
    table, starts = make_plan(z, place, old_section, new_section, lost_pipe, donor_offset)

    grads = Gradients(z, order, table, starts, "group", pair)
    grads.scatter()
    parts = []

    def spread(chunk):
        if chunk >= len(chunk_pairs):
            chunk_pairs.append(swap(state, chunk, z.chunks, "halve_state"))
        parts.append(Donated(z, order, table, starts, chunk_pairs[chunk]))
        parts[chunk].spread()

    early = min(2, z.chunks)
    for chunk in range(early):
        spread(chunk)
    while len(chunk_pairs) < z.chunks:
        chunk_pairs.append(swap(state, len(chunk_pairs), z.chunks, "halve_state"))
    parts[0].across()
    grads.exchange()
    for chunk in range(1, early):
        parts[chunk].across()
    grads.gather()
    for chunk in range(early, z.chunks):
        spread(chunk)
    delivered = 0
    for chunk in range(early, z.chunks):
        parts[delivered].deliver()
        delivered += 1
        parts[chunk].across()
    mean = grads.finish()
    outs = None
    for chunk in range(z.chunks):
        while delivered < min(chunk + early, z.chunks):
            parts[delivered].deliver()
            delivered += 1
        parts[chunk].collect()
        if chunk:
            outs = advance(z, order, table, starts, chunk - 1, state, parts, mean, outs)
    outs = advance(z, order, table, starts, z.chunks - 1, state, parts, mean, outs)
    return tuple(out.reshape((1, 1, z.slots, z.rows, z.cols)) for out in outs)


def advance(z, order, table, starts, chunk, state, parts, mean, outs):
    rebuilt = parts[chunk].rebuilt
    return update(z, order, table, starts["update"], chunk, state, rebuilt, mean, outs)


def solution(mesh):
    split = P("pipe", "section", None, "tp", None)
    return jax.shard_map(
        per_device,
        mesh=mesh,
        in_specs=(split,) * 4 + (P(),) * 4,
        out_specs=(split,) * 3,
        check_vma=False,
    )
```

profile of v0, /device:TPU:0, one launch (start us, length us, event | category | flops | bytes accessed | tf_op | source)
XLA Modules:
  0.0 151.9 jit_solution(14698484167157929595)
XLA Ops:
  0.7 1.7 %copy-done.7 = bf16[1,1,2,1024,512]{4,3,2,1,0:T(8,128)(2,1)S(1)} copy-done((bf16[1,1,2,1024,512]{4,3,2,1,0:T(8,128)(2,1)S(1)}, bf16[1,1,2,1024,512]{4,3,2,1,0:T(8,128)(2,1)}, u32[]{:S(2)}) %copy-start.7) | copy-done | bytes 2097176
  2.5 1.6 %halve_gradients.1 = (bf16[1,2,2,256,512]{4,3,2,1,0:T(8,128)(2,1)S(1)}, bf16[1,2,2,256,512]{4,3,2,1,0:T(8,128)(2,1)}) custom-call(s32[2]{0:T(128)S(1)} %pad_add_fusion.place_ref, bf16[2,2,2,1,256,512]{5,4,3,2,1,0:T(8,128)(2,1)S(1)} %bitcast.108, bf16[2,2,2,1,256,512]{5,4,3,2,1,0:T(8,128)(2,1)S(1)} %bitcast.109), custom_call_target="tpu_custom_call" | custom-call | flops 1572864 | bytes 6291456 | tf_op jit(solution)/shard_map/halve_gradients/pallas_call | solution.py:384
  4.1 1.0 copy-done.10
  5.5 2.2 %copy-done.2 = f32[1,1,2,1024,512]{4,3,2,1,0:T(8,128)S(1)} copy-done((f32[1,1,2,1024,512]{4,3,2,1,0:T(8,128)S(1)}, f32[1,1,2,1024,512]{4,3,2,1,0:T(8,128)}, u32[]{:S(2)}) %copy-start.2) | copy-done | bytes 4194328
  7.7 1.6 %copy-done.5 = bf16[1,1,2,1024,512]{4,3,2,1,0:T(8,128)(2,1)S(1)} copy-done((bf16[1,1,2,1024,512]{4,3,2,1,0:T(8,128)(2,1)S(1)}, bf16[1,1,2,1024,512]{4,3,2,1,0:T(8,128)(2,1)}, u32[]{:S(2)}) %copy-start.5) | copy-done | bytes 2097176
  9.3 1.6 %halve_state.4 = (bf16[3,2,2,64,512]{4,3,2,1,0:T(8,128)(2,1)S(1)}, bf16[3,2,2,64,512]{4,3,2,1,0:T(8,128)(2,1)}) custom-call(s32[2]{0:T(128)S(1)} %pad_add_fusion.place_ref, bf16[2,2,2,4,64,512]{5,4,3,2,1,0:T(8,128)(2,1)S(1)} %bitcast.55, f32[2,2,2,4,64,512]{5,4,3,2,1,0:T(8,128)S(1)} %bitcast.31, f32[2,2,2,4,64,512]{5,4,3,2,1,0:T(8,128)S(1)} %bitcast.43, ...), custom_call_target="tpu_custom_call" | custom-call | flops 1179648 | bytes 4718592 | tf_op jit(solution)/shard_map/halve_state/pallas_call | solution.py:384
  10.9 1.9 %plan.1.table_ref = s32[2048]{0:T(1024)} custom-call(s32[2]{0:T(128)} %copy-done.13, s32[4,3]{1,0:T(4,128)} %old_ref.1, s32[3]{0:T(128)} %new_ref.1, s32[4]{0:T(128)} %lost_ref.1, s32[3]{0:T(128)} %offset_ref.1), custom_call_target="tpu_custom_call" | custom-call | tf_op jit(solution)/shard_map/plan/pallas_call | solution.py:264
  12.9 0.8 copy-done.8
  13.7 1.4 copy-done.11
  15.2 1.5 %grad_out.1.refs_2_ = bf16[3,256,512]{2,1,0:T(8,128)(2,1)S(1)} custom-call(s32[2048]{0:T(1024)S(1)} %copy-done.8, bf16[4,256,512]{2,1,0:T(8,128)(2,1)S(1)} %bitcast.111, bf16[4,256,512]{2,1,0:T(8,128)(2,1)} %bitcast.9.refs_1_, bf16[3,2,2,64,512]{4,3,2,1,0:T(8,128)(2,1)} %get-tuple-element.27.refs_2_), custom_call_target="tpu_custom_call" | custom-call | flops 589824 | bytes 2359296 | tf_op jit(solution)/shard_map/grad_out/pallas_call | solution.py:346
  16.7 1.2 spread.4.refs_6_
  17.9 2.2 %copy-done.3 = f32[1,1,2,1024,512]{4,3,2,1,0:T(8,128)S(1)} copy-done((f32[1,1,2,1024,512]{4,3,2,1,0:T(8,128)S(1)}, f32[1,1,2,1024,512]{4,3,2,1,0:T(8,128)}, u32[]{:S(2)}) %copy-start.3) | copy-done | bytes 4194328
  20.1 0.7 halve_state.5
  20.8 0.5 collective-permute-start.2
  21.3 2.6 %collective-permute-start.5 = (bf16[3,256,512]{2,1,0:T(8,128)(2,1)S(1)}, bf16[3,256,512]{2,1,0:T(8,128)(2,1)S(1)}, u32[]{:S(2)}, u32[]{:S(2)}) collective-permute-start(bf16[3,256,512]{2,1,0:T(8,128)(2,1)S(1)} %grad_out.1.refs_2_), channel_id=1, source_target_pairs={{0,16},{4,20},{8,24},{12,28},{16,0},{20,4},{24,8},{28,12},{1,17},{... | collective-permute-start | bytes 2359304 | tf_op jit(solution)/shard_map/ppermute | solution.py:70
  23.9 1.5 collective-permute-start.6
  25.4 0.7 spread.5.refs_6_
  26.2 0.7 halve_state.6
  26.9 0.7 halve_state.7
  27.6 7.5 %collective-permute-done.6.refs_2_ = bf16[3,2,64,512]{3,2,1,0:T(8,128)(2,1)S(1)} collective-permute-done((bf16[3,2,64,512]{3,2,1,0:T(8,128)(2,1)S(1)}, bf16[3,2,64,512]{3,2,1,0:T(8,128)(2,1)S(1)}, u32[]{:S(2)}, u32[]{:S(2)}) %collective-permute-start.6) | collective-permute-done | bytes 393248 | tf_op jit(solution)/shard_map/ppermute | solution.py:70
  35.1 1.2 across.4.refs_3_
  36.3 5.7 %collective-permute-done.5.refs_2_ = bf16[3,256,512]{2,1,0:T(8,128)(2,1)S(1)} collective-permute-done((bf16[3,256,512]{2,1,0:T(8,128)(2,1)S(1)}, bf16[3,256,512]{2,1,0:T(8,128)(2,1)S(1)}, u32[]{:S(2)}, u32[]{:S(2)}) %collective-permute-start.5) | collective-permute-done | bytes 786464 | tf_op jit(solution)/shard_map/ppermute | solution.py:70
  42.0 1.7 %grad_sum.1.refs_3_.refs_0_ = bf16[3,256,512]{2,1,0:T(8,128)(2,1)S(1)} custom-call(s32[2048]{0:T(1024)S(1)} %copy-done.9, bf16[4,256,512]{2,1,0:T(8,128)(2,1)S(1)} %bitcast.112, bf16[4,256,512]{2,1,0:T(8,128)(2,1)} %bitcast.9.refs_1_, bf16[3,256,512]{2,1,0:T(8,128)(2,1)S(1)} %collective-permute-done.5.refs_2_, bf16[3,3,64,512]{3,2,1,0:T(8,128)(2,1)S(1)} %across.4.refs_3_), custom_call_target="tpu_custom_call" | custom-call | flops 589824 | bytes 2359296 | tf_op jit(solution)/shard_map/grad_sum/pallas_call | solution.py:346
  43.7 1.8 %collective-permute-start.7 = (bf16[3,256,512]{2,1,0:T(8,128)(2,1)S(1)}, bf16[3,256,512]{2,1,0:T(8,128)(2,1)S(1)}, u32[]{:S(2)}, u32[]{:S(2)}) collective-permute-start(bf16[3,256,512]{2,1,0:T(8,128)(2,1)S(1)} %grad_sum.1.refs_3_.refs_0_), channel_id=1, source_target_pairs={{0,4},{4,0},{8,12},{12,8},{16,20},{20,16},{24,28},{28,24},{1,5},{5... | collective-permute-start | bytes 2359304 | tf_op jit(solution)/shard_map/ppermute | solution.py:70
  45.5 0.5 collective-permute-start.3
  46.3 1.8 %collective-permute-start.12 = (bf16[3,3,64,512]{3,2,1,0:T(8,128)(2,1)S(1)}, bf16[3,3,64,512]{3,2,1,0:T(8,128)(2,1)S(1)}, u32[]{:S(2)}, u32[]{:S(2)}) collective-permute-start(bf16[3,3,64,512]{3,2,1,0:T(8,128)(2,1)S(1)} %across.4.refs_3_), channel_id=1, source_target_pairs={{0,16},{4,20},{8,24},{12,28},{16,0},{20,4},{24,8},{28,12},{1,17},{... | collective-permute-start | bytes 1769480 | tf_op jit(solution)/shard_map/ppermute | solution.py:70
  48.1 23.4 %collective-permute-done.8.refs_2_ = bf16[3,2,64,512]{3,2,1,0:T(8,128)(2,1)S(1)} collective-permute-done((bf16[3,2,64,512]{3,2,1,0:T(8,128)(2,1)S(1)}, bf16[3,2,64,512]{3,2,1,0:T(8,128)(2,1)S(1)}, u32[]{:S(2)}, u32[]{:S(2)}) %collective-permute-start.8) | collective-permute-done | bytes 393248 | tf_op jit(solution)/shard_map/ppermute | solution.py:70
  71.5 0.8 across.5.refs_2_
  72.3 1.6 %collective-permute-start.10 = (bf16[3,3,64,512]{3,2,1,0:T(8,128)(2,1)S(1)}, bf16[3,3,64,512]{3,2,1,0:T(8,128)(2,1)S(1)}, u32[]{:S(2)}, u32[]{:S(2)}) collective-permute-start(bf16[3,3,64,512]{3,2,1,0:T(8,128)(2,1)S(1)} %across.5.refs_2_), channel_id=1, source_target_pairs={{0,16},{4,20},{8,24},{12,28},{16,0},{20,4},{24,8},{28,12},{1,17},{... | collective-permute-start | bytes 1769480 | tf_op jit(solution)/shard_map/ppermute | solution.py:70
  73.9 1.0 grad_mean.1.refs_2_
  74.9 0.7 spread.6.refs_2_
  75.6 1.6 %collective-permute-start.11 = (bf16[3,2,64,512]{3,2,1,0:T(8,128)(2,1)S(1)}, bf16[3,2,64,512]{3,2,1,0:T(8,128)(2,1)S(1)}, u32[]{:S(2)}, u32[]{:S(2)}) collective-permute-start(bf16[3,2,64,512]{3,2,1,0:T(8,128)(2,1)S(1)} %spread.6.refs_2_), channel_id=1, source_target_pairs={{0,4},{4,0},{8,12},{12,8},{16,20},{20,16},{24,28},{28,24},{1,5},{5... | collective-permute-start | bytes 1179656 | tf_op jit(solution)/shard_map/ppermute | solution.py:70
  77.2 0.7 spread.7.refs_4_
  77.9 0.6 collective-permute-start.9
  79.0 1.2 deliver.4.refs_3_
  80.2 7.5 %collective-permute-done.11.refs_2_ = bf16[3,2,64,512]{3,2,1,0:T(8,128)(2,1)S(1)} collective-permute-done((bf16[3,2,64,512]{3,2,1,0:T(8,128)(2,1)S(1)}, bf16[3,2,64,512]{3,2,1,0:T(8,128)(2,1)S(1)}, u32[]{:S(2)}, u32[]{:S(2)}) %collective-permute-start.11) | collective-permute-done | bytes 393248 | tf_op jit(solution)/shard_map/ppermute | solution.py:70
  87.7 0.8 across.6.refs_4_
  88.5 0.5 collective-permute-start.15
  89.0 0.7 deliver.5.refs_3_
  89.7 3.9 %collective-permute-done.9.refs_2_ = bf16[3,2,64,512]{3,2,1,0:T(8,128)(2,1)S(1)} collective-permute-done((bf16[3,2,64,512]{3,2,1,0:T(8,128)(2,1)S(1)}, bf16[3,2,64,512]{3,2,1,0:T(8,128)(2,1)S(1)}, u32[]{:S(2)}, u32[]{:S(2)}) %collective-permute-start.9) | collective-permute-done | bytes 393248 | tf_op jit(solution)/shard_map/ppermute | solution.py:70
  93.6 0.8 across.7.refs_2_
  94.4 0.7 collective-permute-start.13
  95.1 1.3 collective-permute-start.16
  96.4 0.7 collective-permute-start.14
  97.1 8.4 %collective-permute-done.17 = bf16[3,256,512]{2,1,0:T(8,128)(2,1)S(1)} collective-permute-done((bf16[3,256,512]{2,1,0:T(8,128)(2,1)S(1)}, bf16[3,256,512]{2,1,0:T(8,128)(2,1)S(1)}, u32[]{:S(2)}, u32[]{:S(2)}) %collective-permute-start.17) | collective-permute-done | bytes 786464 | tf_op jit(solution)/shard_map/ppermute | solution.py:70
  105.5 0.8 sibling_mean.1.refs_2_
  106.3 0.8 mine_mean.1.refs_5_
  107.1 1.3 collect.4.refs_4_
  108.5 9.6 %collective-permute-done.15.refs_3_ = bf16[3,3,64,512]{3,2,1,0:T(8,128)(2,1)S(1)} collective-permute-done((bf16[3,3,64,512]{3,2,1,0:T(8,128)(2,1)S(1)}, bf16[3,3,64,512]{3,2,1,0:T(8,128)(2,1)S(1)}, u32[]{:S(2)}, u32[]{:S(2)}) %collective-permute-start.15) | collective-permute-done | bytes 589856 | tf_op jit(solution)/shard_map/ppermute | solution.py:70
  118.1 0.7 deliver.6.refs_5_
  118.8 1.6 %collective-permute-start.19 = (bf16[3,2,64,512]{3,2,1,0:T(8,128)(2,1)S(1)}, bf16[3,2,64,512]{3,2,1,0:T(8,128)(2,1)S(1)}, u32[]{:S(2)}, u32[]{:S(2)}) collective-permute-start(bf16[3,2,64,512]{3,2,1,0:T(8,128)(2,1)S(1)} %deliver.6.refs_5_), channel_id=1, source_target_pairs={{0,4},{4,0},{8,12},{12,8},{16,20},{20,16},{24,28},{28,24},{1,5},{5... | collective-permute-start | bytes 1179656 | tf_op jit(solution)/shard_map/ppermute | solution.py:70
  120.5 0.8 collect.5.refs_4_.refs_7_
  121.3 7.4 %collective-permute-done.13.refs_3_ = bf16[3,3,64,512]{3,2,1,0:T(8,128)(2,1)S(1)} collective-permute-done((bf16[3,3,64,512]{3,2,1,0:T(8,128)(2,1)S(1)}, bf16[3,3,64,512]{3,2,1,0:T(8,128)(2,1)S(1)}, u32[]{:S(2)}, u32[]{:S(2)}) %collective-permute-start.13) | collective-permute-done | bytes 589856 | tf_op jit(solution)/shard_map/ppermute | solution.py:70
  128.7 0.7 deliver.7.refs_5_
  129.4 1.4 collective-permute-start.18
  130.8 0.5 collective-permute-start.24
  131.3 0.8 collect.6.refs_5_.refs_10_
  132.2 0.6 collective-permute-start.22
  132.8 5.8 %collective-permute-done.18.refs_4_ = bf16[3,2,64,512]{3,2,1,0:T(8,128)(2,1)S(1)} collective-permute-done((bf16[3,2,64,512]{3,2,1,0:T(8,128)(2,1)S(1)}, bf16[3,2,64,512]{3,2,1,0:T(8,128)(2,1)S(1)}, u32[]{:S(2)}, u32[]{:S(2)}) %collective-permute-start.18) | collective-permute-done | bytes 393248 | tf_op jit(solution)/shard_map/ppermute | solution.py:70
  138.6 1.0 collect.7.refs_10_
  139.7 3.1 %update.4 = (bf16[2,2,2,4,64,512]{5,4,3,2,1,0:T(8,128)(2,1)}, f32[2,2,2,4,64,512]{5,4,3,2,1,0:T(8,128)}, f32[2,2,2,4,64,512]{5,4,3,2,1,0:T(8,128)}) custom-call(s32[2048]{0:T(1024)S(1)} %copy-done.9, bf16[2,2,2,4,64,512]{5,4,3,2,1,0:T(8,128)(2,1)S(1)} %bitcast.63, f32[2,2,2,4,64,512]{5,4,3,2,1,0:T(8,128)S(1)} %bitcast.39, ...), custom_call_target="tpu_custom_call" | custom-call | flops 3670016 | bytes 5767168 | tf_op jit(solution)/shard_map/update/pallas_call | solution.py:476
  142.8 3.0 %update.5 = (bf16[2,2,2,4,64,512]{5,4,3,2,1,0:T(8,128)(2,1)}, f32[2,2,2,4,64,512]{5,4,3,2,1,0:T(8,128)}, f32[2,2,2,4,64,512]{5,4,3,2,1,0:T(8,128)}) custom-call(s32[2048]{0:T(1024)S(1)} %copy-done.9, bf16[2,2,2,4,64,512]{5,4,3,2,1,0:T(8,128)(2,1)S(1)} %bitcast.64, ...), custom_call_target="tpu_custom_call", output_to_operand_aliasing={{0}: (8, {}), {1}: (9, {}), {2}: (10, {})} | custom-call | flops 3670016 | bytes 5767168 | tf_op jit(solution)/shard_map/update/pallas_call | solution.py:476
  145.8 3.0 %update.6 = (bf16[2,2,2,4,64,512]{5,4,3,2,1,0:T(8,128)(2,1)}, f32[2,2,2,4,64,512]{5,4,3,2,1,0:T(8,128)}, f32[2,2,2,4,64,512]{5,4,3,2,1,0:T(8,128)}) custom-call(s32[2048]{0:T(1024)S(1)} %copy-done.9, bf16[2,2,2,4,64,512]{5,4,3,2,1,0:T(8,128)(2,1)S(1)} %bitcast.65, ...), custom_call_target="tpu_custom_call", output_to_operand_aliasing={{0}: (8, {}), {1}: (9, {}), {2}: (10, {})} | custom-call | flops 3670016 | bytes 5767168 | tf_op jit(solution)/shard_map/update/pallas_call | solution.py:476
  148.8 3.0 %update.7 = (bf16[2,2,2,4,64,512]{5,4,3,2,1,0:T(8,128)(2,1)}, f32[2,2,2,4,64,512]{5,4,3,2,1,0:T(8,128)}, f32[2,2,2,4,64,512]{5,4,3,2,1,0:T(8,128)}) custom-call(s32[2048]{0:T(1024)S(1)} %copy-done.9, bf16[2,2,2,4,64,512]{5,4,3,2,1,0:T(8,128)(2,1)S(1)} %bitcast.66, ...), custom_call_target="tpu_custom_call", output_to_operand_aliasing={{0}: (8, {}), {1}: (9, {}), {2}: (10, {})} | custom-call | flops 3670016 | bytes 5767168 | tf_op jit(solution)/shard_map/update/pallas_call | solution.py:476
  (48 shorter events, 1.6 us)
Async XLA Ops:
  0.6 4.9 %copy-start = (f32[1,1,2,1024,512]{4,3,2,1,0:T(8,128)S(1)}, f32[1,1,2,1024,512]{4,3,2,1,0:T(8,128)}, u32[]{:S(2)}) copy-start(f32[1,1,2,1024,512]{4,3,2,1,0:T(8,128)} %param.9) | copy-start | bytes 12582916
  0.7 10.2 %copy-start.13 = (s32[2]{0:T(128)}, s32[2]{0:T(128)S(1)}, u32[]{:S(2)}) copy-start(s32[2]{0:T(128)S(1)} %pad_add_fusion.place_ref) | copy-start | bytes 28
  0.7 1.7 %copy-start.7 = (bf16[1,1,2,1024,512]{4,3,2,1,0:T(8,128)(2,1)S(1)}, bf16[1,1,2,1024,512]{4,3,2,1,0:T(8,128)(2,1)}, u32[]{:S(2)}) copy-start(bf16[1,1,2,1024,512]{4,3,2,1,0:T(8,128)(2,1)} %param.11) | copy-start | bytes 6291460
  4.1 1.0 copy-start.10
  5.1 7.8 %collective-permute-start.1 = (bf16[1,2,2,256,512]{4,3,2,1,0:T(8,128)(2,1)}, bf16[1,2,2,256,512]{4,3,2,1,0:T(8,128)(2,1)}, u32[]{:S(2)}, u32[]{:S(2)}) collective-permute-start(bf16[1,2,2,256,512]{4,3,2,1,0:T(8,128)(2,1)} %get-tuple-element.25.refs_6_), channel_id=1, source_target_pairs={{0,8},{4,12},{8,0},{12,4},{16,24},{20,28},{24,16},{28,20},{1,9},{5... | collective-permute-start | bytes 3145736 | tf_op jit(solution)/shard_map/ppermute | solution.py:70
  5.5 2.2 %copy-start.2 = (f32[1,1,2,1024,512]{4,3,2,1,0:T(8,128)S(1)}, f32[1,1,2,1024,512]{4,3,2,1,0:T(8,128)}, u32[]{:S(2)}) copy-start(f32[1,1,2,1024,512]{4,3,2,1,0:T(8,128)} %param.10) | copy-start | bytes 12582916
  7.7 1.6 %copy-start.5 = (bf16[1,1,2,1024,512]{4,3,2,1,0:T(8,128)(2,1)S(1)}, bf16[1,1,2,1024,512]{4,3,2,1,0:T(8,128)(2,1)}, u32[]{:S(2)}) copy-start(bf16[1,1,2,1024,512]{4,3,2,1,0:T(8,128)(2,1)} %param.8) | copy-start | bytes 6291460
  10.9 7.0 %copy-start.6 = (bf16[1,1,2,1024,512]{4,3,2,1,0:T(8,128)(2,1)S(1)}, bf16[1,1,2,1024,512]{4,3,2,1,0:T(8,128)(2,1)}, u32[]{:S(2)}) copy-start(bf16[1,1,2,1024,512]{4,3,2,1,0:T(8,128)(2,1)} %param.8) | copy-start | bytes 6291460
  10.9 5.8 %collective-permute-start = (bf16[3,2,2,64,512]{4,3,2,1,0:T(8,128)(2,1)}, bf16[3,2,2,64,512]{4,3,2,1,0:T(8,128)(2,1)}, u32[]{:S(2)}, u32[]{:S(2)}) collective-permute-start(bf16[3,2,2,64,512]{4,3,2,1,0:T(8,128)(2,1)} %get-tuple-element.27.refs_2_), channel_id=1, source_target_pairs={{0,8},{4,12},{8,0},{12,4},{16,24},{20,28},{24,16},{28,20},{1,9},{5... | collective-permute-start | bytes 2359304 | tf_op jit(solution)/shard_map/ppermute | solution.py:70
  12.9 5.0 %copy-start.1 = (f32[1,1,2,1024,512]{4,3,2,1,0:T(8,128)S(1)}, f32[1,1,2,1024,512]{4,3,2,1,0:T(8,128)}, u32[]{:S(2)}) copy-start(f32[1,1,2,1024,512]{4,3,2,1,0:T(8,128)} %param.9) | copy-start | bytes 12582916
  12.9 0.8 copy-start.8
  13.7 1.4 copy-start.11
  15.2 2.8 %copy-start.14 = (s32[2]{0:T(128)S(1)}, s32[2]{0:T(128)}, u32[]{:S(2)}) copy-start(s32[2]{0:T(128)} %copy-done.13) | copy-start | bytes 28
  17.9 2.2 %copy-start.3 = (f32[1,1,2,1024,512]{4,3,2,1,0:T(8,128)S(1)}, f32[1,1,2,1024,512]{4,3,2,1,0:T(8,128)}, u32[]{:S(2)}) copy-start(f32[1,1,2,1024,512]{4,3,2,1,0:T(8,128)} %param.10) | copy-start | bytes 12582916
  20.1 5.3 %copy-start.9 = (s32[2048]{0:T(1024)S(1)}, s32[2048]{0:T(1024)}, u32[]{:S(2)}) copy-start(s32[2048]{0:T(1024)} %plan.1.table_ref) | copy-start | bytes 24580
  20.1 6.0 %copy-start.4 = (f32[1,1,2,1024,512]{4,3,2,1,0:T(8,128)S(1)}, f32[1,1,2,1024,512]{4,3,2,1,0:T(8,128)}, u32[]{:S(2)}) copy-start(f32[1,1,2,1024,512]{4,3,2,1,0:T(8,128)} %param.10) | copy-start | bytes 12582916
  20.8 4.6 %collective-permute-start.2 = (bf16[3,2,2,64,512]{4,3,2,1,0:T(8,128)(2,1)S(1)}, bf16[3,2,2,64,512]{4,3,2,1,0:T(8,128)(2,1)S(1)}, u32[]{:S(2)}, u32[]{:S(2)}) collective-permute-start(bf16[3,2,2,64,512]{4,3,2,1,0:T(8,128)(2,1)S(1)} %get-tuple-element.30.refs_2_), channel_id=1, source_target_pairs={{0,8},{4,12},{8,0},{12,4},{16,24},{20,28},{24,16},{28,20},{1,9},{5... | collective-permute-start | bytes 2359304 | tf_op jit(solution)/shard_map/ppermute | solution.py:70
  21.3 20.7 %collective-permute-start.5 = (bf16[3,256,512]{2,1,0:T(8,128)(2,1)S(1)}, bf16[3,256,512]{2,1,0:T(8,128)(2,1)S(1)}, u32[]{:S(2)}, u32[]{:S(2)}) collective-permute-start(bf16[3,256,512]{2,1,0:T(8,128)(2,1)S(1)} %grad_out.1.refs_2_), channel_id=1, source_target_pairs={{0,16},{4,20},{8,24},{12,28},{16,0},{20,4},{24,8},{28,12},{1,17},{... | collective-permute-start | bytes 2359304 | tf_op jit(solution)/shard_map/ppermute | solution.py:70
  23.9 11.2 %collective-permute-start.6 = (bf16[3,2,64,512]{3,2,1,0:T(8,128)(2,1)S(1)}, bf16[3,2,64,512]{3,2,1,0:T(8,128)(2,1)S(1)}, u32[]{:S(2)}, u32[]{:S(2)}) collective-permute-start(bf16[3,2,64,512]{3,2,1,0:T(8,128)(2,1)S(1)} %spread.4.refs_6_), channel_id=1, source_target_pairs={{0,4},{4,0},{8,12},{12,8},{16,20},{20,16},{24,28},{28,24},{1,5},{5... | collective-permute-start | bytes 1179656 | tf_op jit(solution)/shard_map/ppermute | solution.py:70
  26.9 15.2 %copy-start.12 = (bf16[1,2,2,256,512]{4,3,2,1,0:T(8,128)(2,1)S(1)}, bf16[1,2,2,256,512]{4,3,2,1,0:T(8,128)(2,1)}, u32[]{:S(2)}) copy-start(bf16[1,2,2,256,512]{4,3,2,1,0:T(8,128)(2,1)} %copy-done.10) | copy-start | bytes 3145732
  43.7 30.2 %collective-permute-start.7 = (bf16[3,256,512]{2,1,0:T(8,128)(2,1)S(1)}, bf16[3,256,512]{2,1,0:T(8,128)(2,1)S(1)}, u32[]{:S(2)}, u32[]{:S(2)}) collective-permute-start(bf16[3,256,512]{2,1,0:T(8,128)(2,1)S(1)} %grad_sum.1.refs_3_.refs_0_), channel_id=1, source_target_pairs={{0,4},{4,0},{8,12},{12,8},{16,20},{20,16},{24,28},{28,24},{1,5},{5... | collective-permute-start | bytes 2359304 | tf_op jit(solution)/shard_map/ppermute | solution.py:70
  45.5 29.3 %collective-permute-start.4 = (bf16[3,2,2,64,512]{4,3,2,1,0:T(8,128)(2,1)S(1)}, bf16[3,2,2,64,512]{4,3,2,1,0:T(8,128)(2,1)S(1)}, u32[]{:S(2)}, u32[]{:S(2)}) collective-permute-start(bf16[3,2,2,64,512]{4,3,2,1,0:T(8,128)(2,1)S(1)} %get-tuple-element.31.refs_6_), channel_id=1, source_target_pairs={{0,8},{4,12},{8,0},{12,4},{16,24},{20,28},{24,16},{28,20},{1,9},{5... | collective-permute-start | bytes 2359304 | tf_op jit(solution)/shard_map/ppermute | solution.py:70
  45.5 31.6 %collective-permute-start.3 = (bf16[3,2,2,64,512]{4,3,2,1,0:T(8,128)(2,1)S(1)}, bf16[3,2,2,64,512]{4,3,2,1,0:T(8,128)(2,1)S(1)}, u32[]{:S(2)}, u32[]{:S(2)}) collective-permute-start(bf16[3,2,2,64,512]{4,3,2,1,0:T(8,128)(2,1)S(1)} %get-tuple-element.33.refs_3_), channel_id=1, source_target_pairs={{0,8},{4,12},{8,0},{12,4},{16,24},{20,28},{24,16},{28,20},{1,9},{5... | collective-permute-start | bytes 2359304 | tf_op jit(solution)/shard_map/ppermute | solution.py:70
  46.0 25.5 %collective-permute-start.8 = (bf16[3,2,64,512]{3,2,1,0:T(8,128)(2,1)S(1)}, bf16[3,2,64,512]{3,2,1,0:T(8,128)(2,1)S(1)}, u32[]{:S(2)}, u32[]{:S(2)}) collective-permute-start(bf16[3,2,64,512]{3,2,1,0:T(8,128)(2,1)S(1)} %spread.5.refs_6_), channel_id=1, source_target_pairs={{0,4},{4,0},{8,12},{12,8},{16,20},{20,16},{24,28},{28,24},{1,5},{5... | collective-permute-start | bytes 1179656 | tf_op jit(solution)/shard_map/ppermute | solution.py:70
  46.3 32.6 %collective-permute-start.12 = (bf16[3,3,64,512]{3,2,1,0:T(8,128)(2,1)S(1)}, bf16[3,3,64,512]{3,2,1,0:T(8,128)(2,1)S(1)}, u32[]{:S(2)}, u32[]{:S(2)}) collective-permute-start(bf16[3,3,64,512]{3,2,1,0:T(8,128)(2,1)S(1)} %across.4.refs_3_), channel_id=1, source_target_pairs={{0,16},{4,20},{8,24},{12,28},{16,0},{20,4},{24,8},{28,12},{1,17},{... | collective-permute-start | bytes 1769480 | tf_op jit(solution)/shard_map/ppermute | solution.py:70
  72.3 16.7 %collective-permute-start.10 = (bf16[3,3,64,512]{3,2,1,0:T(8,128)(2,1)S(1)}, bf16[3,3,64,512]{3,2,1,0:T(8,128)(2,1)S(1)}, u32[]{:S(2)}, u32[]{:S(2)}) collective-permute-start(bf16[3,3,64,512]{3,2,1,0:T(8,128)(2,1)S(1)} %across.5.refs_2_), channel_id=1, source_target_pairs={{0,16},{4,20},{8,24},{12,28},{16,0},{20,4},{24,8},{28,12},{1,17},{... | collective-permute-start | bytes 1769480 | tf_op jit(solution)/shard_map/ppermute | solution.py:70
  75.6 12.1 %collective-permute-start.11 = (bf16[3,2,64,512]{3,2,1,0:T(8,128)(2,1)S(1)}, bf16[3,2,64,512]{3,2,1,0:T(8,128)(2,1)S(1)}, u32[]{:S(2)}, u32[]{:S(2)}) collective-permute-start(bf16[3,2,64,512]{3,2,1,0:T(8,128)(2,1)S(1)} %spread.6.refs_2_), channel_id=1, source_target_pairs={{0,4},{4,0},{8,12},{12,8},{16,20},{20,16},{24,28},{28,24},{1,5},{5... | collective-permute-start | bytes 1179656 | tf_op jit(solution)/shard_map/ppermute | solution.py:70
  77.9 15.7 %collective-permute-start.9 = (bf16[3,2,64,512]{3,2,1,0:T(8,128)(2,1)S(1)}, bf16[3,2,64,512]{3,2,1,0:T(8,128)(2,1)S(1)}, u32[]{:S(2)}, u32[]{:S(2)}) collective-permute-start(bf16[3,2,64,512]{3,2,1,0:T(8,128)(2,1)S(1)} %spread.7.refs_4_), channel_id=1, source_target_pairs={{0,4},{4,0},{8,12},{12,8},{16,20},{20,16},{24,28},{28,24},{1,5},{5... | collective-permute-start | bytes 1179656 | tf_op jit(solution)/shard_map/ppermute | solution.py:70
  78.5 27.0 %collective-permute-start.17 = (bf16[3,256,512]{2,1,0:T(8,128)(2,1)S(1)}, bf16[3,256,512]{2,1,0:T(8,128)(2,1)S(1)}, u32[]{:S(2)}, u32[]{:S(2)}) collective-permute-start(bf16[3,256,512]{2,1,0:T(8,128)(2,1)S(1)} %grad_mean.1.refs_2_), channel_id=1, source_target_pairs={{0,16},{4,20},{8,24},{12,28},{16,0},{20,4},{24,8},{28,12},{1,17},{... | collective-permute-start | bytes 2359304 | tf_op jit(solution)/shard_map/ppermute | solution.py:70
  88.5 29.6 %collective-permute-start.15 = (bf16[3,3,64,512]{3,2,1,0:T(8,128)(2,1)S(1)}, bf16[3,3,64,512]{3,2,1,0:T(8,128)(2,1)S(1)}, u32[]{:S(2)}, u32[]{:S(2)}) collective-permute-start(bf16[3,3,64,512]{3,2,1,0:T(8,128)(2,1)S(1)} %across.6.refs_4_), channel_id=1, source_target_pairs={{0,16},{4,20},{8,24},{12,28},{16,0},{20,4},{24,8},{28,12},{1,17},{... | collective-permute-start | bytes 1769480 | tf_op jit(solution)/shard_map/ppermute | solution.py:70
  94.4 34.3 %collective-permute-start.13 = (bf16[3,3,64,512]{3,2,1,0:T(8,128)(2,1)S(1)}, bf16[3,3,64,512]{3,2,1,0:T(8,128)(2,1)S(1)}, u32[]{:S(2)}, u32[]{:S(2)}) collective-permute-start(bf16[3,3,64,512]{3,2,1,0:T(8,128)(2,1)S(1)} %across.7.refs_2_), channel_id=1, source_target_pairs={{0,16},{4,20},{8,24},{12,28},{16,0},{20,4},{24,8},{28,12},{1,17},{... | collective-permute-start | bytes 1769480 | tf_op jit(solution)/shard_map/ppermute | solution.py:70
  95.1 12.1 %collective-permute-start.16 = (bf16[3,2,64,512]{3,2,1,0:T(8,128)(2,1)S(1)}, bf16[3,2,64,512]{3,2,1,0:T(8,128)(2,1)S(1)}, u32[]{:S(2)}, u32[]{:S(2)}) collective-permute-start(bf16[3,2,64,512]{3,2,1,0:T(8,128)(2,1)S(1)} %deliver.4.refs_3_), channel_id=1, source_target_pairs={{0,4},{4,0},{8,12},{12,8},{16,20},{20,16},{24,28},{28,24},{1,5},{5... | collective-permute-start | bytes 1179656 | tf_op jit(solution)/shard_map/ppermute | solution.py:70
  96.4 24.0 %collective-permute-start.14 = (bf16[3,2,64,512]{3,2,1,0:T(8,128)(2,1)S(1)}, bf16[3,2,64,512]{3,2,1,0:T(8,128)(2,1)S(1)}, u32[]{:S(2)}, u32[]{:S(2)}) collective-permute-start(bf16[3,2,64,512]{3,2,1,0:T(8,128)(2,1)S(1)} %deliver.5.refs_3_), channel_id=1, source_target_pairs={{0,4},{4,0},{8,12},{12,8},{16,20},{20,16},{24,28},{28,24},{1,5},{5... | collective-permute-start | bytes 1179656 | tf_op jit(solution)/shard_map/ppermute | solution.py:70
  118.8 12.5 %collective-permute-start.19 = (bf16[3,2,64,512]{3,2,1,0:T(8,128)(2,1)S(1)}, bf16[3,2,64,512]{3,2,1,0:T(8,128)(2,1)S(1)}, u32[]{:S(2)}, u32[]{:S(2)}) collective-permute-start(bf16[3,2,64,512]{3,2,1,0:T(8,128)(2,1)S(1)} %deliver.6.refs_5_), channel_id=1, source_target_pairs={{0,4},{4,0},{8,12},{12,8},{16,20},{20,16},{24,28},{28,24},{1,5},{5... | collective-permute-start | bytes 1179656 | tf_op jit(solution)/shard_map/ppermute | solution.py:70
  129.4 9.1 %collective-permute-start.18 = (bf16[3,2,64,512]{3,2,1,0:T(8,128)(2,1)S(1)}, bf16[3,2,64,512]{3,2,1,0:T(8,128)(2,1)S(1)}, u32[]{:S(2)}, u32[]{:S(2)}) collective-permute-start(bf16[3,2,64,512]{3,2,1,0:T(8,128)(2,1)S(1)} %deliver.7.refs_5_), channel_id=1, source_target_pairs={{0,4},{4,0},{8,12},{12,8},{16,20},{20,16},{24,28},{28,24},{1,5},{5... | collective-permute-start | bytes 1179656 | tf_op jit(solution)/shard_map/ppermute | solution.py:70
  130.8 8.9 %collective-permute-start.21 = (bf16[1,4,256,512]{3,2,1,0:T(8,128)(2,1)S(1)}, bf16[1,4,256,512]{3,2,1,0:T(8,128)(2,1)S(1)}, u32[]{:S(2)}, u32[]{:S(2)}) collective-permute-start(bf16[1,4,256,512]{3,2,1,0:T(8,128)(2,1)S(1)} %sibling_mean.1.refs_2_), channel_id=1, source_target_pairs={{0,8},{4,12},{8,0},{12,4},{16,24},{20,28},{24,16},{28,20},{1,9},{5... | collective-permute-start | bytes 3145736 | tf_op jit(solution)/shard_map/ppermute | solution.py:70
  130.8 8.9 %collective-permute-start.24 = (bf16[3,4,64,512]{3,2,1,0:T(8,128)(2,1)S(1)}, bf16[3,4,64,512]{3,2,1,0:T(8,128)(2,1)S(1)}, u32[]{:S(2)}, u32[]{:S(2)}) collective-permute-start(bf16[3,4,64,512]{3,2,1,0:T(8,128)(2,1)S(1)} %collect.4.refs_4_), channel_id=1, source_target_pairs={{0,8},{4,12},{8,0},{12,4},{16,24},{20,28},{24,16},{28,20},{1,9},{5... | collective-permute-start | bytes 2359304 | tf_op jit(solution)/shard_map/ppermute | solution.py:70
  131.3 11.4 %collective-permute-start.23 = (bf16[3,4,64,512]{3,2,1,0:T(8,128)(2,1)S(1)}, bf16[3,4,64,512]{3,2,1,0:T(8,128)(2,1)S(1)}, u32[]{:S(2)}, u32[]{:S(2)}) collective-permute-start(bf16[3,4,64,512]{3,2,1,0:T(8,128)(2,1)S(1)} %collect.5.refs_4_.refs_7_), channel_id=1, source_target_pairs={{0,8},{4,12},{8,0},{12,4},{16,24},{20,28},{24,16},{28,20},{1,9},{5... | collective-permute-start | bytes 2359304 | tf_op jit(solution)/shard_map/ppermute | solution.py:70
  132.2 13.6 %collective-permute-start.22 = (bf16[3,4,64,512]{3,2,1,0:T(8,128)(2,1)S(1)}, bf16[3,4,64,512]{3,2,1,0:T(8,128)(2,1)S(1)}, u32[]{:S(2)}, u32[]{:S(2)}) collective-permute-start(bf16[3,4,64,512]{3,2,1,0:T(8,128)(2,1)S(1)} %collect.6.refs_5_.refs_10_), channel_id=1, source_target_pairs={{0,8},{4,12},{8,0},{12,4},{16,24},{20,28},{24,16},{28,20},{1,9},{5... | collective-permute-start | bytes 2359304 | tf_op jit(solution)/shard_map/ppermute | solution.py:70
  139.6 9.2 %collective-permute-start.20 = (bf16[3,4,64,512]{3,2,1,0:T(8,128)(2,1)S(1)}, bf16[3,4,64,512]{3,2,1,0:T(8,128)(2,1)S(1)}, u32[]{:S(2)}, u32[]{:S(2)}) collective-permute-start(bf16[3,4,64,512]{3,2,1,0:T(8,128)(2,1)S(1)} %collect.7.refs_10_), channel_id=1, source_target_pairs={{0,8},{4,12},{8,0},{12,4},{16,24},{20,28},{24,16},{28,20},{1,9},{5... | collective-permute-start | bytes 2359304 | tf_op jit(solution)/shard_map/ppermute | solution.py:70
where the time goes:
time: 153 us; the launch traced here: 152 us
  waiting for transfers between devices  79.4 us (52%)
  Pallas kernels  39.3 us (26%)
  starting transfers between devices  21.1 us (14%)
  local copies, waits for them, and re-layouts  11 us (7%)
    ppermute x25, waiting for transfers between devices, send(): return lax.ppermute(value, AXES, pairs)  79.4 us
    ppermute x25, starting transfers between devices, send(): return lax.ppermute(value, AXES, pairs)  21.1 us
    pallas_call x18, Pallas kernels, pack(): return order.then(call(table, *sources, *order.last))  15.8 us
    pallas_call x4, Pallas kernels, update(): return call(table, *views, *rebuilt, *mean, *outs, *order.last)  12.2 us
    unnamed x30, local copies, waits for them, and re-layouts  11 us
    pallas_call x5, Pallas kernels, halve(): return order.then(call(place, *views, *views, *order.last))  5.26 us
    pallas_call x3, Pallas kernels, add_up(): return order.then(call(table, *sources, *order.last))  4.15 us
  transfers between devices with their start and end apart: 25, of which 10 were waited for; matrix products, arithmetic and copies ran while one was open for 0% of the time, Pallas kernels for 20%

commit v1 on v0

v1 whole, which is shorter than its diff:
```python
import jax
import jax.numpy as jnp
from jax import lax
from jax.experimental import pallas as pl
from jax.experimental.pallas import tpu as pltpu
from jax.sharding import PartitionSpec as P

LEARN_RATE = 0.01
BETA_ONE = 0.9
BETA_TWO = 0.95
EPSILON = 1e-08
DECAY_RATE = 0.1

CORES = 2
CHUNKS = (3, 3, 2)
SEQUENCE = (
    *("ge", "e0", "gs", "s0", "e1", "s1", "a0", "gx", "a1", "e2", "gg", "s2"),
    *("d0", "a2", "d1", "gf", "c0", "u0", "c1", "d2", "u1", "c2", "u2"),
)
VMEM = 24 * 1024 * 1024
AXES = ("pipe", "section")


def both(*terms):
    out = terms[0]
    for term in terms[1:]:
        out = jnp.logical_and(out, term)
    return out


def as_int(flag):
    return jnp.where(flag, 1, 0).astype(jnp.int32)


def total(terms):
    out = jnp.int32(0)
    for term in terms:
        out = out + term
    return out


class Sizes:
    def __init__(self, weights, new_section):
        self.pipes = lax.axis_size("pipe")
        self.sections = lax.axis_size("section")
        self.groups = self.pipes // CORES
        self.slots = weights.shape[2]
        self.rows = weights.shape[3]
        self.cols = weights.shape[4]
        self.layers = new_section.shape[0]
        self.half = self.rows // CORES
        self.band = self.half // self.sections
        units = sum(CHUNKS)
        self.chunks = CHUNKS if self.band % (16 * units) == 0 else (1,)
        self.units = sum(self.chunks)
        self.unit = self.band // self.units
        self.grad_band = self.half // self.groups
        doubles = self.layers - self.sections
        widest = 0
        for at in range(self.sections):
            low = at + max(0, doubles - (self.sections - at))
            high = min(self.layers - self.sections + at, at + min(at, doubles) + 1)
            widest = max(widest, high - low + 1)
        self.channels = min(widest, CORES * self.slots)

    def send(self, value, target):
        pairs = []
        for pipe in range(self.pipes):
            for section in range(self.sections):
                group_to, core, to = target(pipe // CORES, pipe % CORES, section)
                pipe_to = group_to * CORES + core
                pairs.append((pipe * self.sections + section, pipe_to * self.sections + to))
        return lax.ppermute(value, AXES, pairs)

    def to_core(self, value):
        return self.send(value, lambda g, c, s: (g, 1 - c, s))

    def to_group(self, value, shift):
        return self.send(value, lambda g, c, s: ((g + shift) % self.groups, c, s))

    def to_section(self, value, shift):
        return self.send(value, lambda g, c, s: (g, c, (s + shift) % self.sections))


def plan_tables(z, pipe, section, old, new, lost_pipe, offset):
    layers = range(z.layers)
    lost = lost_pipe(0)
    group, core = pipe // CORES, pipe % CORES
    sibling = group * CORES + (1 - core)
    lost_group = lost // CORES
    tables = {}

    def now_of(at):
        return [jnp.where(at == lost, new(l), old(at, l)) for l in layers]

    def slots_of(sections):
        return [total(as_int(sections[k] == sections[l]) for k in range(l)) for l in layers]

    def layer_at(sections, slots, at, slot):
        hits = [both(sections[l] == at, slots[l] == slot) for l in layers]
        index = total(jnp.where(hits[l], l, 0) for l in layers)
        return index, total(as_int(hit) for hit in hits)

    def lookup(values, index):
        out = values[0]
        for l in layers[1:]:
            out = jnp.where(index == l, values[l], out)
        return out

    my_now = now_of(pipe)
    my_slot = slots_of(my_now)
    sib_now = now_of(sibling)
    sib_slot = slots_of(sib_now)
    new_list = [new(l) for l in layers]
    new_slot = slots_of(new_list)

    donor = [lost_pipe(offset(l)) for l in layers]
    source_section = [old(donor[l], l) for l in layers]
    source_slot = [
        total(as_int(old(donor[l], k) == source_section[l]) for k in range(l)) for l in layers
    ]
    source_group = [donor[l] // CORES for l in layers]
    crosses = [as_int(source_group[l] != lost_group) for l in layers]
    rank = [total(crosses[k] for k in range(l)) for l in layers]
    channel = [
        total(
            as_int(both(source_group[k] == source_group[l], source_section[k] == source_section[l]))
            for k in range(l)
        )
        for l in layers
    ]

    def grad_unit(l, band):
        return [
            (as_int(my_now[l] == section), my_slot[l] * z.groups + band),
            (as_int(sib_now[l] == section), sib_slot[l] * z.groups + band),
        ]

    for shift in range(1, z.groups):
        band = lax.rem(group + shift, z.groups)
        tables["grad_out", shift] = [grad_unit(l, band) for l in layers]
    tables["grad_sum"] = [grad_unit(l, group) + [(1, l)] * (z.groups - 1) for l in layers]
    tables["grad_mean"] = [[(1, l)] * z.sections for l in layers]
    for name, sections, slots in (("mine", my_now, my_slot), ("sibling", sib_now, sib_slot)):
        units = []
        for slot in range(z.slots):
            index, found = layer_at(sections, slots, section, slot)
            for band in range(z.groups):
                unit = []
                for shift in range(z.groups):
                    sender = lax.rem(group + z.groups - shift, z.groups)
                    unit.append((found * as_int(sender == band), index))
                units.append(unit)
        tables[name] = units

    here = [as_int(source_group[l] == group) for l in layers]
    my_chip = [here[l] * as_int(source_section[l] == section) for l in layers]
    from_me = [as_int(donor[l] == pipe) for l in layers]

    for shift in range(1, z.sections):
        band = lax.rem(section + shift, z.sections)
        units = []
        for k in range(z.channels):
            hit = [my_chip[l] * as_int(channel[l] == k) for l in layers]
            slot = total(hit[l] * source_slot[l] for l in layers)
            mine = total(hit[l] * from_me[l] for l in layers)
            found = total(hit)
            index = slot * z.sections + band
            units.append([(mine, index), (found - mine, index)])
        tables["spread", shift] = units

    def held(l_my_chip, l_from_me, l_slot, l_here, l_channel, l_section):
        index = l_slot * z.sections + section
        unit = [(l_my_chip * l_from_me, index), (l_my_chip * (1 - l_from_me), index)]
        for shift in range(1, z.sections):
            sender = lax.rem(section + z.sections - shift, z.sections)
            unit.append((l_here * as_int(l_section == sender), l_channel))
        return unit

    def held_at(index):
        return held(
            *(
                lookup(values, index)
                for values in (my_chip, from_me, source_slot, here, channel, source_section)
            )
        )

    units = []
    for u in range(z.layers):
        hit = [crosses[l] * as_int(rank[l] == u) for l in layers]
        index = total(hit[l] * l for l in layers)
        found = total(hit)
        units.append([(flag * found, at) for flag, at in held_at(index)])
    tables["across"] = units

    def arrived(index, found):
        found = found * as_int(group == lost_group)
        unit = [(flag * found, at) for flag, at in held_at(index)]
        from_group = lookup(source_group, index)
        for shift in range(1, z.groups):
            sender = lax.rem(group + z.groups - shift, z.groups)
            unit.append((found * as_int(from_group == sender), lookup(rank, index)))
        return unit

    for shift in range(1, z.sections):
        target = lax.rem(section + shift, z.sections)
        tables["deliver", shift] = [
            arrived(*layer_at(new_list, new_slot, target, slot)) for slot in range(z.slots)
        ]
    units = []
    for slot in range(z.slots):
        own = arrived(*layer_at(new_list, new_slot, section, slot))
        for band in range(z.sections):
            mine = as_int(section == band)
            unit = [(flag * mine, at) for flag, at in own]
            for shift in range(1, z.sections):
                sender = lax.rem(section + z.sections - shift, z.sections)
                unit.append((as_int(both(sender == band, group == lost_group)), slot))
            units.append(unit)
    tables["collect"] = units

    last = [as_int(pipe == lost), core]
    for slot in range(z.slots):
        last.append(layer_at(my_now, my_slot, section, slot)[1])
    tables["update"] = [[tuple(last)]]
    return tables


def table_size(z):
    sources = z.sections + z.groups + z.sections + 2
    units = (z.sections + z.groups) * (4 * z.layers + 4 * z.slots)
    units += z.sections * (z.channels + 2 * z.slots) + z.layers
    return -(-(2 * units * sources + z.slots + 8) // 1024) * 1024


def make_plan(z, place, old_section, new_section, lost_pipe, donor_offset):
    starts = {}
    size = table_size(z)
    smem = pl.BlockSpec(memory_space=pltpu.SMEM)

    def kernel(place_ref, old_ref, new_ref, lost_ref, offset_ref, table_ref):
        tables = plan_tables(
            z,
            place_ref[0],
            place_ref[1],
            lambda at, l: old_ref[at, l],
            lambda l: new_ref[l],
            lambda rank: lost_ref[rank],
            lambda l: offset_ref[l],
        )
        at = 0
        for name, units in tables.items():
            starts[name] = at
            for unit in units:
                for entry in unit:
                    for value in entry:
                        table_ref[at] = jnp.int32(value)
                        at += 1
        assert at <= size

    table = pl.pallas_call(
        kernel,
        out_shape=jax.ShapeDtypeStruct((size,), jnp.int32),
        in_specs=[smem] * 5,
        out_specs=smem,
        name="plan",
    )(place, old_section, new_section, lost_pipe, donor_offset)
    return table, starts


SMEM_SPEC = pl.BlockSpec(memory_space=pltpu.SMEM)
VMEM_SPEC = pl.BlockSpec(memory_space=pltpu.VMEM)


def cost(operands, results):
    moved = sum(math.prod(a.shape) * a.dtype.itemsize for a in (*operands, *results))
    return pl.CostEstimate(flops=moved // 4, bytes_accessed=moved, transcendentals=0)


class Order:
    def __init__(self):
        self.last = []

    def specs(self):
        return [pl.BlockSpec(memory_space=pl.ANY)] * len(self.last)

    def then(self, result):
        self.last = [result[0]]
        return result


SMEM_SPEC = pl.BlockSpec(memory_space=pltpu.SMEM)
VMEM_SPEC = pl.BlockSpec(memory_space=pltpu.VMEM)
PARAMS = pltpu.CompilerParams(vmem_limit_bytes=VMEM)
COST = pl.CostEstimate(flops=1, bytes_accessed=1, transcendentals=0)


class Rows:
    def __init__(self, value, rows, count, arrays=1, base=0):
        self.value, self.rows, self.count = value, rows, count
        self.arrays, self.base = arrays, base

    def block(self, array, index):
        at = self.base + (array * self.count + index) * self.rows
        return pl.ds(at if isinstance(at, int) else pl.multiple_of(at, 16), self.rows)


class Copy:
    def __init__(self, start, units, sources):
        self.start, self.units, self.sources = start, units, sources
        self.arrays, self.rows = sources[0].arrays, sources[0].rows

    def write(self, table_ref, refs, out_ref, out):
        for unit in range(self.units):
            for at, source in enumerate(self.sources):
                entry = self.start + (unit * len(self.sources) + at) * 2

                @pl.when(table_ref[entry] != 0)
                def _(unit=unit, source=source, ref=refs[at], entry=entry):
                    index = table_ref[entry + 1]
                    for array in range(self.arrays):
                        out_ref[out.block(array, unit)] = ref[source.block(array, index)]


class Sum:
    def __init__(self, start, units, sources):
        self.start, self.units, self.sources = start, units, sources
        self.arrays, self.rows = 1, sources[0].rows

    def write(self, table_ref, refs, out_ref, out):
        for unit in range(self.units):
            total_here = None
            for at, source in enumerate(self.sources):
                entry = self.start + (unit * len(self.sources) + at) * 2
                block = refs[at][source.block(0, table_ref[entry + 1])].astype(jnp.float32)
                block = jnp.where(table_ref[entry] != 0, block, 0.0)
                total_here = block if total_here is None else total_here + block
            out_ref[out.block(0, unit)] = total_here.astype(out_ref.dtype)


def stage(z, order, table, outputs, name):
    operands, slots = [], {}
    for job in (job for jobs in outputs for job in jobs):
        for source in job.sources:
            if id(source.value) not in slots:
                slots[id(source.value)] = len(operands)
                operands.append(source.value)
    places, shapes = [], []
    for jobs in outputs:
        at, row = [], 0
        for job in jobs:
            at.append(Rows(None, job.rows, job.units, job.arrays, row))
            row += job.arrays * job.units * job.rows
        places.append(at)
        shapes.append(jax.ShapeDtypeStruct((row, z.cols), jnp.bfloat16))

    def kernel(table_ref, *refs):
        out_refs = refs[-len(outputs) :]
        for jobs, at, out_ref in zip(outputs, places, out_refs):
            for job, place in zip(jobs, at):
                inputs = [refs[slots[id(source.value)]] for source in job.sources]
                job.write(table_ref, inputs, out_ref, place)

    call = pl.pallas_call(
        kernel,
        out_shape=tuple(shapes),
        in_specs=[SMEM_SPEC] + [VMEM_SPEC] * len(operands) + order.specs(),
        out_specs=tuple([VMEM_SPEC] * len(outputs)),
        compiler_params=PARAMS,
        cost_estimate=COST,
        name=name,
    )
    return order.then(call(table, *operands, *order.last))


def halve(z, order, place, arrays, first, count, units):
    unit = z.band // units
    views = [a.reshape(z.slots, CORES, z.sections, units, unit, z.cols) for a in arrays]

    def kernel(place_ref, *refs):
        for part, out_ref in enumerate(refs[-2:]):
            row = 0
            for at in range(len(arrays)):
                ref = refs[part * len(arrays) + at]
                for slot in range(z.slots):
                    for band in range(z.sections):
                        for k in range(count):
                            out_ref[pl.ds(row, unit)] = ref[slot, 0, band, k].astype(jnp.bfloat16)
                            row += unit

    def spec(own):
        def index_map(step, place_ref):
            core = lax.rem(place_ref[0], CORES)
            return (0, core if own else 1 - core, 0, first // count, 0, 0)

        return pl.BlockSpec((z.slots, 1, z.sections, count, unit, z.cols), index_map)

    rows = len(arrays) * z.slots * z.sections * count * unit
    out = jax.ShapeDtypeStruct((rows, z.cols), jnp.bfloat16)
    out_spec = pl.BlockSpec(out.shape, lambda step, place_ref: (0, 0))
    call = pl.pallas_call(
        kernel,
        grid_spec=pltpu.PrefetchScalarGridSpec(
            num_scalar_prefetch=1,
            grid=(1,),
            in_specs=[spec(True)] * len(arrays) + [spec(False)] * len(arrays) + order.specs(),
            out_specs=[out_spec] * 2,
        ),
        out_shape=(out, out),
        compiler_params=PARAMS,
        cost_estimate=COST,
        name="halve_state" if len(arrays) > 1 else "halve_gradients",
    )
    return order.then(call(place, *views, *views, *order.last))


def update(z, order, table, start, first, count, state, halves, mean, outs):
    sub = count * z.unit
    per_slot = z.sections * sub
    views = [a.reshape(z.slots, CORES, z.sections, z.units, z.unit, z.cols) for a in state]
    outs = [] if outs is None else list(outs)

    def kernel(table_ref, *refs):
        local_refs, half_refs, mean_refs = refs[:3], refs[3:5], refs[5:7]
        out_w, out_one, out_two = refs[-3:]
        slot = pl.program_id(0)
        is_lost = table_ref[start] != 0
        core = table_ref[start + 1]
        found = table_ref[start + 2 + slot] != 0

        def step(half, band, unit, weight, one, two, grad):
            grad = grad.astype(jnp.float32) * (1.0 / z.pipes)
            weight = weight.astype(jnp.float32)
            next_one = BETA_ONE * one.astype(jnp.float32) + (1.0 - BETA_ONE) * grad
            next_two = BETA_TWO * two.astype(jnp.float32) + (1.0 - BETA_TWO) * grad * grad
            move = next_one / (jnp.sqrt(next_two) + EPSILON) + DECAY_RATE * weight
            out_w[0, half, band, unit] = (weight - LEARN_RATE * move).astype(out_w.dtype)
            out_one[0, half, band, unit] = next_one
            out_two[0, half, band, unit] = next_two

        def each(half, source, lost):
            for band in range(z.sections):
                for unit in range(count):
                    row = slot * per_slot + band * sub + unit * z.unit

                    def rows(at):
                        return pl.ds(pl.multiple_of(at, 16), z.unit)

                    mean_row = slot * z.half + band * z.band + (first + unit) * z.unit
                    grad = mean_refs[source][rows(mean_row)]
                    if lost:
                        ref = half_refs[source]
                        old = [ref[rows(a * z.slots * per_slot + row)] for a in range(3)]
                    else:
                        old = [ref[0, half, band, unit] for ref in local_refs]
                    step(half, band, unit, *old, grad)

        for half in range(CORES):
            for source in range(2):
                mine = both(found, (core == half) == (source == 0))

                @pl.when(both(mine, is_lost))
                def _(half=half, source=source):
                    each(half, source, True)

                @pl.when(both(mine, jnp.logical_not(is_lost)))
                def _(half=half, source=source):
                    each(half, source, False)

        @pl.when(jnp.logical_not(found))
        def _():
            for ref in (out_w, out_one, out_two):
                ref[...] = jnp.zeros(ref.shape, ref.dtype)

    def local(slot, table_ref):
        return (slot * (1 - table_ref[start]), 0, 0, first // count, 0, 0)

    block = (1, CORES, z.sections, count, z.unit, z.cols)
    out_spec = pl.BlockSpec(block, lambda slot, table_ref: (slot, 0, 0, first // count, 0, 0))
    shape = views[0].shape
    call = pl.pallas_call(
        kernel,
        grid_spec=pltpu.PrefetchScalarGridSpec(
            num_scalar_prefetch=1,
            grid=(z.slots,),
            in_specs=[pl.BlockSpec(block, local)] * 3
            + [VMEM_SPEC] * 4
            + [pl.BlockSpec(memory_space=pl.ANY)] * len(outs)
            + order.specs(),
            out_specs=[out_spec] * 3,
        ),
        out_shape=(
            jax.ShapeDtypeStruct(shape, jnp.bfloat16),
            jax.ShapeDtypeStruct(shape, jnp.float32),
            jax.ShapeDtypeStruct(shape, jnp.float32),
        ),
        input_output_aliases={8 + at: at for at in range(len(outs))},
        compiler_params=PARAMS,
        cost_estimate=COST,
        name="update",
    )
    return order.then(call(table, *views, *halves, *mean, *outs, *order.last))


class Gradients:
    def __init__(self, z, order, grads):
        self.z, self.order, self.grads = z, order, grads

    def run(self, outputs, name):
        return stage(self.z, self.order, self.table, outputs, name)

    def rows(self, value):
        return Rows(value, self.z.grad_band, self.z.layers)

    def enter(self, place):
        z = self.z
        own, theirs = halve(z, self.order, place, (self.grads,), 0, 1, 1)
        self.held = [
            Rows(flat, z.grad_band, z.slots * z.groups) for flat in (own, z.to_core(theirs))
        ]

    def scatter(self):
        z = self.z
        shifts = range(1, z.groups)
        jobs = [[Sum(self.starts["grad_out", s], z.layers, self.held)] for s in shifts]
        parts = self.run(jobs, "grad_out")
        self.held += [self.rows(z.to_group(part, s)) for s, part in zip(shifts, parts)]

    def exchange(self):
        z = self.z
        (part,) = self.run([[Sum(self.starts["grad_sum"], z.layers, self.held)]], "grad_sum")
        others = [z.to_section(part, s) for s in range(1, z.sections)]
        self.held = [self.rows(value) for value in (part, *others)]

    def gather(self):
        z = self.z
        (part,) = self.run([[Sum(self.starts["grad_mean"], z.layers, self.held)]], "grad_mean")
        others = [z.to_group(part, s) for s in range(1, z.groups)]
        self.held = [self.rows(value) for value in (part, *others)]

    def finish(self):
        z = self.z
        theirs, mine = self.run(
            [
                [Copy(self.starts[name], z.slots * z.groups, self.held)]
                for name in ("sibling", "mine")
            ],
            "mean",
        )
        self.mean = (mine, z.to_core(theirs))


class Chunk:
    def __init__(self, z, order, state, first, count):
        self.z, self.order, self.state = z, order, state
        self.first, self.count, self.sub = first, count, count * z.unit

    def run(self, outputs, name):
        return stage(self.z, self.order, self.table, outputs, name)

    def enter(self, place):
        z = self.z
        own, theirs = halve(z, self.order, place, self.state, self.first, self.count, z.units)
        held = z.slots * z.sections
        self.held = [Rows(flat, self.sub, held, 3) for flat in (own, z.to_core(theirs))]

    def spread(self):
        z = self.z
        shifts = range(1, z.sections)
        jobs = [[Copy(self.starts["spread", s], z.channels, self.held)] for s in shifts]
        parts = self.run(jobs, "spread")
        for s, part in zip(shifts, parts):
            self.held.append(Rows(z.to_section(part, s), self.sub, z.channels, 3))

    def across(self):
        z = self.z
        (part,) = self.run([[Copy(self.starts["across"], z.layers, self.held)]], "across")
        for s in range(1, z.groups):
            self.held.append(Rows(z.to_group(part, s), self.sub, z.layers, 3))

    def deliver(self):
        z = self.z
        shifts = range(1, z.sections)
        jobs = [[Copy(self.starts["deliver", s], z.slots, self.held)] for s in shifts]
        parts = self.run(jobs, "deliver")
        for s, part in zip(shifts, parts):
            self.held.append(Rows(z.to_section(part, s), self.sub, z.slots, 3))

    def collect(self):
        z = self.z
        units = z.slots * z.sections
        (half,) = self.run([[Copy(self.starts["collect"], units, self.held)]], "collect")
        self.halves = (half, z.to_core(half))

    def advance(self, mean, outs):
        return update(
            self.z,
            self.order,
            self.table,
            self.starts["update"],
            self.first,
            self.count,
            self.state,
            self.halves,
            mean,
            outs,
        )


def per_device(
    weights,
    first_moment,
    second_moment,
    gradients,
    old_section,
    new_section,
    lost_pipe,
    donor_offset,
):
    z = Sizes(weights, new_section)
    order = Order()
    place = jnp.stack([lax.axis_index("pipe"), lax.axis_index("section")]).astype(jnp.int32)
    state = (weights[0, 0], first_moment[0, 0], second_moment[0, 0])
    grads = Gradients(z, order, gradients[0, 0])
    chunks = [
        Chunk(z, order, state, sum(z.chunks[:at]), count) for at, count in enumerate(z.chunks)
    ]
    table, starts = make_plan(z, place, old_section, new_section, lost_pipe, donor_offset)
    for part in (grads, *chunks):
        part.table, part.starts = table, starts

    outs = None
    for name in SEQUENCE:
        if name[0] == "g":
            part = grads
        elif int(name[1]) < len(chunks):
            part = chunks[int(name[1])]
        else:
            continue
        if name in ("ge", "gs", "gx", "gg", "gf"):
            step = dict(e="enter", s="scatter", x="exchange", g="gather", f="finish")[name[1]]
        else:
            step = dict(e="enter", s="spread", a="across", d="deliver", c="collect", u="")[name[0]]
        if step == "enter":
            part.enter(place)
        elif step:
            getattr(part, step)()
        else:
            outs = part.advance(grads.mean, outs)
    return tuple(out.reshape((1, 1, z.slots, z.rows, z.cols)) for out in outs)


def solution(mesh):
    split = P("pipe", "section", None, "tp", None)
    return jax.shard_map(
        per_device,
        mesh=mesh,
        in_specs=(split,) * 4 + (P(),) * 4,
        out_specs=(split,) * 3,
        check_vma=False,
    )
```

time: 153 us -> 160 us (1.046)
  waiting for transfers between devices: 79.4 us -> 97.3 us
  Pallas kernels: 39.3 us -> 31.9 us
  starting transfers between devices: 21.1 us -> 15.6 us
  local copies, waits for them, and re-layouts: 11 us -> 13.4 us
    ppermute x25 -> x20, waiting for transfers between devices: 79.4 us -> 97.3 us  [send(): return lax.ppermute(value, AXES, pairs)]
    pallas_call x25 -> x19, Pallas kernels: 32.1 us -> 25.3 us  [the longest x16 14.8 us: stage(): return order.then(call(table, *operands, *order.last))]
    ppermute x25 -> x20, starting transfers between devices: 21.1 us -> 15.6 us  [send(): return lax.ppermute(value, AXES, pairs)]
    unnamed x30 -> x28, local copies, waits for them, and re-layouts: 11 us -> 13.4 us
    pallas_call x5 -> x4, Pallas kernels: 5.26 us -> 4.85 us  [halve(): return order.then(call(place, *views, *views, *order.last))]
  transfers between devices with their start and end apart: 25 -> 20, of which waited for: 10 -> 12; matrix products, arithmetic and copies ran while one was open for 0% -> 0% of each run, Pallas kernels for 20% -> 13%
where the time goes in v1:
time: 160 us; the launch traced here: 159 us
  waiting for transfers between devices  97.3 us (61%)
  Pallas kernels  31.9 us (20%)
  starting transfers between devices  15.6 us (10%)
  local copies, waits for them, and re-layouts  13.4 us (8%)
    ppermute x20, waiting for transfers between devices, send(): return lax.ppermute(value, AXES, pairs)  97.3 us
    ppermute x20, starting transfers between devices, send(): return lax.ppermute(value, AXES, pairs)  15.6 us
    pallas_call x16, Pallas kernels, stage(): return order.then(call(table, *operands, *order.last))  14.8 us
    unnamed x28, local copies, waits for them, and re-layouts  13.4 us
    pallas_call x3, Pallas kernels, update(): return order.then(call(table, *views, *halves, *mean, *outs, *order.last))  10.5 us
    pallas_call x4, Pallas kernels, halve(): return order.then(call(place, *views, *views, *order.last))  4.85 us
  transfers between devices with their start and end apart: 20, of which 12 were waited for; matrix products, arithmetic and copies ran while one was open for 0% of the time, Pallas kernels for 13%

profile of v1, /device:TPU:0, one launch (start us, length us, event | category | flops | bytes accessed | tf_op | source)
XLA Modules:
  0.0 159.2 jit_solution(17680153669919132124)
XLA Ops:
  0.6 0.1 pad_add_fusion.place_ref
  0.7 1.6 copy-done.9
  2.3 1.6 %halve_gradients.1 = (bf16[1024,512]{1,0:T(8,128)(2,1)S(1)}, bf16[1024,512]{1,0:T(8,128)(2,1)}) custom-call(s32[2]{0:T(128)S(1)} %pad_add_fusion.place_ref, bf16[2,2,2,1,256,512]{5,4,3,2,1,0:T(8,128)(2,1)S(1)} %bitcast.37, bf16[2,2,2,1,256,512]{5,4,3,2,1,0:T(8,128)(2,1)S(1)} %bitcast.38), custom_call_target="tpu_custom_call" | custom-call | flops 1 | bytes 1 | tf_op jit(solution)/shard_map/halve_gradients/pallas_call | solution.py:414
  4.0 0.9 copy-done
  4.9 2.2 %copy-done.2 = f32[1,1,2,1024,512]{4,3,2,1,0:T(8,128)S(1)} copy-done((f32[1,1,2,1024,512]{4,3,2,1,0:T(8,128)S(1)}, f32[1,1,2,1024,512]{4,3,2,1,0:T(8,128)}, u32[]{:S(2)}) %copy-start.2) | copy-done | bytes 4194328
  7.1 1.6 copy-done.5
  8.7 1.8 %halve_state.3 = (bf16[1152,512]{1,0:T(8,128)(2,1)S(1)}, bf16[1152,512]{1,0:T(8,128)(2,1)}) custom-call(s32[2]{0:T(128)S(1)} %pad_add_fusion.place_ref, bf16[2,2,2,8,32,512]{5,4,3,2,1,0:T(8,128)(2,1)S(1)} %bitcast.27, f32[2,2,2,8,32,512]{5,4,3,2,1,0:T(8,128)S(1)} %bitcast.9, f32[2,2,2,8,32,512]{5,4,3,2,1,0:T(8,128)S(1)} %bitcast.18, ...), custom_call_target="tpu_custom_call" | custom-call | flops 1 | bytes 1 | tf_op jit(solution)/shard_map/halve_state/pallas_call | solution.py:414
  10.4 0.5 collective-permute-start
  10.9 1.7 %plan.1.table_ref = s32[2048]{0:T(1024)} custom-call(s32[2]{0:T(128)} %copy-done.12, s32[4,3]{1,0:T(4,128)} %old_ref.1, s32[3]{0:T(128)} %new_ref.1, s32[4]{0:T(128)} %lost_ref.1, s32[3]{0:T(128)} %offset_ref.1), custom_call_target="tpu_custom_call" | custom-call | tf_op jit(solution)/shard_map/plan/pallas_call | solution.py:261
  12.7 2.5 %collective-permute-done.1.refs_1_ = bf16[1024,512]{1,0:T(8,128)(2,1)} collective-permute-done((bf16[1024,512]{1,0:T(8,128)(2,1)}, bf16[1024,512]{1,0:T(8,128)(2,1)}, u32[]{:S(2)}, u32[]{:S(2)}) %collective-permute-start.1) | collective-permute-done | bytes 1048608 | tf_op jit(solution)/shard_map/ppermute | solution.py:73
  15.2 0.7 copy-done.10
  15.9 1.7 %grad_out.1.refs_2_ = bf16[768,512]{1,0:T(8,128)(2,1)S(1)} custom-call(s32[2048]{0:T(1024)S(1)} %copy-done.10, bf16[1024,512]{1,0:T(8,128)(2,1)S(1)} %get-tuple-element.22.refs_6_.refs_0_, bf16[1024,512]{1,0:T(8,128)(2,1)} %collective-permute-done.1.refs_1_, bf16[1152,512]{1,0:T(8,128)(2,1)S(1)} %get-tuple-element.23.refs_2_.refs_0_), custom_call_target="tpu_custom_call" | custom-call | flops 1 | bytes 1 | tf_op jit(solution)/shard_map/grad_out/pallas_call | solution.py:373
  17.6 0.7 spread.3.refs_6_
  18.4 1.0 copy-done.6
  19.4 2.2 %copy-done.3 = f32[1,1,2,1024,512]{4,3,2,1,0:T(8,128)S(1)} copy-done((f32[1,1,2,1024,512]{4,3,2,1,0:T(8,128)S(1)}, f32[1,1,2,1024,512]{4,3,2,1,0:T(8,128)}, u32[]{:S(2)}) %copy-start.3) | copy-done | bytes 4194328
  21.6 0.7 halve_state.4
  22.3 0.4 collective-permute-start.2
  22.8 2.7 %collective-permute-start.4 = (bf16[768,512]{1,0:T(8,128)(2,1)S(1)}, bf16[768,512]{1,0:T(8,128)(2,1)S(1)}, u32[]{:S(2)}, u32[]{:S(2)}) collective-permute-start(bf16[768,512]{1,0:T(8,128)(2,1)S(1)} %grad_out.1.refs_2_), channel_id=1, source_target_pairs={{0,16},{4,20},{8,24},{12,28},{16,0},{20,4},{24,8},{28,12},{1,17},{... | collective-permute-start | bytes 2359304 | tf_op jit(solution)/shard_map/ppermute | solution.py:73
  25.4 1.5 collective-permute-start.5
  26.9 0.7 spread.4.refs_3_
  27.6 1.2 collective-permute-start.3
  28.9 12.7 %collective-permute-done.5.refs_2_ = bf16[576,512]{1,0:T(8,128)(2,1)S(1)} collective-permute-done((bf16[576,512]{1,0:T(8,128)(2,1)S(1)}, bf16[576,512]{1,0:T(8,128)(2,1)S(1)}, u32[]{:S(2)}, u32[]{:S(2)}) %collective-permute-start.5) | collective-permute-done | bytes 589856 | tf_op jit(solution)/shard_map/ppermute | solution.py:73
  41.6 0.7 across.3.refs_3_
  42.4 1.1 collective-permute-done.4.refs_2_
  43.5 1.7 %grad_sum.1.refs_3_.refs_0_ = bf16[768,512]{1,0:T(8,128)(2,1)S(1)} custom-call(s32[2048]{0:T(1024)S(1)} %copy-done.11, bf16[1024,512]{1,0:T(8,128)(2,1)S(1)} %get-tuple-element.22.refs_6_.refs_0_, bf16[1024,512]{1,0:T(8,128)(2,1)} %collective-permute-done.1.refs_1_, bf16[768,512]{1,0:T(8,128)(2,1)S(1)} %collective-permute-done.4.refs_2_, ...), custom_call_target="tpu_custom_call" | custom-call | flops 1 | bytes 1 | tf_op jit(solution)/shard_map/grad_sum/pallas_call | solution.py:373
  45.2 1.8 %collective-permute-start.7 = (bf16[768,512]{1,0:T(8,128)(2,1)S(1)}, bf16[768,512]{1,0:T(8,128)(2,1)S(1)}, u32[]{:S(2)}, u32[]{:S(2)}) collective-permute-start(bf16[768,512]{1,0:T(8,128)(2,1)S(1)} %grad_sum.1.refs_3_.refs_0_), channel_id=1, source_target_pairs={{0,4},{4,0},{8,12},{12,8},{16,20},{20,16},{24,28},{28,24},{1,5},{5... | collective-permute-start | bytes 2359304 | tf_op jit(solution)/shard_map/ppermute | solution.py:73
  47.0 1.5 collective-permute-start.9
  48.5 5.7 %collective-permute-done.3.refs_2_ = bf16[576,512]{1,0:T(8,128)(2,1)S(1)} collective-permute-done((bf16[576,512]{1,0:T(8,128)(2,1)S(1)}, bf16[576,512]{1,0:T(8,128)(2,1)S(1)}, u32[]{:S(2)}, u32[]{:S(2)}) %collective-permute-start.3) | collective-permute-done | bytes 589856 | tf_op jit(solution)/shard_map/ppermute | solution.py:73
  54.2 0.7 across.4.refs_6_
  55.0 0.7 halve_state.5
  55.7 0.1 collective-permute-start.6
  55.8 0.1 collective-permute-start.11
  55.9 14.4 %collective-permute-done.7.refs_1_ = bf16[768,512]{1,0:T(8,128)(2,1)S(1)} collective-permute-done((bf16[768,512]{1,0:T(8,128)(2,1)S(1)}, bf16[768,512]{1,0:T(8,128)(2,1)S(1)}, u32[]{:S(2)}, u32[]{:S(2)}) %collective-permute-start.7) | collective-permute-done | bytes 786464 | tf_op jit(solution)/shard_map/ppermute | solution.py:73
  70.2 1.0 grad_mean.1.refs_2_.refs_0_
  71.2 0.3 collective-permute-start.14
  71.5 0.7 spread.5.refs_4_
  72.3 0.8 deliver.3.refs_3_
  73.1 1.7 %collective-permute-start.13 = (bf16[576,512]{1,0:T(8,128)(2,1)S(1)}, bf16[576,512]{1,0:T(8,128)(2,1)S(1)}, u32[]{:S(2)}, u32[]{:S(2)}) collective-permute-start(bf16[576,512]{1,0:T(8,128)(2,1)S(1)} %deliver.3.refs_3_), channel_id=1, source_target_pairs={{0,4},{4,0},{8,12},{12,8},{16,20},{20,16},{24,28},{28,24},{1,5},{5... | collective-permute-start | bytes 1769480 | tf_op jit(solution)/shard_map/ppermute | solution.py:73
  74.8 0.4 collective-permute-start.8
  75.2 20.9 %collective-permute-done.8.refs_2_ = bf16[384,512]{1,0:T(8,128)(2,1)S(1)} collective-permute-done((bf16[384,512]{1,0:T(8,128)(2,1)S(1)}, bf16[384,512]{1,0:T(8,128)(2,1)S(1)}, u32[]{:S(2)}, u32[]{:S(2)}) %collective-permute-start.8) | collective-permute-done | bytes 393248 | tf_op jit(solution)/shard_map/ppermute | solution.py:73
  96.1 0.7 across.5.refs_4_
  96.8 0.8 deliver.4.refs_2_
  97.6 6.0 %collective-permute-done.14.refs_1_ = bf16[768,512]{1,0:T(8,128)(2,1)S(1)} collective-permute-done((bf16[768,512]{1,0:T(8,128)(2,1)S(1)}, bf16[768,512]{1,0:T(8,128)(2,1)S(1)}, u32[]{:S(2)}, u32[]{:S(2)}) %collective-permute-start.14) | collective-permute-done | bytes 786464 | tf_op jit(solution)/shard_map/ppermute | solution.py:73
  103.6 0.9 mean.1
  104.5 0.9 collect.3.refs_3_.refs_7_
  105.5 0.1 collective-permute-start.15
  105.5 0.5 collective-permute-start.16
  106.0 0.6 collective-permute-start.12
  106.6 3.3 %collective-permute-done.16.refs_6_ = bf16[1024,512]{1,0:T(8,128)(2,1)S(1)} collective-permute-done((bf16[1024,512]{1,0:T(8,128)(2,1)S(1)}, bf16[1024,512]{1,0:T(8,128)(2,1)S(1)}, u32[]{:S(2)}, u32[]{:S(2)}) %collective-permute-start.16) | collective-permute-done | bytes 1048608 | tf_op jit(solution)/shard_map/ppermute | solution.py:73
  109.9 3.7 %update.3 = (bf16[2,2,2,8,32,512]{5,4,3,2,1,0:T(8,128)(2,1)}, f32[2,2,2,8,32,512]{5,4,3,2,1,0:T(8,128)}, f32[2,2,2,8,32,512]{5,4,3,2,1,0:T(8,128)}) custom-call(s32[2048]{0:T(1024)S(1)} %copy-done.11, bf16[2,2,2,8,32,512]{5,4,3,2,1,0:T(8,128)(2,1)S(1)} %bitcast.33, f32[2,2,2,8,32,512]{5,4,3,2,1,0:T(8,128)S(1)} %bitcast.15, ...), custom_call_target="tpu_custom_call" | custom-call | flops 1 | bytes 1 | tf_op jit(solution)/shard_map/update/pallas_call | solution.py:502
  113.6 7.7 %collective-permute-done.12.refs_4_ = bf16[576,512]{1,0:T(8,128)(2,1)S(1)} collective-permute-done((bf16[576,512]{1,0:T(8,128)(2,1)S(1)}, bf16[576,512]{1,0:T(8,128)(2,1)S(1)}, u32[]{:S(2)}, u32[]{:S(2)}) %collective-permute-start.12) | collective-permute-done | bytes 589856 | tf_op jit(solution)/shard_map/ppermute | solution.py:73
  121.3 1.6 copy-done.7
  122.9 0.9 collect.4.refs_4_.refs_3_
  123.9 1.5 collective-permute-start.10
  125.4 14.3 %collective-permute-done.10.refs_3_ = bf16[576,512]{1,0:T(8,128)(2,1)S(1)} collective-permute-done((bf16[576,512]{1,0:T(8,128)(2,1)S(1)}, bf16[576,512]{1,0:T(8,128)(2,1)S(1)}, u32[]{:S(2)}, u32[]{:S(2)}) %collective-permute-start.10) | collective-permute-done | bytes 589856 | tf_op jit(solution)/shard_map/ppermute | solution.py:73
  139.7 0.9 deliver.5.refs_10_
  140.6 0.6 collective-permute-start.17
  141.3 3.8 %update.4 = (bf16[2,2,2,8,32,512]{5,4,3,2,1,0:T(8,128)(2,1)}, f32[2,2,2,8,32,512]{5,4,3,2,1,0:T(8,128)}, f32[2,2,2,8,32,512]{5,4,3,2,1,0:T(8,128)}) custom-call(s32[2048]{0:T(1024)S(1)} %copy-done.11, bf16[2,2,2,8,32,512]{5,4,3,2,1,0:T(8,128)(2,1)S(1)} %bitcast.34, ...), custom_call_target="tpu_custom_call", output_to_operand_aliasing={{0}: (8, {}), {1}: (9, {}), {2}: (10, {})} | custom-call | flops 1 | bytes 1 | tf_op jit(solution)/shard_map/update/pallas_call | solution.py:502
  145.0 6.3 %collective-permute-done.17.refs_4_ = bf16[384,512]{1,0:T(8,128)(2,1)S(1)} collective-permute-done((bf16[384,512]{1,0:T(8,128)(2,1)S(1)}, bf16[384,512]{1,0:T(8,128)(2,1)S(1)}, u32[]{:S(2)}, u32[]{:S(2)}) %collective-permute-start.17) | collective-permute-done | bytes 393248 | tf_op jit(solution)/shard_map/ppermute | solution.py:73
  151.4 1.6 copy-done.8
  153.0 0.9 collect.5.refs_3_.refs_10_
  153.8 0.1 collective-permute-start.19
  153.9 2.3 %collective-permute-done.19.refs_4_ = bf16[768,512]{1,0:T(8,128)(2,1)S(1)} collective-permute-done((bf16[768,512]{1,0:T(8,128)(2,1)S(1)}, bf16[768,512]{1,0:T(8,128)(2,1)S(1)}, u32[]{:S(2)}, u32[]{:S(2)}) %collective-permute-start.19) | collective-permute-done | bytes 786464 | tf_op jit(solution)/shard_map/ppermute | solution.py:73
  156.2 3.0 %update.5 = (bf16[2,2,2,8,32,512]{5,4,3,2,1,0:T(8,128)(2,1)}, f32[2,2,2,8,32,512]{5,4,3,2,1,0:T(8,128)}, f32[2,2,2,8,32,512]{5,4,3,2,1,0:T(8,128)}) custom-call(s32[2048]{0:T(1024)S(1)} %copy-done.11, bf16[2,2,2,8,32,512]{5,4,3,2,1,0:T(8,128)(2,1)S(1)} %bitcast.35, ...), custom_call_target="tpu_custom_call", output_to_operand_aliasing={{0}: (8, {}), {1}: (9, {}), {2}: (10, {})} | custom-call | flops 1 | bytes 1 | tf_op jit(solution)/shard_map/update/pallas_call | solution.py:502
  (29 shorter events, 0.2 us)
Async XLA Ops:
  0.7 3.3 %copy-start.12 = (s32[2]{0:T(128)}, s32[2]{0:T(128)S(1)}, u32[]{:S(2)}) copy-start(s32[2]{0:T(128)S(1)} %pad_add_fusion.place_ref) | copy-start | bytes 28
  0.7 1.6 %copy-start.9 = (bf16[1,1,2,1024,512]{4,3,2,1,0:T(8,128)(2,1)S(1)}, bf16[1,1,2,1024,512]{4,3,2,1,0:T(8,128)(2,1)}, u32[]{:S(2)}) copy-start(bf16[1,1,2,1024,512]{4,3,2,1,0:T(8,128)(2,1)} %param.11) | copy-start | bytes 6291460
  2.3 2.6 %copy-start = (f32[1,1,2,1024,512]{4,3,2,1,0:T(8,128)S(1)}, f32[1,1,2,1024,512]{4,3,2,1,0:T(8,128)}, u32[]{:S(2)}) copy-start(f32[1,1,2,1024,512]{4,3,2,1,0:T(8,128)} %param.9) | copy-start | bytes 12582916
  4.9 2.2 %copy-start.2 = (f32[1,1,2,1024,512]{4,3,2,1,0:T(8,128)S(1)}, f32[1,1,2,1024,512]{4,3,2,1,0:T(8,128)}, u32[]{:S(2)}) copy-start(f32[1,1,2,1024,512]{4,3,2,1,0:T(8,128)} %param.10) | copy-start | bytes 12582916
  7.1 1.6 copy-start.5
  10.4 7.2 %collective-permute-start = (bf16[1152,512]{1,0:T(8,128)(2,1)}, bf16[1152,512]{1,0:T(8,128)(2,1)S(1)}, u32[]{:S(2)}, u32[]{:S(2)}) collective-permute-start(bf16[1152,512]{1,0:T(8,128)(2,1)} %get-tuple-element.24), channel_id=1, source_target_pairs={{0,8},{4,12},{8,0},{12,4},{16,24},{20,28},{24,16},{28,20},{1,9},{5... | collective-permute-start | bytes 3538952 | tf_op jit(solution)/shard_map/ppermute | solution.py:73
  10.9 4.3 %collective-permute-start.1 = (bf16[1024,512]{1,0:T(8,128)(2,1)}, bf16[1024,512]{1,0:T(8,128)(2,1)}, u32[]{:S(2)}, u32[]{:S(2)}) collective-permute-start(bf16[1024,512]{1,0:T(8,128)(2,1)} %get-tuple-element.25), channel_id=1, source_target_pairs={{0,8},{4,12},{8,0},{12,4},{16,24},{20,28},{24,16},{28,20},{1,9},{5... | collective-permute-start | bytes 3145736 | tf_op jit(solution)/shard_map/ppermute | solution.py:73
  15.2 0.7 copy-start.10
  15.9 2.5 %copy-start.1 = (f32[1,1,2,1024,512]{4,3,2,1,0:T(8,128)S(1)}, f32[1,1,2,1024,512]{4,3,2,1,0:T(8,128)}, u32[]{:S(2)}) copy-start(f32[1,1,2,1024,512]{4,3,2,1,0:T(8,128)} %param.9) | copy-start | bytes 12582916
  17.6 1.8 %copy-start.6 = (bf16[1,1,2,1024,512]{4,3,2,1,0:T(8,128)(2,1)S(1)}, bf16[1,1,2,1024,512]{4,3,2,1,0:T(8,128)(2,1)}, u32[]{:S(2)}) copy-start(bf16[1,1,2,1024,512]{4,3,2,1,0:T(8,128)(2,1)} %param.8) | copy-start | bytes 6291460
  17.6 1.8 %copy-start.13 = (s32[2]{0:T(128)S(1)}, s32[2]{0:T(128)}, u32[]{:S(2)}) copy-start(s32[2]{0:T(128)} %copy-done.12) | copy-start | bytes 28
  19.4 2.2 %copy-start.3 = (f32[1,1,2,1024,512]{4,3,2,1,0:T(8,128)S(1)}, f32[1,1,2,1024,512]{4,3,2,1,0:T(8,128)}, u32[]{:S(2)}) copy-start(f32[1,1,2,1024,512]{4,3,2,1,0:T(8,128)} %param.10) | copy-start | bytes 12582916
  21.6 5.4 %copy-start.11 = (s32[2048]{0:T(1024)S(1)}, s32[2048]{0:T(1024)}, u32[]{:S(2)}) copy-start(s32[2048]{0:T(1024)} %plan.1.table_ref) | copy-start | bytes 24580
  22.3 4.6 %collective-permute-start.2 = (bf16[1152,512]{1,0:T(8,128)(2,1)S(1)}, bf16[1152,512]{1,0:T(8,128)(2,1)S(1)}, u32[]{:S(2)}, u32[]{:S(2)}) collective-permute-start(bf16[1152,512]{1,0:T(8,128)(2,1)S(1)} %get-tuple-element.27), channel_id=1, source_target_pairs={{0,8},{4,12},{8,0},{12,4},{16,24},{20,28},{24,16},{28,20},{1,9},{5... | collective-permute-start | bytes 3538952 | tf_op jit(solution)/shard_map/ppermute | solution.py:73
  22.8 20.7 %collective-permute-start.4 = (bf16[768,512]{1,0:T(8,128)(2,1)S(1)}, bf16[768,512]{1,0:T(8,128)(2,1)S(1)}, u32[]{:S(2)}, u32[]{:S(2)}) collective-permute-start(bf16[768,512]{1,0:T(8,128)(2,1)S(1)} %grad_out.1.refs_2_), channel_id=1, source_target_pairs={{0,16},{4,20},{8,24},{12,28},{16,0},{20,4},{24,8},{28,12},{1,17},{... | collective-permute-start | bytes 2359304 | tf_op jit(solution)/shard_map/ppermute | solution.py:73
  25.4 16.2 %collective-permute-start.5 = (bf16[576,512]{1,0:T(8,128)(2,1)S(1)}, bf16[576,512]{1,0:T(8,128)(2,1)S(1)}, u32[]{:S(2)}, u32[]{:S(2)}) collective-permute-start(bf16[576,512]{1,0:T(8,128)(2,1)S(1)} %spread.3.refs_6_), channel_id=1, source_target_pairs={{0,4},{4,0},{8,12},{12,8},{16,20},{20,16},{24,28},{28,24},{1,5},{5... | collective-permute-start | bytes 1769480 | tf_op jit(solution)/shard_map/ppermute | solution.py:73
  27.6 26.6 %collective-permute-start.3 = (bf16[576,512]{1,0:T(8,128)(2,1)S(1)}, bf16[576,512]{1,0:T(8,128)(2,1)S(1)}, u32[]{:S(2)}, u32[]{:S(2)}) collective-permute-start(bf16[576,512]{1,0:T(8,128)(2,1)S(1)} %spread.4.refs_3_), channel_id=1, source_target_pairs={{0,4},{4,0},{8,12},{12,8},{16,20},{20,16},{24,28},{28,24},{1,5},{5... | collective-permute-start | bytes 1769480 | tf_op jit(solution)/shard_map/ppermute | solution.py:73
  45.2 9.8 %copy-start.4 = (f32[1,1,2,1024,512]{4,3,2,1,0:T(8,128)S(1)}, f32[1,1,2,1024,512]{4,3,2,1,0:T(8,128)}, u32[]{:S(2)}) copy-start(f32[1,1,2,1024,512]{4,3,2,1,0:T(8,128)} %param.10) | copy-start | bytes 12582916
  45.2 25.0 %collective-permute-start.7 = (bf16[768,512]{1,0:T(8,128)(2,1)S(1)}, bf16[768,512]{1,0:T(8,128)(2,1)S(1)}, u32[]{:S(2)}, u32[]{:S(2)}) collective-permute-start(bf16[768,512]{1,0:T(8,128)(2,1)S(1)} %grad_sum.1.refs_3_.refs_0_), channel_id=1, source_target_pairs={{0,4},{4,0},{8,12},{12,8},{16,20},{20,16},{24,28},{28,24},{1,5},{5... | collective-permute-start | bytes 2359304 | tf_op jit(solution)/shard_map/ppermute | solution.py:73
  47.0 25.3 %collective-permute-start.9 = (bf16[864,512]{1,0:T(8,128)(2,1)S(1)}, bf16[864,512]{1,0:T(8,128)(2,1)S(1)}, u32[]{:S(2)}, u32[]{:S(2)}) collective-permute-start(bf16[864,512]{1,0:T(8,128)(2,1)S(1)} %across.3.refs_3_), channel_id=1, source_target_pairs={{0,16},{4,20},{8,24},{12,28},{16,0},{20,4},{24,8},{28,12},{1,17},{... | collective-permute-start | bytes 2654216 | tf_op jit(solution)/shard_map/ppermute | solution.py:73
  55.7 15.8 %collective-permute-start.6 = (bf16[768,512]{1,0:T(8,128)(2,1)S(1)}, bf16[768,512]{1,0:T(8,128)(2,1)S(1)}, u32[]{:S(2)}, u32[]{:S(2)}) collective-permute-start(bf16[768,512]{1,0:T(8,128)(2,1)S(1)} %get-tuple-element.29), channel_id=1, source_target_pairs={{0,8},{4,12},{8,0},{12,4},{16,24},{20,28},{24,16},{28,20},{1,9},{5... | collective-permute-start | bytes 2359304 | tf_op jit(solution)/shard_map/ppermute | solution.py:73
  55.8 41.0 %collective-permute-start.11 = (bf16[864,512]{1,0:T(8,128)(2,1)S(1)}, bf16[864,512]{1,0:T(8,128)(2,1)S(1)}, u32[]{:S(2)}, u32[]{:S(2)}) collective-permute-start(bf16[864,512]{1,0:T(8,128)(2,1)S(1)} %across.4.refs_6_), channel_id=1, source_target_pairs={{0,16},{4,20},{8,24},{12,28},{16,0},{20,4},{24,8},{28,12},{1,17},{... | collective-permute-start | bytes 2654216 | tf_op jit(solution)/shard_map/ppermute | solution.py:73
  71.2 32.4 %collective-permute-start.14 = (bf16[768,512]{1,0:T(8,128)(2,1)S(1)}, bf16[768,512]{1,0:T(8,128)(2,1)S(1)}, u32[]{:S(2)}, u32[]{:S(2)}) collective-permute-start(bf16[768,512]{1,0:T(8,128)(2,1)S(1)} %grad_mean.1.refs_2_.refs_0_), channel_id=1, source_target_pairs={{0,16},{4,20},{8,24},{12,28},{16,0},{20,4},{24,8},{28,12},{1,17},{... | collective-permute-start | bytes 2359304 | tf_op jit(solution)/shard_map/ppermute | solution.py:73
  73.1 31.5 %collective-permute-start.13 = (bf16[576,512]{1,0:T(8,128)(2,1)S(1)}, bf16[576,512]{1,0:T(8,128)(2,1)S(1)}, u32[]{:S(2)}, u32[]{:S(2)}) collective-permute-start(bf16[576,512]{1,0:T(8,128)(2,1)S(1)} %deliver.3.refs_3_), channel_id=1, source_target_pairs={{0,4},{4,0},{8,12},{12,8},{16,20},{20,16},{24,28},{28,24},{1,5},{5... | collective-permute-start | bytes 1769480 | tf_op jit(solution)/shard_map/ppermute | solution.py:73
  74.8 21.3 %collective-permute-start.8 = (bf16[384,512]{1,0:T(8,128)(2,1)S(1)}, bf16[384,512]{1,0:T(8,128)(2,1)S(1)}, u32[]{:S(2)}, u32[]{:S(2)}) collective-permute-start(bf16[384,512]{1,0:T(8,128)(2,1)S(1)} %spread.5.refs_4_), channel_id=1, source_target_pairs={{0,4},{4,0},{8,12},{12,8},{16,20},{20,16},{24,28},{28,24},{1,5},{5... | collective-permute-start | bytes 1179656 | tf_op jit(solution)/shard_map/ppermute | solution.py:73
  105.5 4.4 %collective-permute-start.15 = (bf16[1152,512]{1,0:T(8,128)(2,1)S(1)}, bf16[1152,512]{1,0:T(8,128)(2,1)S(1)}, u32[]{:S(2)}, u32[]{:S(2)}) collective-permute-start(bf16[1152,512]{1,0:T(8,128)(2,1)S(1)} %collect.3.refs_3_.refs_7_), channel_id=1, source_target_pairs={{0,8},{4,12},{8,0},{12,4},{16,24},{20,28},{24,16},{28,20},{1,9},{5... | collective-permute-start | bytes 3538952 | tf_op jit(solution)/shard_map/ppermute | solution.py:73
  105.5 4.3 %collective-permute-start.16 = (bf16[1024,512]{1,0:T(8,128)(2,1)S(1)}, bf16[1024,512]{1,0:T(8,128)(2,1)S(1)}, u32[]{:S(2)}, u32[]{:S(2)}) collective-permute-start(bf16[1024,512]{1,0:T(8,128)(2,1)S(1)} %get-tuple-element.30.refs_5_), channel_id=1, source_target_pairs={{0,8},{4,12},{8,0},{12,4},{16,24},{20,28},{24,16},{28,20},{1,9},{5... | collective-permute-start | bytes 3145736 | tf_op jit(solution)/shard_map/ppermute | solution.py:73
  106.0 15.3 %collective-permute-start.12 = (bf16[576,512]{1,0:T(8,128)(2,1)S(1)}, bf16[576,512]{1,0:T(8,128)(2,1)S(1)}, u32[]{:S(2)}, u32[]{:S(2)}) collective-permute-start(bf16[576,512]{1,0:T(8,128)(2,1)S(1)} %deliver.4.refs_2_), channel_id=1, source_target_pairs={{0,4},{4,0},{8,12},{12,8},{16,20},{20,16},{24,28},{28,24},{1,5},{5... | collective-permute-start | bytes 1769480 | tf_op jit(solution)/shard_map/ppermute | solution.py:73
  121.3 1.6 copy-start.7
  123.8 17.4 %collective-permute-start.18 = (bf16[1152,512]{1,0:T(8,128)(2,1)S(1)}, bf16[1152,512]{1,0:T(8,128)(2,1)S(1)}, u32[]{:S(2)}, u32[]{:S(2)}) collective-permute-start(bf16[1152,512]{1,0:T(8,128)(2,1)S(1)} %collect.4.refs_4_.refs_3_), channel_id=1, source_target_pairs={{0,8},{4,12},{8,0},{12,4},{16,24},{20,28},{24,16},{28,20},{1,9},{5... | collective-permute-start | bytes 3538952 | tf_op jit(solution)/shard_map/ppermute | solution.py:73
  123.9 15.7 %collective-permute-start.10 = (bf16[576,512]{1,0:T(8,128)(2,1)S(1)}, bf16[576,512]{1,0:T(8,128)(2,1)S(1)}, u32[]{:S(2)}, u32[]{:S(2)}) collective-permute-start(bf16[576,512]{1,0:T(8,128)(2,1)S(1)} %across.5.refs_4_), channel_id=1, source_target_pairs={{0,16},{4,20},{8,24},{12,28},{16,0},{20,4},{24,8},{28,12},{1,17},{... | collective-permute-start | bytes 1769480 | tf_op jit(solution)/shard_map/ppermute | solution.py:73
  140.6 10.7 %collective-permute-start.17 = (bf16[384,512]{1,0:T(8,128)(2,1)S(1)}, bf16[384,512]{1,0:T(8,128)(2,1)S(1)}, u32[]{:S(2)}, u32[]{:S(2)}) collective-permute-start(bf16[384,512]{1,0:T(8,128)(2,1)S(1)} %deliver.5.refs_10_), channel_id=1, source_target_pairs={{0,4},{4,0},{8,12},{12,8},{16,20},{20,16},{24,28},{28,24},{1,5},{5... | collective-permute-start | bytes 1179656 | tf_op jit(solution)/shard_map/ppermute | solution.py:73
  151.4 1.6 copy-start.8
  153.8 2.4 %collective-permute-start.19 = (bf16[768,512]{1,0:T(8,128)(2,1)S(1)}, bf16[768,512]{1,0:T(8,128)(2,1)S(1)}, u32[]{:S(2)}, u32[]{:S(2)}) collective-permute-start(bf16[768,512]{1,0:T(8,128)(2,1)S(1)} %collect.5.refs_3_.refs_10_), channel_id=1, source_target_pairs={{0,8},{4,12},{8,0},{12,4},{16,24},{20,28},{24,16},{28,20},{1,9},{5... | collective-permute-start | bytes 2359304 | tf_op jit(solution)/shard_map/ppermute | solution.py:73

commit v2 on v1

--- a/solution.py
+++ b/solution.py
@@ -1,3 +1,5 @@
+import math
+
 import jax
 import jax.numpy as jnp
 from jax import lax
@@ -12,12 +14,9 @@
 DECAY_RATE = 0.1
 
 CORES = 2
-CHUNKS = (3, 3, 2)
-SEQUENCE = (
-    *("ge", "e0", "gs", "s0", "e1", "s1", "a0", "gx", "a1", "e2", "gg", "s2"),
-    *("d0", "a2", "d1", "gf", "c0", "u0", "c1", "d2", "u1", "c2", "u2"),
-)
-VMEM = 24 * 1024 * 1024
+CHUNKS = 1
+AFTER = {}
+VMEM = 40 * 1024 * 1024
 AXES = ("pipe", "section")
 
 
@@ -50,10 +49,9 @@
         self.layers = new_section.shape[0]
         self.half = self.rows // CORES
         self.band = self.half // self.sections
-        units = sum(CHUNKS)
-        self.chunks = CHUNKS if self.band % (16 * units) == 0 else (1,)
-        self.units = sum(self.chunks)
+        self.units = CHUNKS if self.band % (16 * CHUNKS) == 0 else 1
         self.unit = self.band // self.units
+        self.block = math.gcd(self.unit, 32)
         self.grad_band = self.half // self.groups
         doubles = self.layers - self.sections
         widest = 0
@@ -279,13 +277,17 @@
 
 class Order:
     def __init__(self):
-        self.last = []
+        self.results, self.last, self.name = {}, [], None
+
+    def begin(self, name):
+        self.name = name
+        self.last = [self.results[at] for at in AFTER.get(name, ()) if at in self.results]
 
     def specs(self):
         return [pl.BlockSpec(memory_space=pl.ANY)] * len(self.last)
 
     def then(self, result):
-        self.last = [result[0]]
+        self.results[self.name] = result[0]
         return result
 
 
@@ -293,6 +295,8 @@
 VMEM_SPEC = pl.BlockSpec(memory_space=pltpu.VMEM)
 PARAMS = pltpu.CompilerParams(vmem_limit_bytes=VMEM)
 COST = pl.CostEstimate(flops=1, bytes_accessed=1, transcendentals=0)
+
+UPDATE_COST = pl.CostEstimate(flops=1, bytes_accessed=1, transcendentals=0)
 
 
 class Rows:
@@ -373,7 +377,7 @@
     return order.then(call(table, *operands, *order.last))
 
 
-def halve(z, order, place, arrays, first, count, units):
+def halve(z, order, place, arrays, first, count, units, name):
     unit = z.band // units
     views = [a.reshape(z.slots, CORES, z.sections, units, unit, z.cols) for a in arrays]
 
@@ -409,83 +413,81 @@
         out_shape=(out, out),
         compiler_params=PARAMS,
         cost_estimate=COST,
-        name="halve_state" if len(arrays) > 1 else "halve_gradients",
+        name="halve_" + name,
     )
     return order.then(call(place, *views, *views, *order.last))
 
 
-def update(z, order, table, start, first, count, state, halves, mean, outs):
-    sub = count * z.unit
-    per_slot = z.sections * sub
-    views = [a.reshape(z.slots, CORES, z.sections, z.units, z.unit, z.cols) for a in state]
-    outs = [] if outs is None else list(outs)
+def update(z, order, table, start, state, rebuilt, mean):
+    views = [a.reshape(z.slots, CORES, z.half, z.cols) for a in state]
+    halves = [chunk[part] for part in range(2) for chunk in rebuilt]
 
     def kernel(table_ref, *refs):
-        local_refs, half_refs, mean_refs = refs[:3], refs[3:5], refs[5:7]
+        local_refs, mean_refs, half_refs = refs[:3], refs[3:5], refs[5:-3]
         out_w, out_one, out_two = refs[-3:]
-        slot = pl.program_id(0)
+        slot, half = pl.program_id(0), pl.program_id(1)
         is_lost = table_ref[start] != 0
-        core = table_ref[start + 1]
+        mine = table_ref[start + 1] == half
         found = table_ref[start + 2 + slot] != 0
 
-        def step(half, band, unit, weight, one, two, grad):
-            grad = grad.astype(jnp.float32) * (1.0 / z.pipes)
-            weight = weight.astype(jnp.float32)
-            next_one = BETA_ONE * one.astype(jnp.float32) + (1.0 - BETA_ONE) * grad
-            next_two = BETA_TWO * two.astype(jnp.float32) + (1.0 - BETA_TWO) * grad * grad
+        def each(source, lost):
+            @pl.loop(0, z.unit // z.block)
+            def _(at):
+                for band in range(z.sections):
+                    for unit in range(z.units):
+                        one_block(source, lost, band, unit, at)
+
+        def one_block(source, lost, band, unit, at):
+            place = at * z.block
+            row = pl.ds(pl.multiple_of(band * z.band + unit * z.unit + place, 16), z.block)
+            mean_row = pl.multiple_of(slot * z.half + band * z.band + unit * z.unit + place, 16)
+            grad = mean_refs[source][pl.ds(mean_row, z.block)].astype(jnp.float32)
+            grad = grad * (1.0 / z.pipes)
+            if lost:
+                here = half_refs[source * len(rebuilt) : (source + 1) * len(rebuilt)]
+                from_row = (slot * z.sections + band) * z.unit + place
+                from_row = pl.ds(pl.multiple_of(from_row, 16), z.block)
+                old = [here[array * z.units + unit][from_row] for array in range(3)]
+            else:
+                old = [ref[0, 0, row] for ref in local_refs]
+            weight, one, two = [value.astype(jnp.float32) for value in old]
+            next_one = BETA_ONE * one + (1.0 - BETA_ONE) * grad
+            next_two = BETA_TWO * two + (1.0 - BETA_TWO) * grad * grad
             move = next_one / (jnp.sqrt(next_two) + EPSILON) + DECAY_RATE * weight
-            out_w[0, half, band, unit] = (weight - LEARN_RATE * move).astype(out_w.dtype)
-            out_one[0, half, band, unit] = next_one
-            out_two[0, half, band, unit] = next_two
-
-        def each(half, source, lost):
-            for band in range(z.sections):
-                for unit in range(count):
-                    row = slot * per_slot + band * sub + unit * z.unit
-
-                    def rows(at):
-                        return pl.ds(pl.multiple_of(at, 16), z.unit)
-
-                    mean_row = slot * z.half + band * z.band + (first + unit) * z.unit
-                    grad = mean_refs[source][rows(mean_row)]
-                    if lost:
-                        ref = half_refs[source]
-                        old = [ref[rows(a * z.slots * per_slot + row)] for a in range(3)]
-                    else:
-                        old = [ref[0, half, band, unit] for ref in local_refs]
-                    step(half, band, unit, *old, grad)
-
-        for half in range(CORES):
-            for source in range(2):
-                mine = both(found, (core == half) == (source == 0))
-
-                @pl.when(both(mine, is_lost))
-                def _(half=half, source=source):
-                    each(half, source, True)
-
-                @pl.when(both(mine, jnp.logical_not(is_lost)))
-                def _(half=half, source=source):
-                    each(half, source, False)
+            out_w[0, 0, row] = (weight - LEARN_RATE * move).astype(out_w.dtype)
+            out_one[0, 0, row] = next_one
+            out_two[0, 0, row] = next_two
+
+        for source in range(2):
+            ours = both(found, mine == (source == 0))
+
+            @pl.when(both(ours, is_lost))
+            def _(source=source):
+                each(source, True)
+
+            @pl.when(both(ours, jnp.logical_not(is_lost)))
+            def _(source=source):
+                each(source, False)
 
         @pl.when(jnp.logical_not(found))
         def _():
             for ref in (out_w, out_one, out_two):
                 ref[...] = jnp.zeros(ref.shape, ref.dtype)
 
-    def local(slot, table_ref):
-        return (slot * (1 - table_ref[start]), 0, 0, first // count, 0, 0)
-
-    block = (1, CORES, z.sections, count, z.unit, z.cols)
-    out_spec = pl.BlockSpec(block, lambda slot, table_ref: (slot, 0, 0, first // count, 0, 0))
+    def local(slot, half, table_ref):
+        keep = 1 - table_ref[start]
+        return (slot * keep, half * keep, 0, 0)
+
+    block = (1, 1, z.half, z.cols)
+    out_spec = pl.BlockSpec(block, lambda slot, half, table_ref: (slot, half, 0, 0))
     shape = views[0].shape
     call = pl.pallas_call(
         kernel,
         grid_spec=pltpu.PrefetchScalarGridSpec(
             num_scalar_prefetch=1,
-            grid=(z.slots,),
+            grid=(z.slots, CORES),
             in_specs=[pl.BlockSpec(block, local)] * 3
-            + [VMEM_SPEC] * 4
-            + [pl.BlockSpec(memory_space=pl.ANY)] * len(outs)
+            + [VMEM_SPEC] * (2 + len(halves))
             + order.specs(),
             out_specs=[out_spec] * 3,
         ),
@@ -494,12 +496,11 @@
             jax.ShapeDtypeStruct(shape, jnp.float32),
             jax.ShapeDtypeStruct(shape, jnp.float32),
         ),
-        input_output_aliases={8 + at: at for at in range(len(outs))},
         compiler_params=PARAMS,
-        cost_estimate=COST,
+        cost_estimate=UPDATE_COST,
         name="update",
     )
-    return order.then(call(table, *views, *halves, *mean, *outs, *order.last))
+    return order.then(call(table, *views, *mean, *halves, *order.last))
 
 
 class Gradients:
@@ -514,7 +515,7 @@
 
     def enter(self, place):
         z = self.z
-        own, theirs = halve(z, self.order, place, (self.grads,), 0, 1, 1)
+        own, theirs = halve(z, self.order, place, (self.grads,), 0, 1, 1, "gradients")
         self.held = [
             Rows(flat, z.grad_band, z.slots * z.groups) for flat in (own, z.to_core(theirs))
         ]
@@ -551,18 +552,17 @@
 
 
 class Chunk:
-    def __init__(self, z, order, state, first, count):
-        self.z, self.order, self.state = z, order, state
-        self.first, self.count, self.sub = first, count, count * z.unit
+    def __init__(self, z, order, array, first):
+        self.z, self.order, self.array, self.first = z, order, array, first
 
     def run(self, outputs, name):
         return stage(self.z, self.order, self.table, outputs, name)
 
     def enter(self, place):
         z = self.z
-        own, theirs = halve(z, self.order, place, self.state, self.first, self.count, z.units)
+        own, theirs = halve(z, self.order, place, (self.array,), self.first, 1, z.units, "state")
         held = z.slots * z.sections
-        self.held = [Rows(flat, self.sub, held, 3) for flat in (own, z.to_core(theirs))]
+        self.held = [Rows(flat, z.unit, held) for flat in (own, z.to_core(theirs))]
 
     def spread(self):
         z = self.z
@@ -570,13 +570,13 @@
         jobs = [[Copy(self.starts["spread", s], z.channels, self.held)] for s in shifts]
         parts = self.run(jobs, "spread")
         for s, part in zip(shifts, parts):
-            self.held.append(Rows(z.to_section(part, s), self.sub, z.channels, 3))
+            self.held.append(Rows(z.to_section(part, s), z.unit, z.channels))
 
     def across(self):
         z = self.z
         (part,) = self.run([[Copy(self.starts["across"], z.layers, self.held)]], "across")
         for s in range(1, z.groups):
-            self.held.append(Rows(z.to_group(part, s), self.sub, z.layers, 3))
+            self.held.append(Rows(z.to_group(part, s), z.unit, z.layers))
 
     def deliver(self):
         z = self.z
@@ -584,27 +584,13 @@
         jobs = [[Copy(self.starts["deliver", s], z.slots, self.held)] for s in shifts]
         parts = self.run(jobs, "deliver")
         for s, part in zip(shifts, parts):
-            self.held.append(Rows(z.to_section(part, s), self.sub, z.slots, 3))
+            self.held.append(Rows(z.to_section(part, s), z.unit, z.slots))
 
     def collect(self):
         z = self.z
         units = z.slots * z.sections
         (half,) = self.run([[Copy(self.starts["collect"], units, self.held)]], "collect")
         self.halves = (half, z.to_core(half))
-
-    def advance(self, mean, outs):
-        return update(
-            self.z,
-            self.order,
-            self.table,
-            self.starts["update"],
-            self.first,
-            self.count,
-            self.state,
-            self.halves,
-            mean,
-            outs,
-        )
 
 
 def per_device(
@@ -622,31 +608,34 @@
     place = jnp.stack([lax.axis_index("pipe"), lax.axis_index("section")]).astype(jnp.int32)
     state = (weights[0, 0], first_moment[0, 0], second_moment[0, 0])
     grads = Gradients(z, order, gradients[0, 0])
-    chunks = [
-        Chunk(z, order, state, sum(z.chunks[:at]), count) for at, count in enumerate(z.chunks)
-    ]
+    chunks = [Chunk(z, order, array, at) for array in state for at in range(z.units)]
     table, starts = make_plan(z, place, old_section, new_section, lost_pipe, donor_offset)
     for part in (grads, *chunks):
         part.table, part.starts = table, starts
 
-    outs = None
-    for name in SEQUENCE:
-        if name[0] == "g":
-            part = grads
-        elif int(name[1]) < len(chunks):
-            part = chunks[int(name[1])]
-        else:
-            continue
-        if name in ("ge", "gs", "gx", "gg", "gf"):
-            step = dict(e="enter", s="scatter", x="exchange", g="gather", f="finish")[name[1]]
-        else:
-            step = dict(e="enter", s="spread", a="across", d="deliver", c="collect", u="")[name[0]]
-        if step == "enter":
-            part.enter(place)
-        elif step:
-            getattr(part, step)()
-        else:
-            outs = part.advance(grads.mean, outs)
+    def each(step, *args):
+        for at, chunk in enumerate(chunks):
+            order.begin(step[0] + str(at))
+            getattr(chunk, step)(*args)
+
+    order.begin("ge")
+    grads.enter(place)
+    each("enter", place)
+    order.begin("gs")
+    grads.scatter()
+    each("spread")
+    order.begin("gx")
+    grads.exchange()
+    each("across")
+    order.begin("gg")
+    grads.gather()
+    each("deliver")
+    order.begin("gf")
+    grads.finish()
+    each("collect")
+    order.begin("u")
+    rebuilt = [chunk.halves for chunk in chunks]
+    outs = update(z, order, table, starts["update"], state, rebuilt, grads.mean)
     return tuple(out.reshape((1, 1, z.slots, z.rows, z.cols)) for out in outs)
 
 

time: 160 us -> 130 us (0.81)
  waiting for transfers between devices: 97.3 us -> 67 us
  Pallas kernels: 31.9 us -> 38.8 us
  local copies, waits for them, and re-layouts: 13.4 us -> 7.05 us
    ppermute x20, waiting for transfers between devices: 97.3 us -> 67 us  [send(): return lax.ppermute(value, AXES, pairs)]
    pallas_call x16, Pallas kernels: 14.8 us -> 21.3 us  [stage(): return order.then(call(table, *operands, *order.last))]
    unnamed x28, local copies, waits for them, and re-layouts: 13.4 us -> 7.05 us
    pallas_call x4, Pallas kernels: 4.85 us -> 6.77 us  [halve(): return order.then(call(place, *views, *views, *order.last))]
    pallas_call x3 -> x1, Pallas kernels: 10.5 us -> 8.98 us  [update(): return order.then(call(table, *views, *mean, *halves, *order.last))]
  transfers between devices with their start and end apart: 20 -> 20, of which waited for: 12 -> 10; matrix products, arithmetic and copies ran while one was open for 0% -> 0% of each run, Pallas kernels for 13% -> 22%
where the time goes in v2:
time: 130 us; the launch traced here: 129 us
  waiting for transfers between devices  67 us (52%)
  Pallas kernels  38.8 us (30%)
  starting transfers between devices  15 us (12%)
  local copies, waits for them, and re-layouts  7.05 us (5%)
    ppermute x20, waiting for transfers between devices, send(): return lax.ppermute(value, AXES, pairs)  67 us
    pallas_call x16, Pallas kernels, stage(): return order.then(call(table, *operands, *order.last))  21.3 us
    ppermute x20, starting transfers between devices, send(): return lax.ppermute(value, AXES, pairs)  15 us
    pallas_call x1, Pallas kernels, update(): return order.then(call(table, *views, *mean, *halves, *order.last))  8.98 us
    unnamed x28, local copies, waits for them, and re-layouts  7.05 us
    pallas_call x4, Pallas kernels, halve(): return order.then(call(place, *views, *views, *order.last))  6.77 us
  transfers between devices with their start and end apart: 20, of which 10 were waited for; matrix products, arithmetic and copies ran while one was open for 0% of the time, Pallas kernels for 22%

profile of v2, /device:TPU:0, one launch (start us, length us, event | category | flops | bytes accessed | tf_op | source)
XLA Modules:
  0.0 128.8 jit_solution(17821342078894520053)
XLA Ops:
  0.6 0.0 copy-start.1
  0.6 0.1 pad_add_fusion.place_ref
  0.7 1.7 %copy-done.8 = bf16[1,1,2,1024,512]{4,3,2,1,0:T(8,128)(2,1)S(1)} copy-done((bf16[1,1,2,1024,512]{4,3,2,1,0:T(8,128)(2,1)S(1)}, bf16[1,1,2,1024,512]{4,3,2,1,0:T(8,128)(2,1)}, u32[]{:S(2)}) %copy-start.8) | copy-done | bytes 2097176
  2.5 1.6 %halve_gradients.1 = (bf16[1024,512]{1,0:T(8,128)(2,1)S(1)}, bf16[1024,512]{1,0:T(8,128)(2,1)}) custom-call(s32[2]{0:T(128)S(1)} %pad_add_fusion.place_ref, bf16[2,2,2,1,256,512]{5,4,3,2,1,0:T(8,128)(2,1)S(1)} %bitcast.21, bf16[2,2,2,1,256,512]{5,4,3,2,1,0:T(8,128)(2,1)S(1)} %bitcast.22), custom_call_target="tpu_custom_call" | custom-call | flops 1 | bytes 1 | tf_op jit(solution)/shard_map/halve_gradients/pallas_call | solution.py:418
  4.1 0.5 collective-permute-start
  4.6 1.8 %halve_state.5 = (bf16[1024,512]{1,0:T(8,128)(2,1)S(1)}, bf16[1024,512]{1,0:T(8,128)(2,1)}) custom-call(s32[2]{0:T(128)S(1)} %pad_add_fusion.place_ref, f32[2,2,2,1,256,512]{5,4,3,2,1,0:T(8,128)S(1)} %bitcast.16, f32[2,2,2,1,256,512]{5,4,3,2,1,0:T(8,128)S(1)} %bitcast.17), custom_call_target="tpu_custom_call" | custom-call | flops 1 | bytes 1 | tf_op jit(solution)/shard_map/halve_state/pallas_call | solution.py:418
  6.3 1.0 copy-done.5
  7.3 0.1 collective-permute-start.13
  7.4 1.7 %halve_state.4 = (bf16[1024,512]{1,0:T(8,128)(2,1)S(1)}, bf16[1024,512]{1,0:T(8,128)(2,1)}) custom-call(s32[2]{0:T(128)S(1)} %pad_add_fusion.place_ref, f32[2,2,2,1,256,512]{5,4,3,2,1,0:T(8,128)S(1)} %bitcast.13, f32[2,2,2,1,256,512]{5,4,3,2,1,0:T(8,128)S(1)} %bitcast.14), custom_call_target="tpu_custom_call" | custom-call | flops 1 | bytes 1 | tf_op jit(solution)/shard_map/halve_state/pallas_call | solution.py:418
  9.1 1.1 copy-done.3
  10.2 0.5 collective-permute-start.9
  10.7 1.7 %halve_state.3 = (bf16[1024,512]{1,0:T(8,128)(2,1)S(1)}, bf16[1024,512]{1,0:T(8,128)(2,1)}) custom-call(s32[2]{0:T(128)S(1)} %pad_add_fusion.place_ref, bf16[2,2,2,1,256,512]{5,4,3,2,1,0:T(8,128)(2,1)S(1)} %bitcast.18, bf16[2,2,2,1,256,512]{5,4,3,2,1,0:T(8,128)(2,1)S(1)} %bitcast.19), custom_call_target="tpu_custom_call" | custom-call | flops 1 | bytes 1 | tf_op jit(solution)/shard_map/halve_state/pallas_call | solution.py:418
  12.4 0.0 collective-permute-start.5
  12.4 1.7 %plan.1.table_ref = s32[2048]{0:T(1024)} custom-call(s32[2]{0:T(128)} %copy-done.13, s32[4,3]{1,0:T(4,128)} %old_ref.1, s32[3]{0:T(128)} %new_ref.1, s32[4]{0:T(128)} %lost_ref.1, s32[3]{0:T(128)} %offset_ref.1), custom_call_target="tpu_custom_call" | custom-call | tf_op jit(solution)/shard_map/plan/pallas_call | solution.py:259
  14.1 0.0 copy-start.10
  14.2 1.3 %copy-done.10 = bf16[1024,512]{1,0:T(8,128)(2,1)S(1)} copy-done((bf16[1024,512]{1,0:T(8,128)(2,1)S(1)}, bf16[1024,512]{1,0:T(8,128)(2,1)}, u32[]{:S(2)}) %copy-start.10) | copy-done | bytes 1048600
  15.5 0.7 copy-done.12
  16.2 1.6 %grad_out.1 = bf16[768,512]{1,0:T(8,128)(2,1)S(1)} custom-call(s32[2048]{0:T(1024)S(1)} %copy-done.12, bf16[1024,512]{1,0:T(8,128)(2,1)S(1)} %copy-done.10, bf16[1024,512]{1,0:T(8,128)(2,1)} %collective-permute-done.refs_1_), custom_call_target="tpu_custom_call" | custom-call | flops 1 | bytes 1 | tf_op jit(solution)/shard_map/grad_out/pallas_call | solution.py:377
  17.8 3.1 %collective-permute-start.1 = (bf16[768,512]{1,0:T(8,128)(2,1)S(1)}, bf16[768,512]{1,0:T(8,128)(2,1)S(1)}, u32[]{:S(2)}, u32[]{:S(2)}) collective-permute-start(bf16[768,512]{1,0:T(8,128)(2,1)S(1)} %grad_out.1), channel_id=1, source_target_pairs={{0,16},{4,20},{8,24},{12,28},{16,0},{20,4},{24,8},{28,12},{1,17},{... | collective-permute-start | bytes 2359304 | tf_op jit(solution)/shard_map/ppermute | solution.py:71
  20.9 1.2 copy-done.6
  22.1 1.3 spread.5
  23.4 1.6 %collective-permute-start.14 = (bf16[512,512]{1,0:T(8,128)(2,1)S(1)}, bf16[512,512]{1,0:T(8,128)(2,1)S(1)}, u32[]{:S(2)}, u32[]{:S(2)}) collective-permute-start(bf16[512,512]{1,0:T(8,128)(2,1)S(1)} %spread.5), channel_id=1, source_target_pairs={{0,4},{4,0},{8,12},{12,8},{16,20},{20,16},{24,28},{28,24},{1,5},{5... | collective-permute-start | bytes 1572872 | tf_op jit(solution)/shard_map/ppermute | solution.py:71
  24.9 0.0 collective-permute-done.9.refs_1_
  25.0 1.4 %spread.4 = bf16[512,512]{1,0:T(8,128)(2,1)S(1)} custom-call(s32[2048]{0:T(1024)S(1)} %copy-done.12, bf16[1024,512]{1,0:T(8,128)(2,1)S(1)} %copy-done.4, bf16[1024,512]{1,0:T(8,128)(2,1)} %collective-permute-done.9.refs_1_), custom_call_target="tpu_custom_call" | custom-call | flops 1 | bytes 1 | tf_op jit(solution)/shard_map/spread/pallas_call | solution.py:377
  26.3 0.6 collective-permute-start.10
  26.9 0.0 collective-permute-done.5.refs_1_
  26.9 1.3 spread.3
  28.2 1.6 %collective-permute-start.6 = (bf16[512,512]{1,0:T(8,128)(2,1)S(1)}, bf16[512,512]{1,0:T(8,128)(2,1)S(1)}, u32[]{:S(2)}, u32[]{:S(2)}) collective-permute-start(bf16[512,512]{1,0:T(8,128)(2,1)S(1)} %spread.3), channel_id=1, source_target_pairs={{0,4},{4,0},{8,12},{12,8},{16,20},{20,16},{24,28},{28,24},{1,5},{5... | collective-permute-start | bytes 1572872 | tf_op jit(solution)/shard_map/ppermute | solution.py:71
  29.8 8.8 %collective-permute-done.1.refs_2_ = bf16[768,512]{1,0:T(8,128)(2,1)S(1)} collective-permute-done((bf16[768,512]{1,0:T(8,128)(2,1)S(1)}, bf16[768,512]{1,0:T(8,128)(2,1)S(1)}, u32[]{:S(2)}, u32[]{:S(2)}) %collective-permute-start.1) | collective-permute-done | bytes 786464 | tf_op jit(solution)/shard_map/ppermute | solution.py:71
  38.6 1.7 %grad_sum.1.refs_0_ = bf16[768,512]{1,0:T(8,128)(2,1)S(1)} custom-call(s32[2048]{0:T(1024)S(1)} %copy-done.12, bf16[1024,512]{1,0:T(8,128)(2,1)S(1)} %copy-done.11, bf16[1024,512]{1,0:T(8,128)(2,1)} %collective-permute-done.refs_1_, bf16[768,512]{1,0:T(8,128)(2,1)S(1)} %collective-permute-done.1.refs_2_), custom_call_target="tpu_custom_call" | custom-call | flops 1 | bytes 1 | tf_op jit(solution)/shard_map/grad_sum/pallas_call | solution.py:377
  40.2 1.8 %collective-permute-start.2 = (bf16[768,512]{1,0:T(8,128)(2,1)S(1)}, bf16[768,512]{1,0:T(8,128)(2,1)S(1)}, u32[]{:S(2)}, u32[]{:S(2)}) collective-permute-start(bf16[768,512]{1,0:T(8,128)(2,1)S(1)} %grad_sum.1.refs_0_), channel_id=1, source_target_pairs={{0,4},{4,0},{8,12},{12,8},{16,20},{20,16},{24,28},{28,24},{1,5},{5... | collective-permute-start | bytes 2359304 | tf_op jit(solution)/shard_map/ppermute | solution.py:71
  42.0 1.4 %across.5 = bf16[768,512]{1,0:T(8,128)(2,1)S(1)} custom-call(s32[2048]{0:T(1024)S(1)} %copy-done.12, bf16[1024,512]{1,0:T(8,128)(2,1)S(1)} %copy-done.7, bf16[1024,512]{1,0:T(8,128)(2,1)} %collective-permute-done.13.refs_1_, bf16[512,512]{1,0:T(8,128)(2,1)S(1)} %collective-permute-done.14.refs_2_), custom_call_target="tpu_custom_call" | custom-call | flops 1 | bytes 1 | tf_op jit(solution)/shard_map/across/pallas_call | solution.py:377
  43.4 1.5 %collective-permute-start.15 = (bf16[768,512]{1,0:T(8,128)(2,1)S(1)}, bf16[768,512]{1,0:T(8,128)(2,1)S(1)}, u32[]{:S(2)}, u32[]{:S(2)}) collective-permute-start(bf16[768,512]{1,0:T(8,128)(2,1)S(1)} %across.5), channel_id=1, source_target_pairs={{0,16},{4,20},{8,24},{12,28},{16,0},{20,4},{24,8},{28,12},{1,17},{... | collective-permute-start | bytes 2359304 | tf_op jit(solution)/shard_map/ppermute | solution.py:71
  44.9 4.6 %collective-permute-done.10.refs_2_ = bf16[512,512]{1,0:T(8,128)(2,1)S(1)} collective-permute-done((bf16[512,512]{1,0:T(8,128)(2,1)S(1)}, bf16[512,512]{1,0:T(8,128)(2,1)S(1)}, u32[]{:S(2)}, u32[]{:S(2)}) %collective-permute-start.10) | collective-permute-done | bytes 524320 | tf_op jit(solution)/shard_map/ppermute | solution.py:71
  49.5 1.4 %across.4 = bf16[768,512]{1,0:T(8,128)(2,1)S(1)} custom-call(s32[2048]{0:T(1024)S(1)} %copy-done.12, bf16[1024,512]{1,0:T(8,128)(2,1)S(1)} %copy-done.4, bf16[1024,512]{1,0:T(8,128)(2,1)} %collective-permute-done.9.refs_1_, bf16[512,512]{1,0:T(8,128)(2,1)S(1)} %collective-permute-done.10.refs_2_), custom_call_target="tpu_custom_call" | custom-call | flops 1 | bytes 1 | tf_op jit(solution)/shard_map/across/pallas_call | solution.py:377
  50.9 0.1 collective-permute-start.11
  50.9 9.8 %collective-permute-done.6.refs_2_ = bf16[512,512]{1,0:T(8,128)(2,1)S(1)} collective-permute-done((bf16[512,512]{1,0:T(8,128)(2,1)S(1)}, bf16[512,512]{1,0:T(8,128)(2,1)S(1)}, u32[]{:S(2)}, u32[]{:S(2)}) %collective-permute-start.6) | collective-permute-done | bytes 524320 | tf_op jit(solution)/shard_map/ppermute | solution.py:71
  60.7 1.4 %across.3 = bf16[768,512]{1,0:T(8,128)(2,1)S(1)} custom-call(s32[2048]{0:T(1024)S(1)} %copy-done.12, bf16[1024,512]{1,0:T(8,128)(2,1)S(1)} %get-tuple-element.20.refs_0_, bf16[1024,512]{1,0:T(8,128)(2,1)} %collective-permute-done.5.refs_1_, bf16[512,512]{1,0:T(8,128)(2,1)S(1)} %collective-permute-done.6.refs_2_), custom_call_target="tpu_custom_call" | custom-call | flops 1 | bytes 1 | tf_op jit(solution)/shard_map/across/pallas_call | solution.py:377
  62.1 0.1 collective-permute-start.7
  62.2 14.1 %collective-permute-done.2.refs_1_ = bf16[768,512]{1,0:T(8,128)(2,1)S(1)} collective-permute-done((bf16[768,512]{1,0:T(8,128)(2,1)S(1)}, bf16[768,512]{1,0:T(8,128)(2,1)S(1)}, u32[]{:S(2)}, u32[]{:S(2)}) %collective-permute-start.2) | collective-permute-done | bytes 786464 | tf_op jit(solution)/shard_map/ppermute | solution.py:71
  76.3 1.0 grad_mean.1.refs_0_
  77.3 0.3 collective-permute-start.3
  77.6 0.0 collective-permute-done.15.refs_3_
  77.6 1.3 %deliver.5 = bf16[512,512]{1,0:T(8,128)(2,1)S(1)} custom-call(s32[2048]{0:T(1024)S(1)} %copy-done.12, bf16[1024,512]{1,0:T(8,128)(2,1)S(1)} %copy-done.7, bf16[1024,512]{1,0:T(8,128)(2,1)} %collective-permute-done.13.refs_1_, bf16[512,512]{1,0:T(8,128)(2,1)S(1)} %collective-permute-done.14.refs_2_, bf16[768,512]{1,0:T(8,128)(2,1)S(1)} %collective-permute-done.15.refs_3_), custom_call_target="tpu_custom_call" | custom-call | flops 1 | bytes 1 | tf_op jit(solution)/shard_map/deliver/pallas_call | solution.py:377
  78.9 1.8 %collective-permute-start.16 = (bf16[512,512]{1,0:T(8,128)(2,1)S(1)}, bf16[512,512]{1,0:T(8,128)(2,1)S(1)}, u32[]{:S(2)}, u32[]{:S(2)}) collective-permute-start(bf16[512,512]{1,0:T(8,128)(2,1)S(1)} %deliver.5), channel_id=1, source_target_pairs={{0,4},{4,0},{8,12},{12,8},{16,20},{20,16},{24,28},{28,24},{1,5},{5... | collective-permute-start | bytes 1572872 | tf_op jit(solution)/shard_map/ppermute | solution.py:71
  80.7 0.1 collective-permute-done.11.refs_3_
  80.8 1.3 %deliver.4 = bf16[512,512]{1,0:T(8,128)(2,1)S(1)} custom-call(s32[2048]{0:T(1024)S(1)} %copy-done.12, bf16[1024,512]{1,0:T(8,128)(2,1)S(1)} %copy-done.4, bf16[1024,512]{1,0:T(8,128)(2,1)} %collective-permute-done.9.refs_1_, bf16[512,512]{1,0:T(8,128)(2,1)S(1)} %collective-permute-done.10.refs_2_, bf16[768,512]{1,0:T(8,128)(2,1)S(1)} %collective-permute-done.11.refs_3_), custom_call_target="tpu_custom_call" | custom-call | flops 1 | bytes 1 | tf_op jit(solution)/shard_map/deliver/pallas_call | solution.py:377
  82.1 0.4 collective-permute-start.12
  82.5 15.2 %collective-permute-done.7.refs_3_ = bf16[768,512]{1,0:T(8,128)(2,1)S(1)} collective-permute-done((bf16[768,512]{1,0:T(8,128)(2,1)S(1)}, bf16[768,512]{1,0:T(8,128)(2,1)S(1)}, u32[]{:S(2)}, u32[]{:S(2)}) %collective-permute-start.7) | collective-permute-done | bytes 786464 | tf_op jit(solution)/shard_map/ppermute | solution.py:71
  97.6 1.3 %deliver.3 = bf16[512,512]{1,0:T(8,128)(2,1)S(1)} custom-call(s32[2048]{0:T(1024)S(1)} %copy-done.12, bf16[1024,512]{1,0:T(8,128)(2,1)S(1)} %get-tuple-element.20.refs_0_, bf16[1024,512]{1,0:T(8,128)(2,1)} %collective-permute-done.5.refs_1_, bf16[512,512]{1,0:T(8,128)(2,1)S(1)} %collective-permute-done.6.refs_2_, ...), custom_call_target="tpu_custom_call" | custom-call | flops 1 | bytes 1 | tf_op jit(solution)/shard_map/deliver/pallas_call | solution.py:377
  99.0 0.4 collective-permute-start.8
  99.3 1.4 %collect.5.refs_7_ = bf16[1024,512]{1,0:T(8,128)(2,1)S(1)} custom-call(s32[2048]{0:T(1024)S(1)} %copy-done.12, bf16[1024,512]{1,0:T(8,128)(2,1)S(1)} %copy-done.7, bf16[1024,512]{1,0:T(8,128)(2,1)} %collective-permute-done.13.refs_1_, bf16[512,512]{1,0:T(8,128)(2,1)S(1)} %collective-permute-done.14.refs_2_, ...), custom_call_target="tpu_custom_call" | custom-call | flops 1 | bytes 1 | tf_op jit(solution)/shard_map/collect/pallas_call | solution.py:377
  100.8 0.1 collective-permute-start.19
  100.8 4.3 %collective-permute-done.12.refs_4_ = bf16[512,512]{1,0:T(8,128)(2,1)S(1)} collective-permute-done((bf16[512,512]{1,0:T(8,128)(2,1)S(1)}, bf16[512,512]{1,0:T(8,128)(2,1)S(1)}, u32[]{:S(2)}, u32[]{:S(2)}) %collective-permute-start.12) | collective-permute-done | bytes 524320 | tf_op jit(solution)/shard_map/ppermute | solution.py:71
  105.1 1.4 %collect.4.refs_6_ = bf16[1024,512]{1,0:T(8,128)(2,1)S(1)} custom-call(s32[2048]{0:T(1024)S(1)} %copy-done.12, bf16[1024,512]{1,0:T(8,128)(2,1)S(1)} %copy-done.4, bf16[1024,512]{1,0:T(8,128)(2,1)} %collective-permute-done.9.refs_1_, bf16[512,512]{1,0:T(8,128)(2,1)S(1)} %collective-permute-done.10.refs_2_, ...), custom_call_target="tpu_custom_call" | custom-call | flops 1 | bytes 1 | tf_op jit(solution)/shard_map/collect/pallas_call | solution.py:377
  106.5 0.1 collective-permute-start.18
  106.6 7.6 %collective-permute-done.8.refs_4_ = bf16[512,512]{1,0:T(8,128)(2,1)S(1)} collective-permute-done((bf16[512,512]{1,0:T(8,128)(2,1)S(1)}, bf16[512,512]{1,0:T(8,128)(2,1)S(1)}, u32[]{:S(2)}, u32[]{:S(2)}) %collective-permute-start.8) | collective-permute-done | bytes 524320 | tf_op jit(solution)/shard_map/ppermute | solution.py:71
  114.2 1.4 %collect.3.refs_5_ = bf16[1024,512]{1,0:T(8,128)(2,1)S(1)} custom-call(s32[2048]{0:T(1024)S(1)} %copy-done.12, bf16[1024,512]{1,0:T(8,128)(2,1)S(1)} %get-tuple-element.20.refs_0_, bf16[1024,512]{1,0:T(8,128)(2,1)} %collective-permute-done.5.refs_1_, bf16[512,512]{1,0:T(8,128)(2,1)S(1)} %collective-permute-done.6.refs_2_, ...), custom_call_target="tpu_custom_call" | custom-call | flops 1 | bytes 1 | tf_op jit(solution)/shard_map/collect/pallas_call | solution.py:377
  115.6 0.1 collective-permute-start.17
  115.7 0.9 mean.1
  116.6 0.6 collective-permute-start.4
  117.2 1.2 collective-permute-done.17.refs_8_
  118.3 1.5 %collective-permute-done.4.refs_4_ = bf16[1024,512]{1,0:T(8,128)(2,1)S(1)} collective-permute-done((bf16[1024,512]{1,0:T(8,128)(2,1)S(1)}, bf16[1024,512]{1,0:T(8,128)(2,1)S(1)}, u32[]{:S(2)}, u32[]{:S(2)}) %collective-permute-start.4) | collective-permute-done | bytes 1048608 | tf_op jit(solution)/shard_map/ppermute | solution.py:71
  119.8 9.0 %update.1 = (bf16[2,2,512,512]{3,2,1,0:T(8,128)(2,1)}, f32[2,2,512,512]{3,2,1,0:T(8,128)}, f32[2,2,512,512]{3,2,1,0:T(8,128)}) custom-call(s32[2048]{0:T(1024)S(1)} %copy-done.12, bf16[2,2,512,512]{3,2,1,0:T(8,128)(2,1)S(1)} %bitcast.20, f32[2,2,512,512]{3,2,1,0:T(8,128)} %bitcast.12, f32[2,2,512,512]{3,2,1,0:T(8,128)} %bitcast.15, ...), custom_call_target="tpu_custom_call" | custom-call | flops 1 | bytes 1 | tf_op jit(solution)/shard_map/update/pallas_call | solution.py:503
  (27 shorter events, 0.1 us)
Async XLA Ops:
  0.6 3.9 %copy-start.1 = (f32[1,1,2,1024,512]{4,3,2,1,0:T(8,128)S(1)}, f32[1,1,2,1024,512]{4,3,2,1,0:T(8,128)}, u32[]{:S(2)}) copy-start(f32[1,1,2,1024,512]{4,3,2,1,0:T(8,128)} %param.10) | copy-start | bytes 12582916
  0.7 10.0 %copy-start.13 = (s32[2]{0:T(128)}, s32[2]{0:T(128)S(1)}, u32[]{:S(2)}) copy-start(s32[2]{0:T(128)S(1)} %pad_add_fusion.place_ref) | copy-start | bytes 28
  0.7 1.7 %copy-start.8 = (bf16[1,1,2,1024,512]{4,3,2,1,0:T(8,128)(2,1)S(1)}, bf16[1,1,2,1024,512]{4,3,2,1,0:T(8,128)(2,1)}, u32[]{:S(2)}) copy-start(bf16[1,1,2,1024,512]{4,3,2,1,0:T(8,128)(2,1)} %param.11) | copy-start | bytes 6291460
  4.1 2.2 %copy-start.9 = (bf16[1024,512]{1,0:T(8,128)(2,1)}, bf16[1024,512]{1,0:T(8,128)(2,1)S(1)}, u32[]{:S(2)}) copy-start(bf16[1024,512]{1,0:T(8,128)(2,1)S(1)} %get-tuple-element.16.refs_0_) | copy-start | bytes 3145732
  4.1 10.0 %collective-permute-start = (bf16[1024,512]{1,0:T(8,128)(2,1)}, bf16[1024,512]{1,0:T(8,128)(2,1)}, u32[]{:S(2)}, u32[]{:S(2)}) collective-permute-start(bf16[1024,512]{1,0:T(8,128)(2,1)} %get-tuple-element.17), channel_id=1, source_target_pairs={{0,8},{4,12},{8,0},{12,4},{16,24},{20,28},{24,16},{28,20},{1,9},{5... | collective-permute-start | bytes 3145736 | tf_op jit(solution)/shard_map/ppermute | solution.py:71
  4.6 2.8 %copy-start = (f32[1,1,2,1024,512]{4,3,2,1,0:T(8,128)S(1)}, f32[1,1,2,1024,512]{4,3,2,1,0:T(8,128)}, u32[]{:S(2)}) copy-start(f32[1,1,2,1024,512]{4,3,2,1,0:T(8,128)} %param.9) | copy-start | bytes 12582916
  6.3 1.0 copy-start.5
  7.3 13.5 %collective-permute-start.13 = (bf16[1024,512]{1,0:T(8,128)(2,1)}, bf16[1024,512]{1,0:T(8,128)(2,1)}, u32[]{:S(2)}, u32[]{:S(2)}) collective-permute-start(bf16[1024,512]{1,0:T(8,128)(2,1)} %get-tuple-element.25), channel_id=1, source_target_pairs={{0,8},{4,12},{8,0},{12,4},{16,24},{20,28},{24,16},{28,20},{1,9},{5... | collective-permute-start | bytes 3145736 | tf_op jit(solution)/shard_map/ppermute | solution.py:71
  7.4 3.3 %copy-start.2 = (bf16[1,1,2,1024,512]{4,3,2,1,0:T(8,128)(2,1)S(1)}, bf16[1,1,2,1024,512]{4,3,2,1,0:T(8,128)(2,1)}, u32[]{:S(2)}) copy-start(bf16[1,1,2,1024,512]{4,3,2,1,0:T(8,128)(2,1)} %param.8) | copy-start | bytes 6291460
  9.1 1.1 copy-start.3
  10.2 14.8 %collective-permute-start.9 = (bf16[1024,512]{1,0:T(8,128)(2,1)}, bf16[1024,512]{1,0:T(8,128)(2,1)}, u32[]{:S(2)}, u32[]{:S(2)}) collective-permute-start(bf16[1024,512]{1,0:T(8,128)(2,1)} %get-tuple-element.23), channel_id=1, source_target_pairs={{0,8},{4,12},{8,0},{12,4},{16,24},{20,28},{24,16},{28,20},{1,9},{5... | collective-permute-start | bytes 3145736 | tf_op jit(solution)/shard_map/ppermute | solution.py:71
  12.4 14.6 %collective-permute-start.5 = (bf16[1024,512]{1,0:T(8,128)(2,1)}, bf16[1024,512]{1,0:T(8,128)(2,1)}, u32[]{:S(2)}, u32[]{:S(2)}) collective-permute-start(bf16[1024,512]{1,0:T(8,128)(2,1)} %get-tuple-element.21), channel_id=1, source_target_pairs={{0,8},{4,12},{8,0},{12,4},{16,24},{20,28},{24,16},{28,20},{1,9},{5... | collective-permute-start | bytes 3145736 | tf_op jit(solution)/shard_map/ppermute | solution.py:71
  14.1 10.8 %copy-start.4 = (bf16[1024,512]{1,0:T(8,128)(2,1)S(1)}, bf16[1024,512]{1,0:T(8,128)(2,1)}, u32[]{:S(2)}) copy-start(bf16[1024,512]{1,0:T(8,128)(2,1)} %copy-done.3) | copy-start | bytes 3145732
  14.1 1.3 %copy-start.10 = (bf16[1024,512]{1,0:T(8,128)(2,1)S(1)}, bf16[1024,512]{1,0:T(8,128)(2,1)}, u32[]{:S(2)}) copy-start(bf16[1024,512]{1,0:T(8,128)(2,1)} %copy-done.9) | copy-start | bytes 3145732
  15.5 0.7 copy-start.12
  16.2 22.4 %copy-start.11 = (bf16[1024,512]{1,0:T(8,128)(2,1)S(1)}, bf16[1024,512]{1,0:T(8,128)(2,1)}, u32[]{:S(2)}) copy-start(bf16[1024,512]{1,0:T(8,128)(2,1)} %copy-done.9) | copy-start | bytes 3145732
  17.8 20.8 %collective-permute-start.1 = (bf16[768,512]{1,0:T(8,128)(2,1)S(1)}, bf16[768,512]{1,0:T(8,128)(2,1)S(1)}, u32[]{:S(2)}, u32[]{:S(2)}) collective-permute-start(bf16[768,512]{1,0:T(8,128)(2,1)S(1)} %grad_out.1), channel_id=1, source_target_pairs={{0,16},{4,20},{8,24},{12,28},{16,0},{20,4},{24,8},{28,12},{1,17},{... | collective-permute-start | bytes 2359304 | tf_op jit(solution)/shard_map/ppermute | solution.py:71
  20.8 1.2 copy-start.6
  23.4 18.7 %collective-permute-start.14 = (bf16[512,512]{1,0:T(8,128)(2,1)S(1)}, bf16[512,512]{1,0:T(8,128)(2,1)S(1)}, u32[]{:S(2)}, u32[]{:S(2)}) collective-permute-start(bf16[512,512]{1,0:T(8,128)(2,1)S(1)} %spread.5), channel_id=1, source_target_pairs={{0,4},{4,0},{8,12},{12,8},{16,20},{20,16},{24,28},{28,24},{1,5},{5... | collective-permute-start | bytes 1572872 | tf_op jit(solution)/shard_map/ppermute | solution.py:71
  24.9 17.1 %copy-start.7 = (bf16[1024,512]{1,0:T(8,128)(2,1)S(1)}, bf16[1024,512]{1,0:T(8,128)(2,1)}, u32[]{:S(2)}) copy-start(bf16[1024,512]{1,0:T(8,128)(2,1)} %copy-done.5) | copy-start | bytes 3145732
  26.3 23.2 %collective-permute-start.10 = (bf16[512,512]{1,0:T(8,128)(2,1)S(1)}, bf16[512,512]{1,0:T(8,128)(2,1)S(1)}, u32[]{:S(2)}, u32[]{:S(2)}) collective-permute-start(bf16[512,512]{1,0:T(8,128)(2,1)S(1)} %spread.4), channel_id=1, source_target_pairs={{0,4},{4,0},{8,12},{12,8},{16,20},{20,16},{24,28},{28,24},{1,5},{5... | collective-permute-start | bytes 1572872 | tf_op jit(solution)/shard_map/ppermute | solution.py:71
  28.2 32.5 %collective-permute-start.6 = (bf16[512,512]{1,0:T(8,128)(2,1)S(1)}, bf16[512,512]{1,0:T(8,128)(2,1)S(1)}, u32[]{:S(2)}, u32[]{:S(2)}) collective-permute-start(bf16[512,512]{1,0:T(8,128)(2,1)S(1)} %spread.3), channel_id=1, source_target_pairs={{0,4},{4,0},{8,12},{12,8},{16,20},{20,16},{24,28},{28,24},{1,5},{5... | collective-permute-start | bytes 1572872 | tf_op jit(solution)/shard_map/ppermute | solution.py:71
  40.2 36.1 %collective-permute-start.2 = (bf16[768,512]{1,0:T(8,128)(2,1)S(1)}, bf16[768,512]{1,0:T(8,128)(2,1)S(1)}, u32[]{:S(2)}, u32[]{:S(2)}) collective-permute-start(bf16[768,512]{1,0:T(8,128)(2,1)S(1)} %grad_sum.1.refs_0_), channel_id=1, source_target_pairs={{0,4},{4,0},{8,12},{12,8},{16,20},{20,16},{24,28},{28,24},{1,5},{5... | collective-permute-start | bytes 2359304 | tf_op jit(solution)/shard_map/ppermute | solution.py:71
  43.4 34.2 %collective-permute-start.15 = (bf16[768,512]{1,0:T(8,128)(2,1)S(1)}, bf16[768,512]{1,0:T(8,128)(2,1)S(1)}, u32[]{:S(2)}, u32[]{:S(2)}) collective-permute-start(bf16[768,512]{1,0:T(8,128)(2,1)S(1)} %across.5), channel_id=1, source_target_pairs={{0,16},{4,20},{8,24},{12,28},{16,0},{20,4},{24,8},{28,12},{1,17},{... | collective-permute-start | bytes 2359304 | tf_op jit(solution)/shard_map/ppermute | solution.py:71
  50.9 29.9 %collective-permute-start.11 = (bf16[768,512]{1,0:T(8,128)(2,1)S(1)}, bf16[768,512]{1,0:T(8,128)(2,1)S(1)}, u32[]{:S(2)}, u32[]{:S(2)}) collective-permute-start(bf16[768,512]{1,0:T(8,128)(2,1)S(1)} %across.4), channel_id=1, source_target_pairs={{0,16},{4,20},{8,24},{12,28},{16,0},{20,4},{24,8},{28,12},{1,17},{... | collective-permute-start | bytes 2359304 | tf_op jit(solution)/shard_map/ppermute | solution.py:71
  62.1 35.5 %collective-permute-start.7 = (bf16[768,512]{1,0:T(8,128)(2,1)S(1)}, bf16[768,512]{1,0:T(8,128)(2,1)S(1)}, u32[]{:S(2)}, u32[]{:S(2)}) collective-permute-start(bf16[768,512]{1,0:T(8,128)(2,1)S(1)} %across.3), channel_id=1, source_target_pairs={{0,16},{4,20},{8,24},{12,28},{16,0},{20,4},{24,8},{28,12},{1,17},{... | collective-permute-start | bytes 2359304 | tf_op jit(solution)/shard_map/ppermute | solution.py:71
  77.3 38.4 %collective-permute-start.3 = (bf16[768,512]{1,0:T(8,128)(2,1)S(1)}, bf16[768,512]{1,0:T(8,128)(2,1)S(1)}, u32[]{:S(2)}, u32[]{:S(2)}) collective-permute-start(bf16[768,512]{1,0:T(8,128)(2,1)S(1)} %grad_mean.1.refs_0_), channel_id=1, source_target_pairs={{0,16},{4,20},{8,24},{12,28},{16,0},{20,4},{24,8},{28,12},{1,17},{... | collective-permute-start | bytes 2359304 | tf_op jit(solution)/shard_map/ppermute | solution.py:71
  78.9 20.4 %collective-permute-start.16 = (bf16[512,512]{1,0:T(8,128)(2,1)S(1)}, bf16[512,512]{1,0:T(8,128)(2,1)S(1)}, u32[]{:S(2)}, u32[]{:S(2)}) collective-permute-start(bf16[512,512]{1,0:T(8,128)(2,1)S(1)} %deliver.5), channel_id=1, source_target_pairs={{0,4},{4,0},{8,12},{12,8},{16,20},{20,16},{24,28},{28,24},{1,5},{5... | collective-permute-start | bytes 1572872 | tf_op jit(solution)/shard_map/ppermute | solution.py:71
  82.1 23.0 %collective-permute-start.12 = (bf16[512,512]{1,0:T(8,128)(2,1)S(1)}, bf16[512,512]{1,0:T(8,128)(2,1)S(1)}, u32[]{:S(2)}, u32[]{:S(2)}) collective-permute-start(bf16[512,512]{1,0:T(8,128)(2,1)S(1)} %deliver.4), channel_id=1, source_target_pairs={{0,4},{4,0},{8,12},{12,8},{16,20},{20,16},{24,28},{28,24},{1,5},{5... | collective-permute-start | bytes 1572872 | tf_op jit(solution)/shard_map/ppermute | solution.py:71
  99.0 15.2 %collective-permute-start.8 = (bf16[512,512]{1,0:T(8,128)(2,1)S(1)}, bf16[512,512]{1,0:T(8,128)(2,1)S(1)}, u32[]{:S(2)}, u32[]{:S(2)}) collective-permute-start(bf16[512,512]{1,0:T(8,128)(2,1)S(1)} %deliver.3), channel_id=1, source_target_pairs={{0,4},{4,0},{8,12},{12,8},{16,20},{20,16},{24,28},{28,24},{1,5},{5... | collective-permute-start | bytes 1572872 | tf_op jit(solution)/shard_map/ppermute | solution.py:71
  100.8 16.4 %collective-permute-start.19 = (bf16[1024,512]{1,0:T(8,128)(2,1)S(1)}, bf16[1024,512]{1,0:T(8,128)(2,1)S(1)}, u32[]{:S(2)}, u32[]{:S(2)}) collective-permute-start(bf16[1024,512]{1,0:T(8,128)(2,1)S(1)} %collect.5.refs_7_), channel_id=1, source_target_pairs={{0,8},{4,12},{8,0},{12,4},{16,24},{20,28},{24,16},{28,20},{1,9},{5... | collective-permute-start | bytes 3145736 | tf_op jit(solution)/shard_map/ppermute | solution.py:71
  106.5 10.7 %collective-permute-start.18 = (bf16[1024,512]{1,0:T(8,128)(2,1)S(1)}, bf16[1024,512]{1,0:T(8,128)(2,1)S(1)}, u32[]{:S(2)}, u32[]{:S(2)}) collective-permute-start(bf16[1024,512]{1,0:T(8,128)(2,1)S(1)} %collect.4.refs_6_), channel_id=1, source_target_pairs={{0,8},{4,12},{8,0},{12,4},{16,24},{20,28},{24,16},{28,20},{1,9},{5... | collective-permute-start | bytes 3145736 | tf_op jit(solution)/shard_map/ppermute | solution.py:71
  115.6 2.7 %collective-permute-start.17 = (bf16[1024,512]{1,0:T(8,128)(2,1)S(1)}, bf16[1024,512]{1,0:T(8,128)(2,1)S(1)}, u32[]{:S(2)}, u32[]{:S(2)}) collective-permute-start(bf16[1024,512]{1,0:T(8,128)(2,1)S(1)} %collect.3.refs_5_), channel_id=1, source_target_pairs={{0,8},{4,12},{8,0},{12,4},{16,24},{20,28},{24,16},{28,20},{1,9},{5... | collective-permute-start | bytes 3145736 | tf_op jit(solution)/shard_map/ppermute | solution.py:71
  116.6 3.2 %collective-permute-start.4 = (bf16[1024,512]{1,0:T(8,128)(2,1)S(1)}, bf16[1024,512]{1,0:T(8,128)(2,1)S(1)}, u32[]{:S(2)}, u32[]{:S(2)}) collective-permute-start(bf16[1024,512]{1,0:T(8,128)(2,1)S(1)} %get-tuple-element.19), channel_id=1, source_target_pairs={{0,8},{4,12},{8,0},{12,4},{16,24},{20,28},{24,16},{28,20},{1,9},{5... | collective-permute-start | bytes 3145736 | tf_op jit(solution)/shard_map/ppermute | solution.py:71

commit v3 on v2

--- a/solution.py
+++ b/solution.py
@@ -14,9 +14,13 @@
 DECAY_RATE = 0.1
 
 CORES = 2
-CHUNKS = 1
+SEQUENCE = (
+    *("ge", "e0", "gs", "s0", "e1", "e2", "s1", "s2", "gx", "a0", "a1", "a2"),
+    *("gg", "d0", "d1", "d2", "gf", "c0", "c1", "c2"),
+)
 AFTER = {}
 VMEM = 40 * 1024 * 1024
+HALVE_VMEM = 60 * 1024 * 1024
 AXES = ("pipe", "section")
 
 
@@ -49,9 +53,7 @@
         self.layers = new_section.shape[0]
         self.half = self.rows // CORES
         self.band = self.half // self.sections
-        self.units = CHUNKS if self.band % (16 * CHUNKS) == 0 else 1
-        self.unit = self.band // self.units
-        self.block = math.gcd(self.unit, 32)
+        self.block = math.gcd(self.band, 32)
         self.grad_band = self.half // self.groups
         doubles = self.layers - self.sections
         widest = 0
@@ -283,6 +285,10 @@
         self.name = name
         self.last = [self.results[at] for at in AFTER.get(name, ()) if at in self.results]
 
+    def arrived(self, value):
+        self.results[self.name + "r"] = value
+        return value
+
     def specs(self):
         return [pl.BlockSpec(memory_space=pl.ANY)] * len(self.last)
 
@@ -294,7 +300,7 @@
 SMEM_SPEC = pl.BlockSpec(memory_space=pltpu.SMEM)
 VMEM_SPEC = pl.BlockSpec(memory_space=pltpu.VMEM)
 PARAMS = pltpu.CompilerParams(vmem_limit_bytes=VMEM)
-COST = pl.CostEstimate(flops=1, bytes_accessed=1, transcendentals=0)
+COST = pl.CostEstimate(flops=10**9, bytes_accessed=1, transcendentals=0)
 
 UPDATE_COST = pl.CostEstimate(flops=1, bytes_accessed=1, transcendentals=0)
 
@@ -377,49 +383,54 @@
     return order.then(call(table, *operands, *order.last))
 
 
-def halve(z, order, place, arrays, first, count, units, name):
-    unit = z.band // units
-    views = [a.reshape(z.slots, CORES, z.sections, units, unit, z.cols) for a in arrays]
-
-    def kernel(place_ref, *refs):
-        for part, out_ref in enumerate(refs[-2:]):
-            row = 0
-            for at in range(len(arrays)):
-                ref = refs[part * len(arrays) + at]
-                for slot in range(z.slots):
-                    for band in range(z.sections):
-                        for k in range(count):
-                            out_ref[pl.ds(row, unit)] = ref[slot, 0, band, k].astype(jnp.bfloat16)
-                            row += unit
-
-    def spec(own):
-        def index_map(step, place_ref):
-            core = lax.rem(place_ref[0], CORES)
-            return (0, core if own else 1 - core, 0, first // count, 0, 0)
-
-        return pl.BlockSpec((z.slots, 1, z.sections, count, unit, z.cols), index_map)
-
-    rows = len(arrays) * z.slots * z.sections * count * unit
-    out = jax.ShapeDtypeStruct((rows, z.cols), jnp.bfloat16)
-    out_spec = pl.BlockSpec(out.shape, lambda step, place_ref: (0, 0))
+def halve(z, order, place, array, name):
+    view = array.reshape(z.slots, CORES, z.half, z.cols)
+    straight = array.dtype == jnp.bfloat16
+
+    def kernel(place_ref, array_ref, *refs):
+        own_ref, their_ref, sems = refs[-5], refs[-4], refs[-1]
+        landed = refs[-3:-1]
+        core = lax.rem(place_ref[0], CORES)
+        copies = []
+        for part, (half, out_ref) in enumerate(((1 - core, their_ref), (core, own_ref))):
+            for slot in range(z.slots):
+                rows = pl.ds(slot * z.half, z.half)
+                target = out_ref if straight else landed[part]
+                copy = pltpu.make_async_copy(
+                    array_ref.at[slot, half], target.at[rows], sems.at[part, slot]
+                )
+                copy.start()
+                copies.append((copy, part, out_ref, slot))
+        for copy, part, out_ref, slot in copies:
+            copy.wait()
+            if not straight:
+
+                @pl.loop(0, z.half // z.block)
+                def _(at, part=part, out_ref=out_ref, slot=slot):
+                    rows = pl.ds(pl.multiple_of(slot * z.half + at * z.block, 16), z.block)
+                    out_ref[rows] = landed[part][rows].astype(jnp.bfloat16)
+
+    out = jax.ShapeDtypeStruct((z.slots * z.half, z.cols), jnp.bfloat16)
+    scratch = (16, z.cols) if straight else out.shape
     call = pl.pallas_call(
         kernel,
-        grid_spec=pltpu.PrefetchScalarGridSpec(
-            num_scalar_prefetch=1,
-            grid=(1,),
-            in_specs=[spec(True)] * len(arrays) + [spec(False)] * len(arrays) + order.specs(),
-            out_specs=[out_spec] * 2,
-        ),
         out_shape=(out, out),
-        compiler_params=PARAMS,
+        in_specs=[SMEM_SPEC, pl.BlockSpec(memory_space=pltpu.HBM)] + order.specs(),
+        out_specs=(VMEM_SPEC, VMEM_SPEC),
+        scratch_shapes=[
+            pltpu.VMEM(scratch, array.dtype),
+            pltpu.VMEM(scratch, array.dtype),
+            pltpu.SemaphoreType.DMA((2, z.slots)),
+        ],
+        compiler_params=pltpu.CompilerParams(vmem_limit_bytes=HALVE_VMEM),
         cost_estimate=COST,
         name="halve_" + name,
     )
-    return order.then(call(place, *views, *views, *order.last))
+    return order.then(call(place, view, *order.last))
 
 
 def update(z, order, table, start, state, rebuilt, mean):
-    views = [a.reshape(z.slots, CORES, z.half, z.cols) for a in state]
+    views = [a.reshape(z.slots * z.rows, z.cols) for a in state]
     halves = [chunk[part] for part in range(2) for chunk in rebuilt]
 
     def kernel(table_ref, *refs):
@@ -431,25 +442,20 @@
         found = table_ref[start + 2 + slot] != 0
 
         def each(source, lost):
-            @pl.loop(0, z.unit // z.block)
+            @pl.loop(0, z.half // z.block)
             def _(at):
-                for band in range(z.sections):
-                    for unit in range(z.units):
-                        one_block(source, lost, band, unit, at)
-
-        def one_block(source, lost, band, unit, at):
-            place = at * z.block
-            row = pl.ds(pl.multiple_of(band * z.band + unit * z.unit + place, 16), z.block)
-            mean_row = pl.multiple_of(slot * z.half + band * z.band + unit * z.unit + place, 16)
-            grad = mean_refs[source][pl.ds(mean_row, z.block)].astype(jnp.float32)
+                one_block(source, lost, at * z.block)
+
+        def one_block(source, lost, at):
+            row = pl.ds(pl.multiple_of(at, 16), z.block)
+            from_row = pl.ds(pl.multiple_of(slot * z.half + at, 16), z.block)
+            grad = mean_refs[source][from_row].astype(jnp.float32)
             grad = grad * (1.0 / z.pipes)
             if lost:
-                here = half_refs[source * len(rebuilt) : (source + 1) * len(rebuilt)]
-                from_row = (slot * z.sections + band) * z.unit + place
-                from_row = pl.ds(pl.multiple_of(from_row, 16), z.block)
-                old = [here[array * z.units + unit][from_row] for array in range(3)]
+                old = [ref[from_row] for ref in half_refs[source * 3 : source * 3 + 3]]
             else:
-                old = [ref[0, 0, row] for ref in local_refs]
+                local_row = pl.multiple_of(slot * z.rows + half * z.half + at, 16)
+                old = [ref[pl.ds(local_row, z.block)] for ref in local_refs]
             weight, one, two = [value.astype(jnp.float32) for value in old]
             next_one = BETA_ONE * one + (1.0 - BETA_ONE) * grad
             next_two = BETA_TWO * two + (1.0 - BETA_TWO) * grad * grad
@@ -474,21 +480,15 @@
             for ref in (out_w, out_one, out_two):
                 ref[...] = jnp.zeros(ref.shape, ref.dtype)
 
-    def local(slot, half, table_ref):
-        keep = 1 - table_ref[start]
-        return (slot * keep, half * keep, 0, 0)
-
     block = (1, 1, z.half, z.cols)
     out_spec = pl.BlockSpec(block, lambda slot, half, table_ref: (slot, half, 0, 0))
-    shape = views[0].shape
+    shape = (z.slots, CORES, z.half, z.cols)
     call = pl.pallas_call(
         kernel,
         grid_spec=pltpu.PrefetchScalarGridSpec(
             num_scalar_prefetch=1,
             grid=(z.slots, CORES),
-            in_specs=[pl.BlockSpec(block, local)] * 3
-            + [VMEM_SPEC] * (2 + len(halves))
-            + order.specs(),
+            in_specs=[VMEM_SPEC] * (5 + len(halves)) + order.specs(),
             out_specs=[out_spec] * 3,
         ),
         out_shape=(
@@ -515,28 +515,29 @@
 
     def enter(self, place):
         z = self.z
-        own, theirs = halve(z, self.order, place, (self.grads,), 0, 1, 1, "gradients")
-        self.held = [
-            Rows(flat, z.grad_band, z.slots * z.groups) for flat in (own, z.to_core(theirs))
-        ]
+        own, theirs = halve(z, self.order, place, self.grads, "gradients")
+        theirs = self.order.arrived(z.to_core(theirs))
+        self.held = [Rows(flat, z.grad_band, z.slots * z.groups) for flat in (own, theirs)]
 
     def scatter(self):
         z = self.z
         shifts = range(1, z.groups)
         jobs = [[Sum(self.starts["grad_out", s], z.layers, self.held)] for s in shifts]
         parts = self.run(jobs, "grad_out")
-        self.held += [self.rows(z.to_group(part, s)) for s, part in zip(shifts, parts)]
+        self.held += [
+            self.rows(self.order.arrived(z.to_group(part, s))) for s, part in zip(shifts, parts)
+        ]
 
     def exchange(self):
         z = self.z
         (part,) = self.run([[Sum(self.starts["grad_sum"], z.layers, self.held)]], "grad_sum")
-        others = [z.to_section(part, s) for s in range(1, z.sections)]
+        others = [self.order.arrived(z.to_section(part, s)) for s in range(1, z.sections)]
         self.held = [self.rows(value) for value in (part, *others)]
 
     def gather(self):
         z = self.z
         (part,) = self.run([[Sum(self.starts["grad_mean"], z.layers, self.held)]], "grad_mean")
-        others = [z.to_group(part, s) for s in range(1, z.groups)]
+        others = [self.order.arrived(z.to_group(part, s)) for s in range(1, z.groups)]
         self.held = [self.rows(value) for value in (part, *others)]
 
     def finish(self):
@@ -548,21 +549,22 @@
             ],
             "mean",
         )
-        self.mean = (mine, z.to_core(theirs))
+        self.mean = (mine, self.order.arrived(z.to_core(theirs)))
 
 
 class Chunk:
-    def __init__(self, z, order, array, first):
-        self.z, self.order, self.array, self.first = z, order, array, first
+    def __init__(self, z, order, array):
+        self.z, self.order, self.array = z, order, array
 
     def run(self, outputs, name):
         return stage(self.z, self.order, self.table, outputs, name)
 
     def enter(self, place):
         z = self.z
-        own, theirs = halve(z, self.order, place, (self.array,), self.first, 1, z.units, "state")
+        own, theirs = halve(z, self.order, place, self.array, "state")
         held = z.slots * z.sections
-        self.held = [Rows(flat, z.unit, held) for flat in (own, z.to_core(theirs))]
+        theirs = self.order.arrived(z.to_core(theirs))
+        self.held = [Rows(flat, z.band, held) for flat in (own, theirs)]
 
     def spread(self):
         z = self.z
@@ -570,13 +572,13 @@
         jobs = [[Copy(self.starts["spread", s], z.channels, self.held)] for s in shifts]
         parts = self.run(jobs, "spread")
         for s, part in zip(shifts, parts):
-            self.held.append(Rows(z.to_section(part, s), z.unit, z.channels))
+            self.held.append(Rows(self.order.arrived(z.to_section(part, s)), z.band, z.channels))
 
     def across(self):
         z = self.z
         (part,) = self.run([[Copy(self.starts["across"], z.layers, self.held)]], "across")
         for s in range(1, z.groups):
-            self.held.append(Rows(z.to_group(part, s), z.unit, z.layers))
+            self.held.append(Rows(self.order.arrived(z.to_group(part, s)), z.band, z.layers))
 
     def deliver(self):
         z = self.z
@@ -584,13 +586,13 @@
         jobs = [[Copy(self.starts["deliver", s], z.slots, self.held)] for s in shifts]
         parts = self.run(jobs, "deliver")
         for s, part in zip(shifts, parts):
-            self.held.append(Rows(z.to_section(part, s), z.unit, z.slots))
+            self.held.append(Rows(self.order.arrived(z.to_section(part, s)), z.band, z.slots))
 
     def collect(self):
         z = self.z
         units = z.slots * z.sections
         (half,) = self.run([[Copy(self.starts["collect"], units, self.held)]], "collect")
-        self.halves = (half, z.to_core(half))
+        self.halves = (half, self.order.arrived(z.to_core(half)))
 
 
 def per_device(
@@ -608,31 +610,23 @@
     place = jnp.stack([lax.axis_index("pipe"), lax.axis_index("section")]).astype(jnp.int32)
     state = (weights[0, 0], first_moment[0, 0], second_moment[0, 0])
     grads = Gradients(z, order, gradients[0, 0])
-    chunks = [Chunk(z, order, array, at) for array in state for at in range(z.units)]
+    chunks = [Chunk(z, order, array) for array in state]
     table, starts = make_plan(z, place, old_section, new_section, lost_pipe, donor_offset)
     for part in (grads, *chunks):
         part.table, part.starts = table, starts
 
-    def each(step, *args):
-        for at, chunk in enumerate(chunks):
-            order.begin(step[0] + str(at))
-            getattr(chunk, step)(*args)
-
-    order.begin("ge")
-    grads.enter(place)
-    each("enter", place)
-    order.begin("gs")
-    grads.scatter()
-    each("spread")
-    order.begin("gx")
-    grads.exchange()
-    each("across")
-    order.begin("gg")
-    grads.gather()
-    each("deliver")
-    order.begin("gf")
-    grads.finish()
-    each("collect")
+    for name in SEQUENCE:
+        order.begin(name)
+        if name[0] == "g" and name[1] in "esxgf":
+            part = grads
+            step = dict(e="enter", s="scatter", x="exchange", g="gather", f="finish")[name[1]]
+        else:
+            part = chunks[int(name[1])]
+            step = dict(e="enter", s="spread", a="across", d="deliver", c="collect")[name[0]]
+        if step == "enter":
+            part.enter(place)
+        else:
+            getattr(part, step)()
     order.begin("u")
     rebuilt = [chunk.halves for chunk in chunks]
     outs = update(z, order, table, starts["update"], state, rebuilt, grads.mean)

time: 130 us -> 131 us (level)
  Pallas kernels: 38.8 us -> 43.8 us
  local copies, waits for them, and re-layouts: 7.05 us -> 3.17 us
  starting transfers between devices: 15 us -> 16.5 us
  waiting for transfers between devices: 67 us -> 65.5 us
    pallas_call x4, Pallas kernels: 6.77 us -> 15.7 us  [halve(): return order.then(call(place, view, *order.last))]
    pallas_call x16, Pallas kernels: 21.3 us -> 16.6 us  [stage(): return order.then(call(table, *operands, *order.last))]
    unnamed x28 -> x16, local copies, waits for them, and re-layouts: 7.05 us -> 3.17 us
    ppermute x20, starting transfers between devices: 15 us -> 16.5 us  [send(): return lax.ppermute(value, AXES, pairs)]
    ppermute x20, waiting for transfers between devices: 67 us -> 65.5 us  [send(): return lax.ppermute(value, AXES, pairs)]
  transfers between devices with their start and end apart: 20 -> 20, of which waited for: 10 -> 9; matrix products, arithmetic and copies ran while one was open for 0% -> 0% of each run, Pallas kernels for 22% -> 23%
where the time goes in v3:
time: 131 us
  waiting for transfers between devices  65.5 us (50%)
  Pallas kernels  43.8 us (33%)
  starting transfers between devices  16.5 us (13%)
  local copies, waits for them, and re-layouts  3.17 us (2%)
    ppermute x20, waiting for transfers between devices, send(): return lax.ppermute(value, AXES, pairs)  65.5 us
    pallas_call x16, Pallas kernels, stage(): return order.then(call(table, *operands, *order.last))  16.6 us
    ppermute x20, starting transfers between devices, send(): return lax.ppermute(value, AXES, pairs)  16.5 us
    pallas_call x4, Pallas kernels, halve(): return order.then(call(place, view, *order.last))  15.7 us
    pallas_call x1, Pallas kernels, update(): return order.then(call(table, *views, *mean, *halves, *order.last))  9.61 us
    unnamed x16, local copies, waits for them, and re-layouts  3.17 us
  transfers between devices with their start and end apart: 20, of which 9 were waited for; matrix products, arithmetic and copies ran while one was open for 0% of the time, Pallas kernels for 23%

profile of v3, /device:TPU:0, one launch (start us, length us, event | category | flops | bytes accessed | tf_op | source)
XLA Modules:
  0.0 130.6 jit_solution(6521989317047364831)
XLA Ops:
  0.6 0.7 pad_add_fusion.place_ref
  1.3 3.5 %halve_gradients.1 = (bf16[1024,512]{1,0:T(8,128)(2,1)}, bf16[1024,512]{1,0:T(8,128)(2,1)}) custom-call(s32[2]{0:T(128)} %pad_add_fusion.place_ref, bf16[2,2,512,512]{3,2,1,0:T(8,128)(2,1)} %bitcast.20), custom_call_target="tpu_custom_call" | custom-call | flops 1000000000 | bytes 1 | tf_op jit(solution)/shard_map/halve_gradients/pallas_call | solution.py:429
  4.8 0.5 collective-permute-start
  5.3 4.3 %halve_state.5 = (bf16[1024,512]{1,0:T(8,128)(2,1)}, bf16[1024,512]{1,0:T(8,128)(2,1)}) custom-call(s32[2]{0:T(128)} %pad_add_fusion.place_ref, f32[2,2,512,512]{3,2,1,0:T(8,128)} %bitcast.16), custom_call_target="tpu_custom_call" | custom-call | flops 1000000000 | bytes 1 | tf_op jit(solution)/shard_map/halve_state/pallas_call | solution.py:429
  9.7 0.1 collective-permute-start.13
  9.8 4.3 %halve_state.4 = (bf16[1024,512]{1,0:T(8,128)(2,1)}, bf16[1024,512]{1,0:T(8,128)(2,1)}) custom-call(s32[2]{0:T(128)} %pad_add_fusion.place_ref, f32[2,2,512,512]{3,2,1,0:T(8,128)} %bitcast.14), custom_call_target="tpu_custom_call" | custom-call | flops 1000000000 | bytes 1 | tf_op jit(solution)/shard_map/halve_state/pallas_call | solution.py:429
  14.1 0.5 collective-permute-start.9
  14.6 3.6 %halve_state.3 = (bf16[1024,512]{1,0:T(8,128)(2,1)}, bf16[1024,512]{1,0:T(8,128)(2,1)}) custom-call(s32[2]{0:T(128)} %pad_add_fusion.place_ref, bf16[2,2,512,512]{3,2,1,0:T(8,128)(2,1)} %bitcast.12), custom_call_target="tpu_custom_call" | custom-call | flops 1000000000 | bytes 1 | tf_op jit(solution)/shard_map/halve_state/pallas_call | solution.py:429
  18.2 0.1 collective-permute-start.5
  18.4 1.9 %plan.1.table_ref = s32[2048]{0:T(1024)} custom-call(s32[2]{0:T(128)} %pad_add_fusion.place_ref, s32[4,3]{1,0:T(4,128)} %old_ref.1, s32[3]{0:T(128)} %new_ref.1, s32[4]{0:T(128)} %lost_ref.1, s32[3]{0:T(128)} %offset_ref.1), custom_call_target="tpu_custom_call" | custom-call | tf_op jit(solution)/shard_map/plan/pallas_call | solution.py:261
  20.3 0.7 copy-done.5
  21.0 1.2 copy-done.6
  22.2 1.5 %grad_out.1 = bf16[768,512]{1,0:T(8,128)(2,1)S(1)} custom-call(s32[2048]{0:T(1024)S(1)} %copy-done.5, bf16[1024,512]{1,0:T(8,128)(2,1)S(1)} %copy-done.6, bf16[1024,512]{1,0:T(8,128)(2,1)} %collective-permute-done.refs_1_), custom_call_target="tpu_custom_call" | custom-call | flops 1000000000 | bytes 1 | tf_op jit(solution)/shard_map/grad_out/pallas_call | solution.py:383
  23.7 0.0 copy-start
  23.7 2.9 %collective-permute-start.1 = (bf16[768,512]{1,0:T(8,128)(2,1)S(1)}, bf16[768,512]{1,0:T(8,128)(2,1)S(1)}, u32[]{:S(2)}, u32[]{:S(2)}) collective-permute-start(bf16[768,512]{1,0:T(8,128)(2,1)S(1)} %grad_out.1), channel_id=1, source_target_pairs={{0,16},{4,20},{8,24},{12,28},{16,0},{20,4},{24,8},{28,12},{1,17},{... | collective-permute-start | bytes 2359304 | tf_op jit(solution)/shard_map/ppermute | solution.py:73
  26.6 0.0 collective-permute-done.13.refs_1_
  26.6 1.2 copy-done.2
  27.8 1.3 spread.5
  29.1 1.6 %collective-permute-start.14 = (bf16[512,512]{1,0:T(8,128)(2,1)S(1)}, bf16[512,512]{1,0:T(8,128)(2,1)S(1)}, u32[]{:S(2)}, u32[]{:S(2)}) collective-permute-start(bf16[512,512]{1,0:T(8,128)(2,1)S(1)} %spread.5), channel_id=1, source_target_pairs={{0,4},{4,0},{8,12},{12,8},{16,20},{20,16},{24,28},{28,24},{1,5},{5... | collective-permute-start | bytes 1572872 | tf_op jit(solution)/shard_map/ppermute | solution.py:73
  30.7 0.0 collective-permute-done.9.refs_1_
  30.7 0.7 spread.4
  31.4 0.0 copy-start.7
  31.5 0.6 collective-permute-start.10
  32.1 0.0 collective-permute-done.5.refs_1_
  32.1 0.7 spread.3
  32.8 1.6 %collective-permute-start.6 = (bf16[512,512]{1,0:T(8,128)(2,1)S(1)}, bf16[512,512]{1,0:T(8,128)(2,1)S(1)}, u32[]{:S(2)}, u32[]{:S(2)}) collective-permute-start(bf16[512,512]{1,0:T(8,128)(2,1)S(1)} %spread.3), channel_id=1, source_target_pairs={{0,4},{4,0},{8,12},{12,8},{16,20},{20,16},{24,28},{28,24},{1,5},{5... | collective-permute-start | bytes 1572872 | tf_op jit(solution)/shard_map/ppermute | solution.py:73
  34.4 9.6 %collective-permute-done.14.refs_2_ = bf16[512,512]{1,0:T(8,128)(2,1)S(1)} collective-permute-done((bf16[512,512]{1,0:T(8,128)(2,1)S(1)}, bf16[512,512]{1,0:T(8,128)(2,1)S(1)}, u32[]{:S(2)}, u32[]{:S(2)}) %collective-permute-start.14) | collective-permute-done | bytes 524320 | tf_op jit(solution)/shard_map/ppermute | solution.py:73
  44.0 1.4 %across.5 = bf16[768,512]{1,0:T(8,128)(2,1)S(1)} custom-call(s32[2048]{0:T(1024)S(1)} %copy-done.5, bf16[1024,512]{1,0:T(8,128)(2,1)S(1)} %copy-done.2, bf16[1024,512]{1,0:T(8,128)(2,1)} %collective-permute-done.13.refs_1_, bf16[512,512]{1,0:T(8,128)(2,1)S(1)} %collective-permute-done.14.refs_2_), custom_call_target="tpu_custom_call" | custom-call | flops 1000000000 | bytes 1 | tf_op jit(solution)/shard_map/across/pallas_call | solution.py:383
  45.4 0.1 collective-permute-start.15
  45.5 1.7 %grad_sum.1.refs_0_ = bf16[768,512]{1,0:T(8,128)(2,1)S(1)} custom-call(s32[2048]{0:T(1024)S(1)} %copy-done.5, bf16[1024,512]{1,0:T(8,128)(2,1)S(1)} %copy-done.7, bf16[1024,512]{1,0:T(8,128)(2,1)} %collective-permute-done.refs_1_, bf16[768,512]{1,0:T(8,128)(2,1)S(1)} %collective-permute-done.1.refs_2_), custom_call_target="tpu_custom_call" | custom-call | flops 1000000000 | bytes 1 | tf_op jit(solution)/shard_map/grad_sum/pallas_call | solution.py:383
  47.2 2.0 %collective-permute-start.2 = (bf16[768,512]{1,0:T(8,128)(2,1)S(1)}, bf16[768,512]{1,0:T(8,128)(2,1)S(1)}, u32[]{:S(2)}, u32[]{:S(2)}) collective-permute-start(bf16[768,512]{1,0:T(8,128)(2,1)S(1)} %grad_sum.1.refs_0_), channel_id=1, source_target_pairs={{0,4},{4,0},{8,12},{12,8},{16,20},{20,16},{24,28},{28,24},{1,5},{5... | collective-permute-start | bytes 2359304 | tf_op jit(solution)/shard_map/ppermute | solution.py:73
  49.1 6.1 %collective-permute-done.10.refs_2_ = bf16[512,512]{1,0:T(8,128)(2,1)S(1)} collective-permute-done((bf16[512,512]{1,0:T(8,128)(2,1)S(1)}, bf16[512,512]{1,0:T(8,128)(2,1)S(1)}, u32[]{:S(2)}, u32[]{:S(2)}) %collective-permute-start.10) | collective-permute-done | bytes 524320 | tf_op jit(solution)/shard_map/ppermute | solution.py:73
  55.2 0.8 across.4
  56.1 0.1 collective-permute-start.11
  56.1 10.4 %collective-permute-done.6.refs_2_ = bf16[512,512]{1,0:T(8,128)(2,1)S(1)} collective-permute-done((bf16[512,512]{1,0:T(8,128)(2,1)S(1)}, bf16[512,512]{1,0:T(8,128)(2,1)S(1)}, u32[]{:S(2)}, u32[]{:S(2)}) %collective-permute-start.6) | collective-permute-done | bytes 524320 | tf_op jit(solution)/shard_map/ppermute | solution.py:73
  66.5 0.8 across.3
  67.3 0.1 collective-permute-start.7
  67.4 0.0 collective-permute-done.15.refs_3_
  67.4 1.3 deliver.5
  68.7 2.0 %collective-permute-start.16 = (bf16[512,512]{1,0:T(8,128)(2,1)S(1)}, bf16[512,512]{1,0:T(8,128)(2,1)S(1)}, u32[]{:S(2)}, u32[]{:S(2)}) collective-permute-start(bf16[512,512]{1,0:T(8,128)(2,1)S(1)} %deliver.5), channel_id=1, source_target_pairs={{0,4},{4,0},{8,12},{12,8},{16,20},{20,16},{24,28},{28,24},{1,5},{5... | collective-permute-start | bytes 1572872 | tf_op jit(solution)/shard_map/ppermute | solution.py:73
  70.7 12.7 %collective-permute-done.2.refs_1_ = bf16[768,512]{1,0:T(8,128)(2,1)S(1)} collective-permute-done((bf16[768,512]{1,0:T(8,128)(2,1)S(1)}, bf16[768,512]{1,0:T(8,128)(2,1)S(1)}, u32[]{:S(2)}, u32[]{:S(2)}) %collective-permute-start.2) | collective-permute-done | bytes 786464 | tf_op jit(solution)/shard_map/ppermute | solution.py:73
  83.3 1.0 grad_mean.1.refs_0_
  84.3 0.1 collective-permute-start.3
  84.4 0.0 collective-permute-done.11.refs_3_
  84.4 0.7 deliver.4
  85.1 2.0 %collective-permute-start.12 = (bf16[512,512]{1,0:T(8,128)(2,1)S(1)}, bf16[512,512]{1,0:T(8,128)(2,1)S(1)}, u32[]{:S(2)}, u32[]{:S(2)}) collective-permute-start(bf16[512,512]{1,0:T(8,128)(2,1)S(1)} %deliver.4), channel_id=1, source_target_pairs={{0,4},{4,0},{8,12},{12,8},{16,20},{20,16},{24,28},{28,24},{1,5},{5... | collective-permute-start | bytes 1572872 | tf_op jit(solution)/shard_map/ppermute | solution.py:73
  87.2 12.5 %collective-permute-done.7.refs_3_ = bf16[768,512]{1,0:T(8,128)(2,1)S(1)} collective-permute-done((bf16[768,512]{1,0:T(8,128)(2,1)S(1)}, bf16[768,512]{1,0:T(8,128)(2,1)S(1)}, u32[]{:S(2)}, u32[]{:S(2)}) %collective-permute-start.7) | collective-permute-done | bytes 786464 | tf_op jit(solution)/shard_map/ppermute | solution.py:73
  99.6 0.7 deliver.3
  100.4 1.6 %collective-permute-start.8 = (bf16[512,512]{1,0:T(8,128)(2,1)S(1)}, bf16[512,512]{1,0:T(8,128)(2,1)S(1)}, u32[]{:S(2)}, u32[]{:S(2)}) collective-permute-start(bf16[512,512]{1,0:T(8,128)(2,1)S(1)} %deliver.3), channel_id=1, source_target_pairs={{0,4},{4,0},{8,12},{12,8},{16,20},{20,16},{24,28},{28,24},{1,5},{5... | collective-permute-start | bytes 1572872 | tf_op jit(solution)/shard_map/ppermute | solution.py:73
  102.0 0.0 collective-permute-done.16.refs_4_
  102.0 1.4 %collect.5.refs_7_ = bf16[1024,512]{1,0:T(8,128)(2,1)S(1)} custom-call(s32[2048]{0:T(1024)S(1)} %copy-done.5, bf16[1024,512]{1,0:T(8,128)(2,1)S(1)} %copy-done.3, bf16[1024,512]{1,0:T(8,128)(2,1)} %collective-permute-done.13.refs_1_, bf16[512,512]{1,0:T(8,128)(2,1)S(1)} %collective-permute-done.14.refs_2_, ...), custom_call_target="tpu_custom_call" | custom-call | flops 1000000000 | bytes 1 | tf_op jit(solution)/shard_map/collect/pallas_call | solution.py:383
  103.4 0.1 collective-permute-start.19
  103.4 2.4 %collective-permute-done.12.refs_4_ = bf16[512,512]{1,0:T(8,128)(2,1)S(1)} collective-permute-done((bf16[512,512]{1,0:T(8,128)(2,1)S(1)}, bf16[512,512]{1,0:T(8,128)(2,1)S(1)}, u32[]{:S(2)}, u32[]{:S(2)}) %collective-permute-start.12) | collective-permute-done | bytes 524320 | tf_op jit(solution)/shard_map/ppermute | solution.py:73
  105.8 0.8 collect.4.refs_6_
  106.7 0.0 copy-start.4
  106.7 0.1 collective-permute-start.18
  106.7 9.2 %collective-permute-done.8.refs_4_ = bf16[512,512]{1,0:T(8,128)(2,1)S(1)} collective-permute-done((bf16[512,512]{1,0:T(8,128)(2,1)S(1)}, bf16[512,512]{1,0:T(8,128)(2,1)S(1)}, u32[]{:S(2)}, u32[]{:S(2)}) %collective-permute-start.8) | collective-permute-done | bytes 524320 | tf_op jit(solution)/shard_map/ppermute | solution.py:73
  115.9 0.8 collect.3.refs_5_
  116.8 0.1 collective-permute-start.17
  116.9 0.9 mean.1
  117.8 0.6 collective-permute-start.4
  118.3 1.2 collective-permute-done.17.refs_8_
  119.5 1.5 %collective-permute-done.4.refs_4_ = bf16[1024,512]{1,0:T(8,128)(2,1)S(1)} collective-permute-done((bf16[1024,512]{1,0:T(8,128)(2,1)S(1)}, bf16[1024,512]{1,0:T(8,128)(2,1)S(1)}, u32[]{:S(2)}, u32[]{:S(2)}) %collective-permute-start.4) | collective-permute-done | bytes 1048608 | tf_op jit(solution)/shard_map/ppermute | solution.py:73
  121.0 9.6 %update.1 = (bf16[2,2,512,512]{3,2,1,0:T(8,128)(2,1)}, f32[2,2,512,512]{3,2,1,0:T(8,128)}, f32[2,2,512,512]{3,2,1,0:T(8,128)}) custom-call(s32[2048]{0:T(1024)S(1)} %copy-done.5, bf16[2048,512]{1,0:T(8,128)(2,1)S(1)} %bitcast.13, f32[2048,512]{1,0:T(8,128)} %bitcast.15, f32[2048,512]{1,0:T(8,128)} %bitcast.17, ...), custom_call_target="tpu_custom_call" | custom-call | flops 1 | bytes 1 | tf_op jit(solution)/shard_map/update/pallas_call | solution.py:503
  (15 shorter events, 0.0 us)
Async XLA Ops:
  4.8 15.4 %collective-permute-start = (bf16[1024,512]{1,0:T(8,128)(2,1)}, bf16[1024,512]{1,0:T(8,128)(2,1)}, u32[]{:S(2)}, u32[]{:S(2)}) collective-permute-start(bf16[1024,512]{1,0:T(8,128)(2,1)} %get-tuple-element.17), channel_id=1, source_target_pairs={{0,8},{4,12},{8,0},{12,4},{16,24},{20,28},{24,16},{28,20},{1,9},{5... | collective-permute-start | bytes 3145736 | tf_op jit(solution)/shard_map/ppermute | solution.py:73
  9.7 17.0 %collective-permute-start.13 = (bf16[1024,512]{1,0:T(8,128)(2,1)}, bf16[1024,512]{1,0:T(8,128)(2,1)}, u32[]{:S(2)}, u32[]{:S(2)}) collective-permute-start(bf16[1024,512]{1,0:T(8,128)(2,1)} %get-tuple-element.25), channel_id=1, source_target_pairs={{0,8},{4,12},{8,0},{12,4},{16,24},{20,28},{24,16},{28,20},{1,9},{5... | collective-permute-start | bytes 3145736 | tf_op jit(solution)/shard_map/ppermute | solution.py:73
  14.1 16.6 %collective-permute-start.9 = (bf16[1024,512]{1,0:T(8,128)(2,1)}, bf16[1024,512]{1,0:T(8,128)(2,1)S(1)}, u32[]{:S(2)}, u32[]{:S(2)}) collective-permute-start(bf16[1024,512]{1,0:T(8,128)(2,1)} %get-tuple-element.23), channel_id=1, source_target_pairs={{0,8},{4,12},{8,0},{12,4},{16,24},{20,28},{24,16},{28,20},{1,9},{5... | collective-permute-start | bytes 3145736 | tf_op jit(solution)/shard_map/ppermute | solution.py:73
  18.2 12.5 %copy-start.1 = (bf16[1024,512]{1,0:T(8,128)(2,1)S(1)}, bf16[1024,512]{1,0:T(8,128)(2,1)}, u32[]{:S(2)}) copy-start(bf16[1024,512]{1,0:T(8,128)(2,1)} %get-tuple-element.22.refs_0_) | copy-start | bytes 3145732
  18.2 13.8 %collective-permute-start.5 = (bf16[1024,512]{1,0:T(8,128)(2,1)}, bf16[1024,512]{1,0:T(8,128)(2,1)S(1)}, u32[]{:S(2)}, u32[]{:S(2)}) collective-permute-start(bf16[1024,512]{1,0:T(8,128)(2,1)} %get-tuple-element.21), channel_id=1, source_target_pairs={{0,8},{4,12},{8,0},{12,4},{16,24},{20,28},{24,16},{28,20},{1,9},{5... | collective-permute-start | bytes 3145736 | tf_op jit(solution)/shard_map/ppermute | solution.py:73
  20.3 0.7 copy-start.5
  21.0 1.2 copy-start.6
  23.7 8.4 %copy-start = (bf16[1024,512]{1,0:T(8,128)(2,1)S(1)}, bf16[1024,512]{1,0:T(8,128)(2,1)}, u32[]{:S(2)}) copy-start(bf16[1024,512]{1,0:T(8,128)(2,1)} %get-tuple-element.20.refs_0_) | copy-start | bytes 3145732
  23.7 21.7 %collective-permute-start.1 = (bf16[768,512]{1,0:T(8,128)(2,1)S(1)}, bf16[768,512]{1,0:T(8,128)(2,1)S(1)}, u32[]{:S(2)}, u32[]{:S(2)}) collective-permute-start(bf16[768,512]{1,0:T(8,128)(2,1)S(1)} %grad_out.1), channel_id=1, source_target_pairs={{0,16},{4,20},{8,24},{12,28},{16,0},{20,4},{24,8},{28,12},{1,17},{... | collective-permute-start | bytes 2359304 | tf_op jit(solution)/shard_map/ppermute | solution.py:73
  26.6 1.2 copy-start.2
  29.1 14.9 %collective-permute-start.14 = (bf16[512,512]{1,0:T(8,128)(2,1)S(1)}, bf16[512,512]{1,0:T(8,128)(2,1)S(1)}, u32[]{:S(2)}, u32[]{:S(2)}) collective-permute-start(bf16[512,512]{1,0:T(8,128)(2,1)S(1)} %spread.5), channel_id=1, source_target_pairs={{0,4},{4,0},{8,12},{12,8},{16,20},{20,16},{24,28},{28,24},{1,5},{5... | collective-permute-start | bytes 1572872 | tf_op jit(solution)/shard_map/ppermute | solution.py:73
  31.4 14.0 %copy-start.7 = (bf16[1024,512]{1,0:T(8,128)(2,1)S(1)}, bf16[1024,512]{1,0:T(8,128)(2,1)}, u32[]{:S(2)}) copy-start(bf16[1024,512]{1,0:T(8,128)(2,1)} %get-tuple-element.16.refs_0_) | copy-start | bytes 3145732
  31.5 23.8 %collective-permute-start.10 = (bf16[512,512]{1,0:T(8,128)(2,1)S(1)}, bf16[512,512]{1,0:T(8,128)(2,1)S(1)}, u32[]{:S(2)}, u32[]{:S(2)}) collective-permute-start(bf16[512,512]{1,0:T(8,128)(2,1)S(1)} %spread.4), channel_id=1, source_target_pairs={{0,4},{4,0},{8,12},{12,8},{16,20},{20,16},{24,28},{28,24},{1,5},{5... | collective-permute-start | bytes 1572872 | tf_op jit(solution)/shard_map/ppermute | solution.py:73
  32.8 33.7 %collective-permute-start.6 = (bf16[512,512]{1,0:T(8,128)(2,1)S(1)}, bf16[512,512]{1,0:T(8,128)(2,1)S(1)}, u32[]{:S(2)}, u32[]{:S(2)}) collective-permute-start(bf16[512,512]{1,0:T(8,128)(2,1)S(1)} %spread.3), channel_id=1, source_target_pairs={{0,4},{4,0},{8,12},{12,8},{16,20},{20,16},{24,28},{28,24},{1,5},{5... | collective-permute-start | bytes 1572872 | tf_op jit(solution)/shard_map/ppermute | solution.py:73
  45.4 22.0 %collective-permute-start.15 = (bf16[768,512]{1,0:T(8,128)(2,1)S(1)}, bf16[768,512]{1,0:T(8,128)(2,1)S(1)}, u32[]{:S(2)}, u32[]{:S(2)}) collective-permute-start(bf16[768,512]{1,0:T(8,128)(2,1)S(1)} %across.5), channel_id=1, source_target_pairs={{0,16},{4,20},{8,24},{12,28},{16,0},{20,4},{24,8},{28,12},{1,17},{... | collective-permute-start | bytes 2359304 | tf_op jit(solution)/shard_map/ppermute | solution.py:73
  47.2 20.2 %copy-start.3 = (bf16[1024,512]{1,0:T(8,128)(2,1)S(1)}, bf16[1024,512]{1,0:T(8,128)(2,1)}, u32[]{:S(2)}) copy-start(bf16[1024,512]{1,0:T(8,128)(2,1)} %get-tuple-element.24.refs_0_) | copy-start | bytes 3145732
  47.2 36.2 %collective-permute-start.2 = (bf16[768,512]{1,0:T(8,128)(2,1)S(1)}, bf16[768,512]{1,0:T(8,128)(2,1)S(1)}, u32[]{:S(2)}, u32[]{:S(2)}) collective-permute-start(bf16[768,512]{1,0:T(8,128)(2,1)S(1)} %grad_sum.1.refs_0_), channel_id=1, source_target_pairs={{0,4},{4,0},{8,12},{12,8},{16,20},{20,16},{24,28},{28,24},{1,5},{5... | collective-permute-start | bytes 2359304 | tf_op jit(solution)/shard_map/ppermute | solution.py:73
  56.1 28.3 %collective-permute-start.11 = (bf16[768,512]{1,0:T(8,128)(2,1)S(1)}, bf16[768,512]{1,0:T(8,128)(2,1)S(1)}, u32[]{:S(2)}, u32[]{:S(2)}) collective-permute-start(bf16[768,512]{1,0:T(8,128)(2,1)S(1)} %across.4), channel_id=1, source_target_pairs={{0,16},{4,20},{8,24},{12,28},{16,0},{20,4},{24,8},{28,12},{1,17},{... | collective-permute-start | bytes 2359304 | tf_op jit(solution)/shard_map/ppermute | solution.py:73
  67.3 32.3 %collective-permute-start.7 = (bf16[768,512]{1,0:T(8,128)(2,1)S(1)}, bf16[768,512]{1,0:T(8,128)(2,1)S(1)}, u32[]{:S(2)}, u32[]{:S(2)}) collective-permute-start(bf16[768,512]{1,0:T(8,128)(2,1)S(1)} %across.3), channel_id=1, source_target_pairs={{0,16},{4,20},{8,24},{12,28},{16,0},{20,4},{24,8},{28,12},{1,17},{... | collective-permute-start | bytes 2359304 | tf_op jit(solution)/shard_map/ppermute | solution.py:73
  68.7 33.3 %collective-permute-start.16 = (bf16[512,512]{1,0:T(8,128)(2,1)S(1)}, bf16[512,512]{1,0:T(8,128)(2,1)S(1)}, u32[]{:S(2)}, u32[]{:S(2)}) collective-permute-start(bf16[512,512]{1,0:T(8,128)(2,1)S(1)} %deliver.5), channel_id=1, source_target_pairs={{0,4},{4,0},{8,12},{12,8},{16,20},{20,16},{24,28},{28,24},{1,5},{5... | collective-permute-start | bytes 1572872 | tf_op jit(solution)/shard_map/ppermute | solution.py:73
  84.3 32.6 %collective-permute-start.3 = (bf16[768,512]{1,0:T(8,128)(2,1)S(1)}, bf16[768,512]{1,0:T(8,128)(2,1)S(1)}, u32[]{:S(2)}, u32[]{:S(2)}) collective-permute-start(bf16[768,512]{1,0:T(8,128)(2,1)S(1)} %grad_mean.1.refs_0_), channel_id=1, source_target_pairs={{0,16},{4,20},{8,24},{12,28},{16,0},{20,4},{24,8},{28,12},{1,17},{... | collective-permute-start | bytes 2359304 | tf_op jit(solution)/shard_map/ppermute | solution.py:73
  85.1 20.7 %collective-permute-start.12 = (bf16[512,512]{1,0:T(8,128)(2,1)S(1)}, bf16[512,512]{1,0:T(8,128)(2,1)S(1)}, u32[]{:S(2)}, u32[]{:S(2)}) collective-permute-start(bf16[512,512]{1,0:T(8,128)(2,1)S(1)} %deliver.4), channel_id=1, source_target_pairs={{0,4},{4,0},{8,12},{12,8},{16,20},{20,16},{24,28},{28,24},{1,5},{5... | collective-permute-start | bytes 1572872 | tf_op jit(solution)/shard_map/ppermute | solution.py:73
  100.4 15.6 %collective-permute-start.8 = (bf16[512,512]{1,0:T(8,128)(2,1)S(1)}, bf16[512,512]{1,0:T(8,128)(2,1)S(1)}, u32[]{:S(2)}, u32[]{:S(2)}) collective-permute-start(bf16[512,512]{1,0:T(8,128)(2,1)S(1)} %deliver.3), channel_id=1, source_target_pairs={{0,4},{4,0},{8,12},{12,8},{16,20},{20,16},{24,28},{28,24},{1,5},{5... | collective-permute-start | bytes 1572872 | tf_op jit(solution)/shard_map/ppermute | solution.py:73
  103.4 14.9 %collective-permute-start.19 = (bf16[1024,512]{1,0:T(8,128)(2,1)S(1)}, bf16[1024,512]{1,0:T(8,128)(2,1)S(1)}, u32[]{:S(2)}, u32[]{:S(2)}) collective-permute-start(bf16[1024,512]{1,0:T(8,128)(2,1)S(1)} %collect.5.refs_7_), channel_id=1, source_target_pairs={{0,8},{4,12},{8,0},{12,4},{16,24},{20,28},{24,16},{28,20},{1,9},{5... | collective-permute-start | bytes 3145736 | tf_op jit(solution)/shard_map/ppermute | solution.py:73
  106.7 14.4 %copy-start.4 = (bf16[1,1,2,1024,512]{4,3,2,1,0:T(8,128)(2,1)S(1)}, bf16[1,1,2,1024,512]{4,3,2,1,0:T(8,128)(2,1)}, u32[]{:S(2)}) copy-start(bf16[1,1,2,1024,512]{4,3,2,1,0:T(8,128)(2,1)} %param.8) | copy-start | bytes 6291460
  106.7 11.6 %collective-permute-start.18 = (bf16[1024,512]{1,0:T(8,128)(2,1)S(1)}, bf16[1024,512]{1,0:T(8,128)(2,1)S(1)}, u32[]{:S(2)}, u32[]{:S(2)}) collective-permute-start(bf16[1024,512]{1,0:T(8,128)(2,1)S(1)} %collect.4.refs_6_), channel_id=1, source_target_pairs={{0,8},{4,12},{8,0},{12,4},{16,24},{20,28},{24,16},{28,20},{1,9},{5... | collective-permute-start | bytes 3145736 | tf_op jit(solution)/shard_map/ppermute | solution.py:73
  116.8 2.7 %collective-permute-start.17 = (bf16[1024,512]{1,0:T(8,128)(2,1)S(1)}, bf16[1024,512]{1,0:T(8,128)(2,1)S(1)}, u32[]{:S(2)}, u32[]{:S(2)}) collective-permute-start(bf16[1024,512]{1,0:T(8,128)(2,1)S(1)} %collect.3.refs_5_), channel_id=1, source_target_pairs={{0,8},{4,12},{8,0},{12,4},{16,24},{20,28},{24,16},{28,20},{1,9},{5... | collective-permute-start | bytes 3145736 | tf_op jit(solution)/shard_map/ppermute | solution.py:73
  117.8 3.3 %collective-permute-start.4 = (bf16[1024,512]{1,0:T(8,128)(2,1)S(1)}, bf16[1024,512]{1,0:T(8,128)(2,1)S(1)}, u32[]{:S(2)}, u32[]{:S(2)}) collective-permute-start(bf16[1024,512]{1,0:T(8,128)(2,1)S(1)} %get-tuple-element.19), channel_id=1, source_target_pairs={{0,8},{4,12},{8,0},{12,4},{16,24},{20,28},{24,16},{28,20},{1,9},{5... | collective-permute-start | bytes 3145736 | tf_op jit(solution)/shard_map/ppermute | solution.py:73

commit v4 on v3

--- a/solution.py
+++ b/solution.py
@@ -1,5 +1,3 @@
-import math
-
 import jax
 import jax.numpy as jnp
 from jax import lax
@@ -19,8 +17,7 @@
     *("gg", "d0", "d1", "d2", "gf", "c0", "c1", "c2"),
 )
 AFTER = {}
-VMEM = 40 * 1024 * 1024
-HALVE_VMEM = 60 * 1024 * 1024
+VMEM = 24 * 1024 * 1024
 AXES = ("pipe", "section")
 
 
@@ -53,7 +50,6 @@
         self.layers = new_section.shape[0]
         self.half = self.rows // CORES
         self.band = self.half // self.sections
-        self.block = math.gcd(self.band, 32)
         self.grad_band = self.half // self.groups
         doubles = self.layers - self.sections
         widest = 0
@@ -132,7 +128,7 @@
 
     def grad_unit(l, band):
         return [
-            (as_int(my_now[l] == section), my_slot[l] * z.groups + band),
+            (as_int(my_now[l] == section), (my_slot[l] * CORES + core) * z.groups + band),
             (as_int(sib_now[l] == section), sib_slot[l] * z.groups + band),
         ]
 
@@ -165,13 +161,14 @@
             slot = total(hit[l] * source_slot[l] for l in layers)
             mine = total(hit[l] * from_me[l] for l in layers)
             found = total(hit)
-            index = slot * z.sections + band
-            units.append([(mine, index), (found - mine, index)])
+            own = (slot * CORES + core) * z.sections + band
+            units.append([(mine, own), (found - mine, slot * z.sections + band)])
         tables["spread", shift] = units
 
     def held(l_my_chip, l_from_me, l_slot, l_here, l_channel, l_section):
+        own = (l_slot * CORES + core) * z.sections + section
         index = l_slot * z.sections + section
-        unit = [(l_my_chip * l_from_me, index), (l_my_chip * (1 - l_from_me), index)]
+        unit = [(l_my_chip * l_from_me, own), (l_my_chip * (1 - l_from_me), index)]
         for shift in range(1, z.sections):
             sender = lax.rem(section + z.sections - shift, z.sections)
             unit.append((l_here * as_int(l_section == sender), l_channel))
@@ -329,7 +326,8 @@
                 def _(unit=unit, source=source, ref=refs[at], entry=entry):
                     index = table_ref[entry + 1]
                     for array in range(self.arrays):
-                        out_ref[out.block(array, unit)] = ref[source.block(array, index)]
+                        block = ref[source.block(array, index)]
+                        out_ref[out.block(array, unit)] = block.astype(out_ref.dtype)
 
 
 class Sum:
@@ -383,112 +381,91 @@
     return order.then(call(table, *operands, *order.last))
 
 
-def halve(z, order, place, array, name):
+def sibling_half(z, order, place, array, name):
     view = array.reshape(z.slots, CORES, z.half, z.cols)
-    straight = array.dtype == jnp.bfloat16
 
     def kernel(place_ref, array_ref, *refs):
-        own_ref, their_ref, sems = refs[-5], refs[-4], refs[-1]
-        landed = refs[-3:-1]
-        core = lax.rem(place_ref[0], CORES)
-        copies = []
-        for part, (half, out_ref) in enumerate(((1 - core, their_ref), (core, own_ref))):
-            for slot in range(z.slots):
-                rows = pl.ds(slot * z.half, z.half)
-                target = out_ref if straight else landed[part]
-                copy = pltpu.make_async_copy(
-                    array_ref.at[slot, half], target.at[rows], sems.at[part, slot]
-                )
-                copy.start()
-                copies.append((copy, part, out_ref, slot))
-        for copy, part, out_ref, slot in copies:
-            copy.wait()
-            if not straight:
-
-                @pl.loop(0, z.half // z.block)
-                def _(at, part=part, out_ref=out_ref, slot=slot):
-                    rows = pl.ds(pl.multiple_of(slot * z.half + at * z.block, 16), z.block)
-                    out_ref[rows] = landed[part][rows].astype(jnp.bfloat16)
+        refs[-1][...] = array_ref[0, 0].astype(jnp.bfloat16)
+
+    def half_of(slot, place_ref):
+        return (slot, 1 - lax.rem(place_ref[0], CORES), 0, 0)
 
     out = jax.ShapeDtypeStruct((z.slots * z.half, z.cols), jnp.bfloat16)
-    scratch = (16, z.cols) if straight else out.shape
     call = pl.pallas_call(
         kernel,
-        out_shape=(out, out),
-        in_specs=[SMEM_SPEC, pl.BlockSpec(memory_space=pltpu.HBM)] + order.specs(),
-        out_specs=(VMEM_SPEC, VMEM_SPEC),
-        scratch_shapes=[
-            pltpu.VMEM(scratch, array.dtype),
-            pltpu.VMEM(scratch, array.dtype),
-            pltpu.SemaphoreType.DMA((2, z.slots)),
-        ],
-        compiler_params=pltpu.CompilerParams(vmem_limit_bytes=HALVE_VMEM),
+        grid_spec=pltpu.PrefetchScalarGridSpec(
+            num_scalar_prefetch=1,
+            grid=(z.slots,),
+            in_specs=[pl.BlockSpec((1, 1, z.half, z.cols), half_of)] + order.specs(),
+            out_specs=pl.BlockSpec((z.half, z.cols), lambda slot, place_ref: (slot, 0)),
+        ),
+        out_shape=out,
+        compiler_params=PARAMS,
         cost_estimate=COST,
         name="halve_" + name,
     )
-    return order.then(call(place, view, *order.last))
-
-
-def update(z, order, table, start, state, rebuilt, mean):
+    return order.then((call(place, view, *order.last),))[0]
+
+
+def update(z, order, table, start, part, state, rebuilt, mean, outs):
     views = [a.reshape(z.slots * z.rows, z.cols) for a in state]
-    halves = [chunk[part] for part in range(2) for chunk in rebuilt]
+    outs = [] if outs is None else list(outs)
+    rows, cols = 16, min(z.cols, 128)
+
+    def half_now(table_ref):
+        core = table_ref[start + 1]
+        return core if part == 0 else 1 - core
 
     def kernel(table_ref, *refs):
-        local_refs, mean_refs, half_refs = refs[:3], refs[3:5], refs[5:-3]
-        out_w, out_one, out_two = refs[-3:]
-        slot, half = pl.program_id(0), pl.program_id(1)
+        local_refs, lost_refs, mean_ref = refs[:3], refs[3:6], refs[6]
+        out_refs = refs[-3:]
+        slot = pl.program_id(0)
         is_lost = table_ref[start] != 0
-        mine = table_ref[start + 1] == half
         found = table_ref[start + 2 + slot] != 0
 
-        def each(source, lost):
-            @pl.loop(0, z.half // z.block)
+        def each(sources, base):
+            @pl.loop(0, z.half // rows)
             def _(at):
-                one_block(source, lost, at * z.block)
-
-        def one_block(source, lost, at):
-            row = pl.ds(pl.multiple_of(at, 16), z.block)
-            from_row = pl.ds(pl.multiple_of(slot * z.half + at, 16), z.block)
-            grad = mean_refs[source][from_row].astype(jnp.float32)
-            grad = grad * (1.0 / z.pipes)
-            if lost:
-                old = [ref[from_row] for ref in half_refs[source * 3 : source * 3 + 3]]
-            else:
-                local_row = pl.multiple_of(slot * z.rows + half * z.half + at, 16)
-                old = [ref[pl.ds(local_row, z.block)] for ref in local_refs]
-            weight, one, two = [value.astype(jnp.float32) for value in old]
-            next_one = BETA_ONE * one + (1.0 - BETA_ONE) * grad
-            next_two = BETA_TWO * two + (1.0 - BETA_TWO) * grad * grad
-            move = next_one / (jnp.sqrt(next_two) + EPSILON) + DECAY_RATE * weight
-            out_w[0, 0, row] = (weight - LEARN_RATE * move).astype(out_w.dtype)
-            out_one[0, 0, row] = next_one
-            out_two[0, 0, row] = next_two
-
-        for source in range(2):
-            ours = both(found, mine == (source == 0))
-
-            @pl.when(both(ours, is_lost))
-            def _(source=source):
-                each(source, True)
-
-            @pl.when(both(ours, jnp.logical_not(is_lost)))
-            def _(source=source):
-                each(source, False)
+                row = pl.ds(pl.multiple_of(at * rows, rows), rows)
+                mean_row = pl.ds(pl.multiple_of(slot * z.half + at * rows, rows), rows)
+                from_row = pl.ds(pl.multiple_of(base + at * rows, rows), rows)
+                for first in range(0, z.cols, cols):
+                    lanes = pl.ds(first, cols)
+                    weight, one, two = [
+                        ref[from_row, lanes].astype(jnp.float32) for ref in sources
+                    ]
+                    grad = mean_ref[mean_row, lanes].astype(jnp.float32)
+                    next_one = BETA_ONE * one + ((1.0 - BETA_ONE) / z.pipes) * grad
+                    next_two = BETA_TWO * two + ((1.0 - BETA_TWO) / z.pipes**2) * (grad * grad)
+                    move = next_one / (jnp.sqrt(next_two) + EPSILON)
+                    next_weight = (1.0 - LEARN_RATE * DECAY_RATE) * weight - LEARN_RATE * move
+                    for ref, value in zip(out_refs, (next_weight, next_one, next_two)):
+                        ref[0, 0, row, lanes] = value.astype(ref.dtype)
+
+        @pl.when(both(found, is_lost))
+        def _():
+            each(lost_refs, slot * z.half)
+
+        @pl.when(both(found, jnp.logical_not(is_lost)))
+        def _():
+            each(local_refs, slot * z.rows + half_now(table_ref) * z.half)
 
         @pl.when(jnp.logical_not(found))
         def _():
-            for ref in (out_w, out_one, out_two):
+            for ref in out_refs:
                 ref[...] = jnp.zeros(ref.shape, ref.dtype)
 
     block = (1, 1, z.half, z.cols)
-    out_spec = pl.BlockSpec(block, lambda slot, half, table_ref: (slot, half, 0, 0))
+    out_spec = pl.BlockSpec(block, lambda slot, table_ref: (slot, half_now(table_ref), 0, 0))
     shape = (z.slots, CORES, z.half, z.cols)
     call = pl.pallas_call(
         kernel,
         grid_spec=pltpu.PrefetchScalarGridSpec(
             num_scalar_prefetch=1,
-            grid=(z.slots, CORES),
-            in_specs=[VMEM_SPEC] * (5 + len(halves)) + order.specs(),
+            grid=(z.slots,),
+            in_specs=[VMEM_SPEC] * 7
+            + [pl.BlockSpec(memory_space=pl.ANY)] * len(outs)
+            + order.specs(),
             out_specs=[out_spec] * 3,
         ),
         out_shape=(
@@ -496,11 +473,13 @@
             jax.ShapeDtypeStruct(shape, jnp.float32),
             jax.ShapeDtypeStruct(shape, jnp.float32),
         ),
+        input_output_aliases={8 + at: at for at in range(len(outs))},
         compiler_params=PARAMS,
         cost_estimate=UPDATE_COST,
         name="update",
     )
-    return order.then(call(table, *views, *mean, *halves, *order.last))
+    operands = (*views, *(half[part] for half in rebuilt), mean[part], *outs)
+    return order.then(call(table, *operands, *order.last))
 
 
 class Gradients:
@@ -515,9 +494,13 @@
 
     def enter(self, place):
         z = self.z
-        own, theirs = halve(z, self.order, place, self.grads, "gradients")
-        theirs = self.order.arrived(z.to_core(theirs))
-        self.held = [Rows(flat, z.grad_band, z.slots * z.groups) for flat in (own, theirs)]
+        theirs = z.to_core(sibling_half(z, self.order, place, self.grads, "gradients"))
+        own = self.grads.reshape(z.slots * z.rows, z.cols)
+        theirs = self.order.arrived(theirs)
+        self.held = [
+            Rows(own, z.grad_band, z.slots * CORES * z.groups),
+            Rows(theirs, z.grad_band, z.slots * z.groups),
+        ]
 
     def scatter(self):
         z = self.z
@@ -561,10 +544,11 @@
 
     def enter(self, place):
         z = self.z
-        own, theirs = halve(z, self.order, place, self.array, "state")
+        theirs = z.to_core(sibling_half(z, self.order, place, self.array, "state"))
+        own = self.array.reshape(z.slots * z.rows, z.cols)
+        theirs = self.order.arrived(theirs)
         held = z.slots * z.sections
-        theirs = self.order.arrived(z.to_core(theirs))
-        self.held = [Rows(flat, z.band, held) for flat in (own, theirs)]
+        self.held = [Rows(own, z.band, CORES * held), Rows(theirs, z.band, held)]
 
     def spread(self):
         z = self.z
@@ -629,7 +613,9 @@
             getattr(part, step)()
     order.begin("u")
     rebuilt = [chunk.halves for chunk in chunks]
-    outs = update(z, order, table, starts["update"], state, rebuilt, grads.mean)
+    outs = None
+    for part in range(CORES):
+        outs = update(z, order, table, starts["update"], part, state, rebuilt, grads.mean, outs)
     return tuple(out.reshape((1, 1, z.slots, z.rows, z.cols)) for out in outs)
 
 

time: 131 us -> 121 us (0.924)
  Pallas kernels: 43.8 us -> 36.8 us
  waiting for transfers between devices: 65.5 us -> 60.1 us
  local copies, waits for them, and re-layouts: 3.17 us -> 5.92 us
    pallas_call x5 -> x6, Pallas kernels: 25.4 us -> 15.9 us  [the longest x2 9.57 us: update(): return order.then(call(table, *operands, *order.last))]
    ppermute x20, waiting for transfers between devices: 65.5 us -> 60.1 us  [send(): return lax.ppermute(value, AXES, pairs)]
    unnamed x16 -> x20, local copies, waits for them, and re-layouts: 3.17 us -> 5.92 us
    pallas_call x16, Pallas kernels: 16.6 us -> 19.1 us  [stage(): return order.then(call(table, *operands, *order.last))]
  transfers between devices with their start and end apart: 20 -> 20, of which waited for: 9 -> 7; matrix products, arithmetic and copies ran while one was open for 0% -> 0% of each run, Pallas kernels for 23% -> 25%
where the time goes in v4:
time: 121 us
  waiting for transfers between devices  60.1 us (50%)
  Pallas kernels  36.8 us (30%)
  starting transfers between devices  16.8 us (14%)
  local copies, waits for them, and re-layouts  5.92 us (5%)
    ppermute x20, waiting for transfers between devices, send(): return lax.ppermute(value, AXES, pairs)  60.1 us
    pallas_call x16, Pallas kernels, stage(): return order.then(call(table, *operands, *order.last))  19.1 us
    ppermute x20, starting transfers between devices, send(): return lax.ppermute(value, AXES, pairs)  16.8 us
    pallas_call x2, Pallas kernels, update(): return order.then(call(table, *operands, *order.last))  9.57 us
    pallas_call x4, Pallas kernels, sibling_half(): return order.then((call(place, view, *order.last),))[0]  6.33 us
    unnamed x20, local copies, waits for them, and re-layouts  5.92 us
  transfers between devices with their start and end apart: 20, of which 7 were waited for; matrix products, arithmetic and copies ran while one was open for 0% of the time, Pallas kernels for 25%

profile of v4, /device:TPU:0, one launch (start us, length us, event | category | flops | bytes accessed | tf_op | source)
XLA Modules:
  0.0 120.6 jit_solution(6352716815157189799)
XLA Ops:
  0.6 0.0 copy-start
  0.6 0.1 pad_add_fusion.place_ref
  0.7 1.7 %copy-done.6 = bf16[1,1,2,1024,512]{4,3,2,1,0:T(8,128)(2,1)S(1)} copy-done((bf16[1,1,2,1024,512]{4,3,2,1,0:T(8,128)(2,1)S(1)}, bf16[1,1,2,1024,512]{4,3,2,1,0:T(8,128)(2,1)}, u32[]{:S(2)}) %copy-start.6) | copy-done | bytes 2097176
  2.5 1.6 %halve_gradients.1 = bf16[1024,512]{1,0:T(8,128)(2,1)} custom-call(s32[2]{0:T(128)S(1)} %pad_add_fusion.place_ref, bf16[2,2,512,512]{3,2,1,0:T(8,128)(2,1)S(1)} %bitcast.34), custom_call_target="tpu_custom_call" | custom-call | flops 1000000000 | bytes 1 | tf_op jit(solution)/shard_map/halve_gradients/pallas_call | solution.py:407
  4.0 0.5 collective-permute-start.15
  4.5 1.6 %copy-done.4 = bf16[1,1,2,1024,512]{4,3,2,1,0:T(8,128)(2,1)S(1)} copy-done((bf16[1,1,2,1024,512]{4,3,2,1,0:T(8,128)(2,1)S(1)}, bf16[1,1,2,1024,512]{4,3,2,1,0:T(8,128)(2,1)}, u32[]{:S(2)}) %copy-start.4) | copy-done | bytes 2097176
  6.1 1.6 %halve_state.3 = bf16[1024,512]{1,0:T(8,128)(2,1)} custom-call(s32[2]{0:T(128)S(1)} %pad_add_fusion.place_ref, bf16[2,2,512,512]{3,2,1,0:T(8,128)(2,1)S(1)} %bitcast.27), custom_call_target="tpu_custom_call" | custom-call | flops 1000000000 | bytes 1 | tf_op jit(solution)/shard_map/halve_state/pallas_call | solution.py:407
  7.7 0.1 collective-permute-start
  7.7 1.6 %halve_state.4 = bf16[1024,512]{1,0:T(8,128)(2,1)} custom-call(s32[2]{0:T(128)S(1)} %pad_add_fusion.place_ref, f32[2,2,512,512]{3,2,1,0:T(8,128)S(1)} %bitcast.13), custom_call_target="tpu_custom_call" | custom-call | flops 1000000000 | bytes 1 | tf_op jit(solution)/shard_map/halve_state/pallas_call | solution.py:407
  9.3 0.5 collective-permute-start.5
  9.8 1.6 %halve_state.5 = bf16[1024,512]{1,0:T(8,128)(2,1)} custom-call(s32[2]{0:T(128)S(1)} %pad_add_fusion.place_ref, f32[2,2,512,512]{3,2,1,0:T(8,128)S(1)} %bitcast.20), custom_call_target="tpu_custom_call" | custom-call | flops 1000000000 | bytes 1 | tf_op jit(solution)/shard_map/halve_state/pallas_call | solution.py:407
  11.4 0.1 collective-permute-start.10
  11.4 1.8 %plan.1.table_ref = s32[2048]{0:T(1024)} custom-call(s32[2]{0:T(128)} %copy-done.9, s32[4,3]{1,0:T(4,128)} %old_ref.1, s32[3]{0:T(128)} %new_ref.1, s32[4]{0:T(128)} %lost_ref.1, s32[3]{0:T(128)} %offset_ref.1), custom_call_target="tpu_custom_call" | custom-call | tf_op jit(solution)/shard_map/plan/pallas_call | solution.py:258
  13.2 0.0 copy-start.1
  13.2 0.0 collective-permute-done.15.refs_1_
  13.2 0.0 copy-start.7
  13.2 1.7 %copy-done.7 = bf16[1,1,2,1024,512]{4,3,2,1,0:T(8,128)(2,1)S(1)} copy-done((bf16[1,1,2,1024,512]{4,3,2,1,0:T(8,128)(2,1)S(1)}, bf16[1,1,2,1024,512]{4,3,2,1,0:T(8,128)(2,1)}, u32[]{:S(2)}) %copy-start.7) | copy-done | bytes 2097176
  15.0 0.8 copy-done.8
  15.8 1.5 %grad_out.1 = bf16[768,512]{1,0:T(8,128)(2,1)S(1)} custom-call(s32[2048]{0:T(1024)S(1)} %copy-done.8, bf16[2048,512]{1,0:T(8,128)(2,1)S(1)} %bitcast.35, bf16[1024,512]{1,0:T(8,128)(2,1)} %collective-permute-done.15.refs_1_), custom_call_target="tpu_custom_call" | custom-call | flops 1000000000 | bytes 1 | tf_op jit(solution)/shard_map/grad_out/pallas_call | solution.py:381
  17.3 3.0 %collective-permute-start.16 = (bf16[768,512]{1,0:T(8,128)(2,1)S(1)}, bf16[768,512]{1,0:T(8,128)(2,1)S(1)}, u32[]{:S(2)}, u32[]{:S(2)}) collective-permute-start(bf16[768,512]{1,0:T(8,128)(2,1)S(1)} %grad_out.1), channel_id=1, source_target_pairs={{0,16},{4,20},{8,24},{12,28},{16,0},{20,4},{24,8},{28,12},{1,17},{... | collective-permute-start | bytes 2359304 | tf_op jit(solution)/shard_map/ppermute | solution.py:69
  20.3 0.0 collective-permute-done.refs_1_
  20.4 1.4 %spread.3 = bf16[512,512]{1,0:T(8,128)(2,1)S(1)} custom-call(s32[2048]{0:T(1024)S(1)} %copy-done.8, bf16[2048,512]{1,0:T(8,128)(2,1)S(1)} %bitcast.28, bf16[1024,512]{1,0:T(8,128)(2,1)} %collective-permute-done.refs_1_), custom_call_target="tpu_custom_call" | custom-call | flops 1000000000 | bytes 1 | tf_op jit(solution)/shard_map/spread/pallas_call | solution.py:381
  21.8 1.6 %collective-permute-start.1 = (bf16[512,512]{1,0:T(8,128)(2,1)S(1)}, bf16[512,512]{1,0:T(8,128)(2,1)S(1)}, u32[]{:S(2)}, u32[]{:S(2)}) collective-permute-start(bf16[512,512]{1,0:T(8,128)(2,1)S(1)} %spread.3), channel_id=1, source_target_pairs={{0,4},{4,0},{8,12},{12,8},{16,20},{20,16},{24,28},{28,24},{1,5},{5... | collective-permute-start | bytes 1572872 | tf_op jit(solution)/shard_map/ppermute | solution.py:69
  23.3 1.3 %spread.4 = bf16[512,512]{1,0:T(8,128)(2,1)S(1)} custom-call(s32[2048]{0:T(1024)S(1)} %copy-done.8, f32[2048,512]{1,0:T(8,128)S(1)} %bitcast.14, bf16[1024,512]{1,0:T(8,128)(2,1)} %collective-permute-done.5.refs_1_), custom_call_target="tpu_custom_call" | custom-call | flops 1000000000 | bytes 1 | tf_op jit(solution)/shard_map/spread/pallas_call | solution.py:381
  24.6 0.6 collective-permute-start.6
  25.2 0.0 collective-permute-done.10.refs_1_
  25.2 0.7 spread.5
  25.9 1.6 %collective-permute-start.11 = (bf16[512,512]{1,0:T(8,128)(2,1)S(1)}, bf16[512,512]{1,0:T(8,128)(2,1)S(1)}, u32[]{:S(2)}, u32[]{:S(2)}) collective-permute-start(bf16[512,512]{1,0:T(8,128)(2,1)S(1)} %spread.5), channel_id=1, source_target_pairs={{0,4},{4,0},{8,12},{12,8},{16,20},{20,16},{24,28},{28,24},{1,5},{5... | collective-permute-start | bytes 1572872 | tf_op jit(solution)/shard_map/ppermute | solution.py:69
  27.5 9.2 %collective-permute-done.1.refs_2_ = bf16[512,512]{1,0:T(8,128)(2,1)S(1)} collective-permute-done((bf16[512,512]{1,0:T(8,128)(2,1)S(1)}, bf16[512,512]{1,0:T(8,128)(2,1)S(1)}, u32[]{:S(2)}, u32[]{:S(2)}) %collective-permute-start.1) | collective-permute-done | bytes 524320 | tf_op jit(solution)/shard_map/ppermute | solution.py:69
  36.7 1.3 %across.3 = bf16[768,512]{1,0:T(8,128)(2,1)S(1)} custom-call(s32[2048]{0:T(1024)S(1)} %copy-done.8, bf16[2048,512]{1,0:T(8,128)(2,1)S(1)} %bitcast.29, bf16[1024,512]{1,0:T(8,128)(2,1)} %collective-permute-done.refs_1_, bf16[512,512]{1,0:T(8,128)(2,1)S(1)} %collective-permute-done.1.refs_2_), custom_call_target="tpu_custom_call" | custom-call | flops 1000000000 | bytes 1 | tf_op jit(solution)/shard_map/across/pallas_call | solution.py:381
  38.0 0.2 collective-permute-start.2
  38.1 1.7 %grad_sum.1.refs_0_ = bf16[768,512]{1,0:T(8,128)(2,1)S(1)} custom-call(s32[2048]{0:T(1024)S(1)} %copy-done.8, bf16[2048,512]{1,0:T(8,128)(2,1)S(1)} %bitcast.36, bf16[1024,512]{1,0:T(8,128)(2,1)} %collective-permute-done.15.refs_1_, bf16[768,512]{1,0:T(8,128)(2,1)S(1)} %collective-permute-done.16.refs_2_), custom_call_target="tpu_custom_call" | custom-call | flops 1000000000 | bytes 1 | tf_op jit(solution)/shard_map/grad_sum/pallas_call | solution.py:381
  39.8 2.0 %collective-permute-start.17 = (bf16[768,512]{1,0:T(8,128)(2,1)S(1)}, bf16[768,512]{1,0:T(8,128)(2,1)S(1)}, u32[]{:S(2)}, u32[]{:S(2)}) collective-permute-start(bf16[768,512]{1,0:T(8,128)(2,1)S(1)} %grad_sum.1.refs_0_), channel_id=1, source_target_pairs={{0,4},{4,0},{8,12},{12,8},{16,20},{20,16},{24,28},{28,24},{1,5},{5... | collective-permute-start | bytes 2359304 | tf_op jit(solution)/shard_map/ppermute | solution.py:69
  41.9 6.0 %collective-permute-done.6.refs_2_ = bf16[512,512]{1,0:T(8,128)(2,1)S(1)} collective-permute-done((bf16[512,512]{1,0:T(8,128)(2,1)S(1)}, bf16[512,512]{1,0:T(8,128)(2,1)S(1)}, u32[]{:S(2)}, u32[]{:S(2)}) %collective-permute-start.6) | collective-permute-done | bytes 524320 | tf_op jit(solution)/shard_map/ppermute | solution.py:69
  47.9 1.3 %across.4 = bf16[768,512]{1,0:T(8,128)(2,1)S(1)} custom-call(s32[2048]{0:T(1024)S(1)} %copy-done.8, f32[2048,512]{1,0:T(8,128)S(1)} %bitcast.15, bf16[1024,512]{1,0:T(8,128)(2,1)} %collective-permute-done.5.refs_1_, bf16[512,512]{1,0:T(8,128)(2,1)S(1)} %collective-permute-done.6.refs_2_), custom_call_target="tpu_custom_call" | custom-call | flops 1000000000 | bytes 1 | tf_op jit(solution)/shard_map/across/pallas_call | solution.py:381
  49.2 0.2 collective-permute-start.7
  49.4 9.8 %collective-permute-done.11.refs_2_ = bf16[512,512]{1,0:T(8,128)(2,1)S(1)} collective-permute-done((bf16[512,512]{1,0:T(8,128)(2,1)S(1)}, bf16[512,512]{1,0:T(8,128)(2,1)S(1)}, u32[]{:S(2)}, u32[]{:S(2)}) %collective-permute-start.11) | collective-permute-done | bytes 524320 | tf_op jit(solution)/shard_map/ppermute | solution.py:69
  59.1 0.7 across.5
  59.9 0.2 collective-permute-start.12
  60.0 0.0 collective-permute-done.2.refs_3_
  60.0 1.3 %deliver.3 = bf16[512,512]{1,0:T(8,128)(2,1)S(1)} custom-call(s32[2048]{0:T(1024)S(1)} %copy-done.8, bf16[2048,512]{1,0:T(8,128)(2,1)S(1)} %bitcast.30, bf16[1024,512]{1,0:T(8,128)(2,1)} %collective-permute-done.refs_1_, bf16[512,512]{1,0:T(8,128)(2,1)S(1)} %collective-permute-done.1.refs_2_, bf16[768,512]{1,0:T(8,128)(2,1)S(1)} %collective-permute-done.2.refs_3_), custom_call_target="tpu_custom_call" | custom-call | flops 1000000000 | bytes 1 | tf_op jit(solution)/shard_map/deliver/pallas_call | solution.py:381
  61.4 2.1 %collective-permute-start.3 = (bf16[512,512]{1,0:T(8,128)(2,1)S(1)}, bf16[512,512]{1,0:T(8,128)(2,1)S(1)}, u32[]{:S(2)}, u32[]{:S(2)}) collective-permute-start(bf16[512,512]{1,0:T(8,128)(2,1)S(1)} %deliver.3), channel_id=1, source_target_pairs={{0,4},{4,0},{8,12},{12,8},{16,20},{20,16},{24,28},{28,24},{1,5},{5... | collective-permute-start | bytes 1572872 | tf_op jit(solution)/shard_map/ppermute | solution.py:69
  63.4 12.6 %collective-permute-done.17.refs_1_ = bf16[768,512]{1,0:T(8,128)(2,1)S(1)} collective-permute-done((bf16[768,512]{1,0:T(8,128)(2,1)S(1)}, bf16[768,512]{1,0:T(8,128)(2,1)S(1)}, u32[]{:S(2)}, u32[]{:S(2)}) %collective-permute-start.17) | collective-permute-done | bytes 786464 | tf_op jit(solution)/shard_map/ppermute | solution.py:69
  76.0 1.0 grad_mean.1.refs_0_
  77.0 0.1 collective-permute-start.18
  77.1 1.3 %deliver.4 = bf16[512,512]{1,0:T(8,128)(2,1)S(1)} custom-call(s32[2048]{0:T(1024)S(1)} %copy-done.8, f32[2048,512]{1,0:T(8,128)S(1)} %bitcast.16, bf16[1024,512]{1,0:T(8,128)(2,1)} %collective-permute-done.5.refs_1_, bf16[512,512]{1,0:T(8,128)(2,1)S(1)} %collective-permute-done.6.refs_2_, bf16[768,512]{1,0:T(8,128)(2,1)S(1)} %collective-permute-done.7.refs_3_), custom_call_target="tpu_custom_call" | custom-call | flops 1000000000 | bytes 1 | tf_op jit(solution)/shard_map/deliver/pallas_call | solution.py:381
  78.4 2.1 %collective-permute-start.8 = (bf16[512,512]{1,0:T(8,128)(2,1)S(1)}, bf16[512,512]{1,0:T(8,128)(2,1)S(1)}, u32[]{:S(2)}, u32[]{:S(2)}) collective-permute-start(bf16[512,512]{1,0:T(8,128)(2,1)S(1)} %deliver.4), channel_id=1, source_target_pairs={{0,4},{4,0},{8,12},{12,8},{16,20},{20,16},{24,28},{28,24},{1,5},{5... | collective-permute-start | bytes 1572872 | tf_op jit(solution)/shard_map/ppermute | solution.py:69
  80.5 11.8 %collective-permute-done.12.refs_3_ = bf16[768,512]{1,0:T(8,128)(2,1)S(1)} collective-permute-done((bf16[768,512]{1,0:T(8,128)(2,1)S(1)}, bf16[768,512]{1,0:T(8,128)(2,1)S(1)}, u32[]{:S(2)}, u32[]{:S(2)}) %collective-permute-start.12) | collective-permute-done | bytes 786464 | tf_op jit(solution)/shard_map/ppermute | solution.py:69
  92.2 0.8 deliver.5
  93.0 1.6 %collective-permute-start.13 = (bf16[512,512]{1,0:T(8,128)(2,1)S(1)}, bf16[512,512]{1,0:T(8,128)(2,1)S(1)}, u32[]{:S(2)}, u32[]{:S(2)}) collective-permute-start(bf16[512,512]{1,0:T(8,128)(2,1)S(1)} %deliver.5), channel_id=1, source_target_pairs={{0,4},{4,0},{8,12},{12,8},{16,20},{20,16},{24,28},{28,24},{1,5},{5... | collective-permute-start | bytes 1572872 | tf_op jit(solution)/shard_map/ppermute | solution.py:69
  94.6 1.5 %collect.3.refs_3_ = bf16[1024,512]{1,0:T(8,128)(2,1)S(1)} custom-call(s32[2048]{0:T(1024)S(1)} %copy-done.8, bf16[2048,512]{1,0:T(8,128)(2,1)S(1)} %bitcast.31, bf16[1024,512]{1,0:T(8,128)(2,1)} %collective-permute-done.refs_1_, bf16[512,512]{1,0:T(8,128)(2,1)S(1)} %collective-permute-done.1.refs_2_, bf16[768,512]{1,0:T(8,128)(2,1)S(1)} %collective-permute-done.2.refs_3_, ...), custom_call_target="tpu_custom_call" | custom-call | flops 1000000000 | bytes 1 | tf_op jit(solution)/shard_map/collect/pallas_call | solution.py:381
  96.1 0.1 collective-permute-start.4
  96.1 2.3 %collective-permute-done.8.refs_4_ = bf16[512,512]{1,0:T(8,128)(2,1)S(1)} collective-permute-done((bf16[512,512]{1,0:T(8,128)(2,1)S(1)}, bf16[512,512]{1,0:T(8,128)(2,1)S(1)}, u32[]{:S(2)}, u32[]{:S(2)}) %collective-permute-start.8) | collective-permute-done | bytes 524320 | tf_op jit(solution)/shard_map/ppermute | solution.py:69
  98.5 1.5 %collect.4.refs_4_ = bf16[1024,512]{1,0:T(8,128)(2,1)S(1)} custom-call(s32[2048]{0:T(1024)S(1)} %copy-done.8, f32[2048,512]{1,0:T(8,128)S(1)} %bitcast.17, bf16[1024,512]{1,0:T(8,128)(2,1)} %collective-permute-done.5.refs_1_, bf16[512,512]{1,0:T(8,128)(2,1)S(1)} %collective-permute-done.6.refs_2_, bf16[768,512]{1,0:T(8,128)(2,1)S(1)} %collective-permute-done.7.refs_3_, ...), custom_call_target="tpu_custom_call" | custom-call | flops 1000000000 | bytes 1 | tf_op jit(solution)/shard_map/collect/pallas_call | solution.py:381
  99.9 0.1 collective-permute-start.9
  100.0 8.4 %collective-permute-done.13.refs_4_ = bf16[512,512]{1,0:T(8,128)(2,1)S(1)} collective-permute-done((bf16[512,512]{1,0:T(8,128)(2,1)S(1)}, bf16[512,512]{1,0:T(8,128)(2,1)S(1)}, u32[]{:S(2)}, u32[]{:S(2)}) %collective-permute-start.13) | collective-permute-done | bytes 524320 | tf_op jit(solution)/shard_map/ppermute | solution.py:69
  108.4 0.9 collect.5.refs_5_
  109.4 0.1 collective-permute-start.14
  109.4 1.0 mean.1
  110.4 0.6 collective-permute-start.19
  111.0 4.8 %update.2 = (bf16[2,2,512,512]{3,2,1,0:T(8,128)(2,1)}, f32[2,2,512,512]{3,2,1,0:T(8,128)}, f32[2,2,512,512]{3,2,1,0:T(8,128)}) custom-call(s32[2048]{0:T(1024)S(1)} %copy-done.8, bf16[2048,512]{1,0:T(8,128)(2,1)S(1)} %bitcast.32, f32[2048,512]{1,0:T(8,128)S(1)} %bitcast.18, f32[2048,512]{1,0:T(8,128)S(1)} %bitcast.25, bf16[1024,512]{1,0:T(8,128)(2,1)S(1)} %collect.3.refs_3_, ...), custom_call_target="tpu_custom_call" | custom-call | flops 1 | bytes 1 | tf_op jit(solution)/shard_map/update/pallas_call | solution.py:482
  115.7 0.0 collective-permute-done.4.refs_3_
  115.7 0.0 collective-permute-done.9.refs_4_
  115.8 4.8 %update.3 = (bf16[2,2,512,512]{3,2,1,0:T(8,128)(2,1)}, f32[2,2,512,512]{3,2,1,0:T(8,128)}, f32[2,2,512,512]{3,2,1,0:T(8,128)}) custom-call(s32[2048]{0:T(1024)S(1)} %copy-done.8, bf16[2048,512]{1,0:T(8,128)(2,1)S(1)} %bitcast.33, f32[2048,512]{1,0:T(8,128)S(1)} %bitcast.19, ...), custom_call_target="tpu_custom_call", output_to_operand_aliasing={{0}: (8, {}), {1}: (9, {}), {2}: (10, {})} | custom-call | flops 1 | bytes 1 | tf_op jit(solution)/shard_map/update/pallas_call | solution.py:482
  (20 shorter events, 0.0 us)
Async XLA Ops:
  0.6 7.1 %copy-start = (f32[1,1,2,1024,512]{4,3,2,1,0:T(8,128)S(1)}, f32[1,1,2,1024,512]{4,3,2,1,0:T(8,128)}, u32[]{:S(2)}) copy-start(f32[1,1,2,1024,512]{4,3,2,1,0:T(8,128)} %param.9) | copy-start | bytes 12582916
  0.7 9.0 %copy-start.9 = (s32[2]{0:T(128)}, s32[2]{0:T(128)S(1)}, u32[]{:S(2)}) copy-start(s32[2]{0:T(128)S(1)} %pad_add_fusion.place_ref) | copy-start | bytes 28
  0.7 1.7 %copy-start.6 = (bf16[1,1,2,1024,512]{4,3,2,1,0:T(8,128)(2,1)S(1)}, bf16[1,1,2,1024,512]{4,3,2,1,0:T(8,128)(2,1)}, u32[]{:S(2)}) copy-start(bf16[1,1,2,1024,512]{4,3,2,1,0:T(8,128)(2,1)} %param.11) | copy-start | bytes 6291460
  4.0 9.2 %collective-permute-start.15 = (bf16[1024,512]{1,0:T(8,128)(2,1)}, bf16[1024,512]{1,0:T(8,128)(2,1)}, u32[]{:S(2)}, u32[]{:S(2)}) collective-permute-start(bf16[1024,512]{1,0:T(8,128)(2,1)} %halve_gradients.1), channel_id=1, source_target_pairs={{0,8},{4,12},{8,0},{12,4},{16,24},{20,28},{24,16},{28,20},{1,9},{5... | collective-permute-start | bytes 3145736 | tf_op jit(solution)/shard_map/ppermute | solution.py:69
  4.5 1.6 %copy-start.4 = (bf16[1,1,2,1024,512]{4,3,2,1,0:T(8,128)(2,1)S(1)}, bf16[1,1,2,1024,512]{4,3,2,1,0:T(8,128)(2,1)}, u32[]{:S(2)}) copy-start(bf16[1,1,2,1024,512]{4,3,2,1,0:T(8,128)(2,1)} %param.8) | copy-start | bytes 6291460
  6.1 3.7 %copy-start.2 = (f32[1,1,2,1024,512]{4,3,2,1,0:T(8,128)S(1)}, f32[1,1,2,1024,512]{4,3,2,1,0:T(8,128)}, u32[]{:S(2)}) copy-start(f32[1,1,2,1024,512]{4,3,2,1,0:T(8,128)} %param.10) | copy-start | bytes 12582916
  7.7 12.7 %collective-permute-start = (bf16[1024,512]{1,0:T(8,128)(2,1)}, bf16[1024,512]{1,0:T(8,128)(2,1)}, u32[]{:S(2)}, u32[]{:S(2)}) collective-permute-start(bf16[1024,512]{1,0:T(8,128)(2,1)} %halve_state.3), channel_id=1, source_target_pairs={{0,8},{4,12},{8,0},{12,4},{16,24},{20,28},{24,16},{28,20},{1,9},{5... | collective-permute-start | bytes 3145736 | tf_op jit(solution)/shard_map/ppermute | solution.py:69
  9.3 14.0 %collective-permute-start.5 = (bf16[1024,512]{1,0:T(8,128)(2,1)}, bf16[1024,512]{1,0:T(8,128)(2,1)}, u32[]{:S(2)}, u32[]{:S(2)}) collective-permute-start(bf16[1024,512]{1,0:T(8,128)(2,1)} %halve_state.4), channel_id=1, source_target_pairs={{0,8},{4,12},{8,0},{12,4},{16,24},{20,28},{24,16},{28,20},{1,9},{5... | collective-permute-start | bytes 3145736 | tf_op jit(solution)/shard_map/ppermute | solution.py:69
  9.8 10.6 %copy-start.5 = (bf16[1,1,2,1024,512]{4,3,2,1,0:T(8,128)(2,1)S(1)}, bf16[1,1,2,1024,512]{4,3,2,1,0:T(8,128)(2,1)}, u32[]{:S(2)}) copy-start(bf16[1,1,2,1024,512]{4,3,2,1,0:T(8,128)(2,1)} %param.8) | copy-start | bytes 6291460
  11.4 13.9 %collective-permute-start.10 = (bf16[1024,512]{1,0:T(8,128)(2,1)}, bf16[1024,512]{1,0:T(8,128)(2,1)S(1)}, u32[]{:S(2)}, u32[]{:S(2)}) collective-permute-start(bf16[1024,512]{1,0:T(8,128)(2,1)} %halve_state.5), channel_id=1, source_target_pairs={{0,8},{4,12},{8,0},{12,4},{16,24},{20,28},{24,16},{28,20},{1,9},{5... | collective-permute-start | bytes 3145736 | tf_op jit(solution)/shard_map/ppermute | solution.py:69
  13.2 10.1 %copy-start.1 = (f32[1,1,2,1024,512]{4,3,2,1,0:T(8,128)S(1)}, f32[1,1,2,1024,512]{4,3,2,1,0:T(8,128)}, u32[]{:S(2)}) copy-start(f32[1,1,2,1024,512]{4,3,2,1,0:T(8,128)} %param.9) | copy-start | bytes 12582916
  13.2 1.7 %copy-start.7 = (bf16[1,1,2,1024,512]{4,3,2,1,0:T(8,128)(2,1)S(1)}, bf16[1,1,2,1024,512]{4,3,2,1,0:T(8,128)(2,1)}, u32[]{:S(2)}) copy-start(bf16[1,1,2,1024,512]{4,3,2,1,0:T(8,128)(2,1)} %param.11) | copy-start | bytes 6291460
  15.0 0.8 copy-start.8
  17.3 20.8 %collective-permute-start.16 = (bf16[768,512]{1,0:T(8,128)(2,1)S(1)}, bf16[768,512]{1,0:T(8,128)(2,1)S(1)}, u32[]{:S(2)}, u32[]{:S(2)}) collective-permute-start(bf16[768,512]{1,0:T(8,128)(2,1)S(1)} %grad_out.1), channel_id=1, source_target_pairs={{0,16},{4,20},{8,24},{12,28},{16,0},{20,4},{24,8},{28,12},{1,17},{... | collective-permute-start | bytes 2359304 | tf_op jit(solution)/shard_map/ppermute | solution.py:69
  20.4 4.9 %copy-start.3 = (f32[1,1,2,1024,512]{4,3,2,1,0:T(8,128)S(1)}, f32[1,1,2,1024,512]{4,3,2,1,0:T(8,128)}, u32[]{:S(2)}) copy-start(f32[1,1,2,1024,512]{4,3,2,1,0:T(8,128)} %param.10) | copy-start | bytes 12582916
  21.8 14.9 %collective-permute-start.1 = (bf16[512,512]{1,0:T(8,128)(2,1)S(1)}, bf16[512,512]{1,0:T(8,128)(2,1)S(1)}, u32[]{:S(2)}, u32[]{:S(2)}) collective-permute-start(bf16[512,512]{1,0:T(8,128)(2,1)S(1)} %spread.3), channel_id=1, source_target_pairs={{0,4},{4,0},{8,12},{12,8},{16,20},{20,16},{24,28},{28,24},{1,5},{5... | collective-permute-start | bytes 1572872 | tf_op jit(solution)/shard_map/ppermute | solution.py:69
  24.6 23.3 %collective-permute-start.6 = (bf16[512,512]{1,0:T(8,128)(2,1)S(1)}, bf16[512,512]{1,0:T(8,128)(2,1)S(1)}, u32[]{:S(2)}, u32[]{:S(2)}) collective-permute-start(bf16[512,512]{1,0:T(8,128)(2,1)S(1)} %spread.4), channel_id=1, source_target_pairs={{0,4},{4,0},{8,12},{12,8},{16,20},{20,16},{24,28},{28,24},{1,5},{5... | collective-permute-start | bytes 1572872 | tf_op jit(solution)/shard_map/ppermute | solution.py:69
  25.9 33.2 %collective-permute-start.11 = (bf16[512,512]{1,0:T(8,128)(2,1)S(1)}, bf16[512,512]{1,0:T(8,128)(2,1)S(1)}, u32[]{:S(2)}, u32[]{:S(2)}) collective-permute-start(bf16[512,512]{1,0:T(8,128)(2,1)S(1)} %spread.5), channel_id=1, source_target_pairs={{0,4},{4,0},{8,12},{12,8},{16,20},{20,16},{24,28},{28,24},{1,5},{5... | collective-permute-start | bytes 1572872 | tf_op jit(solution)/shard_map/ppermute | solution.py:69
  38.0 22.1 %collective-permute-start.2 = (bf16[768,512]{1,0:T(8,128)(2,1)S(1)}, bf16[768,512]{1,0:T(8,128)(2,1)S(1)}, u32[]{:S(2)}, u32[]{:S(2)}) collective-permute-start(bf16[768,512]{1,0:T(8,128)(2,1)S(1)} %across.3), channel_id=1, source_target_pairs={{0,16},{4,20},{8,24},{12,28},{16,0},{20,4},{24,8},{28,12},{1,17},{... | collective-permute-start | bytes 2359304 | tf_op jit(solution)/shard_map/ppermute | solution.py:69
  39.8 36.2 %collective-permute-start.17 = (bf16[768,512]{1,0:T(8,128)(2,1)S(1)}, bf16[768,512]{1,0:T(8,128)(2,1)S(1)}, u32[]{:S(2)}, u32[]{:S(2)}) collective-permute-start(bf16[768,512]{1,0:T(8,128)(2,1)S(1)} %grad_sum.1.refs_0_), channel_id=1, source_target_pairs={{0,4},{4,0},{8,12},{12,8},{16,20},{20,16},{24,28},{28,24},{1,5},{5... | collective-permute-start | bytes 2359304 | tf_op jit(solution)/shard_map/ppermute | solution.py:69
  49.2 27.8 %collective-permute-start.7 = (bf16[768,512]{1,0:T(8,128)(2,1)S(1)}, bf16[768,512]{1,0:T(8,128)(2,1)S(1)}, u32[]{:S(2)}, u32[]{:S(2)}) collective-permute-start(bf16[768,512]{1,0:T(8,128)(2,1)S(1)} %across.4), channel_id=1, source_target_pairs={{0,16},{4,20},{8,24},{12,28},{16,0},{20,4},{24,8},{28,12},{1,17},{... | collective-permute-start | bytes 2359304 | tf_op jit(solution)/shard_map/ppermute | solution.py:69
  59.9 32.3 %collective-permute-start.12 = (bf16[768,512]{1,0:T(8,128)(2,1)S(1)}, bf16[768,512]{1,0:T(8,128)(2,1)S(1)}, u32[]{:S(2)}, u32[]{:S(2)}) collective-permute-start(bf16[768,512]{1,0:T(8,128)(2,1)S(1)} %across.5), channel_id=1, source_target_pairs={{0,16},{4,20},{8,24},{12,28},{16,0},{20,4},{24,8},{28,12},{1,17},{... | collective-permute-start | bytes 2359304 | tf_op jit(solution)/shard_map/ppermute | solution.py:69
  61.4 33.2 %collective-permute-start.3 = (bf16[512,512]{1,0:T(8,128)(2,1)S(1)}, bf16[512,512]{1,0:T(8,128)(2,1)S(1)}, u32[]{:S(2)}, u32[]{:S(2)}) collective-permute-start(bf16[512,512]{1,0:T(8,128)(2,1)S(1)} %deliver.3), channel_id=1, source_target_pairs={{0,4},{4,0},{8,12},{12,8},{16,20},{20,16},{24,28},{28,24},{1,5},{5... | collective-permute-start | bytes 1572872 | tf_op jit(solution)/shard_map/ppermute | solution.py:69
  77.0 32.5 %collective-permute-start.18 = (bf16[768,512]{1,0:T(8,128)(2,1)S(1)}, bf16[768,512]{1,0:T(8,128)(2,1)S(1)}, u32[]{:S(2)}, u32[]{:S(2)}) collective-permute-start(bf16[768,512]{1,0:T(8,128)(2,1)S(1)} %grad_mean.1.refs_0_), channel_id=1, source_target_pairs={{0,16},{4,20},{8,24},{12,28},{16,0},{20,4},{24,8},{28,12},{1,17},{... | collective-permute-start | bytes 2359304 | tf_op jit(solution)/shard_map/ppermute | solution.py:69
  78.4 20.1 %collective-permute-start.8 = (bf16[512,512]{1,0:T(8,128)(2,1)S(1)}, bf16[512,512]{1,0:T(8,128)(2,1)S(1)}, u32[]{:S(2)}, u32[]{:S(2)}) collective-permute-start(bf16[512,512]{1,0:T(8,128)(2,1)S(1)} %deliver.4), channel_id=1, source_target_pairs={{0,4},{4,0},{8,12},{12,8},{16,20},{20,16},{24,28},{28,24},{1,5},{5... | collective-permute-start | bytes 1572872 | tf_op jit(solution)/shard_map/ppermute | solution.py:69
  93.0 15.4 %collective-permute-start.13 = (bf16[512,512]{1,0:T(8,128)(2,1)S(1)}, bf16[512,512]{1,0:T(8,128)(2,1)S(1)}, u32[]{:S(2)}, u32[]{:S(2)}) collective-permute-start(bf16[512,512]{1,0:T(8,128)(2,1)S(1)} %deliver.5), channel_id=1, source_target_pairs={{0,4},{4,0},{8,12},{12,8},{16,20},{20,16},{24,28},{28,24},{1,5},{5... | collective-permute-start | bytes 1572872 | tf_op jit(solution)/shard_map/ppermute | solution.py:69
  96.1 19.7 %collective-permute-start.4 = (bf16[1024,512]{1,0:T(8,128)(2,1)S(1)}, bf16[1024,512]{1,0:T(8,128)(2,1)S(1)}, u32[]{:S(2)}, u32[]{:S(2)}) collective-permute-start(bf16[1024,512]{1,0:T(8,128)(2,1)S(1)} %collect.3.refs_3_), channel_id=1, source_target_pairs={{0,8},{4,12},{8,0},{12,4},{16,24},{20,28},{24,16},{28,20},{1,9},{5... | collective-permute-start | bytes 3145736 | tf_op jit(solution)/shard_map/ppermute | solution.py:69
  99.9 15.8 %collective-permute-start.9 = (bf16[1024,512]{1,0:T(8,128)(2,1)S(1)}, bf16[1024,512]{1,0:T(8,128)(2,1)S(1)}, u32[]{:S(2)}, u32[]{:S(2)}) collective-permute-start(bf16[1024,512]{1,0:T(8,128)(2,1)S(1)} %collect.4.refs_4_), channel_id=1, source_target_pairs={{0,8},{4,12},{8,0},{12,4},{16,24},{20,28},{24,16},{28,20},{1,9},{5... | collective-permute-start | bytes 3145736 | tf_op jit(solution)/shard_map/ppermute | solution.py:69
  109.4 6.4 %collective-permute-start.14 = (bf16[1024,512]{1,0:T(8,128)(2,1)S(1)}, bf16[1024,512]{1,0:T(8,128)(2,1)S(1)}, u32[]{:S(2)}, u32[]{:S(2)}) collective-permute-start(bf16[1024,512]{1,0:T(8,128)(2,1)S(1)} %collect.5.refs_5_), channel_id=1, source_target_pairs={{0,8},{4,12},{8,0},{12,4},{16,24},{20,28},{24,16},{28,20},{1,9},{5... | collective-permute-start | bytes 3145736 | tf_op jit(solution)/shard_map/ppermute | solution.py:69
  110.4 5.3 %collective-permute-start.19 = (bf16[1024,512]{1,0:T(8,128)(2,1)S(1)}, bf16[1024,512]{1,0:T(8,128)(2,1)S(1)}, u32[]{:S(2)}, u32[]{:S(2)}) collective-permute-start(bf16[1024,512]{1,0:T(8,128)(2,1)S(1)} %get-tuple-element.11), channel_id=1, source_target_pairs={{0,8},{4,12},{8,0},{12,4},{16,24},{20,28},{24,16},{28,20},{1,9},{5... | collective-permute-start | bytes 3145736 | tf_op jit(solution)/shard_map/ppermute | solution.py:69

commit v5 on v4

--- a/solution.py
+++ b/solution.py
@@ -382,29 +382,27 @@
 
 
 def sibling_half(z, order, place, array, name):
-    view = array.reshape(z.slots, CORES, z.half, z.cols)
+    rows = z.half // 2 if z.half % 32 == 0 else z.half
 
     def kernel(place_ref, array_ref, *refs):
-        refs[-1][...] = array_ref[0, 0].astype(jnp.bfloat16)
-
-    def half_of(slot, place_ref):
-        return (slot, 1 - lax.rem(place_ref[0], CORES), 0, 0)
-
-    out = jax.ShapeDtypeStruct((z.slots * z.half, z.cols), jnp.bfloat16)
+        out_ref = refs[-1]
+        half = 1 - lax.rem(place_ref[0], CORES)
+        for slot in range(z.slots):
+            for first in range(0, z.half, rows):
+                at = pl.multiple_of(slot * z.rows + half * z.half + first, 16)
+                block = array_ref[pl.ds(at, rows)].astype(jnp.bfloat16)
+                out_ref[pl.ds(slot * z.half + first, rows)] = block
+
     call = pl.pallas_call(
         kernel,
-        grid_spec=pltpu.PrefetchScalarGridSpec(
-            num_scalar_prefetch=1,
-            grid=(z.slots,),
-            in_specs=[pl.BlockSpec((1, 1, z.half, z.cols), half_of)] + order.specs(),
-            out_specs=pl.BlockSpec((z.half, z.cols), lambda slot, place_ref: (slot, 0)),
-        ),
-        out_shape=out,
+        out_shape=jax.ShapeDtypeStruct((z.slots * z.half, z.cols), jnp.bfloat16),
+        in_specs=[SMEM_SPEC, VMEM_SPEC] + order.specs(),
+        out_specs=VMEM_SPEC,
         compiler_params=PARAMS,
         cost_estimate=COST,
         name="halve_" + name,
     )
-    return order.then((call(place, view, *order.last),))[0]
+    return order.then((call(place, array, *order.last),))[0]
 
 
 def update(z, order, table, start, part, state, rebuilt, mean, outs):
@@ -437,7 +435,8 @@
                     grad = mean_ref[mean_row, lanes].astype(jnp.float32)
                     next_one = BETA_ONE * one + ((1.0 - BETA_ONE) / z.pipes) * grad
                     next_two = BETA_TWO * two + ((1.0 - BETA_TWO) / z.pipes**2) * (grad * grad)
-                    move = next_one / (jnp.sqrt(next_two) + EPSILON)
+                    scale = next_two * lax.rsqrt(next_two) + EPSILON
+                    move = next_one * lax.rsqrt(scale * scale)
                     next_weight = (1.0 - LEARN_RATE * DECAY_RATE) * weight - LEARN_RATE * move
                     for ref, value in zip(out_refs, (next_weight, next_one, next_two)):
                         ref[0, 0, row, lanes] = value.astype(ref.dtype)
@@ -494,8 +493,8 @@
 
     def enter(self, place):
         z = self.z
-        theirs = z.to_core(sibling_half(z, self.order, place, self.grads, "gradients"))
         own = self.grads.reshape(z.slots * z.rows, z.cols)
+        theirs = z.to_core(sibling_half(z, self.order, place, own, "gradients"))
         theirs = self.order.arrived(theirs)
         self.held = [
             Rows(own, z.grad_band, z.slots * CORES * z.groups),
@@ -544,8 +543,8 @@
 
     def enter(self, place):
         z = self.z
-        theirs = z.to_core(sibling_half(z, self.order, place, self.array, "state"))
         own = self.array.reshape(z.slots * z.rows, z.cols)
+        theirs = z.to_core(sibling_half(z, self.order, place, own, "state"))
         theirs = self.order.arrived(theirs)
         held = z.slots * z.sections
         self.held = [Rows(own, z.band, CORES * held), Rows(theirs, z.band, held)]

time: 121 us -> 124 us (1.025)
  local copies, waits for them, and re-layouts: 5.92 us -> 8.56 us
    unnamed x20 -> x22, local copies, waits for them, and re-layouts: 5.92 us -> 8.56 us
  transfers between devices with their start and end apart: 20 -> 20, of which waited for: 7 -> 7; matrix products, arithmetic and copies ran while one was open for 0% -> 0% of each run, Pallas kernels for 25% -> 24%
where the time goes in v5:
time: 124 us; the launch traced here: 123 us
  waiting for transfers between devices  61.2 us (49%)
  Pallas kernels  36.1 us (29%)
  starting transfers between devices  16.3 us (13%)
  local copies, waits for them, and re-layouts  8.56 us (7%)
    ppermute x20, waiting for transfers between devices, send(): return lax.ppermute(value, AXES, pairs)  61.2 us
    pallas_call x16, Pallas kernels, stage(): return order.then(call(table, *operands, *order.last))  18.9 us
    ppermute x20, starting transfers between devices, send(): return lax.ppermute(value, AXES, pairs)  16.3 us
    pallas_call x2, Pallas kernels, update(): return order.then(call(table, *operands, *order.last))  9.04 us
    unnamed x22, local copies, waits for them, and re-layouts  8.56 us
    pallas_call x4, Pallas kernels, sibling_half(): return order.then((call(place, array, *order.last),))[0]  6.41 us
  transfers between devices with their start and end apart: 20, of which 7 were waited for; matrix products, arithmetic and copies ran while one was open for 0% of the time, Pallas kernels for 24%

profile of v5, /device:TPU:0, one launch (start us, length us, event | category | flops | bytes accessed | tf_op | source)
XLA Modules:
  0.0 123.1 jit_solution(10227567698386552548)
XLA Ops:
  0.6 0.1 pad_add_fusion.place_ref
  0.7 1.6 %copy-done.6 = bf16[1,1,2,1024,512]{4,3,2,1,0:T(8,128)(2,1)S(1)} copy-done((bf16[1,1,2,1024,512]{4,3,2,1,0:T(8,128)(2,1)S(1)}, bf16[1,1,2,1024,512]{4,3,2,1,0:T(8,128)(2,1)}, u32[]{:S(2)}) %copy-start.6) | copy-done | bytes 2097176
  2.3 1.6 %halve_gradients.1 = bf16[1024,512]{1,0:T(8,128)(2,1)} custom-call(s32[2]{0:T(128)S(1)} %pad_add_fusion.place_ref, bf16[2048,512]{1,0:T(8,128)(2,1)S(1)} %bitcast.30), custom_call_target="tpu_custom_call" | custom-call | flops 1000000000 | bytes 1 | tf_op jit(solution)/shard_map/halve_gradients/pallas_call | solution.py:405
  3.9 0.5 collective-permute-start.15
  4.3 2.2 %copy-done.2 = f32[1,1,2,1024,512]{4,3,2,1,0:T(8,128)S(1)} copy-done((f32[1,1,2,1024,512]{4,3,2,1,0:T(8,128)S(1)}, f32[1,1,2,1024,512]{4,3,2,1,0:T(8,128)}, u32[]{:S(2)}) %copy-start.2) | copy-done | bytes 4194328
  6.5 1.6 %halve_state.5 = bf16[1024,512]{1,0:T(8,128)(2,1)} custom-call(s32[2]{0:T(128)S(1)} %pad_add_fusion.place_ref, f32[2048,512]{1,0:T(8,128)S(1)} %bitcast.16), custom_call_target="tpu_custom_call" | custom-call | flops 1000000000 | bytes 1 | tf_op jit(solution)/shard_map/halve_state/pallas_call | solution.py:405
  8.2 0.1 collective-permute-start.10
  8.2 1.6 %halve_state.4 = bf16[1024,512]{1,0:T(8,128)(2,1)} custom-call(s32[2]{0:T(128)S(1)} %pad_add_fusion.place_ref, f32[2048,512]{1,0:T(8,128)S(1)} %bitcast.9), custom_call_target="tpu_custom_call" | custom-call | flops 1000000000 | bytes 1 | tf_op jit(solution)/shard_map/halve_state/pallas_call | solution.py:405
  9.8 0.5 collective-permute-start.5
  10.3 1.6 %halve_state.3 = bf16[1024,512]{1,0:T(8,128)(2,1)} custom-call(s32[2]{0:T(128)S(1)} %pad_add_fusion.place_ref, bf16[2048,512]{1,0:T(8,128)(2,1)S(1)} %bitcast.23), custom_call_target="tpu_custom_call" | custom-call | flops 1000000000 | bytes 1 | tf_op jit(solution)/shard_map/halve_state/pallas_call | solution.py:405
  11.9 0.1 collective-permute-start
  11.9 1.8 %plan.1.table_ref = s32[2048]{0:T(1024)} custom-call(s32[2]{0:T(128)} %copy-done.10, s32[4,3]{1,0:T(4,128)} %old_ref.1, s32[3]{0:T(128)} %new_ref.1, s32[4]{0:T(128)} %lost_ref.1, s32[3]{0:T(128)} %offset_ref.1), custom_call_target="tpu_custom_call" | custom-call | tf_op jit(solution)/shard_map/plan/pallas_call | solution.py:258
  13.7 0.0 copy-start.1
  13.7 0.0 collective-permute-done.15.refs_1_
  13.7 0.0 copy-start.7
  13.7 1.7 %copy-done.7 = bf16[1,1,2,1024,512]{4,3,2,1,0:T(8,128)(2,1)S(1)} copy-done((bf16[1,1,2,1024,512]{4,3,2,1,0:T(8,128)(2,1)S(1)}, bf16[1,1,2,1024,512]{4,3,2,1,0:T(8,128)(2,1)}, u32[]{:S(2)}) %copy-start.7) | copy-done | bytes 2097176
  15.5 0.8 copy-done.9
  16.3 1.5 %grad_out.1 = bf16[768,512]{1,0:T(8,128)(2,1)S(1)} custom-call(s32[2048]{0:T(1024)S(1)} %copy-done.9, bf16[2048,512]{1,0:T(8,128)(2,1)S(1)} %bitcast.31, bf16[1024,512]{1,0:T(8,128)(2,1)} %collective-permute-done.15.refs_1_), custom_call_target="tpu_custom_call" | custom-call | flops 1000000000 | bytes 1 | tf_op jit(solution)/shard_map/grad_out/pallas_call | solution.py:381
  17.8 3.0 %collective-permute-start.16 = (bf16[768,512]{1,0:T(8,128)(2,1)S(1)}, bf16[768,512]{1,0:T(8,128)(2,1)S(1)}, u32[]{:S(2)}, u32[]{:S(2)}) collective-permute-start(bf16[768,512]{1,0:T(8,128)(2,1)S(1)} %grad_out.1), channel_id=1, source_target_pairs={{0,16},{4,20},{8,24},{12,28},{16,0},{20,4},{24,8},{28,12},{1,17},{... | collective-permute-start | bytes 2359304 | tf_op jit(solution)/shard_map/ppermute | solution.py:69
  20.9 2.2 %copy-done.3 = f32[1,1,2,1024,512]{4,3,2,1,0:T(8,128)S(1)} copy-done((f32[1,1,2,1024,512]{4,3,2,1,0:T(8,128)S(1)}, f32[1,1,2,1024,512]{4,3,2,1,0:T(8,128)}, u32[]{:S(2)}) %copy-start.3) | copy-done | bytes 4194328
  23.1 1.3 %spread.5 = bf16[512,512]{1,0:T(8,128)(2,1)S(1)} custom-call(s32[2048]{0:T(1024)S(1)} %copy-done.9, f32[2048,512]{1,0:T(8,128)S(1)} %bitcast.17, bf16[1024,512]{1,0:T(8,128)(2,1)} %collective-permute-done.10.refs_1_), custom_call_target="tpu_custom_call" | custom-call | flops 1000000000 | bytes 1 | tf_op jit(solution)/shard_map/spread/pallas_call | solution.py:381
  24.4 0.0 copy-start.4
  24.4 1.5 %collective-permute-start.11 = (bf16[512,512]{1,0:T(8,128)(2,1)S(1)}, bf16[512,512]{1,0:T(8,128)(2,1)S(1)}, u32[]{:S(2)}, u32[]{:S(2)}) collective-permute-start(bf16[512,512]{1,0:T(8,128)(2,1)S(1)} %spread.5), channel_id=1, source_target_pairs={{0,4},{4,0},{8,12},{12,8},{16,20},{20,16},{24,28},{28,24},{1,5},{5... | collective-permute-start | bytes 1572872 | tf_op jit(solution)/shard_map/ppermute | solution.py:69
  25.9 0.0 collective-permute-done.5.refs_1_
  25.9 0.7 spread.4
  26.7 0.6 collective-permute-start.6
  27.3 0.0 collective-permute-done.refs_1_
  27.3 1.3 %spread.3 = bf16[512,512]{1,0:T(8,128)(2,1)S(1)} custom-call(s32[2048]{0:T(1024)S(1)} %copy-done.9, bf16[2048,512]{1,0:T(8,128)(2,1)S(1)} %bitcast.24, bf16[1024,512]{1,0:T(8,128)(2,1)} %collective-permute-done.refs_1_), custom_call_target="tpu_custom_call" | custom-call | flops 1000000000 | bytes 1 | tf_op jit(solution)/shard_map/spread/pallas_call | solution.py:381
  28.6 0.0 copy-start.8
  28.6 1.6 %collective-permute-start.1 = (bf16[512,512]{1,0:T(8,128)(2,1)S(1)}, bf16[512,512]{1,0:T(8,128)(2,1)S(1)}, u32[]{:S(2)}, u32[]{:S(2)}) collective-permute-start(bf16[512,512]{1,0:T(8,128)(2,1)S(1)} %spread.3), channel_id=1, source_target_pairs={{0,4},{4,0},{8,12},{12,8},{16,20},{20,16},{24,28},{28,24},{1,5},{5... | collective-permute-start | bytes 1572872 | tf_op jit(solution)/shard_map/ppermute | solution.py:69
  30.1 9.1 %collective-permute-done.11.refs_2_ = bf16[512,512]{1,0:T(8,128)(2,1)S(1)} collective-permute-done((bf16[512,512]{1,0:T(8,128)(2,1)S(1)}, bf16[512,512]{1,0:T(8,128)(2,1)S(1)}, u32[]{:S(2)}, u32[]{:S(2)}) %collective-permute-start.11) | collective-permute-done | bytes 524320 | tf_op jit(solution)/shard_map/ppermute | solution.py:69
  39.3 1.4 %across.5 = bf16[768,512]{1,0:T(8,128)(2,1)S(1)} custom-call(s32[2048]{0:T(1024)S(1)} %copy-done.9, f32[2048,512]{1,0:T(8,128)S(1)} %bitcast.18, bf16[1024,512]{1,0:T(8,128)(2,1)} %collective-permute-done.10.refs_1_, bf16[512,512]{1,0:T(8,128)(2,1)S(1)} %collective-permute-done.11.refs_2_), custom_call_target="tpu_custom_call" | custom-call | flops 1000000000 | bytes 1 | tf_op jit(solution)/shard_map/across/pallas_call | solution.py:381
  40.6 0.1 collective-permute-start.12
  40.7 1.7 %grad_sum.1.refs_0_ = bf16[768,512]{1,0:T(8,128)(2,1)S(1)} custom-call(s32[2048]{0:T(1024)S(1)} %copy-done.9, bf16[2048,512]{1,0:T(8,128)(2,1)S(1)} %bitcast.32, bf16[1024,512]{1,0:T(8,128)(2,1)} %collective-permute-done.15.refs_1_, bf16[768,512]{1,0:T(8,128)(2,1)S(1)} %collective-permute-done.16.refs_2_), custom_call_target="tpu_custom_call" | custom-call | flops 1000000000 | bytes 1 | tf_op jit(solution)/shard_map/grad_sum/pallas_call | solution.py:381
  42.4 2.0 %collective-permute-start.17 = (bf16[768,512]{1,0:T(8,128)(2,1)S(1)}, bf16[768,512]{1,0:T(8,128)(2,1)S(1)}, u32[]{:S(2)}, u32[]{:S(2)}) collective-permute-start(bf16[768,512]{1,0:T(8,128)(2,1)S(1)} %grad_sum.1.refs_0_), channel_id=1, source_target_pairs={{0,4},{4,0},{8,12},{12,8},{16,20},{20,16},{24,28},{28,24},{1,5},{5... | collective-permute-start | bytes 2359304 | tf_op jit(solution)/shard_map/ppermute | solution.py:69
  44.4 6.1 %collective-permute-done.6.refs_2_ = bf16[512,512]{1,0:T(8,128)(2,1)S(1)} collective-permute-done((bf16[512,512]{1,0:T(8,128)(2,1)S(1)}, bf16[512,512]{1,0:T(8,128)(2,1)S(1)}, u32[]{:S(2)}, u32[]{:S(2)}) %collective-permute-start.6) | collective-permute-done | bytes 524320 | tf_op jit(solution)/shard_map/ppermute | solution.py:69
  50.5 0.8 across.4
  51.3 0.1 collective-permute-start.7
  51.4 10.4 %collective-permute-done.1.refs_2_ = bf16[512,512]{1,0:T(8,128)(2,1)S(1)} collective-permute-done((bf16[512,512]{1,0:T(8,128)(2,1)S(1)}, bf16[512,512]{1,0:T(8,128)(2,1)S(1)}, u32[]{:S(2)}, u32[]{:S(2)}) %collective-permute-start.1) | collective-permute-done | bytes 524320 | tf_op jit(solution)/shard_map/ppermute | solution.py:69
  61.7 1.3 %across.3 = bf16[768,512]{1,0:T(8,128)(2,1)S(1)} custom-call(s32[2048]{0:T(1024)S(1)} %copy-done.9, bf16[2048,512]{1,0:T(8,128)(2,1)S(1)} %bitcast.25, bf16[1024,512]{1,0:T(8,128)(2,1)} %collective-permute-done.refs_1_, bf16[512,512]{1,0:T(8,128)(2,1)S(1)} %collective-permute-done.1.refs_2_), custom_call_target="tpu_custom_call" | custom-call | flops 1000000000 | bytes 1 | tf_op jit(solution)/shard_map/across/pallas_call | solution.py:381
  63.1 0.1 collective-permute-start.2
  63.2 1.3 %deliver.5 = bf16[512,512]{1,0:T(8,128)(2,1)S(1)} custom-call(s32[2048]{0:T(1024)S(1)} %copy-done.9, f32[2048,512]{1,0:T(8,128)S(1)} %bitcast.19, bf16[1024,512]{1,0:T(8,128)(2,1)} %collective-permute-done.10.refs_1_, bf16[512,512]{1,0:T(8,128)(2,1)S(1)} %collective-permute-done.11.refs_2_, bf16[768,512]{1,0:T(8,128)(2,1)S(1)} %collective-permute-done.12.refs_3_), custom_call_target="tpu_custom_call" | custom-call | flops 1000000000 | bytes 1 | tf_op jit(solution)/shard_map/deliver/pallas_call | solution.py:381
  64.5 2.0 %collective-permute-start.13 = (bf16[512,512]{1,0:T(8,128)(2,1)S(1)}, bf16[512,512]{1,0:T(8,128)(2,1)S(1)}, u32[]{:S(2)}, u32[]{:S(2)}) collective-permute-start(bf16[512,512]{1,0:T(8,128)(2,1)S(1)} %deliver.5), channel_id=1, source_target_pairs={{0,4},{4,0},{8,12},{12,8},{16,20},{20,16},{24,28},{28,24},{1,5},{5... | collective-permute-start | bytes 1572872 | tf_op jit(solution)/shard_map/ppermute | solution.py:69
  66.5 12.1 %collective-permute-done.17.refs_1_ = bf16[768,512]{1,0:T(8,128)(2,1)S(1)} collective-permute-done((bf16[768,512]{1,0:T(8,128)(2,1)S(1)}, bf16[768,512]{1,0:T(8,128)(2,1)S(1)}, u32[]{:S(2)}, u32[]{:S(2)}) %collective-permute-start.17) | collective-permute-done | bytes 786464 | tf_op jit(solution)/shard_map/ppermute | solution.py:69
  78.6 1.0 grad_mean.1.refs_0_
  79.5 0.1 collective-permute-start.18
  79.6 0.0 collective-permute-done.7.refs_3_
  79.6 0.7 deliver.4
  80.4 2.0 %collective-permute-start.8 = (bf16[512,512]{1,0:T(8,128)(2,1)S(1)}, bf16[512,512]{1,0:T(8,128)(2,1)S(1)}, u32[]{:S(2)}, u32[]{:S(2)}) collective-permute-start(bf16[512,512]{1,0:T(8,128)(2,1)S(1)} %deliver.4), channel_id=1, source_target_pairs={{0,4},{4,0},{8,12},{12,8},{16,20},{20,16},{24,28},{28,24},{1,5},{5... | collective-permute-start | bytes 1572872 | tf_op jit(solution)/shard_map/ppermute | solution.py:69
  82.4 12.5 %collective-permute-done.2.refs_3_ = bf16[768,512]{1,0:T(8,128)(2,1)S(1)} collective-permute-done((bf16[768,512]{1,0:T(8,128)(2,1)S(1)}, bf16[768,512]{1,0:T(8,128)(2,1)S(1)}, u32[]{:S(2)}, u32[]{:S(2)}) %collective-permute-start.2) | collective-permute-done | bytes 786464 | tf_op jit(solution)/shard_map/ppermute | solution.py:69
  94.9 1.3 %deliver.3 = bf16[512,512]{1,0:T(8,128)(2,1)S(1)} custom-call(s32[2048]{0:T(1024)S(1)} %copy-done.9, bf16[2048,512]{1,0:T(8,128)(2,1)S(1)} %bitcast.26, bf16[1024,512]{1,0:T(8,128)(2,1)} %collective-permute-done.refs_1_, bf16[512,512]{1,0:T(8,128)(2,1)S(1)} %collective-permute-done.1.refs_2_, bf16[768,512]{1,0:T(8,128)(2,1)S(1)} %collective-permute-done.2.refs_3_), custom_call_target="tpu_custom_call" | custom-call | flops 1000000000 | bytes 1 | tf_op jit(solution)/shard_map/deliver/pallas_call | solution.py:381
  96.2 1.5 %collective-permute-start.3 = (bf16[512,512]{1,0:T(8,128)(2,1)S(1)}, bf16[512,512]{1,0:T(8,128)(2,1)S(1)}, u32[]{:S(2)}, u32[]{:S(2)}) collective-permute-start(bf16[512,512]{1,0:T(8,128)(2,1)S(1)} %deliver.3), channel_id=1, source_target_pairs={{0,4},{4,0},{8,12},{12,8},{16,20},{20,16},{24,28},{28,24},{1,5},{5... | collective-permute-start | bytes 1572872 | tf_op jit(solution)/shard_map/ppermute | solution.py:69
  97.7 1.4 %collect.5.refs_5_ = bf16[1024,512]{1,0:T(8,128)(2,1)S(1)} custom-call(s32[2048]{0:T(1024)S(1)} %copy-done.9, f32[2048,512]{1,0:T(8,128)S(1)} %bitcast.20, bf16[1024,512]{1,0:T(8,128)(2,1)} %collective-permute-done.10.refs_1_, bf16[512,512]{1,0:T(8,128)(2,1)S(1)} %collective-permute-done.11.refs_2_, bf16[768,512]{1,0:T(8,128)(2,1)S(1)} %collective-permute-done.12.refs_3_, ...), custom_call_target="tpu_custom_call" | custom-call | flops 1000000000 | bytes 1 | tf_op jit(solution)/shard_map/collect/pallas_call | solution.py:381
  99.1 0.1 collective-permute-start.14
  99.2 1.8 %collective-permute-done.8.refs_4_ = bf16[512,512]{1,0:T(8,128)(2,1)S(1)} collective-permute-done((bf16[512,512]{1,0:T(8,128)(2,1)S(1)}, bf16[512,512]{1,0:T(8,128)(2,1)S(1)}, u32[]{:S(2)}, u32[]{:S(2)}) %collective-permute-start.8) | collective-permute-done | bytes 524320 | tf_op jit(solution)/shard_map/ppermute | solution.py:69
  101.1 0.8 collect.4.refs_4_
  101.9 0.1 collective-permute-start.9
  102.0 9.1 %collective-permute-done.3.refs_4_ = bf16[512,512]{1,0:T(8,128)(2,1)S(1)} collective-permute-done((bf16[512,512]{1,0:T(8,128)(2,1)S(1)}, bf16[512,512]{1,0:T(8,128)(2,1)S(1)}, u32[]{:S(2)}, u32[]{:S(2)}) %collective-permute-start.3) | collective-permute-done | bytes 524320 | tf_op jit(solution)/shard_map/ppermute | solution.py:69
  111.1 1.4 %collect.3.refs_3_ = bf16[1024,512]{1,0:T(8,128)(2,1)S(1)} custom-call(s32[2048]{0:T(1024)S(1)} %copy-done.9, bf16[2048,512]{1,0:T(8,128)(2,1)S(1)} %bitcast.27, bf16[1024,512]{1,0:T(8,128)(2,1)} %collective-permute-done.refs_1_, bf16[512,512]{1,0:T(8,128)(2,1)S(1)} %collective-permute-done.1.refs_2_, bf16[768,512]{1,0:T(8,128)(2,1)S(1)} %collective-permute-done.2.refs_3_, ...), custom_call_target="tpu_custom_call" | custom-call | flops 1000000000 | bytes 1 | tf_op jit(solution)/shard_map/collect/pallas_call | solution.py:381
  112.5 0.1 collective-permute-start.4
  112.6 1.0 mean.1
  113.5 0.6 collective-permute-start.19
  114.1 4.5 %update.2 = (bf16[2,2,512,512]{3,2,1,0:T(8,128)(2,1)}, f32[2,2,512,512]{3,2,1,0:T(8,128)}, f32[2,2,512,512]{3,2,1,0:T(8,128)}) custom-call(s32[2048]{0:T(1024)S(1)} %copy-done.9, bf16[2048,512]{1,0:T(8,128)(2,1)S(1)} %bitcast.28, f32[2048,512]{1,0:T(8,128)S(1)} %bitcast.14, f32[2048,512]{1,0:T(8,128)S(1)} %bitcast.21, bf16[1024,512]{1,0:T(8,128)(2,1)S(1)} %collect.3.refs_3_, ...), custom_call_target="tpu_custom_call" | custom-call | flops 1 | bytes 1 | tf_op jit(solution)/shard_map/update/pallas_call | solution.py:481
  118.6 4.5 %update.3 = (bf16[2,2,512,512]{3,2,1,0:T(8,128)(2,1)}, f32[2,2,512,512]{3,2,1,0:T(8,128)}, f32[2,2,512,512]{3,2,1,0:T(8,128)}) custom-call(s32[2048]{0:T(1024)S(1)} %copy-done.9, bf16[2048,512]{1,0:T(8,128)(2,1)S(1)} %bitcast.29, f32[2048,512]{1,0:T(8,128)S(1)} %bitcast.15, ...), custom_call_target="tpu_custom_call", output_to_operand_aliasing={{0}: (8, {}), {1}: (9, {}), {2}: (10, {})} | custom-call | flops 1 | bytes 1 | tf_op jit(solution)/shard_map/update/pallas_call | solution.py:481
  (22 shorter events, 0.0 us)
Async XLA Ops:
  0.7 9.6 %copy-start.10 = (s32[2]{0:T(128)}, s32[2]{0:T(128)S(1)}, u32[]{:S(2)}) copy-start(s32[2]{0:T(128)S(1)} %pad_add_fusion.place_ref) | copy-start | bytes 28
  0.7 1.6 %copy-start.6 = (bf16[1,1,2,1024,512]{4,3,2,1,0:T(8,128)(2,1)S(1)}, bf16[1,1,2,1024,512]{4,3,2,1,0:T(8,128)(2,1)}, u32[]{:S(2)}) copy-start(bf16[1,1,2,1024,512]{4,3,2,1,0:T(8,128)(2,1)} %param.11) | copy-start | bytes 6291460
  2.3 5.9 %copy-start = (f32[1,1,2,1024,512]{4,3,2,1,0:T(8,128)S(1)}, f32[1,1,2,1024,512]{4,3,2,1,0:T(8,128)}, u32[]{:S(2)}) copy-start(f32[1,1,2,1024,512]{4,3,2,1,0:T(8,128)} %param.9) | copy-start | bytes 12582916
  3.9 9.8 %collective-permute-start.15 = (bf16[1024,512]{1,0:T(8,128)(2,1)}, bf16[1024,512]{1,0:T(8,128)(2,1)}, u32[]{:S(2)}, u32[]{:S(2)}) collective-permute-start(bf16[1024,512]{1,0:T(8,128)(2,1)} %halve_gradients.1), channel_id=1, source_target_pairs={{0,8},{4,12},{8,0},{12,4},{16,24},{20,28},{24,16},{28,20},{1,9},{5... | collective-permute-start | bytes 3145736 | tf_op jit(solution)/shard_map/ppermute | solution.py:69
  4.3 2.2 %copy-start.2 = (f32[1,1,2,1024,512]{4,3,2,1,0:T(8,128)S(1)}, f32[1,1,2,1024,512]{4,3,2,1,0:T(8,128)}, u32[]{:S(2)}) copy-start(f32[1,1,2,1024,512]{4,3,2,1,0:T(8,128)} %param.10) | copy-start | bytes 12582916
  6.5 3.8 %copy-start.5 = (bf16[1,1,2,1024,512]{4,3,2,1,0:T(8,128)(2,1)S(1)}, bf16[1,1,2,1024,512]{4,3,2,1,0:T(8,128)(2,1)}, u32[]{:S(2)}) copy-start(bf16[1,1,2,1024,512]{4,3,2,1,0:T(8,128)(2,1)} %param.8) | copy-start | bytes 6291460
  8.2 12.7 %collective-permute-start.10 = (bf16[1024,512]{1,0:T(8,128)(2,1)}, bf16[1024,512]{1,0:T(8,128)(2,1)}, u32[]{:S(2)}, u32[]{:S(2)}) collective-permute-start(bf16[1024,512]{1,0:T(8,128)(2,1)} %halve_state.5), channel_id=1, source_target_pairs={{0,8},{4,12},{8,0},{12,4},{16,24},{20,28},{24,16},{28,20},{1,9},{5... | collective-permute-start | bytes 3145736 | tf_op jit(solution)/shard_map/ppermute | solution.py:69
  9.8 16.1 %collective-permute-start.5 = (bf16[1024,512]{1,0:T(8,128)(2,1)}, bf16[1024,512]{1,0:T(8,128)(2,1)S(1)}, u32[]{:S(2)}, u32[]{:S(2)}) collective-permute-start(bf16[1024,512]{1,0:T(8,128)(2,1)} %halve_state.4), channel_id=1, source_target_pairs={{0,8},{4,12},{8,0},{12,4},{16,24},{20,28},{24,16},{28,20},{1,9},{5... | collective-permute-start | bytes 3145736 | tf_op jit(solution)/shard_map/ppermute | solution.py:69
  11.9 15.4 %collective-permute-start = (bf16[1024,512]{1,0:T(8,128)(2,1)}, bf16[1024,512]{1,0:T(8,128)(2,1)}, u32[]{:S(2)}, u32[]{:S(2)}) collective-permute-start(bf16[1024,512]{1,0:T(8,128)(2,1)} %halve_state.3), channel_id=1, source_target_pairs={{0,8},{4,12},{8,0},{12,4},{16,24},{20,28},{24,16},{28,20},{1,9},{5... | collective-permute-start | bytes 3145736 | tf_op jit(solution)/shard_map/ppermute | solution.py:69
  13.7 12.2 %copy-start.1 = (f32[1,1,2,1024,512]{4,3,2,1,0:T(8,128)S(1)}, f32[1,1,2,1024,512]{4,3,2,1,0:T(8,128)}, u32[]{:S(2)}) copy-start(f32[1,1,2,1024,512]{4,3,2,1,0:T(8,128)} %param.9) | copy-start | bytes 12582916
  13.7 1.7 %copy-start.7 = (bf16[1,1,2,1024,512]{4,3,2,1,0:T(8,128)(2,1)S(1)}, bf16[1,1,2,1024,512]{4,3,2,1,0:T(8,128)(2,1)}, u32[]{:S(2)}) copy-start(bf16[1,1,2,1024,512]{4,3,2,1,0:T(8,128)(2,1)} %param.11) | copy-start | bytes 6291460
  15.5 0.8 copy-start.9
  17.8 22.9 %collective-permute-start.16 = (bf16[768,512]{1,0:T(8,128)(2,1)S(1)}, bf16[768,512]{1,0:T(8,128)(2,1)S(1)}, u32[]{:S(2)}, u32[]{:S(2)}) collective-permute-start(bf16[768,512]{1,0:T(8,128)(2,1)S(1)} %grad_out.1), channel_id=1, source_target_pairs={{0,16},{4,20},{8,24},{12,28},{16,0},{20,4},{24,8},{28,12},{1,17},{... | collective-permute-start | bytes 2359304 | tf_op jit(solution)/shard_map/ppermute | solution.py:69
  20.9 2.2 %copy-start.3 = (f32[1,1,2,1024,512]{4,3,2,1,0:T(8,128)S(1)}, f32[1,1,2,1024,512]{4,3,2,1,0:T(8,128)}, u32[]{:S(2)}) copy-start(f32[1,1,2,1024,512]{4,3,2,1,0:T(8,128)} %param.10) | copy-start | bytes 12582916
  24.4 14.9 %copy-start.4 = (f32[1,1,2,1024,512]{4,3,2,1,0:T(8,128)S(1)}, f32[1,1,2,1024,512]{4,3,2,1,0:T(8,128)}, u32[]{:S(2)}) copy-start(f32[1,1,2,1024,512]{4,3,2,1,0:T(8,128)} %param.10) | copy-start | bytes 12582916
  24.4 14.9 %collective-permute-start.11 = (bf16[512,512]{1,0:T(8,128)(2,1)S(1)}, bf16[512,512]{1,0:T(8,128)(2,1)S(1)}, u32[]{:S(2)}, u32[]{:S(2)}) collective-permute-start(bf16[512,512]{1,0:T(8,128)(2,1)S(1)} %spread.5), channel_id=1, source_target_pairs={{0,4},{4,0},{8,12},{12,8},{16,20},{20,16},{24,28},{28,24},{1,5},{5... | collective-permute-start | bytes 1572872 | tf_op jit(solution)/shard_map/ppermute | solution.py:69
  26.7 23.8 %collective-permute-start.6 = (bf16[512,512]{1,0:T(8,128)(2,1)S(1)}, bf16[512,512]{1,0:T(8,128)(2,1)S(1)}, u32[]{:S(2)}, u32[]{:S(2)}) collective-permute-start(bf16[512,512]{1,0:T(8,128)(2,1)S(1)} %spread.4), channel_id=1, source_target_pairs={{0,4},{4,0},{8,12},{12,8},{16,20},{20,16},{24,28},{28,24},{1,5},{5... | collective-permute-start | bytes 1572872 | tf_op jit(solution)/shard_map/ppermute | solution.py:69
  28.6 12.2 %copy-start.8 = (bf16[1,1,2,1024,512]{4,3,2,1,0:T(8,128)(2,1)S(1)}, bf16[1,1,2,1024,512]{4,3,2,1,0:T(8,128)(2,1)}, u32[]{:S(2)}) copy-start(bf16[1,1,2,1024,512]{4,3,2,1,0:T(8,128)(2,1)} %param.11) | copy-start | bytes 6291460
  28.6 33.2 %collective-permute-start.1 = (bf16[512,512]{1,0:T(8,128)(2,1)S(1)}, bf16[512,512]{1,0:T(8,128)(2,1)S(1)}, u32[]{:S(2)}, u32[]{:S(2)}) collective-permute-start(bf16[512,512]{1,0:T(8,128)(2,1)S(1)} %spread.3), channel_id=1, source_target_pairs={{0,4},{4,0},{8,12},{12,8},{16,20},{20,16},{24,28},{28,24},{1,5},{5... | collective-permute-start | bytes 1572872 | tf_op jit(solution)/shard_map/ppermute | solution.py:69
  40.6 22.5 %collective-permute-start.12 = (bf16[768,512]{1,0:T(8,128)(2,1)S(1)}, bf16[768,512]{1,0:T(8,128)(2,1)S(1)}, u32[]{:S(2)}, u32[]{:S(2)}) collective-permute-start(bf16[768,512]{1,0:T(8,128)(2,1)S(1)} %across.5), channel_id=1, source_target_pairs={{0,16},{4,20},{8,24},{12,28},{16,0},{20,4},{24,8},{28,12},{1,17},{... | collective-permute-start | bytes 2359304 | tf_op jit(solution)/shard_map/ppermute | solution.py:69
  42.4 36.2 %collective-permute-start.17 = (bf16[768,512]{1,0:T(8,128)(2,1)S(1)}, bf16[768,512]{1,0:T(8,128)(2,1)S(1)}, u32[]{:S(2)}, u32[]{:S(2)}) collective-permute-start(bf16[768,512]{1,0:T(8,128)(2,1)S(1)} %grad_sum.1.refs_0_), channel_id=1, source_target_pairs={{0,4},{4,0},{8,12},{12,8},{16,20},{20,16},{24,28},{28,24},{1,5},{5... | collective-permute-start | bytes 2359304 | tf_op jit(solution)/shard_map/ppermute | solution.py:69
  51.3 28.3 %collective-permute-start.7 = (bf16[768,512]{1,0:T(8,128)(2,1)S(1)}, bf16[768,512]{1,0:T(8,128)(2,1)S(1)}, u32[]{:S(2)}, u32[]{:S(2)}) collective-permute-start(bf16[768,512]{1,0:T(8,128)(2,1)S(1)} %across.4), channel_id=1, source_target_pairs={{0,16},{4,20},{8,24},{12,28},{16,0},{20,4},{24,8},{28,12},{1,17},{... | collective-permute-start | bytes 2359304 | tf_op jit(solution)/shard_map/ppermute | solution.py:69
  63.1 31.8 %collective-permute-start.2 = (bf16[768,512]{1,0:T(8,128)(2,1)S(1)}, bf16[768,512]{1,0:T(8,128)(2,1)S(1)}, u32[]{:S(2)}, u32[]{:S(2)}) collective-permute-start(bf16[768,512]{1,0:T(8,128)(2,1)S(1)} %across.3), channel_id=1, source_target_pairs={{0,16},{4,20},{8,24},{12,28},{16,0},{20,4},{24,8},{28,12},{1,17},{... | collective-permute-start | bytes 2359304 | tf_op jit(solution)/shard_map/ppermute | solution.py:69
  64.5 33.2 %collective-permute-start.13 = (bf16[512,512]{1,0:T(8,128)(2,1)S(1)}, bf16[512,512]{1,0:T(8,128)(2,1)S(1)}, u32[]{:S(2)}, u32[]{:S(2)}) collective-permute-start(bf16[512,512]{1,0:T(8,128)(2,1)S(1)} %deliver.5), channel_id=1, source_target_pairs={{0,4},{4,0},{8,12},{12,8},{16,20},{20,16},{24,28},{28,24},{1,5},{5... | collective-permute-start | bytes 1572872 | tf_op jit(solution)/shard_map/ppermute | solution.py:69
  79.5 33.0 %collective-permute-start.18 = (bf16[768,512]{1,0:T(8,128)(2,1)S(1)}, bf16[768,512]{1,0:T(8,128)(2,1)S(1)}, u32[]{:S(2)}, u32[]{:S(2)}) collective-permute-start(bf16[768,512]{1,0:T(8,128)(2,1)S(1)} %grad_mean.1.refs_0_), channel_id=1, source_target_pairs={{0,16},{4,20},{8,24},{12,28},{16,0},{20,4},{24,8},{28,12},{1,17},{... | collective-permute-start | bytes 2359304 | tf_op jit(solution)/shard_map/ppermute | solution.py:69
  80.4 20.7 %collective-permute-start.8 = (bf16[512,512]{1,0:T(8,128)(2,1)S(1)}, bf16[512,512]{1,0:T(8,128)(2,1)S(1)}, u32[]{:S(2)}, u32[]{:S(2)}) collective-permute-start(bf16[512,512]{1,0:T(8,128)(2,1)S(1)} %deliver.4), channel_id=1, source_target_pairs={{0,4},{4,0},{8,12},{12,8},{16,20},{20,16},{24,28},{28,24},{1,5},{5... | collective-permute-start | bytes 1572872 | tf_op jit(solution)/shard_map/ppermute | solution.py:69
  96.2 14.9 %collective-permute-start.3 = (bf16[512,512]{1,0:T(8,128)(2,1)S(1)}, bf16[512,512]{1,0:T(8,128)(2,1)S(1)}, u32[]{:S(2)}, u32[]{:S(2)}) collective-permute-start(bf16[512,512]{1,0:T(8,128)(2,1)S(1)} %deliver.3), channel_id=1, source_target_pairs={{0,4},{4,0},{8,12},{12,8},{16,20},{20,16},{24,28},{28,24},{1,5},{5... | collective-permute-start | bytes 1572872 | tf_op jit(solution)/shard_map/ppermute | solution.py:69
  99.1 19.5 %collective-permute-start.14 = (bf16[1024,512]{1,0:T(8,128)(2,1)S(1)}, bf16[1024,512]{1,0:T(8,128)(2,1)S(1)}, u32[]{:S(2)}, u32[]{:S(2)}) collective-permute-start(bf16[1024,512]{1,0:T(8,128)(2,1)S(1)} %collect.5.refs_5_), channel_id=1, source_target_pairs={{0,8},{4,12},{8,0},{12,4},{16,24},{20,28},{24,16},{28,20},{1,9},{5... | collective-permute-start | bytes 3145736 | tf_op jit(solution)/shard_map/ppermute | solution.py:69
  101.9 16.7 %collective-permute-start.9 = (bf16[1024,512]{1,0:T(8,128)(2,1)S(1)}, bf16[1024,512]{1,0:T(8,128)(2,1)S(1)}, u32[]{:S(2)}, u32[]{:S(2)}) collective-permute-start(bf16[1024,512]{1,0:T(8,128)(2,1)S(1)} %collect.4.refs_4_), channel_id=1, source_target_pairs={{0,8},{4,12},{8,0},{12,4},{16,24},{20,28},{24,16},{28,20},{1,9},{5... | collective-permute-start | bytes 3145736 | tf_op jit(solution)/shard_map/ppermute | solution.py:69
  112.5 6.1 %collective-permute-start.4 = (bf16[1024,512]{1,0:T(8,128)(2,1)S(1)}, bf16[1024,512]{1,0:T(8,128)(2,1)S(1)}, u32[]{:S(2)}, u32[]{:S(2)}) collective-permute-start(bf16[1024,512]{1,0:T(8,128)(2,1)S(1)} %collect.3.refs_3_), channel_id=1, source_target_pairs={{0,8},{4,12},{8,0},{12,4},{16,24},{20,28},{24,16},{28,20},{1,9},{5... | collective-permute-start | bytes 3145736 | tf_op jit(solution)/shard_map/ppermute | solution.py:69
  113.5 5.1 %collective-permute-start.19 = (bf16[1024,512]{1,0:T(8,128)(2,1)S(1)}, bf16[1024,512]{1,0:T(8,128)(2,1)S(1)}, u32[]{:S(2)}, u32[]{:S(2)}) collective-permute-start(bf16[1024,512]{1,0:T(8,128)(2,1)S(1)} %get-tuple-element.11), channel_id=1, source_target_pairs={{0,8},{4,12},{8,0},{12,4},{16,24},{20,28},{24,16},{28,20},{1,9},{5... | collective-permute-start | bytes 3145736 | tf_op jit(solution)/shard_map/ppermute | solution.py:69

commit v6 on v4

--- a/solution.py
+++ b/solution.py
@@ -1,3 +1,5 @@
+import math
+
 import jax
 import jax.numpy as jnp
 from jax import lax
@@ -307,9 +309,9 @@
         self.value, self.rows, self.count = value, rows, count
         self.arrays, self.base = arrays, base
 
-    def block(self, array, index):
-        at = self.base + (array * self.count + index) * self.rows
-        return pl.ds(at if isinstance(at, int) else pl.multiple_of(at, 16), self.rows)
+    def part(self, array, index, first, rows):
+        at = self.base + (array * self.count + index) * self.rows + first
+        return pl.ds(pl.multiple_of(at, 16), rows)
 
 
 class Copy:
@@ -325,9 +327,14 @@
                 @pl.when(table_ref[entry] != 0)
                 def _(unit=unit, source=source, ref=refs[at], entry=entry):
                     index = table_ref[entry + 1]
+                    step = math.gcd(self.rows, 64)
                     for array in range(self.arrays):
-                        block = ref[source.block(array, index)]
-                        out_ref[out.block(array, unit)] = block.astype(out_ref.dtype)
+
+                        @pl.loop(0, self.rows // step)
+                        def _(at):
+                            block = ref[source.part(array, index, at * step, step)]
+                            place = out.part(array, unit, at * step, step)
+                            out_ref[place] = block.astype(out_ref.dtype)
 
 
 class Sum:
@@ -336,14 +343,23 @@
         self.arrays, self.rows = 1, sources[0].rows
 
     def write(self, table_ref, refs, out_ref, out):
+        step = math.gcd(self.rows, 32)
         for unit in range(self.units):
-            total_here = None
-            for at, source in enumerate(self.sources):
-                entry = self.start + (unit * len(self.sources) + at) * 2
-                block = refs[at][source.block(0, table_ref[entry + 1])].astype(jnp.float32)
-                block = jnp.where(table_ref[entry] != 0, block, 0.0)
-                total_here = block if total_here is None else total_here + block
-            out_ref[out.block(0, unit)] = total_here.astype(out_ref.dtype)
+            entries = [
+                self.start + (unit * len(self.sources) + at) * 2
+                for at in range(len(self.sources))
+            ]
+            flags = [table_ref[entry] != 0 for entry in entries]
+            places = [table_ref[entry + 1] for entry in entries]
+
+            @pl.loop(0, self.rows // step)
+            def _(at, unit=unit, flags=flags, places=places):
+                total_here = None
+                for source, ref, flag, index in zip(self.sources, refs, flags, places):
+                    block = ref[source.part(0, index, at * step, step)].astype(jnp.float32)
+                    block = jnp.where(flag, block, 0.0)
+                    total_here = block if total_here is None else total_here + block
+                out_ref[out.part(0, unit, at * step, step)] = total_here.astype(out_ref.dtype)
 
 
 def stage(z, order, table, outputs, name):
@@ -384,8 +400,13 @@
 def sibling_half(z, order, place, array, name):
     view = array.reshape(z.slots, CORES, z.half, z.cols)
 
+    step = math.gcd(z.half, 64)
+
     def kernel(place_ref, array_ref, *refs):
-        refs[-1][...] = array_ref[0, 0].astype(jnp.bfloat16)
+        @pl.loop(0, z.half // step)
+        def _(at):
+            rows = pl.ds(pl.multiple_of(at * step, 16), step)
+            refs[-1][rows] = array_ref[0, 0, rows].astype(jnp.bfloat16)
 
     def half_of(slot, place_ref):
         return (slot, 1 - lax.rem(place_ref[0], CORES), 0, 0)
@@ -411,6 +432,7 @@
     views = [a.reshape(z.slots * z.rows, z.cols) for a in state]
     outs = [] if outs is None else list(outs)
     rows, cols = 16, min(z.cols, 128)
+    unroll = math.gcd(z.half // rows, 4)
 
     def half_now(table_ref):
         core = table_ref[start + 1]
@@ -424,23 +446,26 @@
         found = table_ref[start + 2 + slot] != 0
 
         def each(sources, base):
-            @pl.loop(0, z.half // rows)
+            @pl.loop(0, z.half // (rows * unroll))
             def _(at):
-                row = pl.ds(pl.multiple_of(at * rows, rows), rows)
-                mean_row = pl.ds(pl.multiple_of(slot * z.half + at * rows, rows), rows)
-                from_row = pl.ds(pl.multiple_of(base + at * rows, rows), rows)
-                for first in range(0, z.cols, cols):
-                    lanes = pl.ds(first, cols)
-                    weight, one, two = [
-                        ref[from_row, lanes].astype(jnp.float32) for ref in sources
-                    ]
-                    grad = mean_ref[mean_row, lanes].astype(jnp.float32)
-                    next_one = BETA_ONE * one + ((1.0 - BETA_ONE) / z.pipes) * grad
-                    next_two = BETA_TWO * two + ((1.0 - BETA_TWO) / z.pipes**2) * (grad * grad)
-                    move = next_one / (jnp.sqrt(next_two) + EPSILON)
-                    next_weight = (1.0 - LEARN_RATE * DECAY_RATE) * weight - LEARN_RATE * move
-                    for ref, value in zip(out_refs, (next_weight, next_one, next_two)):
-                        ref[0, 0, row, lanes] = value.astype(ref.dtype)
+                for first in range(unroll):
+                    for lane in range(0, z.cols, cols):
+                        one_block(sources, base, (at * unroll + first) * rows, lane)
+
+        def one_block(sources, base, at, lane):
+            row = pl.ds(pl.multiple_of(at, rows), rows)
+            mean_row = pl.ds(pl.multiple_of(slot * z.half + at, rows), rows)
+            from_row = pl.ds(pl.multiple_of(base + at, rows), rows)
+            lanes = pl.ds(lane, cols)
+            weight, one, two = [ref[from_row, lanes].astype(jnp.float32) for ref in sources]
+            grad = mean_ref[mean_row, lanes].astype(jnp.float32)
+            next_one = BETA_ONE * one + ((1.0 - BETA_ONE) / z.pipes) * grad
+            next_two = BETA_TWO * two + ((1.0 - BETA_TWO) / z.pipes**2) * (grad * grad)
+            scale = next_two * lax.rsqrt(next_two) + EPSILON
+            move = next_one * lax.rsqrt(scale * scale)
+            next_weight = (1.0 - LEARN_RATE * DECAY_RATE) * weight - LEARN_RATE * move
+            for ref, value in zip(out_refs, (next_weight, next_one, next_two)):
+                ref[0, 0, row, lanes] = value.astype(ref.dtype)
 
         @pl.when(both(found, is_lost))
         def _():
@@ -452,8 +477,11 @@
 
         @pl.when(jnp.logical_not(found))
         def _():
-            for ref in out_refs:
-                ref[...] = jnp.zeros(ref.shape, ref.dtype)
+            @pl.loop(0, z.half // rows)
+            def _(at):
+                for ref in out_refs:
+                    row = pl.ds(pl.multiple_of(at * rows, rows), rows)
+                    ref[0, 0, row] = jnp.zeros((rows, z.cols), ref.dtype)
 
     block = (1, 1, z.half, z.cols)
     out_spec = pl.BlockSpec(block, lambda slot, table_ref: (slot, half_now(table_ref), 0, 0))

time: 121 us -> 120 us (level)
    pallas_call x2, Pallas kernels: 9.57 us -> 8.04 us  [update(): return order.then(call(table, *operands, *order.last))]
  transfers between devices with their start and end apart: 20 -> 20, of which waited for: 7 -> 7; matrix products, arithmetic and copies ran while one was open for 0% -> 0% of each run, Pallas kernels for 25% -> 26%
where the time goes in v6:
time: 120 us; the launch traced here: 119 us
  waiting for transfers between devices  59.6 us (50%)
  Pallas kernels  36.1 us (30%)
  starting transfers between devices  16.8 us (14%)
  local copies, waits for them, and re-layouts  5.92 us (5%)
    ppermute x20, waiting for transfers between devices, send(): return lax.ppermute(value, AXES, pairs)  59.6 us
    pallas_call x16, Pallas kernels, stage(): return order.then(call(table, *operands, *order.last))  19.9 us
    ppermute x20, starting transfers between devices, send(): return lax.ppermute(value, AXES, pairs)  16.8 us
    pallas_call x2, Pallas kernels, update(): return order.then(call(table, *operands, *order.last))  8.04 us
    pallas_call x4, Pallas kernels, sibling_half(): return order.then((call(place, view, *order.last),))[0]  6.44 us
    unnamed x20, local copies, waits for them, and re-layouts  5.92 us
  transfers between devices with their start and end apart: 20, of which 7 were waited for; matrix products, arithmetic and copies ran while one was open for 0% of the time, Pallas kernels for 26%

profile of v6, /device:TPU:0, one launch (start us, length us, event | category | flops | bytes accessed | tf_op | source)
XLA Modules:
  0.0 119.4 jit_solution(2103484145485631062)
XLA Ops:
  0.6 0.0 copy-start
  0.6 0.1 pad_add_fusion.place_ref
  0.7 1.7 %copy-done.6 = bf16[1,1,2,1024,512]{4,3,2,1,0:T(8,128)(2,1)S(1)} copy-done((bf16[1,1,2,1024,512]{4,3,2,1,0:T(8,128)(2,1)S(1)}, bf16[1,1,2,1024,512]{4,3,2,1,0:T(8,128)(2,1)}, u32[]{:S(2)}) %copy-start.6) | copy-done | bytes 2097176
  2.5 1.6 %halve_gradients.1 = bf16[1024,512]{1,0:T(8,128)(2,1)} custom-call(s32[2]{0:T(128)S(1)} %pad_add_fusion.place_ref, bf16[2,2,512,512]{3,2,1,0:T(8,128)(2,1)S(1)} %bitcast.34), custom_call_target="tpu_custom_call" | custom-call | flops 1000000000 | bytes 1 | tf_op jit(solution)/shard_map/halve_gradients/pallas_call | solution.py:428
  4.1 0.5 collective-permute-start.15
  4.5 1.6 %copy-done.4 = bf16[1,1,2,1024,512]{4,3,2,1,0:T(8,128)(2,1)S(1)} copy-done((bf16[1,1,2,1024,512]{4,3,2,1,0:T(8,128)(2,1)S(1)}, bf16[1,1,2,1024,512]{4,3,2,1,0:T(8,128)(2,1)}, u32[]{:S(2)}) %copy-start.4) | copy-done | bytes 2097176
  6.1 1.6 %halve_state.3 = bf16[1024,512]{1,0:T(8,128)(2,1)} custom-call(s32[2]{0:T(128)S(1)} %pad_add_fusion.place_ref, bf16[2,2,512,512]{3,2,1,0:T(8,128)(2,1)S(1)} %bitcast.27), custom_call_target="tpu_custom_call" | custom-call | flops 1000000000 | bytes 1 | tf_op jit(solution)/shard_map/halve_state/pallas_call | solution.py:428
  7.7 0.1 collective-permute-start
  7.8 1.6 %halve_state.4 = bf16[1024,512]{1,0:T(8,128)(2,1)} custom-call(s32[2]{0:T(128)S(1)} %pad_add_fusion.place_ref, f32[2,2,512,512]{3,2,1,0:T(8,128)S(1)} %bitcast.13), custom_call_target="tpu_custom_call" | custom-call | flops 1000000000 | bytes 1 | tf_op jit(solution)/shard_map/halve_state/pallas_call | solution.py:428
  9.4 0.5 collective-permute-start.5
  9.9 1.6 %halve_state.5 = bf16[1024,512]{1,0:T(8,128)(2,1)} custom-call(s32[2]{0:T(128)S(1)} %pad_add_fusion.place_ref, f32[2,2,512,512]{3,2,1,0:T(8,128)S(1)} %bitcast.20), custom_call_target="tpu_custom_call" | custom-call | flops 1000000000 | bytes 1 | tf_op jit(solution)/shard_map/halve_state/pallas_call | solution.py:428
  11.5 0.1 collective-permute-start.10
  11.5 1.8 %plan.1.table_ref = s32[2048]{0:T(1024)} custom-call(s32[2]{0:T(128)} %copy-done.9, s32[4,3]{1,0:T(4,128)} %old_ref.1, s32[3]{0:T(128)} %new_ref.1, s32[4]{0:T(128)} %lost_ref.1, s32[3]{0:T(128)} %offset_ref.1), custom_call_target="tpu_custom_call" | custom-call | tf_op jit(solution)/shard_map/plan/pallas_call | solution.py:260
  13.3 0.0 copy-start.1
  13.3 0.0 collective-permute-done.15.refs_1_
  13.3 0.0 copy-start.7
  13.3 1.7 %copy-done.7 = bf16[1,1,2,1024,512]{4,3,2,1,0:T(8,128)(2,1)S(1)} copy-done((bf16[1,1,2,1024,512]{4,3,2,1,0:T(8,128)(2,1)S(1)}, bf16[1,1,2,1024,512]{4,3,2,1,0:T(8,128)(2,1)}, u32[]{:S(2)}) %copy-start.7) | copy-done | bytes 2097176
  15.1 0.8 copy-done.8
  15.9 1.7 %grad_out.1 = bf16[768,512]{1,0:T(8,128)(2,1)S(1)} custom-call(s32[2048]{0:T(1024)S(1)} %copy-done.8, bf16[2048,512]{1,0:T(8,128)(2,1)S(1)} %bitcast.35, bf16[1024,512]{1,0:T(8,128)(2,1)} %collective-permute-done.15.refs_1_), custom_call_target="tpu_custom_call" | custom-call | flops 1000000000 | bytes 1 | tf_op jit(solution)/shard_map/grad_out/pallas_call | solution.py:397
  17.6 3.0 %collective-permute-start.16 = (bf16[768,512]{1,0:T(8,128)(2,1)S(1)}, bf16[768,512]{1,0:T(8,128)(2,1)S(1)}, u32[]{:S(2)}, u32[]{:S(2)}) collective-permute-start(bf16[768,512]{1,0:T(8,128)(2,1)S(1)} %grad_out.1), channel_id=1, source_target_pairs={{0,16},{4,20},{8,24},{12,28},{16,0},{20,4},{24,8},{28,12},{1,17},{... | collective-permute-start | bytes 2359304 | tf_op jit(solution)/shard_map/ppermute | solution.py:71
  20.6 1.4 %spread.3 = bf16[512,512]{1,0:T(8,128)(2,1)S(1)} custom-call(s32[2048]{0:T(1024)S(1)} %copy-done.8, bf16[2048,512]{1,0:T(8,128)(2,1)S(1)} %bitcast.28, bf16[1024,512]{1,0:T(8,128)(2,1)} %collective-permute-done.refs_1_), custom_call_target="tpu_custom_call" | custom-call | flops 1000000000 | bytes 1 | tf_op jit(solution)/shard_map/spread/pallas_call | solution.py:397
  22.1 1.5 %collective-permute-start.1 = (bf16[512,512]{1,0:T(8,128)(2,1)S(1)}, bf16[512,512]{1,0:T(8,128)(2,1)S(1)}, u32[]{:S(2)}, u32[]{:S(2)}) collective-permute-start(bf16[512,512]{1,0:T(8,128)(2,1)S(1)} %spread.3), channel_id=1, source_target_pairs={{0,4},{4,0},{8,12},{12,8},{16,20},{20,16},{24,28},{28,24},{1,5},{5... | collective-permute-start | bytes 1572872 | tf_op jit(solution)/shard_map/ppermute | solution.py:71
  23.6 1.3 %spread.4 = bf16[512,512]{1,0:T(8,128)(2,1)S(1)} custom-call(s32[2048]{0:T(1024)S(1)} %copy-done.8, f32[2048,512]{1,0:T(8,128)S(1)} %bitcast.14, bf16[1024,512]{1,0:T(8,128)(2,1)} %collective-permute-done.5.refs_1_), custom_call_target="tpu_custom_call" | custom-call | flops 1000000000 | bytes 1 | tf_op jit(solution)/shard_map/spread/pallas_call | solution.py:397
  24.9 0.6 collective-permute-start.6
  25.5 0.0 collective-permute-done.10.refs_1_
  25.5 0.7 spread.5
  26.3 1.5 %collective-permute-start.11 = (bf16[512,512]{1,0:T(8,128)(2,1)S(1)}, bf16[512,512]{1,0:T(8,128)(2,1)S(1)}, u32[]{:S(2)}, u32[]{:S(2)}) collective-permute-start(bf16[512,512]{1,0:T(8,128)(2,1)S(1)} %spread.5), channel_id=1, source_target_pairs={{0,4},{4,0},{8,12},{12,8},{16,20},{20,16},{24,28},{28,24},{1,5},{5... | collective-permute-start | bytes 1572872 | tf_op jit(solution)/shard_map/ppermute | solution.py:71
  27.8 9.2 %collective-permute-done.1.refs_2_ = bf16[512,512]{1,0:T(8,128)(2,1)S(1)} collective-permute-done((bf16[512,512]{1,0:T(8,128)(2,1)S(1)}, bf16[512,512]{1,0:T(8,128)(2,1)S(1)}, u32[]{:S(2)}, u32[]{:S(2)}) %collective-permute-start.1) | collective-permute-done | bytes 524320 | tf_op jit(solution)/shard_map/ppermute | solution.py:71
  37.0 1.3 %across.3 = bf16[768,512]{1,0:T(8,128)(2,1)S(1)} custom-call(s32[2048]{0:T(1024)S(1)} %copy-done.8, bf16[2048,512]{1,0:T(8,128)(2,1)S(1)} %bitcast.29, bf16[1024,512]{1,0:T(8,128)(2,1)} %collective-permute-done.refs_1_, bf16[512,512]{1,0:T(8,128)(2,1)S(1)} %collective-permute-done.1.refs_2_), custom_call_target="tpu_custom_call" | custom-call | flops 1000000000 | bytes 1 | tf_op jit(solution)/shard_map/across/pallas_call | solution.py:397
  38.3 0.1 collective-permute-start.2
  38.4 0.0 collective-permute-done.16.refs_2_
  38.4 1.9 %grad_sum.1.refs_0_ = bf16[768,512]{1,0:T(8,128)(2,1)S(1)} custom-call(s32[2048]{0:T(1024)S(1)} %copy-done.8, bf16[2048,512]{1,0:T(8,128)(2,1)S(1)} %bitcast.36, bf16[1024,512]{1,0:T(8,128)(2,1)} %collective-permute-done.15.refs_1_, bf16[768,512]{1,0:T(8,128)(2,1)S(1)} %collective-permute-done.16.refs_2_), custom_call_target="tpu_custom_call" | custom-call | flops 1000000000 | bytes 1 | tf_op jit(solution)/shard_map/grad_sum/pallas_call | solution.py:397
  40.3 2.1 %collective-permute-start.17 = (bf16[768,512]{1,0:T(8,128)(2,1)S(1)}, bf16[768,512]{1,0:T(8,128)(2,1)S(1)}, u32[]{:S(2)}, u32[]{:S(2)}) collective-permute-start(bf16[768,512]{1,0:T(8,128)(2,1)S(1)} %grad_sum.1.refs_0_), channel_id=1, source_target_pairs={{0,4},{4,0},{8,12},{12,8},{16,20},{20,16},{24,28},{28,24},{1,5},{5... | collective-permute-start | bytes 2359304 | tf_op jit(solution)/shard_map/ppermute | solution.py:71
  42.4 5.8 %collective-permute-done.6.refs_2_ = bf16[512,512]{1,0:T(8,128)(2,1)S(1)} collective-permute-done((bf16[512,512]{1,0:T(8,128)(2,1)S(1)}, bf16[512,512]{1,0:T(8,128)(2,1)S(1)}, u32[]{:S(2)}, u32[]{:S(2)}) %collective-permute-start.6) | collective-permute-done | bytes 524320 | tf_op jit(solution)/shard_map/ppermute | solution.py:71
  48.2 1.3 %across.4 = bf16[768,512]{1,0:T(8,128)(2,1)S(1)} custom-call(s32[2048]{0:T(1024)S(1)} %copy-done.8, f32[2048,512]{1,0:T(8,128)S(1)} %bitcast.15, bf16[1024,512]{1,0:T(8,128)(2,1)} %collective-permute-done.5.refs_1_, bf16[512,512]{1,0:T(8,128)(2,1)S(1)} %collective-permute-done.6.refs_2_), custom_call_target="tpu_custom_call" | custom-call | flops 1000000000 | bytes 1 | tf_op jit(solution)/shard_map/across/pallas_call | solution.py:397
  49.5 0.1 collective-permute-start.7
  49.6 9.8 %collective-permute-done.11.refs_2_ = bf16[512,512]{1,0:T(8,128)(2,1)S(1)} collective-permute-done((bf16[512,512]{1,0:T(8,128)(2,1)S(1)}, bf16[512,512]{1,0:T(8,128)(2,1)S(1)}, u32[]{:S(2)}, u32[]{:S(2)}) %collective-permute-start.11) | collective-permute-done | bytes 524320 | tf_op jit(solution)/shard_map/ppermute | solution.py:71
  59.4 0.7 across.5
  60.2 0.1 collective-permute-start.12
  60.3 1.3 %deliver.3 = bf16[512,512]{1,0:T(8,128)(2,1)S(1)} custom-call(s32[2048]{0:T(1024)S(1)} %copy-done.8, bf16[2048,512]{1,0:T(8,128)(2,1)S(1)} %bitcast.30, bf16[1024,512]{1,0:T(8,128)(2,1)} %collective-permute-done.refs_1_, bf16[512,512]{1,0:T(8,128)(2,1)S(1)} %collective-permute-done.1.refs_2_, bf16[768,512]{1,0:T(8,128)(2,1)S(1)} %collective-permute-done.2.refs_3_), custom_call_target="tpu_custom_call" | custom-call | flops 1000000000 | bytes 1 | tf_op jit(solution)/shard_map/deliver/pallas_call | solution.py:397
  61.6 2.2 %collective-permute-start.3 = (bf16[512,512]{1,0:T(8,128)(2,1)S(1)}, bf16[512,512]{1,0:T(8,128)(2,1)S(1)}, u32[]{:S(2)}, u32[]{:S(2)}) collective-permute-start(bf16[512,512]{1,0:T(8,128)(2,1)S(1)} %deliver.3), channel_id=1, source_target_pairs={{0,4},{4,0},{8,12},{12,8},{16,20},{20,16},{24,28},{28,24},{1,5},{5... | collective-permute-start | bytes 1572872 | tf_op jit(solution)/shard_map/ppermute | solution.py:71
  63.8 12.5 %collective-permute-done.17.refs_1_ = bf16[768,512]{1,0:T(8,128)(2,1)S(1)} collective-permute-done((bf16[768,512]{1,0:T(8,128)(2,1)S(1)}, bf16[768,512]{1,0:T(8,128)(2,1)S(1)}, u32[]{:S(2)}, u32[]{:S(2)}) %collective-permute-start.17) | collective-permute-done | bytes 786464 | tf_op jit(solution)/shard_map/ppermute | solution.py:71
  76.3 1.1 grad_mean.1.refs_0_
  77.4 0.1 collective-permute-start.18
  77.5 0.0 collective-permute-done.7.refs_3_
  77.5 1.3 %deliver.4 = bf16[512,512]{1,0:T(8,128)(2,1)S(1)} custom-call(s32[2048]{0:T(1024)S(1)} %copy-done.8, f32[2048,512]{1,0:T(8,128)S(1)} %bitcast.16, bf16[1024,512]{1,0:T(8,128)(2,1)} %collective-permute-done.5.refs_1_, bf16[512,512]{1,0:T(8,128)(2,1)S(1)} %collective-permute-done.6.refs_2_, bf16[768,512]{1,0:T(8,128)(2,1)S(1)} %collective-permute-done.7.refs_3_), custom_call_target="tpu_custom_call" | custom-call | flops 1000000000 | bytes 1 | tf_op jit(solution)/shard_map/deliver/pallas_call | solution.py:397
  78.9 2.1 %collective-permute-start.8 = (bf16[512,512]{1,0:T(8,128)(2,1)S(1)}, bf16[512,512]{1,0:T(8,128)(2,1)S(1)}, u32[]{:S(2)}, u32[]{:S(2)}) collective-permute-start(bf16[512,512]{1,0:T(8,128)(2,1)S(1)} %deliver.4), channel_id=1, source_target_pairs={{0,4},{4,0},{8,12},{12,8},{16,20},{20,16},{24,28},{28,24},{1,5},{5... | collective-permute-start | bytes 1572872 | tf_op jit(solution)/shard_map/ppermute | solution.py:71
  81.0 11.6 %collective-permute-done.12.refs_3_ = bf16[768,512]{1,0:T(8,128)(2,1)S(1)} collective-permute-done((bf16[768,512]{1,0:T(8,128)(2,1)S(1)}, bf16[768,512]{1,0:T(8,128)(2,1)S(1)}, u32[]{:S(2)}, u32[]{:S(2)}) %collective-permute-start.12) | collective-permute-done | bytes 786464 | tf_op jit(solution)/shard_map/ppermute | solution.py:71
  92.5 0.8 deliver.5
  93.3 1.6 %collective-permute-start.13 = (bf16[512,512]{1,0:T(8,128)(2,1)S(1)}, bf16[512,512]{1,0:T(8,128)(2,1)S(1)}, u32[]{:S(2)}, u32[]{:S(2)}) collective-permute-start(bf16[512,512]{1,0:T(8,128)(2,1)S(1)} %deliver.5), channel_id=1, source_target_pairs={{0,4},{4,0},{8,12},{12,8},{16,20},{20,16},{24,28},{28,24},{1,5},{5... | collective-permute-start | bytes 1572872 | tf_op jit(solution)/shard_map/ppermute | solution.py:71
  94.9 0.0 collective-permute-done.3.refs_4_
  94.9 1.5 %collect.3.refs_3_ = bf16[1024,512]{1,0:T(8,128)(2,1)S(1)} custom-call(s32[2048]{0:T(1024)S(1)} %copy-done.8, bf16[2048,512]{1,0:T(8,128)(2,1)S(1)} %bitcast.31, bf16[1024,512]{1,0:T(8,128)(2,1)} %collective-permute-done.refs_1_, bf16[512,512]{1,0:T(8,128)(2,1)S(1)} %collective-permute-done.1.refs_2_, bf16[768,512]{1,0:T(8,128)(2,1)S(1)} %collective-permute-done.2.refs_3_, ...), custom_call_target="tpu_custom_call" | custom-call | flops 1000000000 | bytes 1 | tf_op jit(solution)/shard_map/collect/pallas_call | solution.py:397
  96.4 0.1 collective-permute-start.4
  96.5 2.3 %collective-permute-done.8.refs_4_ = bf16[512,512]{1,0:T(8,128)(2,1)S(1)} collective-permute-done((bf16[512,512]{1,0:T(8,128)(2,1)S(1)}, bf16[512,512]{1,0:T(8,128)(2,1)S(1)}, u32[]{:S(2)}, u32[]{:S(2)}) %collective-permute-start.8) | collective-permute-done | bytes 524320 | tf_op jit(solution)/shard_map/ppermute | solution.py:71
  98.8 1.5 %collect.4.refs_4_ = bf16[1024,512]{1,0:T(8,128)(2,1)S(1)} custom-call(s32[2048]{0:T(1024)S(1)} %copy-done.8, f32[2048,512]{1,0:T(8,128)S(1)} %bitcast.17, bf16[1024,512]{1,0:T(8,128)(2,1)} %collective-permute-done.5.refs_1_, bf16[512,512]{1,0:T(8,128)(2,1)S(1)} %collective-permute-done.6.refs_2_, bf16[768,512]{1,0:T(8,128)(2,1)S(1)} %collective-permute-done.7.refs_3_, ...), custom_call_target="tpu_custom_call" | custom-call | flops 1000000000 | bytes 1 | tf_op jit(solution)/shard_map/collect/pallas_call | solution.py:397
  100.3 0.1 collective-permute-start.9
  100.4 8.4 %collective-permute-done.13.refs_4_ = bf16[512,512]{1,0:T(8,128)(2,1)S(1)} collective-permute-done((bf16[512,512]{1,0:T(8,128)(2,1)S(1)}, bf16[512,512]{1,0:T(8,128)(2,1)S(1)}, u32[]{:S(2)}, u32[]{:S(2)}) %collective-permute-start.13) | collective-permute-done | bytes 524320 | tf_op jit(solution)/shard_map/ppermute | solution.py:71
  108.7 1.0 collect.5.refs_5_
  109.7 0.1 collective-permute-start.14
  109.8 1.0 mean.1
  110.8 0.6 collective-permute-start.19
  111.3 4.0 %update.2 = (bf16[2,2,512,512]{3,2,1,0:T(8,128)(2,1)}, f32[2,2,512,512]{3,2,1,0:T(8,128)}, f32[2,2,512,512]{3,2,1,0:T(8,128)}) custom-call(s32[2048]{0:T(1024)S(1)} %copy-done.8, bf16[2048,512]{1,0:T(8,128)(2,1)S(1)} %bitcast.32, f32[2048,512]{1,0:T(8,128)S(1)} %bitcast.18, f32[2048,512]{1,0:T(8,128)S(1)} %bitcast.25, bf16[1024,512]{1,0:T(8,128)(2,1)S(1)} %collect.3.refs_3_, ...), custom_call_target="tpu_custom_call" | custom-call | flops 1 | bytes 1 | tf_op jit(solution)/shard_map/update/pallas_call | solution.py:510
  115.4 0.0 collective-permute-done.19.refs_6_
  115.4 4.0 %update.3 = (bf16[2,2,512,512]{3,2,1,0:T(8,128)(2,1)}, f32[2,2,512,512]{3,2,1,0:T(8,128)}, f32[2,2,512,512]{3,2,1,0:T(8,128)}) custom-call(s32[2048]{0:T(1024)S(1)} %copy-done.8, bf16[2048,512]{1,0:T(8,128)(2,1)S(1)} %bitcast.33, f32[2048,512]{1,0:T(8,128)S(1)} %bitcast.19, ...), custom_call_target="tpu_custom_call", output_to_operand_aliasing={{0}: (8, {}), {1}: (9, {}), {2}: (10, {})} | custom-call | flops 1 | bytes 1 | tf_op jit(solution)/shard_map/update/pallas_call | solution.py:510
  (20 shorter events, 0.0 us)
Async XLA Ops:
  0.6 7.1 %copy-start = (f32[1,1,2,1024,512]{4,3,2,1,0:T(8,128)S(1)}, f32[1,1,2,1024,512]{4,3,2,1,0:T(8,128)}, u32[]{:S(2)}) copy-start(f32[1,1,2,1024,512]{4,3,2,1,0:T(8,128)} %param.9) | copy-start | bytes 12582916
  0.7 9.1 %copy-start.9 = (s32[2]{0:T(128)}, s32[2]{0:T(128)S(1)}, u32[]{:S(2)}) copy-start(s32[2]{0:T(128)S(1)} %pad_add_fusion.place_ref) | copy-start | bytes 28
  0.7 1.7 %copy-start.6 = (bf16[1,1,2,1024,512]{4,3,2,1,0:T(8,128)(2,1)S(1)}, bf16[1,1,2,1024,512]{4,3,2,1,0:T(8,128)(2,1)}, u32[]{:S(2)}) copy-start(bf16[1,1,2,1024,512]{4,3,2,1,0:T(8,128)(2,1)} %param.11) | copy-start | bytes 6291460
  4.1 9.2 %collective-permute-start.15 = (bf16[1024,512]{1,0:T(8,128)(2,1)}, bf16[1024,512]{1,0:T(8,128)(2,1)}, u32[]{:S(2)}, u32[]{:S(2)}) collective-permute-start(bf16[1024,512]{1,0:T(8,128)(2,1)} %halve_gradients.1), channel_id=1, source_target_pairs={{0,8},{4,12},{8,0},{12,4},{16,24},{20,28},{24,16},{28,20},{1,9},{5... | collective-permute-start | bytes 3145736 | tf_op jit(solution)/shard_map/ppermute | solution.py:71
  4.5 1.6 %copy-start.4 = (bf16[1,1,2,1024,512]{4,3,2,1,0:T(8,128)(2,1)S(1)}, bf16[1,1,2,1024,512]{4,3,2,1,0:T(8,128)(2,1)}, u32[]{:S(2)}) copy-start(bf16[1,1,2,1024,512]{4,3,2,1,0:T(8,128)(2,1)} %param.8) | copy-start | bytes 6291460
  6.1 3.7 %copy-start.2 = (f32[1,1,2,1024,512]{4,3,2,1,0:T(8,128)S(1)}, f32[1,1,2,1024,512]{4,3,2,1,0:T(8,128)}, u32[]{:S(2)}) copy-start(f32[1,1,2,1024,512]{4,3,2,1,0:T(8,128)} %param.10) | copy-start | bytes 12582916
  7.7 12.9 %collective-permute-start = (bf16[1024,512]{1,0:T(8,128)(2,1)}, bf16[1024,512]{1,0:T(8,128)(2,1)}, u32[]{:S(2)}, u32[]{:S(2)}) collective-permute-start(bf16[1024,512]{1,0:T(8,128)(2,1)} %halve_state.3), channel_id=1, source_target_pairs={{0,8},{4,12},{8,0},{12,4},{16,24},{20,28},{24,16},{28,20},{1,9},{5... | collective-permute-start | bytes 3145736 | tf_op jit(solution)/shard_map/ppermute | solution.py:71
  9.4 14.2 %collective-permute-start.5 = (bf16[1024,512]{1,0:T(8,128)(2,1)}, bf16[1024,512]{1,0:T(8,128)(2,1)}, u32[]{:S(2)}, u32[]{:S(2)}) collective-permute-start(bf16[1024,512]{1,0:T(8,128)(2,1)} %halve_state.4), channel_id=1, source_target_pairs={{0,8},{4,12},{8,0},{12,4},{16,24},{20,28},{24,16},{28,20},{1,9},{5... | collective-permute-start | bytes 3145736 | tf_op jit(solution)/shard_map/ppermute | solution.py:71
  9.9 10.8 %copy-start.5 = (bf16[1,1,2,1024,512]{4,3,2,1,0:T(8,128)(2,1)S(1)}, bf16[1,1,2,1024,512]{4,3,2,1,0:T(8,128)(2,1)}, u32[]{:S(2)}) copy-start(bf16[1,1,2,1024,512]{4,3,2,1,0:T(8,128)(2,1)} %param.8) | copy-start | bytes 6291460
  11.5 14.0 %collective-permute-start.10 = (bf16[1024,512]{1,0:T(8,128)(2,1)}, bf16[1024,512]{1,0:T(8,128)(2,1)S(1)}, u32[]{:S(2)}, u32[]{:S(2)}) collective-permute-start(bf16[1024,512]{1,0:T(8,128)(2,1)} %halve_state.5), channel_id=1, source_target_pairs={{0,8},{4,12},{8,0},{12,4},{16,24},{20,28},{24,16},{28,20},{1,9},{5... | collective-permute-start | bytes 3145736 | tf_op jit(solution)/shard_map/ppermute | solution.py:71
  13.3 10.3 %copy-start.1 = (f32[1,1,2,1024,512]{4,3,2,1,0:T(8,128)S(1)}, f32[1,1,2,1024,512]{4,3,2,1,0:T(8,128)}, u32[]{:S(2)}) copy-start(f32[1,1,2,1024,512]{4,3,2,1,0:T(8,128)} %param.9) | copy-start | bytes 12582916
  13.3 1.7 %copy-start.7 = (bf16[1,1,2,1024,512]{4,3,2,1,0:T(8,128)(2,1)S(1)}, bf16[1,1,2,1024,512]{4,3,2,1,0:T(8,128)(2,1)}, u32[]{:S(2)}) copy-start(bf16[1,1,2,1024,512]{4,3,2,1,0:T(8,128)(2,1)} %param.11) | copy-start | bytes 6291460
  15.1 0.8 copy-start.8
  17.6 20.8 %collective-permute-start.16 = (bf16[768,512]{1,0:T(8,128)(2,1)S(1)}, bf16[768,512]{1,0:T(8,128)(2,1)S(1)}, u32[]{:S(2)}, u32[]{:S(2)}) collective-permute-start(bf16[768,512]{1,0:T(8,128)(2,1)S(1)} %grad_out.1), channel_id=1, source_target_pairs={{0,16},{4,20},{8,24},{12,28},{16,0},{20,4},{24,8},{28,12},{1,17},{... | collective-permute-start | bytes 2359304 | tf_op jit(solution)/shard_map/ppermute | solution.py:71
  20.6 4.9 %copy-start.3 = (f32[1,1,2,1024,512]{4,3,2,1,0:T(8,128)S(1)}, f32[1,1,2,1024,512]{4,3,2,1,0:T(8,128)}, u32[]{:S(2)}) copy-start(f32[1,1,2,1024,512]{4,3,2,1,0:T(8,128)} %param.10) | copy-start | bytes 12582916
  22.1 14.9 %collective-permute-start.1 = (bf16[512,512]{1,0:T(8,128)(2,1)S(1)}, bf16[512,512]{1,0:T(8,128)(2,1)S(1)}, u32[]{:S(2)}, u32[]{:S(2)}) collective-permute-start(bf16[512,512]{1,0:T(8,128)(2,1)S(1)} %spread.3), channel_id=1, source_target_pairs={{0,4},{4,0},{8,12},{12,8},{16,20},{20,16},{24,28},{28,24},{1,5},{5... | collective-permute-start | bytes 1572872 | tf_op jit(solution)/shard_map/ppermute | solution.py:71
  24.9 23.3 %collective-permute-start.6 = (bf16[512,512]{1,0:T(8,128)(2,1)S(1)}, bf16[512,512]{1,0:T(8,128)(2,1)S(1)}, u32[]{:S(2)}, u32[]{:S(2)}) collective-permute-start(bf16[512,512]{1,0:T(8,128)(2,1)S(1)} %spread.4), channel_id=1, source_target_pairs={{0,4},{4,0},{8,12},{12,8},{16,20},{20,16},{24,28},{28,24},{1,5},{5... | collective-permute-start | bytes 1572872 | tf_op jit(solution)/shard_map/ppermute | solution.py:71
  26.3 33.2 %collective-permute-start.11 = (bf16[512,512]{1,0:T(8,128)(2,1)S(1)}, bf16[512,512]{1,0:T(8,128)(2,1)S(1)}, u32[]{:S(2)}, u32[]{:S(2)}) collective-permute-start(bf16[512,512]{1,0:T(8,128)(2,1)S(1)} %spread.5), channel_id=1, source_target_pairs={{0,4},{4,0},{8,12},{12,8},{16,20},{20,16},{24,28},{28,24},{1,5},{5... | collective-permute-start | bytes 1572872 | tf_op jit(solution)/shard_map/ppermute | solution.py:71
  38.3 22.0 %collective-permute-start.2 = (bf16[768,512]{1,0:T(8,128)(2,1)S(1)}, bf16[768,512]{1,0:T(8,128)(2,1)S(1)}, u32[]{:S(2)}, u32[]{:S(2)}) collective-permute-start(bf16[768,512]{1,0:T(8,128)(2,1)S(1)} %across.3), channel_id=1, source_target_pairs={{0,16},{4,20},{8,24},{12,28},{16,0},{20,4},{24,8},{28,12},{1,17},{... | collective-permute-start | bytes 2359304 | tf_op jit(solution)/shard_map/ppermute | solution.py:71
  40.3 36.0 %collective-permute-start.17 = (bf16[768,512]{1,0:T(8,128)(2,1)S(1)}, bf16[768,512]{1,0:T(8,128)(2,1)S(1)}, u32[]{:S(2)}, u32[]{:S(2)}) collective-permute-start(bf16[768,512]{1,0:T(8,128)(2,1)S(1)} %grad_sum.1.refs_0_), channel_id=1, source_target_pairs={{0,4},{4,0},{8,12},{12,8},{16,20},{20,16},{24,28},{28,24},{1,5},{5... | collective-permute-start | bytes 2359304 | tf_op jit(solution)/shard_map/ppermute | solution.py:71
  49.5 28.0 %collective-permute-start.7 = (bf16[768,512]{1,0:T(8,128)(2,1)S(1)}, bf16[768,512]{1,0:T(8,128)(2,1)S(1)}, u32[]{:S(2)}, u32[]{:S(2)}) collective-permute-start(bf16[768,512]{1,0:T(8,128)(2,1)S(1)} %across.4), channel_id=1, source_target_pairs={{0,16},{4,20},{8,24},{12,28},{16,0},{20,4},{24,8},{28,12},{1,17},{... | collective-permute-start | bytes 2359304 | tf_op jit(solution)/shard_map/ppermute | solution.py:71
  60.2 32.3 %collective-permute-start.12 = (bf16[768,512]{1,0:T(8,128)(2,1)S(1)}, bf16[768,512]{1,0:T(8,128)(2,1)S(1)}, u32[]{:S(2)}, u32[]{:S(2)}) collective-permute-start(bf16[768,512]{1,0:T(8,128)(2,1)S(1)} %across.5), channel_id=1, source_target_pairs={{0,16},{4,20},{8,24},{12,28},{16,0},{20,4},{24,8},{28,12},{1,17},{... | collective-permute-start | bytes 2359304 | tf_op jit(solution)/shard_map/ppermute | solution.py:71
  61.6 33.2 %collective-permute-start.3 = (bf16[512,512]{1,0:T(8,128)(2,1)S(1)}, bf16[512,512]{1,0:T(8,128)(2,1)S(1)}, u32[]{:S(2)}, u32[]{:S(2)}) collective-permute-start(bf16[512,512]{1,0:T(8,128)(2,1)S(1)} %deliver.3), channel_id=1, source_target_pairs={{0,4},{4,0},{8,12},{12,8},{16,20},{20,16},{24,28},{28,24},{1,5},{5... | collective-permute-start | bytes 1572872 | tf_op jit(solution)/shard_map/ppermute | solution.py:71
  77.4 32.4 %collective-permute-start.18 = (bf16[768,512]{1,0:T(8,128)(2,1)S(1)}, bf16[768,512]{1,0:T(8,128)(2,1)S(1)}, u32[]{:S(2)}, u32[]{:S(2)}) collective-permute-start(bf16[768,512]{1,0:T(8,128)(2,1)S(1)} %grad_mean.1.refs_0_), channel_id=1, source_target_pairs={{0,16},{4,20},{8,24},{12,28},{16,0},{20,4},{24,8},{28,12},{1,17},{... | collective-permute-start | bytes 2359304 | tf_op jit(solution)/shard_map/ppermute | solution.py:71
  78.9 19.9 %collective-permute-start.8 = (bf16[512,512]{1,0:T(8,128)(2,1)S(1)}, bf16[512,512]{1,0:T(8,128)(2,1)S(1)}, u32[]{:S(2)}, u32[]{:S(2)}) collective-permute-start(bf16[512,512]{1,0:T(8,128)(2,1)S(1)} %deliver.4), channel_id=1, source_target_pairs={{0,4},{4,0},{8,12},{12,8},{16,20},{20,16},{24,28},{28,24},{1,5},{5... | collective-permute-start | bytes 1572872 | tf_op jit(solution)/shard_map/ppermute | solution.py:71
  93.3 15.4 %collective-permute-start.13 = (bf16[512,512]{1,0:T(8,128)(2,1)S(1)}, bf16[512,512]{1,0:T(8,128)(2,1)S(1)}, u32[]{:S(2)}, u32[]{:S(2)}) collective-permute-start(bf16[512,512]{1,0:T(8,128)(2,1)S(1)} %deliver.5), channel_id=1, source_target_pairs={{0,4},{4,0},{8,12},{12,8},{16,20},{20,16},{24,28},{28,24},{1,5},{5... | collective-permute-start | bytes 1572872 | tf_op jit(solution)/shard_map/ppermute | solution.py:71
  96.4 19.0 %collective-permute-start.4 = (bf16[1024,512]{1,0:T(8,128)(2,1)S(1)}, bf16[1024,512]{1,0:T(8,128)(2,1)S(1)}, u32[]{:S(2)}, u32[]{:S(2)}) collective-permute-start(bf16[1024,512]{1,0:T(8,128)(2,1)S(1)} %collect.3.refs_3_), channel_id=1, source_target_pairs={{0,8},{4,12},{8,0},{12,4},{16,24},{20,28},{24,16},{28,20},{1,9},{5... | collective-permute-start | bytes 3145736 | tf_op jit(solution)/shard_map/ppermute | solution.py:71
  100.3 15.1 %collective-permute-start.9 = (bf16[1024,512]{1,0:T(8,128)(2,1)S(1)}, bf16[1024,512]{1,0:T(8,128)(2,1)S(1)}, u32[]{:S(2)}, u32[]{:S(2)}) collective-permute-start(bf16[1024,512]{1,0:T(8,128)(2,1)S(1)} %collect.4.refs_4_), channel_id=1, source_target_pairs={{0,8},{4,12},{8,0},{12,4},{16,24},{20,28},{24,16},{28,20},{1,9},{5... | collective-permute-start | bytes 3145736 | tf_op jit(solution)/shard_map/ppermute | solution.py:71
  109.7 5.7 %collective-permute-start.14 = (bf16[1024,512]{1,0:T(8,128)(2,1)S(1)}, bf16[1024,512]{1,0:T(8,128)(2,1)S(1)}, u32[]{:S(2)}, u32[]{:S(2)}) collective-permute-start(bf16[1024,512]{1,0:T(8,128)(2,1)S(1)} %collect.5.refs_5_), channel_id=1, source_target_pairs={{0,8},{4,12},{8,0},{12,4},{16,24},{20,28},{24,16},{28,20},{1,9},{5... | collective-permute-start | bytes 3145736 | tf_op jit(solution)/shard_map/ppermute | solution.py:71
  110.8 4.6 %collective-permute-start.19 = (bf16[1024,512]{1,0:T(8,128)(2,1)S(1)}, bf16[1024,512]{1,0:T(8,128)(2,1)S(1)}, u32[]{:S(2)}, u32[]{:S(2)}) collective-permute-start(bf16[1024,512]{1,0:T(8,128)(2,1)S(1)} %get-tuple-element.11), channel_id=1, source_target_pairs={{0,8},{4,12},{8,0},{12,4},{16,24},{20,28},{24,16},{28,20},{1,9},{5... | collective-permute-start | bytes 3145736 | tf_op jit(solution)/shard_map/ppermute | solution.py:71

commit v7 on v6

--- a/solution.py
+++ b/solution.py
@@ -130,7 +130,7 @@
 
     def grad_unit(l, band):
         return [
-            (as_int(my_now[l] == section), (my_slot[l] * CORES + core) * z.groups + band),
+            (as_int(my_now[l] == section), my_slot[l] * z.groups + band),
             (as_int(sib_now[l] == section), sib_slot[l] * z.groups + band),
         ]
 
@@ -226,10 +226,13 @@
 
 
 def table_size(z):
-    sources = z.sections + z.groups + z.sections + 2
-    units = (z.sections + z.groups) * (4 * z.layers + 4 * z.slots)
-    units += z.sections * (z.channels + 2 * z.slots) + z.layers
-    return -(-(2 * units * sources + z.slots + 8) // 1024) * 1024
+    held = z.sections + 1
+    arrived = held + z.groups - 1
+    entries = z.layers * (2 * (z.groups - 1) + z.groups + 1 + z.sections + held)
+    entries += 2 * z.slots * z.groups**2 + 2 * (z.sections - 1) * z.channels
+    entries += z.slots * (z.sections - 1) * arrived
+    entries += z.slots * z.sections * (arrived + z.sections - 1)
+    return -(-(2 * entries + z.slots + 2) // 256) * 256
 
 
 def make_plan(z, place, old_section, new_section, lost_pipe, donor_offset):
@@ -397,35 +400,41 @@
     return order.then(call(table, *operands, *order.last))
 
 
-def sibling_half(z, order, place, array, name):
+def halves_of(z, order, place, array, parts, name):
     view = array.reshape(z.slots, CORES, z.half, z.cols)
-
     step = math.gcd(z.half, 64)
 
-    def kernel(place_ref, array_ref, *refs):
+    def kernel(place_ref, *refs):
         @pl.loop(0, z.half // step)
         def _(at):
             rows = pl.ds(pl.multiple_of(at * step, 16), step)
-            refs[-1][rows] = array_ref[0, 0, rows].astype(jnp.bfloat16)
-
-    def half_of(slot, place_ref):
-        return (slot, 1 - lax.rem(place_ref[0], CORES), 0, 0)
+            for array_ref, out_ref in zip(refs, refs[-len(parts) :]):
+                out_ref[rows] = array_ref[0, 0, rows].astype(jnp.bfloat16)
+
+    def half_of(part):
+        def index_map(slot, place_ref):
+            core = lax.rem(place_ref[0], CORES)
+            return (slot, 1 - core if part else core, 0, 0)
+
+        return index_map
 
     out = jax.ShapeDtypeStruct((z.slots * z.half, z.cols), jnp.bfloat16)
+    out_spec = pl.BlockSpec((z.half, z.cols), lambda slot, place_ref: (slot, 0))
     call = pl.pallas_call(
         kernel,
         grid_spec=pltpu.PrefetchScalarGridSpec(
             num_scalar_prefetch=1,
             grid=(z.slots,),
-            in_specs=[pl.BlockSpec((1, 1, z.half, z.cols), half_of)] + order.specs(),
-            out_specs=pl.BlockSpec((z.half, z.cols), lambda slot, place_ref: (slot, 0)),
+            in_specs=[pl.BlockSpec((1, 1, z.half, z.cols), half_of(part)) for part in parts]
+            + order.specs(),
+            out_specs=[out_spec] * len(parts),
         ),
-        out_shape=out,
+        out_shape=[out] * len(parts),
         compiler_params=PARAMS,
         cost_estimate=COST,
         name="halve_" + name,
     )
-    return order.then((call(place, view, *order.last),))[0]
+    return order.then(call(place, *[view] * len(parts), *order.last))
 
 
 def update(z, order, table, start, part, state, rebuilt, mean, outs):
@@ -522,13 +531,9 @@
 
     def enter(self, place):
         z = self.z
-        theirs = z.to_core(sibling_half(z, self.order, place, self.grads, "gradients"))
-        own = self.grads.reshape(z.slots * z.rows, z.cols)
-        theirs = self.order.arrived(theirs)
-        self.held = [
-            Rows(own, z.grad_band, z.slots * CORES * z.groups),
-            Rows(theirs, z.grad_band, z.slots * z.groups),
-        ]
+        theirs, own = halves_of(z, self.order, place, self.grads, (1, 0), "gradients")
+        theirs = self.order.arrived(z.to_core(theirs))
+        self.held = [Rows(half, z.grad_band, z.slots * z.groups) for half in (own, theirs)]
 
     def scatter(self):
         z = self.z
@@ -572,7 +577,8 @@
 
     def enter(self, place):
         z = self.z
-        theirs = z.to_core(sibling_half(z, self.order, place, self.array, "state"))
+        (theirs,) = halves_of(z, self.order, place, self.array, (1,), "state")
+        theirs = z.to_core(theirs)
         own = self.array.reshape(z.slots * z.rows, z.cols)
         theirs = self.order.arrived(theirs)
         held = z.slots * z.sections

time: 120 us -> 117 us (0.975)
  local copies, waits for them, and re-layouts: 5.92 us -> 3.98 us
  Pallas kernels: 36.1 us -> 34.8 us
    unnamed x20, local copies, waits for them, and re-layouts: 5.92 us -> 3.98 us
  transfers between devices with their start and end apart: 20 -> 20, of which waited for: 7 -> 7; matrix products, arithmetic and copies ran while one was open for 0% -> 0% of each run, Pallas kernels for 26% -> 25%
where the time goes in v7:
time: 117 us
  waiting for transfers between devices  60.6 us (52%)
  Pallas kernels  34.8 us (30%)
  starting transfers between devices  16.3 us (14%)
  local copies, waits for them, and re-layouts  3.98 us (3%)
    ppermute x20, waiting for transfers between devices, send(): return lax.ppermute(value, AXES, pairs)  60.6 us
    pallas_call x16, Pallas kernels, stage(): return order.then(call(table, *operands, *order.last))  18.9 us
    ppermute x20, starting transfers between devices, send(): return lax.ppermute(value, AXES, pairs)  16.3 us
    pallas_call x2, Pallas kernels, update(): return order.then(call(table, *operands, *order.last))  7.63 us
    pallas_call x4, Pallas kernels, halves_of(): return order.then(call(place, *[view] * len(parts), *order.last))  6.53 us
    unnamed x20, local copies, waits for them, and re-layouts  3.98 us
  transfers between devices with their start and end apart: 20, of which 7 were waited for; matrix products, arithmetic and copies ran while one was open for 0% of the time, Pallas kernels for 25%

profile of v7, /device:TPU:0, one launch (start us, length us, event | category | flops | bytes accessed | tf_op | source)
XLA Modules:
  0.0 116.7 jit_solution(6276728083781066722)
XLA Ops:
  0.6 0.0 copy-start
  0.7 0.1 pad_add_fusion.place_ref
  0.7 1.7 %copy-done.5 = bf16[1,1,2,1024,512]{4,3,2,1,0:T(8,128)(2,1)S(1)} copy-done((bf16[1,1,2,1024,512]{4,3,2,1,0:T(8,128)(2,1)S(1)}, bf16[1,1,2,1024,512]{4,3,2,1,0:T(8,128)(2,1)}, u32[]{:S(2)}) %copy-start.5) | copy-done | bytes 2097176
  2.5 1.7 %halve_gradients.1 = (bf16[1024,512]{1,0:T(8,128)(2,1)}, bf16[1024,512]{1,0:T(8,128)(2,1)S(1)}) custom-call(s32[2]{0:T(128)S(1)} %pad_add_fusion.place_ref, bf16[2,2,512,512]{3,2,1,0:T(8,128)(2,1)S(1)} %bitcast.33, bf16[2,2,512,512]{3,2,1,0:T(8,128)(2,1)S(1)} %bitcast.34), custom_call_target="tpu_custom_call" | custom-call | flops 1000000000 | bytes 1 | tf_op jit(solution)/shard_map/halve_gradients/pallas_call | solution.py:437
  4.2 0.5 collective-permute-start.15
  4.6 1.6 %halve_state.3 = bf16[1024,512]{1,0:T(8,128)(2,1)} custom-call(s32[2]{0:T(128)S(1)} %pad_add_fusion.place_ref, bf16[2,2,512,512]{3,2,1,0:T(8,128)(2,1)S(1)} %bitcast.26), custom_call_target="tpu_custom_call" | custom-call | flops 1000000000 | bytes 1 | tf_op jit(solution)/shard_map/halve_state/pallas_call | solution.py:437
  6.2 0.1 collective-permute-start
  6.3 1.6 %halve_state.4 = bf16[1024,512]{1,0:T(8,128)(2,1)} custom-call(s32[2]{0:T(128)S(1)} %pad_add_fusion.place_ref, f32[2,2,512,512]{3,2,1,0:T(8,128)S(1)} %bitcast.12), custom_call_target="tpu_custom_call" | custom-call | flops 1000000000 | bytes 1 | tf_op jit(solution)/shard_map/halve_state/pallas_call | solution.py:437
  7.9 0.5 collective-permute-start.5
  8.4 1.6 %halve_state.5 = bf16[1024,512]{1,0:T(8,128)(2,1)} custom-call(s32[2]{0:T(128)S(1)} %pad_add_fusion.place_ref, f32[2,2,512,512]{3,2,1,0:T(8,128)S(1)} %bitcast.19), custom_call_target="tpu_custom_call" | custom-call | flops 1000000000 | bytes 1 | tf_op jit(solution)/shard_map/halve_state/pallas_call | solution.py:437
  10.0 0.1 collective-permute-start.10
  10.0 1.7 %plan.1.table_ref = s32[256]{0:T(256)} custom-call(s32[2]{0:T(128)} %copy-done.7, s32[4,3]{1,0:T(4,128)} %old_ref.1, s32[3]{0:T(128)} %new_ref.1, s32[4]{0:T(128)} %lost_ref.1, s32[3]{0:T(128)} %offset_ref.1), custom_call_target="tpu_custom_call" | custom-call | tf_op jit(solution)/shard_map/plan/pallas_call | solution.py:263
  11.7 0.0 copy-start.1
  11.8 0.0 collective-permute-done.15.refs_1_
  11.8 0.8 copy-done.6
  12.6 1.4 %copy-done.9 = bf16[1024,512]{1,0:T(8,128)(2,1)S(1)} copy-done((bf16[1024,512]{1,0:T(8,128)(2,1)S(1)}, bf16[1024,512]{1,0:T(8,128)(2,1)}, u32[]{:S(2)}) %copy-start.9) | copy-done | bytes 1048600
  14.0 1.7 %grad_out.1 = bf16[768,512]{1,0:T(8,128)(2,1)S(1)} custom-call(s32[256]{0:T(256)S(1)} %copy-done.6, bf16[1024,512]{1,0:T(8,128)(2,1)S(1)} %copy-done.9, bf16[1024,512]{1,0:T(8,128)(2,1)} %collective-permute-done.15.refs_1_), custom_call_target="tpu_custom_call" | custom-call | flops 1000000000 | bytes 1 | tf_op jit(solution)/shard_map/grad_out/pallas_call | solution.py:400
  15.7 3.0 %collective-permute-start.16 = (bf16[768,512]{1,0:T(8,128)(2,1)S(1)}, bf16[768,512]{1,0:T(8,128)(2,1)S(1)}, u32[]{:S(2)}, u32[]{:S(2)}) collective-permute-start(bf16[768,512]{1,0:T(8,128)(2,1)S(1)} %grad_out.1), channel_id=1, source_target_pairs={{0,16},{4,20},{8,24},{12,28},{16,0},{20,4},{24,8},{28,12},{1,17},{... | collective-permute-start | bytes 2359304 | tf_op jit(solution)/shard_map/ppermute | solution.py:71
  18.7 0.0 collective-permute-done.refs_1_
  18.7 1.4 %spread.3 = bf16[512,512]{1,0:T(8,128)(2,1)S(1)} custom-call(s32[256]{0:T(256)S(1)} %copy-done.6, bf16[2048,512]{1,0:T(8,128)(2,1)S(1)} %bitcast.27, bf16[1024,512]{1,0:T(8,128)(2,1)} %collective-permute-done.refs_1_), custom_call_target="tpu_custom_call" | custom-call | flops 1000000000 | bytes 1 | tf_op jit(solution)/shard_map/spread/pallas_call | solution.py:400
  20.2 1.6 %collective-permute-start.1 = (bf16[512,512]{1,0:T(8,128)(2,1)S(1)}, bf16[512,512]{1,0:T(8,128)(2,1)S(1)}, u32[]{:S(2)}, u32[]{:S(2)}) collective-permute-start(bf16[512,512]{1,0:T(8,128)(2,1)S(1)} %spread.3), channel_id=1, source_target_pairs={{0,4},{4,0},{8,12},{12,8},{16,20},{20,16},{24,28},{28,24},{1,5},{5... | collective-permute-start | bytes 1572872 | tf_op jit(solution)/shard_map/ppermute | solution.py:71
  21.7 0.0 collective-permute-done.5.refs_1_
  21.7 1.3 %spread.4 = bf16[512,512]{1,0:T(8,128)(2,1)S(1)} custom-call(s32[256]{0:T(256)S(1)} %copy-done.6, f32[2048,512]{1,0:T(8,128)S(1)} %bitcast.13, bf16[1024,512]{1,0:T(8,128)(2,1)} %collective-permute-done.5.refs_1_), custom_call_target="tpu_custom_call" | custom-call | flops 1000000000 | bytes 1 | tf_op jit(solution)/shard_map/spread/pallas_call | solution.py:400
  23.0 0.6 collective-permute-start.6
  23.6 0.0 collective-permute-done.10.refs_1_
  23.6 0.6 spread.5
  24.3 1.6 %collective-permute-start.11 = (bf16[512,512]{1,0:T(8,128)(2,1)S(1)}, bf16[512,512]{1,0:T(8,128)(2,1)S(1)}, u32[]{:S(2)}, u32[]{:S(2)}) collective-permute-start(bf16[512,512]{1,0:T(8,128)(2,1)S(1)} %spread.5), channel_id=1, source_target_pairs={{0,4},{4,0},{8,12},{12,8},{16,20},{20,16},{24,28},{28,24},{1,5},{5... | collective-permute-start | bytes 1572872 | tf_op jit(solution)/shard_map/ppermute | solution.py:71
  25.8 9.2 %collective-permute-done.1.refs_2_ = bf16[512,512]{1,0:T(8,128)(2,1)S(1)} collective-permute-done((bf16[512,512]{1,0:T(8,128)(2,1)S(1)}, bf16[512,512]{1,0:T(8,128)(2,1)S(1)}, u32[]{:S(2)}, u32[]{:S(2)}) %collective-permute-start.1) | collective-permute-done | bytes 524320 | tf_op jit(solution)/shard_map/ppermute | solution.py:71
  35.1 1.4 %across.3 = bf16[768,512]{1,0:T(8,128)(2,1)S(1)} custom-call(s32[256]{0:T(256)S(1)} %copy-done.6, bf16[2048,512]{1,0:T(8,128)(2,1)S(1)} %bitcast.28, bf16[1024,512]{1,0:T(8,128)(2,1)} %collective-permute-done.refs_1_, bf16[512,512]{1,0:T(8,128)(2,1)S(1)} %collective-permute-done.1.refs_2_), custom_call_target="tpu_custom_call" | custom-call | flops 1000000000 | bytes 1 | tf_op jit(solution)/shard_map/across/pallas_call | solution.py:400
  36.4 0.1 collective-permute-start.2
  36.5 0.0 collective-permute-done.16.refs_2_
  36.6 1.9 %grad_sum.1.refs_0_ = bf16[768,512]{1,0:T(8,128)(2,1)S(1)} custom-call(s32[256]{0:T(256)S(1)} %copy-done.6, bf16[1024,512]{1,0:T(8,128)(2,1)S(1)} %copy-done.9, bf16[1024,512]{1,0:T(8,128)(2,1)} %collective-permute-done.15.refs_1_, bf16[768,512]{1,0:T(8,128)(2,1)S(1)} %collective-permute-done.16.refs_2_), custom_call_target="tpu_custom_call" | custom-call | flops 1000000000 | bytes 1 | tf_op jit(solution)/shard_map/grad_sum/pallas_call | solution.py:400
  38.4 1.9 %collective-permute-start.17 = (bf16[768,512]{1,0:T(8,128)(2,1)S(1)}, bf16[768,512]{1,0:T(8,128)(2,1)S(1)}, u32[]{:S(2)}, u32[]{:S(2)}) collective-permute-start(bf16[768,512]{1,0:T(8,128)(2,1)S(1)} %grad_sum.1.refs_0_), channel_id=1, source_target_pairs={{0,4},{4,0},{8,12},{12,8},{16,20},{20,16},{24,28},{28,24},{1,5},{5... | collective-permute-start | bytes 2359304 | tf_op jit(solution)/shard_map/ppermute | solution.py:71
  40.4 5.9 %collective-permute-done.6.refs_2_ = bf16[512,512]{1,0:T(8,128)(2,1)S(1)} collective-permute-done((bf16[512,512]{1,0:T(8,128)(2,1)S(1)}, bf16[512,512]{1,0:T(8,128)(2,1)S(1)}, u32[]{:S(2)}, u32[]{:S(2)}) %collective-permute-start.6) | collective-permute-done | bytes 524320 | tf_op jit(solution)/shard_map/ppermute | solution.py:71
  46.3 1.4 %across.4 = bf16[768,512]{1,0:T(8,128)(2,1)S(1)} custom-call(s32[256]{0:T(256)S(1)} %copy-done.6, f32[2048,512]{1,0:T(8,128)S(1)} %bitcast.14, bf16[1024,512]{1,0:T(8,128)(2,1)} %collective-permute-done.5.refs_1_, bf16[512,512]{1,0:T(8,128)(2,1)S(1)} %collective-permute-done.6.refs_2_), custom_call_target="tpu_custom_call" | custom-call | flops 1000000000 | bytes 1 | tf_op jit(solution)/shard_map/across/pallas_call | solution.py:400
  47.7 0.1 collective-permute-start.7
  47.8 9.8 %collective-permute-done.11.refs_2_ = bf16[512,512]{1,0:T(8,128)(2,1)S(1)} collective-permute-done((bf16[512,512]{1,0:T(8,128)(2,1)S(1)}, bf16[512,512]{1,0:T(8,128)(2,1)S(1)}, u32[]{:S(2)}, u32[]{:S(2)}) %collective-permute-start.11) | collective-permute-done | bytes 524320 | tf_op jit(solution)/shard_map/ppermute | solution.py:71
  57.5 0.7 across.5
  58.2 0.1 collective-permute-start.12
  58.3 0.0 collective-permute-done.2.refs_3_
  58.3 1.3 %deliver.3 = bf16[512,512]{1,0:T(8,128)(2,1)S(1)} custom-call(s32[256]{0:T(256)S(1)} %copy-done.6, bf16[2048,512]{1,0:T(8,128)(2,1)S(1)} %bitcast.29, bf16[1024,512]{1,0:T(8,128)(2,1)} %collective-permute-done.refs_1_, bf16[512,512]{1,0:T(8,128)(2,1)S(1)} %collective-permute-done.1.refs_2_, bf16[768,512]{1,0:T(8,128)(2,1)S(1)} %collective-permute-done.2.refs_3_), custom_call_target="tpu_custom_call" | custom-call | flops 1000000000 | bytes 1 | tf_op jit(solution)/shard_map/deliver/pallas_call | solution.py:400
  59.6 2.0 %collective-permute-start.3 = (bf16[512,512]{1,0:T(8,128)(2,1)S(1)}, bf16[512,512]{1,0:T(8,128)(2,1)S(1)}, u32[]{:S(2)}, u32[]{:S(2)}) collective-permute-start(bf16[512,512]{1,0:T(8,128)(2,1)S(1)} %deliver.3), channel_id=1, source_target_pairs={{0,4},{4,0},{8,12},{12,8},{16,20},{20,16},{24,28},{28,24},{1,5},{5... | collective-permute-start | bytes 1572872 | tf_op jit(solution)/shard_map/ppermute | solution.py:71
  61.6 12.8 %collective-permute-done.17.refs_1_ = bf16[768,512]{1,0:T(8,128)(2,1)S(1)} collective-permute-done((bf16[768,512]{1,0:T(8,128)(2,1)S(1)}, bf16[768,512]{1,0:T(8,128)(2,1)S(1)}, u32[]{:S(2)}, u32[]{:S(2)}) %collective-permute-start.17) | collective-permute-done | bytes 786464 | tf_op jit(solution)/shard_map/ppermute | solution.py:71
  74.4 1.0 grad_mean.1.refs_0_
  75.4 0.1 collective-permute-start.18
  75.5 1.3 %deliver.4 = bf16[512,512]{1,0:T(8,128)(2,1)S(1)} custom-call(s32[256]{0:T(256)S(1)} %copy-done.6, f32[2048,512]{1,0:T(8,128)S(1)} %bitcast.15, bf16[1024,512]{1,0:T(8,128)(2,1)} %collective-permute-done.5.refs_1_, bf16[512,512]{1,0:T(8,128)(2,1)S(1)} %collective-permute-done.6.refs_2_, bf16[768,512]{1,0:T(8,128)(2,1)S(1)} %collective-permute-done.7.refs_3_), custom_call_target="tpu_custom_call" | custom-call | flops 1000000000 | bytes 1 | tf_op jit(solution)/shard_map/deliver/pallas_call | solution.py:400
  76.8 2.0 %collective-permute-start.8 = (bf16[512,512]{1,0:T(8,128)(2,1)S(1)}, bf16[512,512]{1,0:T(8,128)(2,1)S(1)}, u32[]{:S(2)}, u32[]{:S(2)}) collective-permute-start(bf16[512,512]{1,0:T(8,128)(2,1)S(1)} %deliver.4), channel_id=1, source_target_pairs={{0,4},{4,0},{8,12},{12,8},{16,20},{20,16},{24,28},{28,24},{1,5},{5... | collective-permute-start | bytes 1572872 | tf_op jit(solution)/shard_map/ppermute | solution.py:71
  78.8 11.8 %collective-permute-done.12.refs_3_ = bf16[768,512]{1,0:T(8,128)(2,1)S(1)} collective-permute-done((bf16[768,512]{1,0:T(8,128)(2,1)S(1)}, bf16[768,512]{1,0:T(8,128)(2,1)S(1)}, u32[]{:S(2)}, u32[]{:S(2)}) %collective-permute-start.12) | collective-permute-done | bytes 786464 | tf_op jit(solution)/shard_map/ppermute | solution.py:71
  90.7 0.6 deliver.5
  91.3 1.6 %collective-permute-start.13 = (bf16[512,512]{1,0:T(8,128)(2,1)S(1)}, bf16[512,512]{1,0:T(8,128)(2,1)S(1)}, u32[]{:S(2)}, u32[]{:S(2)}) collective-permute-start(bf16[512,512]{1,0:T(8,128)(2,1)S(1)} %deliver.5), channel_id=1, source_target_pairs={{0,4},{4,0},{8,12},{12,8},{16,20},{20,16},{24,28},{28,24},{1,5},{5... | collective-permute-start | bytes 1572872 | tf_op jit(solution)/shard_map/ppermute | solution.py:71
  92.9 1.4 %collect.3.refs_3_ = bf16[1024,512]{1,0:T(8,128)(2,1)S(1)} custom-call(s32[256]{0:T(256)S(1)} %copy-done.6, bf16[2048,512]{1,0:T(8,128)(2,1)S(1)} %bitcast.30, bf16[1024,512]{1,0:T(8,128)(2,1)} %collective-permute-done.refs_1_, bf16[512,512]{1,0:T(8,128)(2,1)S(1)} %collective-permute-done.1.refs_2_, bf16[768,512]{1,0:T(8,128)(2,1)S(1)} %collective-permute-done.2.refs_3_, ...), custom_call_target="tpu_custom_call" | custom-call | flops 1000000000 | bytes 1 | tf_op jit(solution)/shard_map/collect/pallas_call | solution.py:400
  94.3 0.1 collective-permute-start.4
  94.4 2.5 %collective-permute-done.8.refs_4_ = bf16[512,512]{1,0:T(8,128)(2,1)S(1)} collective-permute-done((bf16[512,512]{1,0:T(8,128)(2,1)S(1)}, bf16[512,512]{1,0:T(8,128)(2,1)S(1)}, u32[]{:S(2)}, u32[]{:S(2)}) %collective-permute-start.8) | collective-permute-done | bytes 524320 | tf_op jit(solution)/shard_map/ppermute | solution.py:71
  96.9 1.4 %collect.4.refs_4_ = bf16[1024,512]{1,0:T(8,128)(2,1)S(1)} custom-call(s32[256]{0:T(256)S(1)} %copy-done.6, f32[2048,512]{1,0:T(8,128)S(1)} %bitcast.16, bf16[1024,512]{1,0:T(8,128)(2,1)} %collective-permute-done.5.refs_1_, bf16[512,512]{1,0:T(8,128)(2,1)S(1)} %collective-permute-done.6.refs_2_, bf16[768,512]{1,0:T(8,128)(2,1)S(1)} %collective-permute-done.7.refs_3_, ...), custom_call_target="tpu_custom_call" | custom-call | flops 1000000000 | bytes 1 | tf_op jit(solution)/shard_map/collect/pallas_call | solution.py:400
  98.3 0.1 collective-permute-start.9
  98.3 8.5 %collective-permute-done.13.refs_4_ = bf16[512,512]{1,0:T(8,128)(2,1)S(1)} collective-permute-done((bf16[512,512]{1,0:T(8,128)(2,1)S(1)}, bf16[512,512]{1,0:T(8,128)(2,1)S(1)}, u32[]{:S(2)}, u32[]{:S(2)}) %collective-permute-start.13) | collective-permute-done | bytes 524320 | tf_op jit(solution)/shard_map/ppermute | solution.py:71
  106.8 0.7 collect.5.refs_5_
  107.6 0.1 collective-permute-start.14
  107.6 0.0 collective-permute-done.18.refs_1_
  107.6 0.8 mean.1
  108.5 0.6 collective-permute-start.19
  109.0 3.8 %update.2 = (bf16[2,2,512,512]{3,2,1,0:T(8,128)(2,1)}, f32[2,2,512,512]{3,2,1,0:T(8,128)}, f32[2,2,512,512]{3,2,1,0:T(8,128)}) custom-call(s32[256]{0:T(256)S(1)} %copy-done.6, bf16[2048,512]{1,0:T(8,128)(2,1)S(1)} %bitcast.31, f32[2048,512]{1,0:T(8,128)S(1)} %bitcast.17, f32[2048,512]{1,0:T(8,128)S(1)} %bitcast.24, bf16[1024,512]{1,0:T(8,128)(2,1)S(1)} %collect.3.refs_3_, ...), custom_call_target="tpu_custom_call" | custom-call | flops 1 | bytes 1 | tf_op jit(solution)/shard_map/update/pallas_call | solution.py:519
  112.8 0.0 collective-permute-done.14.refs_5_
  112.8 3.8 %update.3 = (bf16[2,2,512,512]{3,2,1,0:T(8,128)(2,1)}, f32[2,2,512,512]{3,2,1,0:T(8,128)}, f32[2,2,512,512]{3,2,1,0:T(8,128)}) custom-call(s32[256]{0:T(256)S(1)} %copy-done.6, bf16[2048,512]{1,0:T(8,128)(2,1)S(1)} %bitcast.32, f32[2048,512]{1,0:T(8,128)S(1)} %bitcast.18, ...), custom_call_target="tpu_custom_call", output_to_operand_aliasing={{0}: (8, {}), {1}: (9, {}), {2}: (10, {})} | custom-call | flops 1 | bytes 1 | tf_op jit(solution)/shard_map/update/pallas_call | solution.py:519
  (20 shorter events, 0.0 us)
Async XLA Ops:
  0.6 4.0 %copy-start.4 = (bf16[1,1,2,1024,512]{4,3,2,1,0:T(8,128)(2,1)S(1)}, bf16[1,1,2,1024,512]{4,3,2,1,0:T(8,128)(2,1)}, u32[]{:S(2)}) copy-start(bf16[1,1,2,1024,512]{4,3,2,1,0:T(8,128)(2,1)} %param.8) | copy-start | bytes 6291460
  0.6 5.6 %copy-start = (f32[1,1,2,1024,512]{4,3,2,1,0:T(8,128)S(1)}, f32[1,1,2,1024,512]{4,3,2,1,0:T(8,128)}, u32[]{:S(2)}) copy-start(f32[1,1,2,1024,512]{4,3,2,1,0:T(8,128)} %param.9) | copy-start | bytes 12582916
  0.7 7.6 %copy-start.7 = (s32[2]{0:T(128)}, s32[2]{0:T(128)S(1)}, u32[]{:S(2)}) copy-start(s32[2]{0:T(128)S(1)} %pad_add_fusion.place_ref) | copy-start | bytes 28
  0.7 1.7 %copy-start.5 = (bf16[1,1,2,1024,512]{4,3,2,1,0:T(8,128)(2,1)S(1)}, bf16[1,1,2,1024,512]{4,3,2,1,0:T(8,128)(2,1)}, u32[]{:S(2)}) copy-start(bf16[1,1,2,1024,512]{4,3,2,1,0:T(8,128)(2,1)} %param.11) | copy-start | bytes 6291460
  4.2 3.7 %copy-start.8 = (bf16[1024,512]{1,0:T(8,128)(2,1)}, bf16[1024,512]{1,0:T(8,128)(2,1)S(1)}, u32[]{:S(2)}) copy-start(bf16[1024,512]{1,0:T(8,128)(2,1)S(1)} %get-tuple-element.13.refs_0_) | copy-start | bytes 3145732
  4.2 7.6 %collective-permute-start.15 = (bf16[1024,512]{1,0:T(8,128)(2,1)}, bf16[1024,512]{1,0:T(8,128)(2,1)}, u32[]{:S(2)}, u32[]{:S(2)}) collective-permute-start(bf16[1024,512]{1,0:T(8,128)(2,1)} %get-tuple-element.14), channel_id=1, source_target_pairs={{0,8},{4,12},{8,0},{12,4},{16,24},{20,28},{24,16},{28,20},{1,9},{5... | collective-permute-start | bytes 3145736 | tf_op jit(solution)/shard_map/ppermute | solution.py:71
  4.6 3.7 %copy-start.2 = (f32[1,1,2,1024,512]{4,3,2,1,0:T(8,128)S(1)}, f32[1,1,2,1024,512]{4,3,2,1,0:T(8,128)}, u32[]{:S(2)}) copy-start(f32[1,1,2,1024,512]{4,3,2,1,0:T(8,128)} %param.10) | copy-start | bytes 12582916
  6.2 12.5 %collective-permute-start = (bf16[1024,512]{1,0:T(8,128)(2,1)}, bf16[1024,512]{1,0:T(8,128)(2,1)}, u32[]{:S(2)}, u32[]{:S(2)}) collective-permute-start(bf16[1024,512]{1,0:T(8,128)(2,1)} %halve_state.3), channel_id=1, source_target_pairs={{0,8},{4,12},{8,0},{12,4},{16,24},{20,28},{24,16},{28,20},{1,9},{5... | collective-permute-start | bytes 3145736 | tf_op jit(solution)/shard_map/ppermute | solution.py:71
  7.9 13.8 %collective-permute-start.5 = (bf16[1024,512]{1,0:T(8,128)(2,1)}, bf16[1024,512]{1,0:T(8,128)(2,1)}, u32[]{:S(2)}, u32[]{:S(2)}) collective-permute-start(bf16[1024,512]{1,0:T(8,128)(2,1)} %halve_state.4), channel_id=1, source_target_pairs={{0,8},{4,12},{8,0},{12,4},{16,24},{20,28},{24,16},{28,20},{1,9},{5... | collective-permute-start | bytes 3145736 | tf_op jit(solution)/shard_map/ppermute | solution.py:71
  10.0 13.6 %collective-permute-start.10 = (bf16[1024,512]{1,0:T(8,128)(2,1)}, bf16[1024,512]{1,0:T(8,128)(2,1)S(1)}, u32[]{:S(2)}, u32[]{:S(2)}) collective-permute-start(bf16[1024,512]{1,0:T(8,128)(2,1)} %halve_state.5), channel_id=1, source_target_pairs={{0,8},{4,12},{8,0},{12,4},{16,24},{20,28},{24,16},{28,20},{1,9},{5... | collective-permute-start | bytes 3145736 | tf_op jit(solution)/shard_map/ppermute | solution.py:71
  11.7 10.0 %copy-start.1 = (f32[1,1,2,1024,512]{4,3,2,1,0:T(8,128)S(1)}, f32[1,1,2,1024,512]{4,3,2,1,0:T(8,128)}, u32[]{:S(2)}) copy-start(f32[1,1,2,1024,512]{4,3,2,1,0:T(8,128)} %param.9) | copy-start | bytes 12582916
  11.8 0.8 copy-start.6
  12.6 1.4 %copy-start.9 = (bf16[1024,512]{1,0:T(8,128)(2,1)S(1)}, bf16[1024,512]{1,0:T(8,128)(2,1)}, u32[]{:S(2)}) copy-start(bf16[1024,512]{1,0:T(8,128)(2,1)} %copy-done.8) | copy-start | bytes 3145732
  15.7 20.9 %collective-permute-start.16 = (bf16[768,512]{1,0:T(8,128)(2,1)S(1)}, bf16[768,512]{1,0:T(8,128)(2,1)S(1)}, u32[]{:S(2)}, u32[]{:S(2)}) collective-permute-start(bf16[768,512]{1,0:T(8,128)(2,1)S(1)} %grad_out.1), channel_id=1, source_target_pairs={{0,16},{4,20},{8,24},{12,28},{16,0},{20,4},{24,8},{28,12},{1,17},{... | collective-permute-start | bytes 2359304 | tf_op jit(solution)/shard_map/ppermute | solution.py:71
  18.7 4.9 %copy-start.3 = (f32[1,1,2,1024,512]{4,3,2,1,0:T(8,128)S(1)}, f32[1,1,2,1024,512]{4,3,2,1,0:T(8,128)}, u32[]{:S(2)}) copy-start(f32[1,1,2,1024,512]{4,3,2,1,0:T(8,128)} %param.10) | copy-start | bytes 12582916
  20.2 14.9 %collective-permute-start.1 = (bf16[512,512]{1,0:T(8,128)(2,1)S(1)}, bf16[512,512]{1,0:T(8,128)(2,1)S(1)}, u32[]{:S(2)}, u32[]{:S(2)}) collective-permute-start(bf16[512,512]{1,0:T(8,128)(2,1)S(1)} %spread.3), channel_id=1, source_target_pairs={{0,4},{4,0},{8,12},{12,8},{16,20},{20,16},{24,28},{28,24},{1,5},{5... | collective-permute-start | bytes 1572872 | tf_op jit(solution)/shard_map/ppermute | solution.py:71
  23.0 23.2 %collective-permute-start.6 = (bf16[512,512]{1,0:T(8,128)(2,1)S(1)}, bf16[512,512]{1,0:T(8,128)(2,1)S(1)}, u32[]{:S(2)}, u32[]{:S(2)}) collective-permute-start(bf16[512,512]{1,0:T(8,128)(2,1)S(1)} %spread.4), channel_id=1, source_target_pairs={{0,4},{4,0},{8,12},{12,8},{16,20},{20,16},{24,28},{28,24},{1,5},{5... | collective-permute-start | bytes 1572872 | tf_op jit(solution)/shard_map/ppermute | solution.py:71
  24.3 33.3 %collective-permute-start.11 = (bf16[512,512]{1,0:T(8,128)(2,1)S(1)}, bf16[512,512]{1,0:T(8,128)(2,1)S(1)}, u32[]{:S(2)}, u32[]{:S(2)}) collective-permute-start(bf16[512,512]{1,0:T(8,128)(2,1)S(1)} %spread.5), channel_id=1, source_target_pairs={{0,4},{4,0},{8,12},{12,8},{16,20},{20,16},{24,28},{28,24},{1,5},{5... | collective-permute-start | bytes 1572872 | tf_op jit(solution)/shard_map/ppermute | solution.py:71
  36.4 21.9 %collective-permute-start.2 = (bf16[768,512]{1,0:T(8,128)(2,1)S(1)}, bf16[768,512]{1,0:T(8,128)(2,1)S(1)}, u32[]{:S(2)}, u32[]{:S(2)}) collective-permute-start(bf16[768,512]{1,0:T(8,128)(2,1)S(1)} %across.3), channel_id=1, source_target_pairs={{0,16},{4,20},{8,24},{12,28},{16,0},{20,4},{24,8},{28,12},{1,17},{... | collective-permute-start | bytes 2359304 | tf_op jit(solution)/shard_map/ppermute | solution.py:71
  38.4 36.0 %collective-permute-start.17 = (bf16[768,512]{1,0:T(8,128)(2,1)S(1)}, bf16[768,512]{1,0:T(8,128)(2,1)S(1)}, u32[]{:S(2)}, u32[]{:S(2)}) collective-permute-start(bf16[768,512]{1,0:T(8,128)(2,1)S(1)} %grad_sum.1.refs_0_), channel_id=1, source_target_pairs={{0,4},{4,0},{8,12},{12,8},{16,20},{20,16},{24,28},{28,24},{1,5},{5... | collective-permute-start | bytes 2359304 | tf_op jit(solution)/shard_map/ppermute | solution.py:71
  47.7 27.8 %collective-permute-start.7 = (bf16[768,512]{1,0:T(8,128)(2,1)S(1)}, bf16[768,512]{1,0:T(8,128)(2,1)S(1)}, u32[]{:S(2)}, u32[]{:S(2)}) collective-permute-start(bf16[768,512]{1,0:T(8,128)(2,1)S(1)} %across.4), channel_id=1, source_target_pairs={{0,16},{4,20},{8,24},{12,28},{16,0},{20,4},{24,8},{28,12},{1,17},{... | collective-permute-start | bytes 2359304 | tf_op jit(solution)/shard_map/ppermute | solution.py:71
  58.2 32.5 %collective-permute-start.12 = (bf16[768,512]{1,0:T(8,128)(2,1)S(1)}, bf16[768,512]{1,0:T(8,128)(2,1)S(1)}, u32[]{:S(2)}, u32[]{:S(2)}) collective-permute-start(bf16[768,512]{1,0:T(8,128)(2,1)S(1)} %across.5), channel_id=1, source_target_pairs={{0,16},{4,20},{8,24},{12,28},{16,0},{20,4},{24,8},{28,12},{1,17},{... | collective-permute-start | bytes 2359304 | tf_op jit(solution)/shard_map/ppermute | solution.py:71
  59.6 33.2 %collective-permute-start.3 = (bf16[512,512]{1,0:T(8,128)(2,1)S(1)}, bf16[512,512]{1,0:T(8,128)(2,1)S(1)}, u32[]{:S(2)}, u32[]{:S(2)}) collective-permute-start(bf16[512,512]{1,0:T(8,128)(2,1)S(1)} %deliver.3), channel_id=1, source_target_pairs={{0,4},{4,0},{8,12},{12,8},{16,20},{20,16},{24,28},{28,24},{1,5},{5... | collective-permute-start | bytes 1572872 | tf_op jit(solution)/shard_map/ppermute | solution.py:71
  75.4 32.2 %collective-permute-start.18 = (bf16[768,512]{1,0:T(8,128)(2,1)S(1)}, bf16[768,512]{1,0:T(8,128)(2,1)S(1)}, u32[]{:S(2)}, u32[]{:S(2)}) collective-permute-start(bf16[768,512]{1,0:T(8,128)(2,1)S(1)} %grad_mean.1.refs_0_), channel_id=1, source_target_pairs={{0,16},{4,20},{8,24},{12,28},{16,0},{20,4},{24,8},{28,12},{1,17},{... | collective-permute-start | bytes 2359304 | tf_op jit(solution)/shard_map/ppermute | solution.py:71
  76.8 20.1 %collective-permute-start.8 = (bf16[512,512]{1,0:T(8,128)(2,1)S(1)}, bf16[512,512]{1,0:T(8,128)(2,1)S(1)}, u32[]{:S(2)}, u32[]{:S(2)}) collective-permute-start(bf16[512,512]{1,0:T(8,128)(2,1)S(1)} %deliver.4), channel_id=1, source_target_pairs={{0,4},{4,0},{8,12},{12,8},{16,20},{20,16},{24,28},{28,24},{1,5},{5... | collective-permute-start | bytes 1572872 | tf_op jit(solution)/shard_map/ppermute | solution.py:71
  91.3 15.5 %collective-permute-start.13 = (bf16[512,512]{1,0:T(8,128)(2,1)S(1)}, bf16[512,512]{1,0:T(8,128)(2,1)S(1)}, u32[]{:S(2)}, u32[]{:S(2)}) collective-permute-start(bf16[512,512]{1,0:T(8,128)(2,1)S(1)} %deliver.5), channel_id=1, source_target_pairs={{0,4},{4,0},{8,12},{12,8},{16,20},{20,16},{24,28},{28,24},{1,5},{5... | collective-permute-start | bytes 1572872 | tf_op jit(solution)/shard_map/ppermute | solution.py:71
  94.3 18.5 %collective-permute-start.4 = (bf16[1024,512]{1,0:T(8,128)(2,1)S(1)}, bf16[1024,512]{1,0:T(8,128)(2,1)S(1)}, u32[]{:S(2)}, u32[]{:S(2)}) collective-permute-start(bf16[1024,512]{1,0:T(8,128)(2,1)S(1)} %collect.3.refs_3_), channel_id=1, source_target_pairs={{0,8},{4,12},{8,0},{12,4},{16,24},{20,28},{24,16},{28,20},{1,9},{5... | collective-permute-start | bytes 3145736 | tf_op jit(solution)/shard_map/ppermute | solution.py:71
  98.3 14.6 %collective-permute-start.9 = (bf16[1024,512]{1,0:T(8,128)(2,1)S(1)}, bf16[1024,512]{1,0:T(8,128)(2,1)S(1)}, u32[]{:S(2)}, u32[]{:S(2)}) collective-permute-start(bf16[1024,512]{1,0:T(8,128)(2,1)S(1)} %collect.4.refs_4_), channel_id=1, source_target_pairs={{0,8},{4,12},{8,0},{12,4},{16,24},{20,28},{24,16},{28,20},{1,9},{5... | collective-permute-start | bytes 3145736 | tf_op jit(solution)/shard_map/ppermute | solution.py:71
  107.6 5.3 %collective-permute-start.14 = (bf16[1024,512]{1,0:T(8,128)(2,1)S(1)}, bf16[1024,512]{1,0:T(8,128)(2,1)S(1)}, u32[]{:S(2)}, u32[]{:S(2)}) collective-permute-start(bf16[1024,512]{1,0:T(8,128)(2,1)S(1)} %collect.5.refs_5_), channel_id=1, source_target_pairs={{0,8},{4,12},{8,0},{12,4},{16,24},{20,28},{24,16},{28,20},{1,9},{5... | collective-permute-start | bytes 3145736 | tf_op jit(solution)/shard_map/ppermute | solution.py:71
  108.5 4.4 %collective-permute-start.19 = (bf16[1024,512]{1,0:T(8,128)(2,1)S(1)}, bf16[1024,512]{1,0:T(8,128)(2,1)S(1)}, u32[]{:S(2)}, u32[]{:S(2)}) collective-permute-start(bf16[1024,512]{1,0:T(8,128)(2,1)S(1)} %get-tuple-element.15), channel_id=1, source_target_pairs={{0,8},{4,12},{8,0},{12,4},{16,24},{20,28},{24,16},{28,20},{1,9},{5... | collective-permute-start | bytes 3145736 | tf_op jit(solution)/shard_map/ppermute | solution.py:71
